TPU v7x, 32 devices: a whole 2x2x4 slice. The times are simulated.
32 devices in a mesh: ctx: 16 (over z, y, x), wshard: 2 (over core).
Axes of the slice: x: 2, y: 2, z: 4, core: 2. Of those that a mesh axis runs over, the one named last changes fastest.
Arguments:
- tokens: bfloat16 [2, 2048, 1536], P('wshard', 'ctx'), may hold values from -6 to 6
- cotangent: bfloat16 [2, 2048, 1536], P('wshard', 'ctx'), may hold values from -6 to 6
- doc_lengths: int32 [2, 4], P('wshard'), may hold values from 1 to 1024, 2048 in all within a row
- norm_attn: bfloat16 [1536], P(('ctx', 'wshard')), may hold values from 0.5 to 1.5
- w_qkv: bfloat16 [1536, 2048], P(('ctx', 'wshard')), may hold values from -0.15625 to 0.15625
- b_qkv: bfloat16 [2048], P(('ctx', 'wshard')), may hold values from -1.1953125 to 1.1953125
- w_out: bfloat16 [1536, 1536], P(None, ('ctx', 'wshard')), may hold values from -0.625 to 0.625
- norm_mlp: bfloat16 [1536], P(('ctx', 'wshard')), may hold values from 0.5 to 1.5
- w_gate: bfloat16 [1536, 8960], P(('ctx', 'wshard')), may hold values from -0.15625 to 0.15625
- w_up: bfloat16 [1536, 8960], P(('ctx', 'wshard')), may hold values from -0.15625 to 0.15625
- w_down: bfloat16 [8960, 1536], P(('ctx', 'wshard')), may hold values from -0.0625 to 0.0625
Outputs:
- output: bfloat16 [2, 2048, 1536], P('wshard', 'ctx')
- grad_tokens: float32 [2, 2048, 1536], P('wshard', 'ctx')
- grad_norm_attn: float32 [1536], P(('ctx', 'wshard'))
- grad_w_qkv: float32 [1536, 2048], P(('ctx', 'wshard'))
- grad_b_qk: float32 [1792], P(('ctx', 'wshard'))
- grad_b_v: float32 [256], P(('ctx', 'wshard'))
- grad_w_out: float32 [1536, 1536], P(None, ('ctx', 'wshard'))
- grad_norm_mlp: float32 [1536], P(('ctx', 'wshard'))
- grad_w_gate: float32 [1536, 8960], P(('ctx', 'wshard'))
- grad_w_up: float32 [1536, 8960], P(('ctx', 'wshard'))
- grad_w_down: float32 [8960, 1536], P(('ctx', 'wshard'))
Inputs may be any that keep to these rules, and one draw needn't show every extreme that they name: Each row of doc_lengths lists the lengths of its stream's 4 documents in stream order; a row sums to 2048 and its largest entry is 1024.
All inputs are finite; a program needn't handle non-finite values.
Results may differ from a plain program's by a relative error of at most 0.022.
Values may be sent and summed in bfloat16 or wider, within the bound.
No kernel may reach another device: no remote copies, remote signals or barrier semaphores. Data moves between devices by JAX's collectives and lax.ppermute only.
A program may use at most 640 MiB of HBM per device.

v0:
```python
import math

import jax
import jax.numpy as jnp
from jax import lax
from jax.sharding import PartitionSpec as P

H = 12
KVH = 2
HD = 128
KEY_BLOCK = 512


EPSILON = 1e-06
ROPE_BASE = 1000000.0


def split_up(array, dim, devices):
    shape = array.shape
    tiles = array.reshape(*shape[:dim], devices, shape[dim] // devices, *shape[dim + 1 :])
    return jnp.moveaxis(tiles, dim, 0)


def sum_at_owner(array, axis, dim):
    tiles = split_up(array, dim, lax.axis_size(axis))
    arrived = lax.all_to_all(tiles, axis, split_axis=0, concat_axis=0, tiled=True)
    return arrived.astype(jnp.float32).sum(axis=0)


def in_one_piece(arrays, axis, dim, along):
    both = jnp.concatenate(arrays, axis=along)
    whole, at, finished = (sum_at_owner(both, axis, dim), 0, [])
    for a in arrays:
        finished.append(lax.slice_in_dim(whole, at, at + a.shape[along], axis=along))
        at += a.shape[along]
    return tuple(finished)


def stream_places(row_count, tok_dev, ctx_size, first_row):
    row_ids = first_row + jnp.arange(row_count, dtype=jnp.int32)
    half_rows = tok_dev // 2
    device = row_ids // tok_dev
    inner_row = row_ids % tok_dev
    blocks = jnp.where(inner_row < half_rows, device, 2 * ctx_size - 1 - device)
    return blocks * half_rows + inner_row % half_rows


def documents_positions(lengths, places):
    ends_at = jnp.cumsum(lengths)
    passed = ends_at[None, :] <= places[:, None]
    documents = jnp.sum(passed.astype(jnp.int32), axis=1)
    starts = jnp.sum(jnp.where(passed, lengths[None, :], 0), axis=1)
    return (documents, places - starts)


def rope_tables(positions):
    half_width = HD // 2
    frequency = ROPE_BASE ** (-jnp.arange(half_width, dtype=jnp.float32) * 2.0 / HD)
    angles = positions.astype(jnp.float32)[:, None] * frequency[None, :]
    cos_table = jnp.concatenate([jnp.cos(angles), jnp.cos(angles)], axis=-1)[:, None, :]
    sin_table = jnp.concatenate([jnp.sin(angles), jnp.sin(angles)], axis=-1)[:, None, :]
    return (cos_table, sin_table)


def rotate(values, cos_table, sin_table):
    half_width = values.shape[-1] // 2
    turned = jnp.concatenate([-values[..., half_width:], values[..., :half_width]], axis=-1)
    return values * cos_table + turned * sin_table


def unrotate(gradient, cos_table, sin_table):
    half_width = gradient.shape[-1] // 2
    scaled = gradient * sin_table
    turned = jnp.concatenate([scaled[..., half_width:], -scaled[..., :half_width]], axis=-1)
    return gradient * cos_table + turned


def contract_rows(left_side, right_side):
    return lax.dot_general(
        left_side, right_side, (((0,), (0,)), ((), ())), preferred_element_type=jnp.float32
    )


def times_transpose(left_side, right_side):
    return lax.dot_general(
        left_side, right_side, (((1,), (1,)), ((), ())), preferred_element_type=jnp.float32
    )


def rms_back(grad_in, values, scale_rows, gain_row):
    weighted = grad_in * gain_row
    return scale_rows * weighted - values * scale_rows**3 * jnp.mean(
        weighted * values, axis=-1, keepdims=True
    )


def on_device(
    tokens, cotangent, doc_lengths, norm_attn, w_qkv, b_qkv, w_out, norm_mlp, w_gate, w_up, w_down
):
    gathered = (
        lax.all_gather(norm_attn, ("ctx", "wshard"), axis=0, tiled=True),
        lax.all_gather(w_qkv, ("ctx", "wshard"), axis=0, tiled=True),
        lax.all_gather(b_qkv, ("ctx", "wshard"), axis=0, tiled=True),
        lax.all_gather(w_out, ("ctx", "wshard"), axis=1, tiled=True),
        lax.all_gather(norm_mlp, ("ctx", "wshard"), axis=0, tiled=True),
        lax.all_gather(w_gate, ("ctx", "wshard"), axis=0, tiled=True),
        lax.all_gather(w_up, ("ctx", "wshard"), axis=0, tiled=True),
        lax.all_gather(w_down, ("ctx", "wshard"), axis=0, tiled=True),
    )
    gain_attn, full_qkv, full_bias, full_out, gain_mlp, full_gate, full_up, full_down = gathered
    tok_dev = tokens.shape[1]
    ctx_size = lax.axis_size("ctx")
    stream_len = tok_dev * ctx_size
    q_width = H * HD
    kv_width = KVH * HD
    groups = H // KVH
    block_count = stream_len // KEY_BLOCK
    score_scale = 1.0 / math.sqrt(HD)
    lengths = doc_lengths[0]
    local_docs, local_pos = documents_positions(
        lengths, stream_places(tok_dev, tok_dev, ctx_size, lax.axis_index("ctx") * tok_dev)
    )
    every_docs, every_pos = documents_positions(
        lengths, stream_places(stream_len, tok_dev, ctx_size, 0)
    )
    cos_table, sin_table = rope_tables(local_pos)
    inputs = tokens[0].astype(jnp.float32)
    gain_one = gain_attn.astype(jnp.float32)
    scale_one = lax.rsqrt(jnp.mean(inputs * inputs, axis=-1, keepdims=True) + EPSILON)
    normed_one = (inputs * scale_one * gain_one).astype(jnp.bfloat16)
    project = jnp.dot(normed_one, full_qkv, preferred_element_type=jnp.float32) + full_bias.astype(
        jnp.float32
    )
    queries = rotate(project[:, :q_width].reshape(tok_dev, H, HD), cos_table, sin_table).astype(
        jnp.bfloat16
    )
    queries = queries.reshape(tok_dev, KVH, groups, HD)
    keys_local = rotate(
        project[:, q_width : q_width + kv_width].reshape(tok_dev, KVH, HD), cos_table, sin_table
    )
    keys_local = keys_local.astype(jnp.bfloat16).reshape(tok_dev, kv_width)
    values_local = project[:, q_width + kv_width :].astype(jnp.bfloat16)
    all_keys, all_values = (
        lax.all_gather(keys_local, "ctx", axis=0, tiled=True),
        lax.all_gather(values_local, "ctx", axis=0, tiled=True),
    )
    key_blocks = all_keys.reshape(block_count, KEY_BLOCK, KVH, HD)
    value_blocks = all_values.reshape(block_count, KEY_BLOCK, KVH, HD)
    doc_blocks = every_docs.reshape(block_count, KEY_BLOCK)
    pos_blocks = every_pos.reshape(block_count, KEY_BLOCK)

    def block_scores(key_block, doc_block, pos_block):
        scores = (
            jnp.einsum("tkgd,skd->tkgs", queries, key_block, preferred_element_type=jnp.float32)
            * score_scale
        )
        allowed = (local_docs[:, None] == doc_block[None, :]) & (
            pos_block[None, :] <= local_pos[:, None]
        )
        return (scores, allowed[:, None, None, :])

    def max_sum(state_pair, block_in):
        running_max, running_sum = state_pair
        key_block, doc_block, pos_block = block_in
        scores, allowed = block_scores(key_block, doc_block, pos_block)
        masked = jnp.where(allowed, scores, -1e30)
        new_max = jnp.maximum(running_max, jnp.max(masked, axis=-1))
        added = jnp.sum(jnp.where(allowed, jnp.exp(masked - new_max[..., None]), 0.0), axis=-1)
        return ((new_max, running_sum * jnp.exp(running_max - new_max) + added), None)

    start_max = jnp.full((tok_dev, KVH, groups), -1e30, jnp.float32)
    start_sum = jnp.zeros((tok_dev, KVH, groups), jnp.float32)
    (running_max, running_sum), _ = lax.scan(
        max_sum, (start_max, start_sum), (key_blocks, doc_blocks, pos_blocks)
    )
    log_total = running_max + jnp.log(running_sum)

    def block_probability(key_block, doc_block, pos_block):
        scores, allowed = block_scores(key_block, doc_block, pos_block)
        return jnp.where(allowed, jnp.exp(scores - log_total[..., None]), 0.0)

    def weigh_values(accum_out, block_in):
        key_block, value_block, doc_block, pos_block = block_in
        probability = block_probability(key_block, doc_block, pos_block).astype(jnp.bfloat16)
        return (
            accum_out
            + jnp.einsum(
                "tkgs,skd->tkgd", probability, value_block, preferred_element_type=jnp.float32
            ),
            None,
        )

    start_out = jnp.zeros((tok_dev, KVH, groups, HD), jnp.float32)
    attended, _ = lax.scan(
        weigh_values, start_out, (key_blocks, value_blocks, doc_blocks, pos_blocks)
    )
    attended_b = attended.reshape(tok_dev, q_width).astype(jnp.bfloat16)
    hidden_res = inputs + jnp.dot(attended_b, full_out, preferred_element_type=jnp.float32)
    gain_two = gain_mlp.astype(jnp.float32)
    scale_two = lax.rsqrt(jnp.mean(hidden_res * hidden_res, axis=-1, keepdims=True) + EPSILON)
    normed_two = (hidden_res * scale_two * gain_two).astype(jnp.bfloat16)
    gate_pre = jnp.dot(normed_two, full_gate, preferred_element_type=jnp.float32)
    up_pre = jnp.dot(normed_two, full_up, preferred_element_type=jnp.float32)
    gate_sig = jax.nn.sigmoid(gate_pre)
    gate_act = gate_pre * gate_sig
    activated = (gate_act * up_pre).astype(jnp.bfloat16)
    branch_mlp = jnp.dot(activated, full_down, preferred_element_type=jnp.float32)
    output = (hidden_res + branch_mlp).astype(jnp.bfloat16)
    again = (
        lax.all_gather(norm_attn, ("ctx", "wshard"), axis=0, tiled=True),
        lax.all_gather(w_qkv, ("ctx", "wshard"), axis=0, tiled=True),
        lax.all_gather(w_out, ("ctx", "wshard"), axis=1, tiled=True),
        lax.all_gather(norm_mlp, ("ctx", "wshard"), axis=0, tiled=True),
        lax.all_gather(w_gate, ("ctx", "wshard"), axis=0, tiled=True),
        lax.all_gather(w_up, ("ctx", "wshard"), axis=0, tiled=True),
        lax.all_gather(w_down, ("ctx", "wshard"), axis=0, tiled=True),
    )
    back_gain_one, back_qkv, back_out, back_gain_two, back_gate, back_up, back_down = again
    back_gain_one = back_gain_one.astype(jnp.float32)
    back_gain_two = back_gain_two.astype(jnp.float32)
    out_grad_b = cotangent[0]
    out_grad = out_grad_b.astype(jnp.float32)
    act_grad = times_transpose(out_grad_b, back_down)
    gate_grad_b = (act_grad * up_pre * gate_sig * (1.0 + gate_pre * (1.0 - gate_sig))).astype(
        jnp.bfloat16
    )
    up_grad_b = (act_grad * gate_act).astype(jnp.bfloat16)
    normed_two_grad = times_transpose(gate_grad_b, back_gate) + times_transpose(up_grad_b, back_up)
    gain_two_grad = jnp.sum(normed_two_grad * hidden_res * scale_two, axis=0)
    hidden_grad = out_grad + rms_back(normed_two_grad, hidden_res, scale_two, back_gain_two)
    mlp_sum = (
        lax.psum_scatter(
            contract_rows(normed_two, gate_grad_b),
            ("ctx", "wshard"),
            scatter_dimension=0,
            tiled=True,
        ),
        lax.psum_scatter(
            contract_rows(normed_two, up_grad_b), ("ctx", "wshard"), scatter_dimension=0, tiled=True
        ),
    )
    down_sum = lax.psum_scatter(
        contract_rows(activated, out_grad_b), ("ctx", "wshard"), scatter_dimension=0, tiled=True
    )
    branch_grad_b = hidden_grad.astype(jnp.bfloat16)
    attended_grad_b = times_transpose(branch_grad_b, back_out).astype(jnp.bfloat16)
    grad_heads = attended_grad_b.reshape(tok_dev, KVH, groups, HD)
    delta_rows = jnp.sum(grad_heads.astype(jnp.float32) * attended, axis=-1)

    def backward_block(query_grad, block_in):
        key_block, value_block, doc_block, pos_block = block_in
        probability = block_probability(key_block, doc_block, pos_block)
        prob_grad = jnp.einsum(
            "tkgd,skd->tkgs", grad_heads, value_block, preferred_element_type=jnp.float32
        )
        score_grad_b = (probability * (prob_grad - delta_rows[..., None])).astype(jnp.bfloat16)
        query_grad = (
            query_grad
            + jnp.einsum(
                "tkgs,skd->tkgd", score_grad_b, key_block, preferred_element_type=jnp.float32
            )
            * score_scale
        )
        key_grad = (
            jnp.einsum("tkgs,tkgd->skd", score_grad_b, queries, preferred_element_type=jnp.float32)
            * score_scale
        )
        value_grad = jnp.einsum(
            "tkgs,tkgd->skd",
            probability.astype(jnp.bfloat16),
            grad_heads,
            preferred_element_type=jnp.float32,
        )
        return (
            query_grad,
            (key_grad.reshape(KEY_BLOCK, kv_width), value_grad.reshape(KEY_BLOCK, kv_width)),
        )

    query_grad, (key_parts, value_parts) = lax.scan(
        backward_block, start_out, (key_blocks, value_blocks, doc_blocks, pos_blocks)
    )
    key_sum, value_sum = in_one_piece(
        (
            key_parts.reshape(stream_len, kv_width).astype(jnp.bfloat16),
            value_parts.reshape(stream_len, kv_width).astype(jnp.bfloat16),
        ),
        "ctx",
        0,
        1,
    )
    query_pre = unrotate(query_grad.reshape(tok_dev, H, HD), cos_table, sin_table).reshape(
        tok_dev, q_width
    )
    key_pre = unrotate(key_sum.reshape(tok_dev, KVH, HD), cos_table, sin_table).reshape(
        tok_dev, kv_width
    )
    project_grad_b = jnp.concatenate([query_pre, key_pre, value_sum], axis=1).astype(jnp.bfloat16)
    bias_grad = jnp.sum(project_grad_b.astype(jnp.float32), axis=0)
    normed_one_grad = times_transpose(project_grad_b, back_qkv)
    gain_one_grad = jnp.sum(normed_one_grad * inputs * scale_one, axis=0)
    input_grad = hidden_grad + rms_back(normed_one_grad, inputs, scale_one, back_gain_one)
    attn_sum = (
        lax.psum_scatter(
            contract_rows(normed_one, project_grad_b),
            ("ctx", "wshard"),
            scatter_dimension=0,
            tiled=True,
        ),
        lax.psum_scatter(
            contract_rows(attended_b, branch_grad_b),
            ("ctx", "wshard"),
            scatter_dimension=1,
            tiled=True,
        ),
    )
    qk_width = q_width + kv_width
    small_sums = (
        lax.psum_scatter(gain_one_grad, ("ctx", "wshard"), scatter_dimension=0, tiled=True),
        lax.psum_scatter(bias_grad[:qk_width], ("ctx", "wshard"), scatter_dimension=0, tiled=True),
        lax.psum_scatter(bias_grad[qk_width:], ("ctx", "wshard"), scatter_dimension=0, tiled=True),
        lax.psum_scatter(gain_two_grad, ("ctx", "wshard"), scatter_dimension=0, tiled=True),
    )
    return (
        output[None],
        input_grad[None],
        small_sums[0],
        attn_sum[0],
        small_sums[1],
        small_sums[2],
        attn_sum[1],
        small_sums[3],
        mlp_sum[0],
        mlp_sum[1],
        down_sum,
    )


def solution(mesh):
    placed = (
        P("wshard", "ctx", None),
        P("wshard", "ctx", None),
        P("wshard", None),
        P(("ctx", "wshard")),
        P(("ctx", "wshard"), None),
        P(("ctx", "wshard")),
        P(None, ("ctx", "wshard")),
        P(("ctx", "wshard")),
        P(("ctx", "wshard"), None),
        P(("ctx", "wshard"), None),
        P(("ctx", "wshard"), None),
    )
    return jax.shard_map(
        on_device,
        mesh=mesh,
        in_specs=placed,
        out_specs=(
            P("wshard", "ctx", None),
            P("wshard", "ctx", None),
            P(("ctx", "wshard")),
            P(("ctx", "wshard"), None),
            P(("ctx", "wshard")),
            P(("ctx", "wshard")),
            P(None, ("ctx", "wshard")),
            P(("ctx", "wshard")),
            P(("ctx", "wshard"), None),
            P(("ctx", "wshard"), None),
            P(("ctx", "wshard"), None),
        ),
        check_vma=False,
    )
```

profile of v0, /device:TPU:0, one launch (start us, length us, event | category | flops | bytes accessed | tf_op | source)
XLA Modules:
  0.0 2573.2 jit_solution(11463339890385587523)
XLA Ops:
  10.5 43.0 %all-reduce.9 = (bf16[2048]{0:T(1024)(128)(2,1)S(1)}, bf16[1536]{0:T(1024)(128)(2,1)S(1)}, bf16[1536]{0:T(1024)(128)(2,1)S(1)}) all-reduce(bf16[2048]{0:T(1024)(128)(2,1)S(1)} %dynamic-update-slice.1, bf16[1536]{0:T(1024)(128)(2,1)S(1)} %dynamic-update-slice, ...), channel_id=1, replica_groups=mesh['ctx'=16,'wshard'=2] {'ctx','wshard'}, use_global_device_ids=true, to_apply=%add.1 | all-reduce | flops 5120 | bytes 20480
  58.4 24.9 all-gather.8.cloned.1.call-done
  83.2 4.0 convolution_add_fusion.3
  96.0 47.1 %all-gather.12.cloned.1.call-done = bf16[2048,256]{1,0:T(8,128)(2,1)} async-done(((bf16[128,256]{1,0:T(8,128)(2,1)}), bf16[2048,256]{1,0:T(8,128)(2,1)}) %all-gather.12.cloned.1.call-update) | async-done | bytes 1048592 | tf_op jit(solution)/shard_map/all_gather | solution.py:144
  145.5 55.0 %all-gather.10.cloned.1.call-done = bf16[2048,256]{1,0:T(8,128)(2,1)} async-done(((bf16[128,256]{1,0:T(8,128)(2,1)}), bf16[2048,256]{1,0:T(8,128)(2,1)}) %all-gather.10.cloned.1.call-update) | async-done | bytes 1048592 | tf_op jit(solution)/shard_map/all_gather | solution.py:145
  200.5 2.1 reshape.403
  202.7 24.7 while.39
  228.0 24.6 while.40
  231.0 2.9 fusion.160
  236.8 3.2 fusion.160
  242.9 3.2 fusion.160
  249.0 3.2 fusion.160
  253.9 11.9 all-gather.14.cloned.1.call-done
  265.8 4.1 multiply_reduce_fusion.3
  270.6 162.7 %all-gather.16.cloned.1.call-done = bf16[1536,8960]{1,0:T(8,128)(2,1)} async-done(((bf16[48,8960]{1,0:T(8,128)(2,1)}), bf16[1536,8960]{1,0:T(8,128)(2,1)}) %all-gather.16.cloned.1.call-update) | async-done | bytes 27525136 | tf_op jit(solution)/shard_map/all_gather | solution.py:106
  433.3 14.8 fusion.98
  448.1 152.1 %all-gather.18.cloned.1.call-done = bf16[1536,8960]{1,0:T(8,128)(2,1)} async-done(((bf16[48,8960]{1,0:T(8,128)(2,1)}), bf16[1536,8960]{1,0:T(8,128)(2,1)}) %all-gather.18.cloned.1.call-update) | async-done | bytes 27525136 | tf_op jit(solution)/shard_map/all_gather | solution.py:107
  600.2 14.8 fusion.99
  615.0 152.2 %all-gather.20.cloned.1.call-done = bf16[8960,1536]{1,0:T(8,128)(2,1)} async-done(((bf16[280,1536]{1,0:T(8,128)(2,1)}), bf16[8960,1536]{1,0:T(8,128)(2,1)}) %all-gather.20.cloned.1.call-update) | async-done | bytes 27525136 | tf_op jit(solution)/shard_map/all_gather | solution.py:108
  767.3 17.8 multiply_convert_fusion
  785.1 15.6 fusion.100
  800.7 15.6 multiply_reduce_fusion
  817.3 5.1 fusion.61
  822.4 3.2 convolution_convert_fusion
  828.7 51.1 %while.41 = (s32[]{:T(128)}, f32[128,2,6,128]{0,3,2,1:T(8,128)S(1)}, bf16[4,512,256]{2,1,0:T(8,128)(2,1)}, bf16[4,512,256]{2,1,0:T(8,128)(2,1)}, bf16[4,512,2,12...) while((s32[]{:T(128)}, ...), condition=%wide.region_16.17_spmd.clone, body=%wide.region_15.16_spmd.clone.sunk | while | flops 1015545856 | bytes 46628084 | solution.py:279
  833.8 2.1 fusion.171
  838.0 1.8 fusion.173
  846.6 2.1 fusion.171
  850.8 1.8 fusion.173
  859.5 2.0 fusion.171
  863.7 1.8 fusion.173
  872.3 2.0 fusion.171
  876.3 1.8 fusion.173
  879.8 3.1 pad_maximum_fusion
  882.9 4.6 all-to-all-start
  888.5 56.4 %all-to-all-done = bf16[16,128,512]{2,1,0:T(8,128)(2,1)} async-done(((bf16[16,128,512]{2,1,0:T(8,128)(2,1)}), bf16[16,128,512]{2,1,0:T(8,128)(2,1)}, u32[]{:S(2)}, u32[]{:S(2)}) %all-to-all-start) | async-done | bytes 2097184 | tf_op jit(solution)/shard_map/all_to_all | solution.py:26
  944.8 1.9 convert_reduce_fusion
  947.7 6.4 fusion.66
  955.8 21.6 fusion.101
  979.0 21.3 fusion.102
  1002.0 24.2 fusion.57
  1027.5 13.3 fusion.43
  1041.0 5.6 fusion.53
  1046.6 49.8 %all-reduce.8 = (f32[1536]{0:T(1024)S(1)}, f32[1792]{0:T(1024)S(1)}, f32[256]{0:T(256)S(1)}, f32[1536]{0:T(1024)S(1)}) all-reduce(f32[1536]{0:T(1024)S(1)} %get-tuple-element.433, f32[1792]{0:T(1024)S(1)} %bitcast.280, f32[256]{0:T(256)S(1)} %slice.76, ...), channel_id=2, replica_groups=mesh['ctx'=16,'wshard'=2] {'ctx','wshard'}, use_global_device_ids=true, to_apply=%region_20.21.clone | all-reduce | flops 5120 | bytes 40960
  1100.0 59.7 %reduce-scatter.8.cloned.1.call-done = f32[48,2048]{1,0:T(8,128)} async-done(((f32[1536,2048]{1,0:T(8,128)}), f32[48,2048]{1,0:T(8,128)}) %reduce-scatter.8.cloned.1.call-update) | async-done | bytes 393232 | tf_op jit(solution)/shard_map/reduce_scatter | solution.py:303
  1159.7 468.2 %reduce-scatter.12.cloned.1.call-done = f32[48,8960]{1,0:T(8,128)} async-done(((f32[1536,8960]{1,0:T(8,128)}), f32[48,8960]{1,0:T(8,128)}) %reduce-scatter.12.cloned.1.call-update) | async-done | bytes 1720336 | tf_op jit(solution)/shard_map/reduce_scatter | solution.py:232
  1627.9 469.6 %reduce-scatter.14.cloned.1.call-done = f32[48,8960]{1,0:T(8,128)} async-done(((f32[1536,8960]{1,0:T(8,128)}), f32[48,8960]{1,0:T(8,128)}) %reduce-scatter.14.cloned.1.call-update) | async-done | bytes 1720336 | tf_op jit(solution)/shard_map/reduce_scatter | solution.py:238
  2097.5 468.4 %reduce-scatter.16.cloned.1.call-done = f32[280,1536]{1,0:T(8,128)} async-done(((f32[8960,1536]{1,0:T(8,128)}), f32[280,1536]{1,0:T(8,128)}) %reduce-scatter.16.cloned.1.call-update) | async-done | bytes 1720336
  (302 shorter events, 108.7 us)
Async XLA Ops:
  7.2 76.1 %all-gather.8.cloned.1.call-start = ((), (), s32[]{:S(2)}) async-start(), calls=%async_computation.6 | async-start | bytes 6488064 | tf_op jit(solution)/shard_map/all_gather | solution.py:102
  7.9 135.2 %all-gather.12.cloned.1.call-start = ((), (), s32[]{:S(2)}) async-start(), calls=%async_computation.8 | async-start | bytes 1114112 | tf_op jit(solution)/shard_map/all_gather | solution.py:144
  53.6 33.7 %copy-start.35 = (f32[1536]{0:T(1024)}, f32[1536]{0:T(1024)S(1)}, u32[]{:S(2)}) copy-start(f32[1536]{0:T(1024)S(1)} %convert_element_type.107) | copy-start | bytes 18436
  56.4 38.5 %copy-start.27 = (f32[128,128]{0,1:T(8,128)}, f32[128,128]{0,1:T(8,128)S(1)}, u32[]{:S(2)}) copy-start(f32[128,128]{0,1:T(8,128)S(1)} %pad_maximum_fusion.5) | copy-start | bytes 196612
  56.5 31.0 %copy-start.31 = (f32[128,128]{1,0:T(8,128)}, f32[128,128]{1,0:T(8,128)S(1)}, u32[]{:S(2)}) copy-start(f32[128,128]{1,0:T(8,128)S(1)} %copy.95) | copy-start | bytes 196612
  56.6 38.3 %copy-start.25 = (f32[128,128]{0,1:T(8,128)}, f32[128,128]{0,1:T(8,128)S(1)}, u32[]{:S(2)}) copy-start(f32[128,128]{0,1:T(8,128)S(1)} %pad_maximum_fusion.4) | copy-start | bytes 196612
  58.4 28.9 %copy-start.39 = (f32[128]{0:T(128)}, f32[128]{0:T(128)S(1)}, u32[]{:S(2)}) copy-start(f32[128]{0:T(128)S(1)} %get-tuple-element.536) | copy-start | bytes 1540
  87.2 5.3 copy-start.42
  89.2 111.4 %all-gather.10.cloned.1.call-start = ((), (), s32[]{:S(2)}) async-start(), calls=%async_computation.7 | async-start | bytes 1114112 | tf_op jit(solution)/shard_map/all_gather | solution.py:145
  89.9 175.9 %all-gather.14.cloned.1.call-start = ((), (), s32[]{:S(2)}) async-start(), calls=%async_computation.9 | async-start | bytes 4866048 | tf_op jit(solution)/shard_map/all_gather | solution.py:104
  90.5 342.9 %all-gather.16.cloned.1.call-start = ((), (), s32[]{:S(2)}) async-start(), calls=%async_computation.10 | async-start | bytes 28385280 | tf_op jit(solution)/shard_map/all_gather | solution.py:106
  91.1 509.2 %all-gather.18.cloned.1.call-start = ((), (), s32[]{:S(2)}) async-start(), calls=%async_computation.11 | async-start | bytes 28385280 | tf_op jit(solution)/shard_map/all_gather | solution.py:107
  91.6 675.6 %all-gather.20.cloned.1.call-start = ((), (), s32[]{:S(2)}) async-start(), calls=%async_computation.12 | async-start | bytes 28385280 | tf_op jit(solution)/shard_map/all_gather | solution.py:108
  92.4 1007.6 %reduce-scatter.10.cloned.1.call-start = ((), (), s32[]{:S(2)}) async-start(), calls=%async_computation.14 | async-start | bytes 9732096 | tf_op jit(solution)/shard_map/reduce_scatter | solution.py:309
  228.0 37.7 %copy-start.12 = (bf16[1,128,1536]{2,1,0:T(8,128)(2,1)S(1)}, bf16[1,128,1536]{2,1,0:T(8,128)(2,1)}, u32[]{:S(2)}) copy-start(bf16[1,128,1536]{2,1,0:T(8,128)(2,1)} %param.17) | copy-start | bytes 1179652
  253.9 16.0 copy-start.16
  265.8 4.7 copy-start.37
  269.9 546.4 %copy-start.3 = (f32[128,1536]{1,0:T(8,128)}, f32[128,1536]{1,0:T(8,128)S(1)}, u32[]{:S(2)}) copy-start(f32[128,1536]{1,0:T(8,128)S(1)} %get-tuple-element.540) | copy-start | bytes 2359300
  270.5 177.7 %copy-start.41 = (f32[128]{0:T(128)}, f32[128]{0:T(128)S(1)}, u32[]{:S(2)}) copy-start(f32[128]{0:T(128)S(1)} %get-tuple-element.538) | copy-start | bytes 1540
  270.6 329.6 %copy-start.14 = (bf16[128,1536]{1,0:T(8,128)(2,1)}, bf16[128,1536]{1,0:T(8,128)(2,1)S(1)}, u32[]{:S(2)}) copy-start(bf16[128,1536]{1,0:T(8,128)(2,1)S(1)} %multiply_convert_fusion.3) | copy-start | bytes 1179652
  785.1 15.6 copy-start.5
  800.7 15.6 copy-start.21
  800.7 16.5 copy-start.17
  817.2 5.1 copy-start.10
  822.4 4.1 copy-start.20
  830.3 5.6 copy-start
  835.9 2.1 copy-start.1
  843.1 5.6 copy-start
  855.9 5.6 copy-start
  868.7 5.6 copy-start
  882.9 4.9 copy-start.28
  882.9 61.9 %all-to-all-start = ((bf16[16,128,512]{2,1,0:T(8,128)(2,1)}), bf16[16,128,512]{2,1,0:T(8,128)(2,1)}, u32[]{:S(2)}, u32[]{:S(2)}) async-start(bf16[16,128,512]{2,1,0:T(8,128)(2,1)} %pad_maximum_fusion), calls=%async_computation | async-start | bytes 4194304 | tf_op jit(solution)/shard_map/all_to_all | solution.py:26
  887.5 272.2 %reduce-scatter.8.cloned.1.call-start = ((), (), s32[]{:S(2)}) async-start(), calls=%async_computation.13 | async-start | bytes 12976128 | tf_op jit(solution)/shard_map/reduce_scatter | solution.py:303
  887.9 59.0 %copy-start.32 = (f32[128,128]{1,0:T(8,128)S(1)}, f32[128,128]{1,0:T(8,128)}, u32[]{:S(2)}) copy-start(f32[128,128]{1,0:T(8,128)} %copy-done.31) | copy-start | bytes 196612
  888.3 59.1 %copy-start.24 = (f32[128,2,128]{2,1,0:T(2,128)S(1)}, f32[128,2,128]{2,1,0:T(2,128)}, u32[]{:S(2)}) copy-start(f32[128,2,128]{2,1,0:T(2,128)} %copy-done.23) | copy-start | bytes 393220
  888.3 59.3 %copy-start.13 = (bf16[1,128,1536]{2,1,0:T(8,128)(2,1)S(1)}, bf16[1,128,1536]{2,1,0:T(8,128)(2,1)}, u32[]{:S(2)}) copy-start(bf16[1,128,1536]{2,1,0:T(8,128)(2,1)} %param.17) | copy-start | bytes 1179652
  888.3 59.3 %copy-start.36 = (f32[1536]{0:T(1024)S(1)}, f32[1536]{0:T(1024)}, u32[]{:S(2)}) copy-start(f32[1536]{0:T(1024)} %copy-done.35) | copy-start | bytes 18436
  888.3 59.3 %copy-start.40 = (f32[128]{0:T(128)S(1)}, f32[128]{0:T(128)}, u32[]{:S(2)}) copy-start(f32[128]{0:T(128)} %copy-done.39) | copy-start | bytes 1540
  888.5 65.6 %copy-start.18 = (bf16[128,1536]{0,1:T(8,128)(2,1)}, bf16[128,1536]{0,1:T(8,128)(2,1)S(1)}, u32[]{:S(2)}) copy-start(bf16[128,1536]{0,1:T(8,128)(2,1)S(1)} %fusion.56) | copy-start | bytes 1179652
  947.7 6.4 copy-start.29
  954.1 673.8 %reduce-scatter.12.cloned.1.call-start = ((), (), s32[]{:S(2)}) async-start(), calls=%async_computation.15 | async-start | bytes 56770560 | tf_op jit(solution)/shard_map/reduce_scatter | solution.py:232
  977.4 1120.1 %reduce-scatter.14.cloned.1.call-start = ((), (), s32[]{:S(2)}) async-start(), calls=%async_computation.16 | async-start | bytes 56770560 | tf_op jit(solution)/shard_map/reduce_scatter | solution.py:238
  1000.4 1565.5 %reduce-scatter.16.cloned.1.call-start = ((), (), s32[]{:S(2)}) async-start(), calls=%async_computation.17 | async-start | bytes 56770560
  1027.5 13.3 copy-start.19
  1027.5 13.3 copy-start.30
  1041.0 5.6 copy-start.38
  1041.0 57.8 %copy-start.11 = (f32[128,1536]{1,0:T(8,128)S(1)}, f32[128,1536]{1,0:T(8,128)}, u32[]{:S(2)}) copy-start(f32[128,1536]{1,0:T(8,128)} %copy-done.10) | copy-start | bytes 2359300
  1041.0 57.7 %copy-start.43 = (f32[128]{0:T(128)S(1)}, f32[128]{0:T(128)}, u32[]{:S(2)}) copy-start(f32[128]{0:T(128)} %get-tuple-element.535) | copy-start | bytes 1540
  (24 other events, 29.8 us)
Sparse Core Ops, SparseCore 0:
  10.9 72.3 all-gather.7
  89.3 53.7 all-gather.11
  146.4 54.0 all-gather.9
  203.3 62.4 all-gather.13
  268.5 164.7 all-gather.15
  436.1 164.0 all-gather.17
  603.1 164.0 all-gather.19
  827.8 168.3 reduce-scatter.9
  1003.8 155.7 reduce-scatter.7
  1166.5 461.3 reduce-scatter.11
  1636.1 461.3 reduce-scatter.13
  2104.3 461.4 reduce-scatter.15
where the time goes:
time: 2580 us; the launch traced here: 2570 us
  waiting for transfers between devices  2130 us (83%)
  matrix products  237 us (9%)
  blocking collectives  92.8 us (4%)
  local copies, waits for them, and re-layouts  53.9 us (2%)
  other arithmetic  35.9 us (1%)
    unnamed x13, waiting for transfers between devices  471 us
    reduce_scatter x1, waiting for transfers between devices, on_device(): lax.psum_scatter(contract_rows(normed_two, up_grad_b), ('ctx', 'wshard'),...  470 us
    reduce_scatter x1, waiting for transfers between devices, on_device(): lax.psum_scatter(contract_rows(normed_two, gate_grad_b), ('ctx', 'wshard'...  468 us
    all_gather x1, waiting for transfers between devices, on_device(): lax.all_gather(w_gate, ('ctx', 'wshard'), axis=0, tiled=True)  163 us
    all_gather x1, waiting for transfers between devices, on_device(): lax.all_gather(w_down, ('ctx', 'wshard'), axis=0, tiled=True)  152 us
    all_gather x1, waiting for transfers between devices, on_device(): lax.all_gather(w_up, ('ctx', 'wshard'), axis=0, tiled=True)  152 us
    unnamed x2, blocking collectives  92.8 us
    dot_general x5, matrix products, contract_rows(): lax.dot_general(left_side, right_side, (((0,), (0,)), ((), ())), preferre...  78.7 us
  transfers between devices with their start and end apart: 13, of which 12 were waited for; matrix products, arithmetic and copies ran while one was open for 10% of the time, Pallas kernels for 0%

commit v1 on v0

v1 whole, which is shorter than its diff:
```python
import math

import jax
import jax.numpy as jnp
from jax import lax
from jax.sharding import PartitionSpec as P

H = 12
KVH = 2
HD = 128
EPSILON = 1e-06
ROPE_BASE = 1000000.0
CUBE = (0, 1, 2)
ORDERS = ((0, 1, 2), (1, 2, 0), (2, 0, 1))
bf16 = jnp.bfloat16
f32 = jnp.float32


def core_swap(x):
    return lax.ppermute(x, "wshard", [(0, 1), (1, 0)])


def chip_swap(x, flip):
    count = lax.axis_size("ctx")
    return lax.ppermute(x, "ctx", [(i, i ^ flip) for i in range(count)])


def high_bits():
    return tuple(range(3, lax.axis_size("ctx").bit_length() - 1))


def my_bit(bit):
    return (lax.axis_index("ctx") >> bit) & 1


def gather_relative(x, bits):
    for bit in bits:
        x = jnp.concatenate([x, chip_swap(x, 1 << bit)], axis=0)
    return x


def relative_flips(bits):
    flips = [0]
    for bit in bits:
        flips = flips + [f ^ (1 << bit) for f in flips]
    return flips


def scatter_relative(x, bits):
    total = x
    for at, bit in enumerate(reversed(bits)):
        half = total.shape[0] // 2
        keep, send = total[:half], total[half:]
        total = keep.astype(f32) + chip_swap(send.astype(bf16), 1 << bit).astype(f32)
        if at < len(bits) - 1:
            total = total.astype(bf16)
    return total


def gather_ordered(x, bits):
    names = []
    for bit in bits:
        other = chip_swap(x, 1 << bit)
        upper = my_bit(bit) == 1
        x = jnp.stack([jnp.where(upper, other, x), jnp.where(upper, x, other)])
        names = [bit] + names
    want = sorted(names, reverse=True)
    rest = tuple(range(len(names), x.ndim))
    x = x.transpose(tuple(names.index(b) for b in want) + rest)
    return x.reshape((2 ** len(names),) + x.shape[len(names) :])


def scatter_ordered(x, bits):
    count = len(bits)
    names = sorted(bits, reverse=True)
    x = x.reshape((2,) * count + x.shape[1:])
    for at, bit in enumerate(bits):
        axis = names.index(bit)
        mine = my_bit(bit)
        keep = lax.dynamic_index_in_dim(x, mine, axis, keepdims=False)
        send = lax.dynamic_index_in_dim(x, 1 - mine, axis, keepdims=False)
        x = keep.astype(f32) + chip_swap(send.astype(bf16), 1 << bit).astype(f32)
        if at < count - 1:
            x = x.astype(bf16)
        names.pop(axis)
    return x


def row_parts(rows):
    third = rows * 3 // 8
    return ((0, third), (third, 2 * third), (2 * third, rows))


def documents_positions(lengths, places):
    ends_at = jnp.cumsum(lengths)
    passed = ends_at[None, :] <= places[:, None]
    documents = jnp.sum(passed.astype(jnp.int32), axis=1)
    starts = jnp.sum(jnp.where(passed, lengths[None, :], 0), axis=1)
    return (documents, places - starts)


def places_of(device, inner_row, tok_dev):
    ctx_size = lax.axis_size("ctx")
    half_rows = tok_dev // 2
    blocks = jnp.where(inner_row < half_rows, device, 2 * ctx_size - 1 - device)
    return blocks * half_rows + inner_row % half_rows


def rope_tables(positions):
    half_width = HD // 2
    frequency = ROPE_BASE ** (-jnp.arange(half_width, dtype=f32) * 2.0 / HD)
    angles = positions.astype(f32)[:, None] * frequency[None, :]
    cos_table = jnp.concatenate([jnp.cos(angles), jnp.cos(angles)], axis=-1)[:, None, :]
    sin_table = jnp.concatenate([jnp.sin(angles), jnp.sin(angles)], axis=-1)[:, None, :]
    return (cos_table, sin_table)


def rotate(values, cos_table, sin_table):
    half_width = values.shape[-1] // 2
    turned = jnp.concatenate([-values[..., half_width:], values[..., :half_width]], axis=-1)
    return values * cos_table + turned * sin_table


def unrotate(gradient, cos_table, sin_table):
    half_width = gradient.shape[-1] // 2
    scaled = gradient * sin_table
    turned = jnp.concatenate([scaled[..., half_width:], -scaled[..., :half_width]], axis=-1)
    return gradient * cos_table + turned


def dot(left, right, left_axis, right_axis):
    return lax.dot_general(
        left, right, (((left_axis,), (right_axis,)), ((), ())), preferred_element_type=f32
    )


def rms_back(grad_in, values, scale_rows, gain_row):
    weighted = grad_in * gain_row
    return scale_rows * weighted - values * scale_rows**3 * jnp.mean(
        weighted * values, axis=-1, keepdims=True
    )


def half_of(x, which, axis):
    size = x.shape[axis] // 2
    return lax.dynamic_slice_in_dim(x, which * size, size, axis)


def head_columns(x, core):
    q_width, kv_width = H * HD, KVH * HD
    return jnp.concatenate(
        [
            half_of(x[:, :q_width], core, 1),
            half_of(x[:, q_width : q_width + kv_width], core, 1),
            half_of(x[:, q_width + kv_width :], core, 1),
        ],
        axis=1,
    )


def by_core(mine, other, core):
    return jnp.stack([jnp.where(core == 0, mine, other), jnp.where(core == 0, other, mine)])


def gather_rows(x, bits):
    high = tuple(b for b in bits if b > 2)
    rows = x.shape[0]
    parts = []
    cuts = (0, rows // 48 * 16, rows // 48 * 32, rows) if rows >= 48 else (0, rows)
    for (start, stop), order in zip(zip(cuts[:-1], cuts[1:]), ORDERS):
        parts.append(gather_ordered(x[start:stop], high + order))
    whole = jnp.concatenate(parts, axis=1)
    return whole.reshape((-1,) + x.shape[1:])


def scatter_rows(x, bits):
    high = tuple(b for b in bits if b > 2)
    chips = 2 ** len(bits)
    rows = x.shape[0] // chips
    x = x.reshape(chips, rows, x.shape[1])
    cuts = (0, rows // 48 * 16, rows // 48 * 32, rows) if rows >= 48 else (0, rows)
    parts = [
        scatter_ordered(x[:, start:stop], order + high)
        for (start, stop), order in zip(zip(cuts[:-1], cuts[1:]), ORDERS)
    ]
    return jnp.concatenate(parts, axis=0)


def on_device(
    tokens, cotangent, doc_lengths, norm_attn, w_qkv, b_qkv, w_out, norm_mlp, w_gate, w_up, w_down
):
    ctx_size = lax.axis_size("ctx")
    chip = lax.axis_index("ctx")
    core = lax.axis_index("wshard")
    high = high_bits()
    bits = tuple(range(3)) + high
    groups = ctx_size // 8
    member, group = chip % 8, chip // 8
    tok_dev, width = tokens.shape[1], tokens.shape[2]
    ff = w_gate.shape[1]
    ff_chip = ff // ctx_size
    ff_own = ff // 8
    heads = H // KVH
    hq = heads * HD
    score_scale = 1.0 / math.sqrt(HD)

    mine = head_columns(w_qkv, core)
    other = core_swap(head_columns(w_qkv, 1 - core))
    qkv_w = gather_rows(by_core(mine, other, core).reshape(-1, mine.shape[1]), bits)
    small = jnp.concatenate([norm_attn, b_qkv, norm_mlp])
    small_all = gather_ordered(by_core(small, core_swap(small), core), bits).reshape(
        2 * ctx_size, -1
    )
    n_gain, n_bias = norm_attn.shape[0], b_qkv.shape[0]
    gain_one = small_all[:, :n_gain].reshape(-1).astype(f32)
    bias = small_all[:, n_gain : n_gain + n_bias].reshape(1, -1).astype(f32)
    gain_two = small_all[:, n_gain + n_bias :].reshape(-1).astype(f32)
    bias = head_columns(bias, core)
    out_t = w_out.T
    out_mine = half_of(out_t, core, 1)
    out_other = core_swap(half_of(out_t, 1 - core, 1))
    out_w = gather_rows(by_core(out_mine, out_other, core).reshape(-1, hq), bits)

    rows_dev = w_gate.shape[0]

    def by_member(w):
        return w.reshape(rows_dev, groups, 8, ff_chip).transpose(2, 0, 1, 3).reshape(8, rows_dev, ff_own)

    both = jnp.concatenate([by_member(w_gate), by_member(w_up)], axis=2)
    arrived = [lax.dynamic_index_in_dim(both, member, 0, keepdims=False)]
    for k in range(1, 8):
        send = lax.dynamic_index_in_dim(both, member ^ k, 0, keepdims=False)
        arrived.append(chip_swap(send, k))
    arrived = jnp.stack(arrived)
    cube_rows = jnp.stack(
        [lax.dynamic_index_in_dim(arrived, member ^ k, 0, keepdims=False) for k in range(8)]
    )
    all_rows = gather_ordered(cube_rows, high)
    all_rows = by_core(all_rows, core_swap(all_rows), core)
    gate_up = all_rows.transpose(1, 2, 0, 3, 4).reshape(width, 2 * ff_own)
    down = by_core(w_down, core_swap(w_down), core).reshape(ff_chip, width)
    down = gather_ordered(down, high).reshape(ff_own, width)

    def streams(x):
        return jnp.stack([x, core_swap(x)])

    token_pair = streams(tokens[0])
    length_pair = streams(doc_lengths[0])
    inner = jnp.arange(tok_dev, dtype=jnp.int32)
    parts = row_parts(tok_dev)
    key_places = jnp.concatenate(
        [
            places_of(
                (chip ^ jnp.array(relative_flips(high + order), jnp.int32))[:, None],
                inner[None, start:stop],
                tok_dev,
            ).reshape(-1)
            for (start, stop), order in zip(parts, ORDERS)
        ]
    )
    own_places = places_of(chip, inner, tok_dev)
    own_docs, own_pos = jax.vmap(lambda l: documents_positions(l, own_places))(length_pair)
    key_docs, key_pos = jax.vmap(lambda l: documents_positions(l, key_places))(length_pair)
    cos_table, sin_table = rope_tables(own_pos.reshape(-1))

    inputs_pair = token_pair.reshape(2 * tok_dev, width).astype(f32)
    scale_one = lax.rsqrt(jnp.mean(inputs_pair * inputs_pair, axis=-1, keepdims=True) + EPSILON)
    normed_one = (inputs_pair * scale_one * gain_one).astype(bf16)
    project = dot(normed_one, qkv_w, 1, 0) + bias
    queries = rotate(project[:, :hq].reshape(-1, heads, HD), cos_table, sin_table).astype(bf16)
    keys_own = rotate(project[:, hq : hq + HD].reshape(-1, 1, HD), cos_table, sin_table)
    keys_own = keys_own.reshape(2, tok_dev, HD).astype(bf16)
    values_own = project[:, hq + HD :].reshape(2, tok_dev, HD).astype(bf16)
    kv_own = jnp.concatenate([keys_own, values_own], axis=2)
    kv_parts = [
        gather_relative(kv_own[None, :, start:stop], high + order)
        .transpose(1, 0, 2, 3)
        .reshape(2, -1, 2 * HD)
        for (start, stop), order in zip(parts, ORDERS)
    ]
    kv_all = jnp.concatenate(kv_parts, axis=1)
    keys, values = kv_all[..., :HD], kv_all[..., HD:]

    queries = queries.reshape(2, tok_dev, heads, HD)
    allowed = (own_docs[:, :, None] == key_docs[:, None, :]) & (
        key_pos[:, None, :] <= own_pos[:, :, None]
    )
    allowed = allowed[:, None]
    scores = (
        jnp.einsum("sthd,skd->shtk", queries, keys, preferred_element_type=f32) * score_scale
    )
    masked = jnp.where(allowed, scores, -1e30)
    top = jnp.max(masked, axis=-1, keepdims=True)
    shifted = jnp.exp(masked - top)
    probability = shifted / jnp.sum(shifted, axis=-1, keepdims=True)
    probability_b = probability.astype(bf16)
    attended = jnp.einsum("shtk,skd->sthd", probability_b, values, preferred_element_type=f32)
    attended_b = attended.reshape(2 * tok_dev, hq).astype(bf16)
    branch = dot(attended_b, out_w, 1, 1)
    inputs = inputs_pair[:tok_dev]
    hidden_res = inputs + branch[:tok_dev] + core_swap(branch[tok_dev:])
    scale_two = lax.rsqrt(jnp.mean(hidden_res * hidden_res, axis=-1, keepdims=True) + EPSILON)
    normed_two = (hidden_res * scale_two * gain_two).astype(bf16)

    def cube_gather(x):
        return jnp.concatenate(
            [
                gather_relative(x[start:stop], order)
                for (start, stop), order in zip(parts, ORDERS)
            ]
        )

    def cube_scatter(x):
        sums = []
        for (start, stop), order in zip(parts, ORDERS):
            sums.append(scatter_relative(x[8 * start : 8 * stop], order))
        return jnp.concatenate(sums)

    out_grad_b = cotangent[0]
    out_grad = out_grad_b.astype(f32)
    out_grad_all = cube_gather(out_grad_b)
    act_grad = dot(out_grad_all, down, 1, 1)
    normed_all = cube_gather(normed_two)
    pre = dot(normed_all, gate_up, 1, 0)
    gate_pre, up_pre = pre[:, :ff_own], pre[:, ff_own:]
    gate_sig = jax.nn.sigmoid(gate_pre)
    gate_act = gate_pre * gate_sig
    activated = (gate_act * up_pre).astype(bf16)
    gate_grad = (act_grad * up_pre * gate_sig * (1.0 + gate_pre * (1.0 - gate_sig))).astype(bf16)
    up_grad = (act_grad * gate_act).astype(bf16)
    pre_grad = jnp.concatenate([gate_grad, up_grad], axis=1)
    normed_two_grad = cube_scatter(dot(pre_grad, gate_up, 1, 1).astype(bf16))
    branch_mlp = cube_scatter(dot(activated, down, 1, 0).astype(bf16))
    output = (hidden_res + branch_mlp).astype(bf16)

    down_part = dot(activated, out_grad_all, 0, 0).astype(bf16).reshape(groups, 2, -1, width)
    keep = lax.dynamic_index_in_dim(down_part, core, 1, keepdims=False)
    send = lax.dynamic_index_in_dim(down_part, 1 - core, 1, keepdims=False)
    down_sum = (keep.astype(f32) + core_swap(send).astype(f32)).astype(bf16)
    grad_down = scatter_ordered(down_sum, tuple(reversed(high)))

    gu_part = dot(normed_all, pre_grad, 0, 0).astype(bf16)
    gu_part = gu_part.reshape(groups, 8, 2, rows_dev, 2 * ff_own)
    keep = lax.dynamic_index_in_dim(gu_part, core, 2, keepdims=False)
    send = lax.dynamic_index_in_dim(gu_part, 1 - core, 2, keepdims=False)
    gu_sum = (keep.astype(f32) + core_swap(send).astype(f32)).astype(bf16)
    gu_sum = scatter_ordered(gu_sum, tuple(reversed(high))).astype(bf16)
    arrived = [lax.dynamic_index_in_dim(gu_sum, member, 0, keepdims=False)]
    for k in range(1, 8):
        send = lax.dynamic_index_in_dim(gu_sum, member ^ k, 0, keepdims=False)
        arrived.append(chip_swap(send, k))
    arrived = jnp.stack(arrived)
    from_members = jnp.stack(
        [lax.dynamic_index_in_dim(arrived, member ^ k, 0, keepdims=False) for k in range(8)]
    )

    def to_columns(x):
        x = x.reshape(8, rows_dev, groups, ff_chip).transpose(1, 2, 0, 3)
        return x.reshape(rows_dev, ff).astype(f32)

    grad_gate = to_columns(from_members[:, :, :ff_own])
    grad_up = to_columns(from_members[:, :, ff_own:])

    gain_two_grad = jnp.sum(normed_two_grad * hidden_res * scale_two, axis=0)
    hidden_grad = out_grad + rms_back(normed_two_grad, hidden_res, scale_two, gain_two)

    branch_grad = streams(hidden_grad.astype(bf16)).reshape(2 * tok_dev, width)
    attended_grad = dot(branch_grad, out_w, 1, 0).astype(bf16)
    grad_out_t = scatter_rows(dot(branch_grad, attended_b, 0, 0).astype(bf16), bits)
    grad_heads = attended_grad.reshape(2, tok_dev, heads, HD)
    delta = jnp.sum(grad_heads.astype(f32) * attended, axis=-1).transpose(0, 2, 1)[..., None]
    prob_grad = jnp.einsum("sthd,skd->shtk", grad_heads, values, preferred_element_type=f32)
    score_grad = (probability * (prob_grad - delta)).astype(bf16)
    query_grad = (
        jnp.einsum("shtk,skd->sthd", score_grad, keys, preferred_element_type=f32) * score_scale
    )
    key_grad = (
        jnp.einsum("shtk,sthd->skd", score_grad, queries, preferred_element_type=f32) * score_scale
    )
    value_grad = jnp.einsum("shtk,sthd->skd", probability_b, grad_heads, preferred_element_type=f32)
    kv_grad = jnp.concatenate([key_grad, value_grad], axis=2).astype(bf16)
    kv_sums = []
    for (start, stop), order in zip(parts, ORDERS):
        own = kv_grad[:, ctx_size * start : ctx_size * stop]
        own = own.reshape(2, ctx_size, stop - start, 2 * HD).transpose(1, 0, 2, 3)
        kv_sums.append(scatter_relative(own, high + order)[0])
    kv_sum = jnp.concatenate(kv_sums, axis=1).reshape(2 * tok_dev, 2 * HD)
    query_pre = unrotate(query_grad.reshape(-1, heads, HD), cos_table, sin_table)
    key_pre = unrotate(kv_sum[:, None, :HD], cos_table, sin_table)
    project_grad_q = query_pre.reshape(-1, hq).astype(bf16)
    project_grad_kv = jnp.concatenate([key_pre[:, 0], kv_sum[:, HD:]], axis=1).astype(bf16)
    grad_q = scatter_rows(dot(normed_one, project_grad_q, 0, 0).astype(bf16), bits)
    grad_kv = scatter_rows(dot(normed_one, project_grad_kv, 0, 0).astype(bf16), bits)
    project_grad = jnp.concatenate([project_grad_q, project_grad_kv], axis=1)
    normed_one_grad = dot(project_grad, qkv_w, 1, 1)
    normed_one_grad = normed_one_grad[:tok_dev] + core_swap(normed_one_grad[tok_dev:])
    gain_one_grad = jnp.sum(normed_one_grad * inputs * scale_one[:tok_dev], axis=0)
    input_grad = hidden_grad + rms_back(normed_one_grad, inputs, scale_one[:tok_dev], gain_one)

    mine = half_of(jnp.concatenate([grad_q, grad_kv], axis=1), core, 0)
    other = half_of(jnp.concatenate([grad_q, grad_kv], axis=1), 1 - core, 0)
    pair = by_core(mine, core_swap(other), core)

    def whole_columns(x):
        return jnp.concatenate(
            [
                x[0, :, :hq],
                x[1, :, :hq],
                x[0, :, hq : hq + HD],
                x[1, :, hq : hq + HD],
                x[0, :, hq + HD :],
                x[1, :, hq + HD :],
            ],
            axis=1,
        )

    grad_qkv = whole_columns(pair)
    out_mine = half_of(grad_out_t, core, 0)
    out_other = half_of(grad_out_t, 1 - core, 0)
    out_pair = by_core(out_mine, core_swap(out_other), core)
    grad_out = out_pair.transpose(1, 0, 2).reshape(-1, 2 * hq).T

    bias_grad = jnp.sum(project_grad.astype(f32), axis=0, keepdims=True)
    zeros = jnp.zeros_like(bias_grad)
    bias_full = jnp.stack(
        [jnp.where(core == 0, bias_grad, zeros), jnp.where(core == 0, zeros, bias_grad)]
    )
    sums = jnp.concatenate([gain_one_grad, gain_two_grad, whole_columns(bias_full)[0]])
    sums = sums.reshape(-1, 128)
    sums = sums + core_swap(sums)
    for bit in bits:
        sums = sums + chip_swap(sums, 1 << bit)
    sums = sums.reshape(-1)
    at = 2 * chip + core

    def owned(x):
        size = x.shape[0] // (2 * ctx_size)
        return lax.dynamic_slice_in_dim(x, at * size, size, 0)

    qk_width = (H + KVH) * HD
    bias_sum = sums[2 * width :]
    return (
        output[None],
        input_grad[None],
        owned(sums[:width]),
        grad_qkv,
        owned(bias_sum[:qk_width]),
        owned(bias_sum[qk_width:]),
        grad_out,
        owned(sums[width : 2 * width]),
        grad_gate,
        grad_up,
        grad_down,
    )


def solution(mesh):
    whole = ("ctx", "wshard")
    rows, columns, flat = P(whole, None), P(None, whole), P(whole)
    tokens = P("wshard", "ctx", None)
    return jax.shard_map(
        on_device,
        mesh=mesh,
        in_specs=(tokens, tokens, P("wshard", None), flat, rows, flat, columns, flat, rows, rows, rows),
        out_specs=(tokens, tokens, flat, rows, flat, flat, columns, flat, rows, rows, rows),
        check_vma=False,
    )
```

time: 2580 us -> 830 us (0.32)
  waiting for transfers between devices: 2130 us -> 362 us
  starting transfers between devices: 5.52 us -> 181 us
  matrix products: 237 us -> 89.3 us
  blocking collectives: 92.8 us -> 0 us
  local copies, waits for them, and re-layouts: 53.9 us -> 112 us
  other arithmetic: 35.9 us -> 73.8 us
    reduce_scatter x4 -> x0, waiting for transfers between devices: 998 us -> none  [the longest x1 470 us: on_device(): lax.psum_scatter(contract_rows(normed_two, up_grad_b), ('ctx', 'wshard'),...]
    all_gather x7 -> x0, waiting for transfers between devices: 606 us -> none  [the longest x1 163 us: on_device(): lax.all_gather(w_gate, ('ctx', 'wshard'), axis=0, tiled=True)]
    unnamed x13 -> x0, waiting for transfers between devices: 471 us -> none
    ppermute x0 -> x161, waiting for transfers between devices: none -> 362 us  [the longest x146 361 us: chip_swap(): return lax.ppermute(x, 'ctx', [(i, i ^ flip) for i in range(count)])]
    ppermute x0 -> x161, starting transfers between devices: none -> 181 us  [the longest x146 178 us: chip_swap(): return lax.ppermute(x, 'ctx', [(i, i ^ flip) for i in range(count)])]
    dot_general x43 -> x18, matrix products: 237 us -> 81.9 us  [the longest x13 62.1 us: dot(): lax.dot_general(left, right, (((left_axis,), (right_axis,)), ((), ())), p...]
    unnamed x2 -> x0, blocking collectives: 92.8 us -> none
    all_to_all x1 -> x0, waiting for transfers between devices: 56.4 us -> none  [sum_at_owner(): lax.all_to_all(tiles, axis, split_axis=0, concat_axis=0, tiled=True)]
  transfers between devices with their start and end apart: 13 -> 161, of which waited for: 12 -> 88; matrix products, arithmetic and copies ran while one was open for 10% -> 23% of each run, Pallas kernels for 0% -> 0%
where the time goes in v1:
time: 830 us; the launch traced here: 822 us
  waiting for transfers between devices  362 us (44%)
  starting transfers between devices  181 us (22%)
  local copies, waits for them, and re-layouts  112 us (13%)
  matrix products  89.3 us (11%)
  other arithmetic  73.8 us (9%)
    ppermute x146, waiting for transfers between devices, chip_swap(): return lax.ppermute(x, 'ctx', [(i, i ^ flip) for i in range(count)])  361 us
    ppermute x146, starting transfers between devices, chip_swap(): return lax.ppermute(x, 'ctx', [(i, i ^ flip) for i in range(count)])  178 us
    dot_general x13, matrix products, dot(): lax.dot_general(left, right, (((left_axis,), (right_axis,)), ((), ())), p...  62.1 us
    unnamed x253, local copies, waits for them, and re-layouts  29.9 us
    convert_element_type x6, local copies, waits for them, and re-layouts, to_columns(): return x.reshape(rows_dev, ff).astype(f32)  16.7 us
  transfers between devices with their start and end apart: 161, of which 88 were waited for; matrix products, arithmetic and copies ran while one was open for 23% of the time, Pallas kernels for 0%

profile of v1, /device:TPU:0, one launch (start us, length us, event | category | flops | bytes accessed | tf_op | source)
XLA Modules:
  0.0 822.5 jit_solution(9522408080097883423)
XLA Ops:
  32.9 3.5 collective-permute-done.2
  64.1 4.8 collective-permute-done.78
  106.3 3.3 collective-permute-done.38
  110.5 4.0 collective-permute-done.8
  117.5 5.2 collective-permute-done.16
  123.9 3.7 collective-permute-done.12
  133.5 3.2 collective-permute-done.35
  144.2 24.7 %collective-permute-done.39 = bf16[2,2,32,768]{3,2,1,0:T(8,128)(2,1)S(1)} collective-permute-done((bf16[2,2,32,768]{3,2,1,0:T(8,128)(2,1)S(1)}, bf16[2,2,32,768]{3,2,1,0:T(8,128)(2,1)S(1)}, u32[]{:S(2)}, u32[]{:S(2)}) %collective-permute-start.39) | collective-permute-done | bytes 196640 | tf_op jit(solution)/shard_map/ppermute | solution.py:25
  177.9 27.2 %collective-permute-done.13 = bf16[2,2,32,1024]{3,2,1,0:T(8,128)(2,1)S(1)} collective-permute-done((bf16[2,2,32,1024]{3,2,1,0:T(8,128)(2,1)S(1)}, bf16[2,2,32,1024]{3,2,1,0:T(8,128)(2,1)S(1)}, u32[]{:S(2)}, u32[]{:S(2)}) %collective-permute-start.13) | collective-permute-done | bytes 262176 | tf_op jit(solution)/shard_map/ppermute | solution.py:25
  206.2 4.2 collective-permute-done.36
  212.9 8.5 %collective-permute-done.40 = bf16[2,2,2,32,768]{4,3,2,1,0:T(8,128)(2,1)S(1)} collective-permute-done((bf16[2,2,2,32,768]{4,3,2,1,0:T(8,128)(2,1)S(1)}, bf16[2,2,2,32,768]{4,3,2,1,0:T(8,128)(2,1)S(1)}, u32[]{:S(2)}, u32[]{:S(2)}) %collective-permute-start.40) | collective-permute-done | bytes 393248 | tf_op jit(solution)/shard_map/ppermute | solution.py:25
  237.1 7.4 collective-permute-done.14
  276.9 3.8 collective-permute-done.27
  280.8 5.6 collective-permute-done.23
  287.5 7.4 fusion.152
  294.9 5.9 fusion.8
  300.9 4.2 fusion.157
  326.2 3.0 collective-permute-start.50
  329.3 3.3 collective-permute-done.47
  334.9 11.4 %collective-permute-done.50 = bf16[96,1536]{1,0:T(8,128)(2,1)S(1)} collective-permute-done((bf16[96,1536]{1,0:T(8,128)(2,1)S(1)}, bf16[96,1536]{1,0:T(8,128)(2,1)S(1)}, u32[]{:S(2)}, u32[]{:S(2)}) %collective-permute-start.50) | collective-permute-done | bytes 294944 | tf_op jit(solution)/shard_map/ppermute | solution.py:25
  347.7 11.1 %collective-permute-done.48 = bf16[192,1536]{1,0:T(8,128)(2,1)S(1)} collective-permute-done((bf16[192,1536]{1,0:T(8,128)(2,1)S(1)}, bf16[192,1536]{1,0:T(8,128)(2,1)S(1)}, u32[]{:S(2)}, u32[]{:S(2)}) %collective-permute-start.48) | collective-permute-done | bytes 589856 | tf_op jit(solution)/shard_map/ppermute | solution.py:25
  373.5 6.4 collective-permute-done.54
  383.0 11.3 %fusion.158 = f32[1024,2240]{0,1:T(8,128)} fusion(bf16[1024,1536]{1,0:T(8,128)(2,1)} %copy-done.71, bf16[1536,2240]{1,0:T(8,128)(2,1)S(1)} %bitcast.815), kind=kOutput, calls=%fused_computation.696 | convolution fusion | flops 7046430720 | bytes 19202048 | tf_op jit(solution)/shard_map/dot_general | solution.py:132
  394.3 10.7 %multiply_convert_fusion.1 = (bf16[1024,1120]{0,1:T(8,128)(2,1)}, bf16[1024,1120]{0,1:T(8,128)(2,1)}, bf16[1024,1120]{0,1:T(8,128)(2,1)}) fusion(f32[1024,2240]{0,1:T(8,128)} %fusion.158, bf16[1024,1536]{1,0:T(8,128)(2,1)} %constant_dynamic-update-slice_fusion.28, bf16[1120,1536]{1,0:T(8,128)(2,1)S(1)} %bitcast.831), kind=kOutput, calls=%fused_computation.19 | convolution fusion | flops 3540418560 | bytes 22642688 | tf_op jit(solution)/shard_map/dot_general | solution.py:132
  405.0 9.6 %convolution_convert_fusion.2 = bf16[1024,1536]{1,0:T(8,128)(2,1)S(1)} fusion(bf16[1536,2240]{1,0:T(8,128)(2,1)S(1)} %bitcast.816, bf16[1024,1120]{0,1:T(8,128)(2,1)} %get-tuple-element.32, bf16[1024,1120]{0,1:T(8,128)(2,1)} %get-tuple-element.31), kind=kOutput, calls=%fused_computation.23 | convolution fusion | flops 7057178624 | bytes 14614528 | tf_op jit(solution)/shard_map/dot_general | solution.py:132
  417.9 10.9 %convolution_convert_fusion = bf16[1536,2240]{0,1:T(8,128)(2,1)} fusion(bf16[1024,1536]{1,0:T(8,128)(2,1)S(1)} %copy-done.72, bf16[1024,1120]{0,1:T(8,128)(2,1)} %get-tuple-element.32, bf16[1024,1120]{0,1:T(8,128)(2,1)S(1)} %copy-done.88), kind=kOutput, calls=%fused_computation.6 | convolution fusion | flops 7059046400 | bytes 14614528 | tf_op jit(solution)/shard_map/dot_general | solution.py:132
  428.8 4.6 convolution_convert_fusion.3
  433.5 7.4 convolution_convert_fusion.1
  448.2 10.2 %copy.224 = bf16[1536,2240]{1,0:T(8,128)(2,1)} copy(bf16[1536,2240]{0,1:T(8,128)(2,1)} %convolution_convert_fusion) | data formatting | bytes 13762560 | tf_op jit(solution)/shard_map/convert_element_type | solution.py:342
  466.2 3.6 collective-permute-done.66
  477.8 4.8 collective-permute-done.92
  483.8 3.4 collective-permute-done.74
  504.5 5.1 fusion.14
  509.7 5.8 fusion.2
  557.4 3.4 collective-permute-done.112
  572.0 13.0 %collective-permute-done.104 = bf16[2,2,32,256]{3,2,1,0:T(8,128)(2,1)S(1)} collective-permute-done((bf16[2,2,32,256]{3,2,1,0:T(8,128)(2,1)S(1)}, bf16[2,2,32,256]{3,2,1,0:T(8,128)(2,1)S(1)}, u32[]{:S(2)}, u32[]{:S(2)}) %collective-permute-start.104) | collective-permute-done | bytes 65568 | tf_op jit(solution)/shard_map/ppermute | solution.py:25
  587.6 13.4 %collective-permute-done.105 = bf16[1,2,32,256]{3,2,1,0:T(8,128)(2,1)S(1)} collective-permute-done((bf16[1,2,32,256]{3,2,1,0:T(8,128)(2,1)S(1)}, bf16[1,2,32,256]{3,2,1,0:T(8,128)(2,1)S(1)}, u32[]{:S(2)}, u32[]{:S(2)}) %collective-permute-start.105) | collective-permute-done | bytes 32800 | tf_op jit(solution)/shard_map/ppermute | solution.py:25
  603.9 3.1 collective-permute-done.121
  636.7 3.0 fusion.71
  642.8 3.6 collective-permute-done.144
  647.1 4.7 collective-permute-done.140
  692.9 2.9 fusion.4
  698.3 3.7 collective-permute-done.109
  702.6 34.2 %collective-permute-done.110 = f32[40,128]{1,0:T(8,128)S(1)} collective-permute-done((f32[40,128]{1,0:T(8,128)S(1)}, f32[40,128]{1,0:T(8,128)S(1)}, u32[]{:S(2)}, u32[]{:S(2)}) %collective-permute-start.110) | collective-permute-done | bytes 20512 | tf_op jit(solution)/shard_map/ppermute | solution.py:25
  739.2 36.6 %collective-permute-done.111 = f32[40,128]{1,0:T(8,128)S(1)} collective-permute-done((f32[40,128]{1,0:T(8,128)S(1)}, f32[40,128]{1,0:T(8,128)S(1)}, u32[]{:S(2)}, u32[]{:S(2)}) %collective-permute-start.111) | collective-permute-done | bytes 20512 | tf_op jit(solution)/shard_map/ppermute | solution.py:25
  795.8 4.7 collective-permute-done.157
  810.8 3.1 reshape.795
  819.2 3.1 reshape.796
  (961 shorter events, 436.3 us)
Async XLA Ops:
  2.3 48.4 %collective-permute-start.32 = (bf16[48,768]{1,0:T(8,128)(2,1)}, bf16[48,768]{1,0:T(8,128)(2,1)}, u32[]{:S(2)}, u32[]{:S(2)}) collective-permute-start(bf16[48,768]{1,0:T(8,128)(2,1)} %dynamic-slice_bitcast_fusion.25), channel_id=1, source_target_pairs={{0,1},{1,0},{2,3},{3,2},{4,5},{5,4},{6,7},{7,6},{8,9},{9,8},{10,11... | collective-permute-start | bytes 221192 | tf_op jit(solution)/shard_map/ppermute | solution.py:20
  2.7 23.1 %collective-permute-start.19 = (s32[4]{0:T(128)}, s32[4]{0:T(128)}, u32[]{:S(2)}, u32[]{:S(2)}) collective-permute-start(s32[4]{0:T(128)} %bitcast.905), channel_id=1, source_target_pairs={{0,1},{1,0},{2,3},{3,2},{4,5},{5,4},{6,7},{7,6},{8,9},{9,8},{10,11... | collective-permute-start | bytes 56 | tf_op jit(solution)/shard_map/ppermute | solution.py:20
  4.1 28.0 %collective-permute-start.1 = (bf16[160]{0:T(256)(128)(2,1)}, bf16[160]{0:T(256)(128)(2,1)}, u32[]{:S(2)}, u32[]{:S(2)}) collective-permute-start(bf16[160]{0:T(256)(128)(2,1)} %pad_maximum_fusion.73), channel_id=1, source_target_pairs={{0,1},{1,0},{2,3},{3,2},{4,5},{5,4},{6,7},{7,6},{8,9},{9,8},{10,11... | collective-permute-start | bytes 968 | tf_op jit(solution)/shard_map/ppermute | solution.py:20
  4.5 124.4 %collective-permute-start = (bf16[128,1536]{1,0:T(8,128)(2,1)}, bf16[128,1536]{1,0:T(8,128)(2,1)S(1)}, u32[]{:S(2)}, u32[]{:S(2)}) collective-permute-start(bf16[128,1536]{1,0:T(8,128)(2,1)} %bitcast.825), channel_id=1, source_target_pairs={{0,1},{1,0},{2,3},{3,2},{4,5},{5,4},{6,7},{7,6},{8,9},{9,8},{10,11... | collective-permute-start | bytes 1179656 | tf_op jit(solution)/shard_map/ppermute | solution.py:20
  8.2 48.2 %collective-permute-start.6 = (bf16[48,1024]{1,0:T(8,128)(2,1)}, bf16[48,1024]{1,0:T(8,128)(2,1)}, u32[]{:S(2)}, u32[]{:S(2)}) collective-permute-start(bf16[48,1024]{1,0:T(8,128)(2,1)} %pad_maximum_fusion.59), channel_id=1, source_target_pairs={{0,1},{1,0},{2,3},{3,2},{4,5},{5,4},{6,7},{7,6},{8,9},{9,8},{10,11... | collective-permute-start | bytes 294920 | tf_op jit(solution)/shard_map/ppermute | solution.py:20
  25.9 51.5 %collective-permute-start.55 = (bf16[48,2240]{1,0:T(8,128)(2,1)}, bf16[48,2240]{1,0:T(8,128)(2,1)}, u32[]{:S(2)}, u32[]{:S(2)}) collective-permute-start(bf16[48,2240]{1,0:T(8,128)(2,1)} %get-tuple-element.68), channel_id=1, source_target_pairs={{0,2},{2,0},{4,6},{6,4},{8,10},{10,8},{12,14},{14,12},{16,18},{18,... | collective-permute-start | bytes 645128 | tf_op jit(solution)/shard_map/ppermute | solution.py:25
  48.5 32.5 %collective-permute-start.56 = (bf16[48,2240]{1,0:T(8,128)(2,1)}, bf16[48,2240]{1,0:T(8,128)(2,1)}, u32[]{:S(2)}, u32[]{:S(2)}) collective-permute-start(bf16[48,2240]{1,0:T(8,128)(2,1)} %get-tuple-element.69), channel_id=1, source_target_pairs={{0,4},{2,6},{4,0},{6,2},{8,12},{10,14},{12,8},{14,10},{16,20},{18,... | collective-permute-start | bytes 645128 | tf_op jit(solution)/shard_map/ppermute | solution.py:25
  85.2 136.3 %collective-permute-start.64 = (bf16[280,1536]{1,0:T(8,128)(2,1)S(1)}, bf16[280,1536]{1,0:T(8,128)(2,1)S(1)}, u32[]{:S(2)}, u32[]{:S(2)}) collective-permute-start(bf16[280,1536]{1,0:T(8,128)(2,1)S(1)} %copy-done.44), channel_id=1, source_target_pairs={{0,1},{1,0},{2,3},{3,2},{4,5},{5,4},{6,7},{7,6},{8,9},{9,8},{10,11... | collective-permute-start | bytes 2580488 | tf_op jit(solution)/shard_map/ppermute | solution.py:20
  86.2 28.6 %collective-permute-start.82 = (bf16[64,1536]{1,0:T(8,128)(2,1)S(1)}, bf16[64,1536]{1,0:T(8,128)(2,1)S(1)}, u32[]{:S(2)}, u32[]{:S(2)}) collective-permute-start(bf16[64,1536]{1,0:T(8,128)(2,1)S(1)} %pad_maximum_fusion.48), channel_id=1, source_target_pairs={{0,2},{2,0},{4,6},{6,4},{8,10},{10,8},{12,14},{14,12},{16,18},{18,... | collective-permute-start | bytes 589832 | tf_op jit(solution)/shard_map/ppermute | solution.py:25
  105.9 32.5 %collective-permute-start.76 = (bf16[96,1536]{1,0:T(8,128)(2,1)S(1)}, bf16[96,1536]{1,0:T(8,128)(2,1)S(1)}, u32[]{:S(2)}, u32[]{:S(2)}) collective-permute-start(bf16[96,1536]{1,0:T(8,128)(2,1)S(1)} %pad_maximum_fusion.32), channel_id=1, source_target_pairs={{0,4},{2,6},{4,0},{6,2},{8,12},{10,14},{12,8},{14,10},{16,20},{18,... | collective-permute-start | bytes 884744 | tf_op jit(solution)/shard_map/ppermute | solution.py:25
  114.5 24.9 %collective-permute-start.79 = (bf16[96,1536]{1,0:T(8,128)(2,1)S(1)}, bf16[96,1536]{1,0:T(8,128)(2,1)S(1)}, u32[]{:S(2)}, u32[]{:S(2)}) collective-permute-start(bf16[96,1536]{1,0:T(8,128)(2,1)S(1)} %pad_maximum_fusion.33), channel_id=1, source_target_pairs={{0,8},{2,10},{4,12},{6,14},{8,0},{10,2},{12,4},{14,6},{16,24},{18,... | collective-permute-start | bytes 884744 | tf_op jit(solution)/shard_map/ppermute | solution.py:25
  127.6 190.3 %collective-permute-start.62 = (bf16[8,48,2240]{2,1,0:T(8,128)(2,1)}, bf16[8,48,2240]{2,1,0:T(8,128)(2,1)}, u32[]{:S(2)}, u32[]{:S(2)}) collective-permute-start(bf16[8,48,2240]{2,1,0:T(8,128)(2,1)} %dynamic-slice_dynamic-update-slice_fusion.9), channel_id=1, source_target_pairs={{0,16},{2,18},{4,20},{6,22},{8,24},{10,26},{12,28},{14,30},{16,0},... | collective-permute-start | bytes 5160968 | tf_op jit(solution)/shard_map/ppermute | solution.py:25
  138.4 30.5 %collective-permute-start.39 = (bf16[2,2,32,768]{3,2,1,0:T(8,128)(2,1)S(1)}, bf16[2,2,32,768]{3,2,1,0:T(8,128)(2,1)S(1)}, u32[]{:S(2)}, u32[]{:S(2)}) collective-permute-start(bf16[2,2,32,768]{3,2,1,0:T(8,128)(2,1)S(1)} %pad_maximum_fusion.45), channel_id=1, source_target_pairs={{0,8},{2,10},{4,12},{6,14},{8,0},{10,2},{12,4},{14,6},{16,24},{18,... | collective-permute-start | bytes 589832 | tf_op jit(solution)/shard_map/ppermute | solution.py:25
  139.4 30.4 %collective-permute-start.9 = (bf16[2,2,32,1024]{3,2,0,1:T(8,128)(2,1)S(1)}, bf16[2,2,32,1024]{3,2,0,1:T(8,128)(2,1)S(1)}, u32[]{:S(2)}, u32[]{:S(2)}) collective-permute-start(bf16[2,2,32,1024]{3,2,0,1:T(8,128)(2,1)S(1)} %pad_maximum_fusion.35), channel_id=1, source_target_pairs={{0,4},{2,6},{4,0},{6,2},{8,12},{10,14},{12,8},{14,10},{16,20},{18,... | collective-permute-start | bytes 786440 | tf_op jit(solution)/shard_map/ppermute | solution.py:25
  142.4 167.8 %collective-permute-start.83 = (bf16[128,1536]{1,0:T(8,128)(2,1)}, bf16[128,1536]{1,0:T(8,128)(2,1)}, u32[]{:S(2)}, u32[]{:S(2)}) collective-permute-start(bf16[128,1536]{1,0:T(8,128)(2,1)} %pad_maximum_fusion.29), channel_id=1, source_target_pairs={{0,4},{2,6},{4,0},{6,2},{8,12},{10,14},{12,8},{14,10},{16,20},{18,... | collective-permute-start | bytes 1179656 | tf_op jit(solution)/shard_map/ppermute | solution.py:25
  169.8 35.2 %collective-permute-start.13 = (bf16[2,2,32,1024]{3,2,1,0:T(8,128)(2,1)S(1)}, bf16[2,2,32,1024]{3,2,1,0:T(8,128)(2,1)S(1)}, u32[]{:S(2)}, u32[]{:S(2)}) collective-permute-start(bf16[2,2,32,1024]{3,2,1,0:T(8,128)(2,1)S(1)} %pad_maximum_fusion.36), channel_id=1, source_target_pairs={{0,8},{2,10},{4,12},{6,14},{8,0},{10,2},{12,4},{14,6},{16,24},{18,... | collective-permute-start | bytes 786440 | tf_op jit(solution)/shard_map/ppermute | solution.py:25
  175.3 35.2 %collective-permute-start.36 = (bf16[2,2,2,32,768]{4,3,1,0,2:T(8,128)(2,1)S(1)}, bf16[2,2,2,32,768]{4,3,1,0,2:T(8,128)(2,1)S(1)}, u32[]{:S(2)}, u32[]{:S(2)}) collective-permute-start(bf16[2,2,2,32,768]{4,3,1,0,2:T(8,128)(2,1)S(1)} %pad_maximum_fusion.25), channel_id=1, source_target_pairs={{0,8},{2,10},{4,12},{6,14},{8,0},{10,2},{12,4},{14,6},{16,24},{18,... | collective-permute-start | bytes 1179656 | tf_op jit(solution)/shard_map/ppermute | solution.py:25
  212.8 14.9 %collective-permute-start.77 = (bf16[192,1536]{1,0:T(8,128)(2,1)S(1)}, bf16[192,1536]{1,0:T(8,128)(2,1)S(1)}, u32[]{:S(2)}, u32[]{:S(2)}) collective-permute-start(bf16[192,1536]{1,0:T(8,128)(2,1)S(1)} %pad_maximum_fusion.16), channel_id=1, source_target_pairs={{0,8},{2,10},{4,12},{6,14},{8,0},{10,2},{12,4},{14,6},{16,24},{18,... | collective-permute-start | bytes 1769480 | tf_op jit(solution)/shard_map/ppermute | solution.py:25
  221.5 14.7 %collective-permute-start.10 = (bf16[2,2,2,32,1024]{4,3,1,0,2:T(8,128)(2,1)S(1)}, bf16[2,2,2,32,1024]{4,3,1,0,2:T(8,128)(2,1)S(1)}, u32[]{:S(2)}, u32[]{:S(2)}) collective-permute-start(bf16[2,2,2,32,1024]{4,3,1,0,2:T(8,128)(2,1)S(1)} %pad_maximum_fusion.19), channel_id=1, source_target_pairs={{0,8},{2,10},{4,12},{6,14},{8,0},{10,2},{12,4},{14,6},{16,24},{18,... | collective-permute-start | bytes 1572872 | tf_op jit(solution)/shard_map/ppermute | solution.py:25
  275.6 86.1 %collective-permute-start.65 = (bf16[560,1536]{1,0:T(8,128)(2,1)}, bf16[560,1536]{1,0:T(8,128)(2,1)}, u32[]{:S(2)}, u32[]{:S(2)}) collective-permute-start(bf16[560,1536]{1,0:T(8,128)(2,1)} %bitcast.136), channel_id=1, source_target_pairs={{0,16},{2,18},{4,20},{6,22},{8,24},{10,26},{12,28},{14,30},{16,0},... | collective-permute-start | bytes 5160968 | tf_op jit(solution)/shard_map/ppermute | solution.py:25
  324.8 55.1 %collective-permute-start.63 = (bf16[2,8,48,2240]{3,2,1,0:T(8,128)(2,1)S(1)}, bf16[2,8,48,2240]{3,2,1,0:T(8,128)(2,1)S(1)}, u32[]{:S(2)}, u32[]{:S(2)}) collective-permute-start(bf16[2,8,48,2240]{3,2,1,0:T(8,128)(2,1)S(1)} %pad_maximum_fusion.1), channel_id=1, source_target_pairs={{0,1},{1,0},{2,3},{3,2},{4,5},{5,4},{6,7},{7,6},{8,9},{9,8},{10,11... | collective-permute-start | bytes 10321928 | tf_op jit(solution)/shard_map/ppermute | solution.py:20
  326.2 20.0 %collective-permute-start.50 = (bf16[96,1536]{1,0:T(8,128)(2,1)S(1)}, bf16[96,1536]{1,0:T(8,128)(2,1)S(1)}, u32[]{:S(2)}, u32[]{:S(2)}) collective-permute-start(bf16[96,1536]{1,0:T(8,128)(2,1)S(1)} %pad_maximum_fusion.31), channel_id=1, source_target_pairs={{0,8},{2,10},{4,12},{6,14},{8,0},{10,2},{12,4},{14,6},{16,24},{18,... | collective-permute-start | bytes 884744 | tf_op jit(solution)/shard_map/ppermute | solution.py:25
  332.6 26.2 %collective-permute-start.48 = (bf16[192,1536]{1,0:T(8,128)(2,1)S(1)}, bf16[192,1536]{1,0:T(8,128)(2,1)S(1)}, u32[]{:S(2)}, u32[]{:S(2)}) collective-permute-start(bf16[192,1536]{1,0:T(8,128)(2,1)S(1)} %pad_maximum_fusion.14), channel_id=1, source_target_pairs={{0,8},{2,10},{4,12},{6,14},{8,0},{10,2},{12,4},{14,6},{16,24},{18,... | collective-permute-start | bytes 1769480 | tf_op jit(solution)/shard_map/ppermute | solution.py:25
  346.3 15.2 %collective-permute-start.51 = (bf16[192,1536]{1,0:T(8,128)(2,1)S(1)}, bf16[192,1536]{1,0:T(8,128)(2,1)S(1)}, u32[]{:S(2)}, u32[]{:S(2)}) collective-permute-start(bf16[192,1536]{1,0:T(8,128)(2,1)S(1)} %pad_maximum_fusion.15), channel_id=1, source_target_pairs={{0,2},{2,0},{4,6},{6,4},{8,10},{10,8},{12,14},{14,12},{16,18},{18,... | collective-permute-start | bytes 1769480 | tf_op jit(solution)/shard_map/ppermute | solution.py:25
  440.9 17.5 %collective-permute-start.90 = (bf16[128,1536]{1,0:T(8,128)(2,1)}, bf16[128,1536]{1,0:T(8,128)(2,1)}, u32[]{:S(2)}, u32[]{:S(2)}) collective-permute-start(bf16[128,1536]{1,0:T(8,128)(2,1)} %slice.694), channel_id=1, source_target_pairs={{0,4},{2,6},{4,0},{6,2},{8,12},{10,14},{12,8},{14,10},{16,20},{18,... | collective-permute-start | bytes 1179656 | tf_op jit(solution)/shard_map/ppermute | solution.py:25
  442.3 20.6 %collective-permute-start.84 = (bf16[192,1536]{1,0:T(8,128)(2,1)}, bf16[192,1536]{1,0:T(8,128)(2,1)}, u32[]{:S(2)}, u32[]{:S(2)}) collective-permute-start(bf16[192,1536]{1,0:T(8,128)(2,1)} %get-tuple-element.42), channel_id=1, source_target_pairs={{0,8},{2,10},{4,12},{6,14},{8,0},{10,2},{12,4},{14,6},{16,24},{18,... | collective-permute-start | bytes 1769480 | tf_op jit(solution)/shard_map/ppermute | solution.py:25
  442.8 20.9 %collective-permute-start.87 = (bf16[192,1536]{1,0:T(8,128)(2,1)}, bf16[192,1536]{1,0:T(8,128)(2,1)}, u32[]{:S(2)}, u32[]{:S(2)}) collective-permute-start(bf16[192,1536]{1,0:T(8,128)(2,1)} %get-tuple-element.43), channel_id=1, source_target_pairs={{0,2},{2,0},{4,6},{6,4},{8,10},{10,8},{12,14},{14,12},{16,18},{18,... | collective-permute-start | bytes 1769480 | tf_op jit(solution)/shard_map/ppermute | solution.py:25
  444.9 15.5 %collective-permute-start.72 = (bf16[128,1536]{1,0:T(8,128)(2,1)}, bf16[128,1536]{1,0:T(8,128)(2,1)}, u32[]{:S(2)}, u32[]{:S(2)}) collective-permute-start(bf16[128,1536]{1,0:T(8,128)(2,1)} %slice.676), channel_id=1, source_target_pairs={{0,4},{2,6},{4,0},{6,2},{8,12},{10,14},{12,8},{14,10},{16,20},{18,... | collective-permute-start | bytes 1179656 | tf_op jit(solution)/shard_map/ppermute | solution.py:25
  446.6 23.1 %collective-permute-start.66 = (bf16[192,1536]{1,0:T(8,128)(2,1)}, bf16[192,1536]{1,0:T(8,128)(2,1)}, u32[]{:S(2)}, u32[]{:S(2)}) collective-permute-start(bf16[192,1536]{1,0:T(8,128)(2,1)} %get-tuple-element.46), channel_id=1, source_target_pairs={{0,8},{2,10},{4,12},{6,14},{8,0},{10,2},{12,4},{14,6},{16,24},{18,... | collective-permute-start | bytes 1769480 | tf_op jit(solution)/shard_map/ppermute | solution.py:25
  465.6 21.6 %collective-permute-start.88 = (bf16[96,1536]{1,0:T(8,128)(2,1)S(1)}, bf16[96,1536]{1,0:T(8,128)(2,1)S(1)}, u32[]{:S(2)}, u32[]{:S(2)}) collective-permute-start(bf16[96,1536]{1,0:T(8,128)(2,1)S(1)} %slice.690), channel_id=1, source_target_pairs={{0,8},{2,10},{4,12},{6,14},{8,0},{10,2},{12,4},{14,6},{16,24},{18,... | collective-permute-start | bytes 884744 | tf_op jit(solution)/shard_map/ppermute | solution.py:25
  469.8 19.0 %collective-permute-start.85 = (bf16[96,1536]{1,0:T(8,128)(2,1)S(1)}, bf16[96,1536]{1,0:T(8,128)(2,1)S(1)}, u32[]{:S(2)}, u32[]{:S(2)}) collective-permute-start(bf16[96,1536]{1,0:T(8,128)(2,1)S(1)} %slice.684), channel_id=1, source_target_pairs={{0,4},{2,6},{4,0},{6,2},{8,12},{10,14},{12,8},{14,10},{16,20},{18,... | collective-permute-start | bytes 884744 | tf_op jit(solution)/shard_map/ppermute | solution.py:25
  473.7 16.0 %collective-permute-start.70 = (bf16[96,1536]{1,0:T(8,128)(2,1)S(1)}, bf16[96,1536]{1,0:T(8,128)(2,1)S(1)}, u32[]{:S(2)}, u32[]{:S(2)}) collective-permute-start(bf16[96,1536]{1,0:T(8,128)(2,1)S(1)} %slice.672), channel_id=1, source_target_pairs={{0,8},{2,10},{4,12},{6,14},{8,0},{10,2},{12,4},{14,6},{16,24},{18,... | collective-permute-start | bytes 884744 | tf_op jit(solution)/shard_map/ppermute | solution.py:25
  475.0 15.5 %collective-permute-start.67 = (bf16[96,1536]{1,0:T(8,128)(2,1)S(1)}, bf16[96,1536]{1,0:T(8,128)(2,1)S(1)}, u32[]{:S(2)}, u32[]{:S(2)}) collective-permute-start(bf16[96,1536]{1,0:T(8,128)(2,1)S(1)} %slice.666), channel_id=1, source_target_pairs={{0,4},{2,6},{4,0},{6,2},{8,12},{10,14},{12,8},{14,10},{16,20},{18,... | collective-permute-start | bytes 884744 | tf_op jit(solution)/shard_map/ppermute | solution.py:25
  499.4 193.5 %collective-permute-start.150 = (bf16[2,8,48,2240]{3,2,1,0:T(8,128)(2,1)}, bf16[2,8,48,2240]{3,2,1,0:T(8,128)(2,1)}, u32[]{:S(2)}, u32[]{:S(2)}) collective-permute-start(bf16[2,8,48,2240]{3,2,1,0:T(8,128)(2,1)} %dynamic-slice_bitcast_fusion), channel_id=1, source_target_pairs={{0,1},{1,0},{2,3},{3,2},{4,5},{5,4},{6,7},{7,6},{8,9},{9,8},{10,11... | collective-permute-start | bytes 10321928 | tf_op jit(solution)/shard_map/ppermute | solution.py:20
  501.9 43.7 %collective-permute-start.159 = (bf16[2,280,1536]{2,1,0:T(8,128)(2,1)}, bf16[2,280,1536]{2,1,0:T(8,128)(2,1)}, u32[]{:S(2)}, u32[]{:S(2)}) collective-permute-start(bf16[2,280,1536]{2,1,0:T(8,128)(2,1)} %dynamic-slice_bitcast_fusion.2), channel_id=1, source_target_pairs={{0,1},{1,0},{2,3},{3,2},{4,5},{5,4},{6,7},{7,6},{8,9},{9,8},{10,11... | collective-permute-start | bytes 5160968 | tf_op jit(solution)/shard_map/ppermute | solution.py:20
  533.6 17.6 %collective-permute-start.98 = (bf16[8,2,48,256]{3,2,1,0:T(8,128)(2,1)}, bf16[8,2,48,256]{3,2,1,0:T(8,128)(2,1)}, u32[]{:S(2)}, u32[]{:S(2)}) collective-permute-start(bf16[8,2,48,256]{3,2,1,0:T(8,128)(2,1)} %slice.714), channel_id=1, source_target_pairs={{0,2},{2,0},{4,6},{6,4},{8,10},{10,8},{12,14},{14,12},{16,18},{18,... | collective-permute-start | bytes 1179656 | tf_op jit(solution)/shard_map/ppermute | solution.py:25
  536.1 17.1 %collective-permute-start.94 = (bf16[8,2,48,256]{3,2,0,1:T(8,128)(2,1)}, bf16[8,2,48,256]{3,2,0,1:T(8,128)(2,1)}, u32[]{:S(2)}, u32[]{:S(2)}) collective-permute-start(bf16[8,2,48,256]{3,2,0,1:T(8,128)(2,1)} %slice.704), channel_id=1, source_target_pairs={{0,8},{2,10},{4,12},{6,14},{8,0},{10,2},{12,4},{14,6},{16,24},{18,... | collective-permute-start | bytes 1179656 | tf_op jit(solution)/shard_map/ppermute | solution.py:25
  562.6 124.2 %collective-permute-start.160 = (bf16[280,1536]{1,0:T(8,128)(2,1)}, bf16[280,1536]{1,0:T(8,128)(2,1)}, u32[]{:S(2)}, u32[]{:S(2)}) collective-permute-start(bf16[280,1536]{1,0:T(8,128)(2,1)} %dynamic-slice_bitcast_fusion.3), channel_id=1, source_target_pairs={{0,16},{2,18},{4,20},{6,22},{8,24},{10,26},{12,28},{14,30},{16,0},... | collective-permute-start | bytes 2580488 | tf_op jit(solution)/shard_map/ppermute | solution.py:25
  566.2 18.8 %collective-permute-start.104 = (bf16[2,2,32,256]{3,2,1,0:T(8,128)(2,1)S(1)}, bf16[2,2,32,256]{3,2,1,0:T(8,128)(2,1)S(1)}, u32[]{:S(2)}, u32[]{:S(2)}) collective-permute-start(bf16[2,2,32,256]{3,2,1,0:T(8,128)(2,1)S(1)} %slice.726), channel_id=1, source_target_pairs={{0,8},{2,10},{4,12},{6,14},{8,0},{10,2},{12,4},{14,6},{16,24},{18,... | collective-permute-start | bytes 196616 | tf_op jit(solution)/shard_map/ppermute | solution.py:25
  569.3 32.9 %collective-permute-start.99 = (bf16[4,2,48,256]{3,2,1,0:T(8,128)(2,1)S(1)}, bf16[4,2,48,256]{3,2,1,0:T(8,128)(2,1)S(1)}, u32[]{:S(2)}, u32[]{:S(2)}) collective-permute-start(bf16[4,2,48,256]{3,2,1,0:T(8,128)(2,1)S(1)} %slice.716), channel_id=1, source_target_pairs={{0,8},{2,10},{4,12},{6,14},{8,0},{10,2},{12,4},{14,6},{16,24},{18,... | collective-permute-start | bytes 589832 | tf_op jit(solution)/shard_map/ppermute | solution.py:25
  570.4 32.0 %collective-permute-start.95 = (bf16[4,2,48,256]{3,2,0,1:T(8,128)(2,1)S(1)}, bf16[4,2,48,256]{3,2,0,1:T(8,128)(2,1)S(1)}, u32[]{:S(2)}, u32[]{:S(2)}) collective-permute-start(bf16[4,2,48,256]{3,2,0,1:T(8,128)(2,1)S(1)} %slice.706), channel_id=1, source_target_pairs={{0,4},{2,6},{4,0},{6,2},{8,12},{10,14},{12,8},{14,10},{16,20},{18,... | collective-permute-start | bytes 589832 | tf_op jit(solution)/shard_map/ppermute | solution.py:25
  585.0 16.0 %collective-permute-start.105 = (bf16[1,2,32,256]{3,2,1,0:T(8,128)(2,1)S(1)}, bf16[1,2,32,256]{3,2,1,0:T(8,128)(2,1)S(1)}, u32[]{:S(2)}, u32[]{:S(2)}) collective-permute-start(bf16[1,2,32,256]{3,2,1,0:T(8,128)(2,1)S(1)} %slice.728), channel_id=1, source_target_pairs={{0,16},{2,18},{4,20},{6,22},{8,24},{10,26},{12,28},{14,30},{16,0},... | collective-permute-start | bytes 98312 | tf_op jit(solution)/shard_map/ppermute | solution.py:25
  630.8 21.4 %collective-permute-start.123 = (bf16[32,768]{1,0:T(8,128)(2,1)}, bf16[32,768]{1,0:T(8,128)(2,1)}, u32[]{:S(2)}, u32[]{:S(2)}) collective-permute-start(bf16[32,768]{1,0:T(8,128)(2,1)} %dynamic-slice_bitcast_fusion.32), channel_id=1, source_target_pairs={{0,16},{2,18},{4,20},{6,22},{8,24},{10,26},{12,28},{14,30},{16,0},... | collective-permute-start | bytes 147464 | tf_op jit(solution)/shard_map/ppermute | solution.py:25
  633.0 20.6 %collective-permute-start.119 = (bf16[32,768]{1,0:T(8,128)(2,1)}, bf16[32,768]{1,0:T(8,128)(2,1)}, u32[]{:S(2)}, u32[]{:S(2)}) collective-permute-start(bf16[32,768]{1,0:T(8,128)(2,1)} %dynamic-slice_bitcast_fusion.33), channel_id=1, source_target_pairs={{0,16},{2,18},{4,20},{6,22},{8,24},{10,26},{12,28},{14,30},{16,0},... | collective-permute-start | bytes 147464 | tf_op jit(solution)/shard_map/ppermute | solution.py:25
  652.2 37.4 %collective-permute-start.106 = (f32[128,1536]{1,0:T(8,128)S(1)}, f32[128,1536]{1,0:T(8,128)S(1)}, u32[]{:S(2)}, u32[]{:S(2)}) collective-permute-start(f32[128,1536]{1,0:T(8,128)S(1)} %slice.734), channel_id=1, source_target_pairs={{0,1},{1,0},{2,3},{3,2},{4,5},{5,4},{6,7},{7,6},{8,9},{9,8},{10,11... | collective-permute-start | bytes 2359304 | tf_op jit(solution)/shard_map/ppermute | solution.py:20
  695.9 81.6 %collective-permute-start.151 = (bf16[8,48,2240]{2,1,0:T(8,128)(2,1)S(1)}, bf16[8,48,2240]{2,1,0:T(8,128)(2,1)S(1)}, u32[]{:S(2)}, u32[]{:S(2)}) collective-permute-start(bf16[8,48,2240]{2,1,0:T(8,128)(2,1)S(1)} %dynamic-slice_bitcast_fusion.1), channel_id=1, source_target_pairs={{0,16},{2,18},{4,20},{6,22},{8,24},{10,26},{12,28},{14,30},{16,0},... | collective-permute-start | bytes 5160968 | tf_op jit(solution)/shard_map/ppermute | solution.py:25
  702.1 34.7 %collective-permute-start.110 = (f32[40,128]{1,0:T(8,128)S(1)}, f32[40,128]{1,0:T(8,128)S(1)}, u32[]{:S(2)}, u32[]{:S(2)}) collective-permute-start(f32[40,128]{1,0:T(8,128)S(1)} %add.690), channel_id=1, source_target_pairs={{0,8},{2,10},{4,12},{6,14},{8,0},{10,2},{12,4},{14,6},{16,24},{18,... | collective-permute-start | bytes 61448 | tf_op jit(solution)/shard_map/ppermute | solution.py:25
  736.8 39.0 %collective-permute-start.111 = (f32[40,128]{1,0:T(8,128)S(1)}, f32[40,128]{1,0:T(8,128)S(1)}, u32[]{:S(2)}, u32[]{:S(2)}) collective-permute-start(f32[40,128]{1,0:T(8,128)S(1)} %add.691), channel_id=1, source_target_pairs={{0,16},{2,18},{4,20},{6,22},{8,24},{10,26},{12,28},{14,30},{16,0},... | collective-permute-start | bytes 61448 | tf_op jit(solution)/shard_map/ppermute | solution.py:25
  (206 other events, 2475.6 us)

commit v2 on v1

v2 whole, which is shorter than its diff:
```python
import functools
import math

import jax
import jax.numpy as jnp
from jax import lax
from jax.experimental import pallas as pl
from jax.experimental.pallas import tpu as pltpu
from jax.sharding import PartitionSpec as P

H = 12
KVH = 2
HD = 128
EPSILON = 1e-06
ROPE_BASE = 1000000.0
ORDERS = ((0, 1, 2), (1, 2, 0), (2, 0, 1))
CHUNK = 256
NEVER = -1e30
SCALE = 1.0 / math.sqrt(HD)
bf16 = jnp.bfloat16
f32 = jnp.float32
VMEM = pl.BlockSpec(memory_space=pltpu.VMEM)
SMEM = pl.BlockSpec(memory_space=pltpu.SMEM)
BIG = pltpu.CompilerParams(vmem_limit_bytes=56 * 1024 * 1024)


def after(x, *others):
    return lax.optimization_barrier((x,) + others)[0]


def together(*groups):
    flat, tree = jax.tree.flatten(groups)
    return jax.tree.unflatten(tree, lax.optimization_barrier(flat))


def core_swap(x):
    return lax.ppermute(x, "wshard", [(0, 1), (1, 0)])


def chip_swap(x, flip):
    count = lax.axis_size("ctx")
    return lax.ppermute(x, "ctx", [(i, i ^ flip) for i in range(count)])


def cubes():
    count = lax.axis_size("ctx")
    return [list(range(i, i + 8)) for i in range(0, count, 8)]


def cube_exchange(x):
    return lax.all_to_all(
        x, "ctx", split_axis=0, concat_axis=0, tiled=True, axis_index_groups=cubes()
    )


def group_bits():
    return tuple(range(lax.axis_size("ctx").bit_length() - 4))


def member_bits():
    first = len(group_bits())
    return (first, first + 1, first + 2)


def group_lists():
    groups = lax.axis_size("ctx") // 8
    return [[g + groups * m for m in range(8)] for g in range(groups)]


def group_exchange(x):
    return lax.all_to_all(
        x, "ctx", split_axis=0, concat_axis=0, tiled=True, axis_index_groups=group_lists()
    )


def high_bits():
    return tuple(range(3, lax.axis_size("ctx").bit_length() - 1))


def my_bit(bit):
    return (lax.axis_index("ctx") >> bit) & 1


def gather_relative(x, bits):
    for bit in bits:
        x = jnp.concatenate([x, chip_swap(x, 1 << bit)], axis=0)
    return x


def gather_list(x, bits):
    found = [x]
    for bit in bits:
        found = found + [chip_swap(y, 1 << bit) for y in found]
    return found


def relative_flips(bits):
    flips = [0]
    for bit in bits:
        flips = flips + [f ^ (1 << bit) for f in flips]
    return flips


def sum_over(x, axis, bits):
    for at, bit in enumerate(bits):
        shape = x.shape
        x = x.reshape(shape[:axis] + (2, shape[axis] // 2) + shape[axis + 1 :])
        keep = lax.dynamic_index_in_dim(x, my_bit(bit), axis, keepdims=False)
        send = lax.dynamic_index_in_dim(x, 1 - my_bit(bit), axis, keepdims=False)
        x = keep.astype(f32) + chip_swap(send.astype(bf16), 1 << bit).astype(f32)
        if at < len(bits) - 1:
            x = x.astype(bf16)
    return jnp.squeeze(x, axis).astype(f32)


def sum_over_high(x, high):
    return sum_over(x, 0, tuple(reversed(high)))


def row_parts(rows):
    third = rows * 3 // 8
    return ((0, third), (third, 2 * third), (2 * third, rows))


def doubled(parts, bits):
    return [jnp.concatenate([x, chip_swap(x, 1 << bit)]) for x, bit in zip(parts, bits)]


def with_arrived(parts, bits):
    found = []
    for x, bit in zip(parts, bits):
        found.extend([x, chip_swap(x, 1 << bit)])
    return found


def both_halves(x, layout, bit):
    axis = layout.index(bit)
    keep = lax.dynamic_index_in_dim(x, my_bit(bit), axis, keepdims=False)
    send = lax.dynamic_index_in_dim(x, 1 - my_bit(bit), axis, keepdims=False)
    return keep, send


class Scatter:
    def __init__(self, parts, layout):
        self.parts = list(parts)
        self.layouts = [list(layout) for _ in self.parts]

    def split(self, bits):
        pairs = [both_halves(x, l, b) for x, l, b in zip(self.parts, self.layouts, bits)]
        for layout, bit in zip(self.layouts, bits):
            layout.remove(bit)
        return [k for k, _ in pairs], [s.astype(bf16) for _, s in pairs]

    def step(self, bits, kept=None, sent=None):
        if kept is None:
            kept, sent = self.split(bits)
        self.add(kept, [chip_swap(x, 1 << bit) for x, bit in zip(sent, bits)])

    def add(self, kept, arrived):
        self.parts = [k.astype(f32) + a.astype(f32) for k, a in zip(kept, arrived)]
        if self.layouts[0]:
            self.parts = [x.astype(bf16) for x in self.parts]


def dot(left, right, left_axis, right_axis):
    return lax.dot_general(
        left, right, (((left_axis,), (right_axis,)), ((), ())), preferred_element_type=f32
    )


def rms_back(grad_in, values, scale_rows, gain_row):
    weighted = grad_in * gain_row
    return scale_rows * weighted - values * scale_rows**3 * jnp.mean(
        weighted * values, axis=-1, keepdims=True
    )


def half_of(x, which, axis):
    size = x.shape[axis] // 2
    return lax.dynamic_slice_in_dim(x, which * size, size, axis)


def head_columns(x, core):
    q_width, kv_width = H * HD, KVH * HD
    return jnp.concatenate(
        [
            half_of(x[:, :q_width], core, 1),
            half_of(x[:, q_width : q_width + kv_width], core, 1),
            half_of(x[:, q_width + kv_width :], core, 1),
        ],
        axis=1,
    )


def by_core(mine, other, core):
    return jnp.stack([jnp.where(core == 0, mine, other), jnp.where(core == 0, other, mine)])


def order_weights_kernel(flips, extra_rows, where_ref, *refs):
    parts, out = refs[: 2 * len(flips)], refs[2 * len(flips)]
    chip, core = where_ref[0], where_ref[1]
    count, rows = parts[0].shape[0], out.shape[2]
    at = 0
    for p, part_flips in enumerate(flips):
        columns = parts[2 * p].shape[3]
        for k, flip in enumerate(part_flips):
            part = parts[2 * p + k // count]
            for h in range(2):
                out[chip ^ flip, core ^ h, :, at : at + columns] = part[k % count, h, :rows]
                if extra_rows and p == len(flips) - 1:
                    extra = part[k % count, h, rows:].astype(f32)[:1]
                    refs[-1][chip ^ flip, core ^ h] = extra
        at += columns


def order_weights(parts, flips, where):
    count, _, rows, _ = parts[0].shape
    columns = sum(p.shape[3] for p in parts[::2])
    extra = parts[-1].shape[2] > rows
    shapes = [jax.ShapeDtypeStruct((2 * count, 2, rows, columns), bf16)]
    if extra:
        shapes.append(jax.ShapeDtypeStruct((2 * count, 2, 1, parts[-1].shape[3]), f32))
    return pl.pallas_call(
        functools.partial(order_weights_kernel, flips, extra),
        out_shape=shapes,
        in_specs=[SMEM] + [VMEM] * len(parts),
        out_specs=[VMEM] * len(shapes),
        compiler_params=BIG,
        name="order_weights",
    )(where, *parts)


def order_rows_kernel(flips, where_ref, *refs):
    out = refs[-1]
    chip, core = where_ref[0], where_ref[1]
    group = chip % len(flips)
    for k, flip in enumerate(flips):
        out[:, group ^ flip, core] = refs[k][...]
        out[:, group ^ flip, 1 - core] = refs[len(flips) + k][...]


def order_rows(own, other, flips, where):
    members, rows, columns = own[0].shape
    groups = len(own)
    tile = columns // 2 if columns % 256 == 0 else columns
    source = pl.BlockSpec((1, rows, tile), lambda m, n: (m, 0, n))
    return pl.pallas_call(
        functools.partial(order_rows_kernel, flips),
        grid=(members, columns // tile),
        out_shape=jax.ShapeDtypeStruct((members, groups, 2, rows, columns), bf16),
        in_specs=[SMEM] + [source] * (2 * groups),
        out_specs=pl.BlockSpec((1, groups, 2, rows, tile), lambda m, n: (m, 0, 0, 0, n)),
        compiler_params=BIG,
        name="order_rows",
    )(where, *own, *other)


def order_tokens_kernel(flips, cuts, groups, where_ref, *refs):
    out = refs[-1]
    member = where_ref[0] // groups
    for p, (start, stop) in enumerate(cuts):
        for k, flip in enumerate(flips[p]):
            half = refs[2 * p + k // 4]
            out[member ^ (flip // groups), start:stop, :] = half[k % 4]


def order_tokens(halves, flips, cuts, groups, where):
    rows, width = cuts[-1][1], halves[0].shape[2]
    return pl.pallas_call(
        functools.partial(order_tokens_kernel, flips, cuts, groups),
        out_shape=jax.ShapeDtypeStruct((8, rows, width), bf16),
        in_specs=[SMEM] + [VMEM] * len(halves),
        out_specs=VMEM,
        compiler_params=BIG,
        name="order_tokens",
    )(where, *halves)


def padded(ff_own):
    return -(-ff_own // 128) * 128


def pack_members_kernel(gate, up, out):
    own, wide = gate.shape[1] // 8, out.shape[2] // 2
    for m in range(8):
        for at, source in ((0, gate), (wide, up)):
            out[m, :, at : at + own] = source[:, m * own : (m + 1) * own]
            out[m, :, at + own : at + wide] = jnp.zeros((out.shape[1], wide - own), bf16)


def pack_members(gate, up):
    rows, ff = gate.shape
    return pl.pallas_call(
        pack_members_kernel,
        out_shape=jax.ShapeDtypeStruct((8, rows, 2 * padded(ff // 8)), bf16),
        in_specs=[VMEM] * 2,
        out_specs=VMEM,
        compiler_params=BIG,
        name="pack_members",
    )(gate, up)


def unpack_members_kernel(packed_gate, packed_up, gate, up):
    own = gate.shape[1] // 8
    for m in range(8):
        for packed, target in ((packed_gate, gate), (packed_up, up)):
            target[:, m * own : (m + 1) * own] = packed[m, :, :own].astype(f32)


def unpack_members(packed_gate, packed_up, ff):
    rows = packed_gate.shape[1]
    return pl.pallas_call(
        unpack_members_kernel,
        out_shape=[jax.ShapeDtypeStruct((rows, ff), f32)] * 2,
        in_specs=[VMEM] * 2,
        out_specs=[VMEM] * 2,
        compiler_params=BIG,
        name="unpack_members",
    )(packed_gate, packed_up)


def mlp_kernel(loads, groups, where_ref, normed, out_grad, down, *refs):
    sources = refs[: len(loads)]
    pre_grad, activated, normed_grad, gate_up, arrived = refs[len(loads) :]
    chip, core = where_ref[0], where_ref[1]

    @pl.when(pl.program_id(0) == 0)
    def _():
        copies = []
        for source, (flip, other, first) in zip(sources, loads):
            if flip is None:
                copies.append(pltpu.make_async_copy(source, gate_up, arrived.at[len(copies)]))
                continue
            rows = source.shape[1]
            for i in range(source.shape[0]):
                device = 2 * ((first + i) * groups + (chip % groups ^ flip)) + (core ^ other)
                target = gate_up.at[pl.ds(pl.multiple_of(device * rows, 16), rows), :]
                copies.append(pltpu.make_async_copy(source.at[i], target, arrived.at[len(copies)]))
        for copy in copies:
            copy.start()
        for copy in copies:
            copy.wait()

    ff_own = down.shape[0]
    wide = gate_up.shape[1] // 2
    gates, ups = slice(0, ff_own), slice(wide, wide + ff_own)
    n = normed[...]
    gate = dot(n, gate_up[:, gates], 1, 0)
    up = dot(n, gate_up[:, ups], 1, 0)
    act_grad = dot(out_grad[...], down[...], 1, 1)
    sig = jax.nn.sigmoid(gate)
    act = gate * sig
    activated[...] = (act * up).astype(bf16)
    if wide > ff_own:
        gap = jnp.zeros((n.shape[0], wide - ff_own), bf16)
        pre_grad[:, ff_own:wide] = gap
        pre_grad[:, wide + ff_own :] = gap
    pre_grad[:, gates] = (act_grad * up * sig * (1.0 + gate * (1.0 - sig))).astype(bf16)
    pre_grad[:, ups] = (act_grad * act).astype(bf16)
    normed_grad[...] = dot(pre_grad[...], gate_up[...], 1, 1).astype(bf16)


def mlp(where, groups, normed, out_grad, down, sources, loads, tile=256):
    rows, width = normed.shape
    ff_own, wide = down.shape[0], sources[0].shape[-1]
    count = sum(1 if flip is None else x.shape[0] for x, (flip, _, _) in zip(sources, loads))

    def by_rows(columns):
        return pl.BlockSpec((tile, columns), lambda i: (i, 0))

    return pl.pallas_call(
        functools.partial(mlp_kernel, loads, groups),
        grid=(rows // tile,),
        out_shape=[
            jax.ShapeDtypeStruct((rows, wide), bf16),
            jax.ShapeDtypeStruct((rows, ff_own), bf16),
            jax.ShapeDtypeStruct((rows, width), bf16),
        ],
        in_specs=[
            SMEM,
            by_rows(width),
            by_rows(width),
            pl.BlockSpec(down.shape, lambda i: (0, 0), pipeline_mode=pl.Buffered(1)),
        ]
        + [pl.BlockSpec(memory_space=pl.ANY)] * len(sources),
        out_specs=[by_rows(wide), by_rows(ff_own), by_rows(width)],
        scratch_shapes=[pltpu.VMEM((width, wide), bf16), pltpu.SemaphoreType.DMA((count,))],
        compiler_params=BIG,
        name="mlp",
    )(where, normed, out_grad, down, *sources)


def gate_up_grads_kernel(rows_dev, where_ref, normed, pre_grad, keep, send):
    grads = dot(normed[...], pre_grad[...], 0, 0)
    core = where_ref[1]
    for i in range(keep.shape[0]):
        low = grads[2 * i * rows_dev : (2 * i + 1) * rows_dev].astype(bf16)
        upper = grads[(2 * i + 1) * rows_dev : (2 * i + 2) * rows_dev].astype(bf16)
        keep[i] = jnp.where(core == 0, low, upper)
        send[i] = jnp.where(core == 0, upper, low)


def gate_up_grads(normed, pre_grad, rows_dev, where, tile=384):
    rows, width = normed.shape
    wide = pre_grad.shape[1]
    chips, step = width // (2 * rows_dev), tile // (2 * rows_dev)
    result = pl.BlockSpec((step, rows_dev, wide), lambda i: (i, 0, 0))
    return pl.pallas_call(
        functools.partial(gate_up_grads_kernel, rows_dev),
        grid=(width // tile,),
        out_shape=[jax.ShapeDtypeStruct((chips, rows_dev, wide), bf16)] * 2,
        in_specs=[
            SMEM,
            pl.BlockSpec((rows, tile), lambda i: (0, i)),
            pl.BlockSpec((rows, wide), lambda i: (0, 0), pipeline_mode=pl.Buffered(1)),
        ],
        out_specs=[result] * 2,
        compiler_params=BIG,
        name="gate_up_grads",
    )(where, normed, pre_grad)


def down_grads_kernel(where_ref, activated, out_grad, keep, send):
    grads = dot(activated[...], out_grad[...], 0, 0)
    core = where_ref[1]
    rows_dev = keep.shape[1]
    for i in range(keep.shape[0]):
        low = grads[2 * i * rows_dev : (2 * i + 1) * rows_dev].astype(bf16)
        upper = grads[(2 * i + 1) * rows_dev : (2 * i + 2) * rows_dev].astype(bf16)
        keep[i] = jnp.where(core == 0, low, upper)
        send[i] = jnp.where(core == 0, upper, low)


def down_grads(activated, out_grad, groups, where, tile=512):
    rows, ff_own = activated.shape
    width = out_grad.shape[1]
    rows_dev = ff_own // (2 * groups)
    result = pl.BlockSpec((groups, rows_dev, tile), lambda i: (0, 0, i))
    return pl.pallas_call(
        down_grads_kernel,
        grid=(width // tile,),
        out_shape=[jax.ShapeDtypeStruct((groups, rows_dev, width), bf16)] * 2,
        in_specs=[
            SMEM,
            pl.BlockSpec((rows, ff_own), lambda i: (0, 0), pipeline_mode=pl.Buffered(1)),
            pl.BlockSpec((rows, tile), lambda i: (0, i)),
        ],
        out_specs=[result] * 2,
        compiler_params=BIG,
        name="down_grads",
    )(where, activated, out_grad)


def project_kernel(heads, own, other, gain, weight, bias, cos, sin, normed, queries, kv):
    hq = heads * HD
    for s, tokens in enumerate((own, other)):
        x = tokens[...].astype(f32)
        scale = lax.rsqrt(jnp.mean(x * x, axis=-1, keepdims=True) + EPSILON)
        n = (x * scale * gain[...]).astype(bf16)
        normed[s] = n
        cos_s, sin_s = cos[s], sin[s]
        project = dot(n, weight[...], 1, 0) + bias[...]

        def turn(z):
            return z * cos_s + pltpu.roll(z, HD // 2, 1) * sin_s

        for h in range(heads):
            queries[s, h] = turn(project[:, h * HD : (h + 1) * HD]).astype(bf16)
        kv[s, :, :HD] = turn(project[:, hq : hq + HD]).astype(bf16)
        kv[s, :, HD:] = project[:, hq + HD :].astype(bf16)


def project(own, other, gain, weight, bias, cos, sin):
    rows, width = own.shape
    heads = H // KVH
    return pl.pallas_call(
        functools.partial(project_kernel, heads),
        out_shape=[
            jax.ShapeDtypeStruct((2, rows, width), bf16),
            jax.ShapeDtypeStruct((2, heads, rows, HD), bf16),
            jax.ShapeDtypeStruct((2, rows, 2 * HD), bf16),
        ],
        in_specs=[VMEM] * 7,
        out_specs=[VMEM] * 3,
        compiler_params=BIG,
        name="project",
    )(own, other, gain, weight, bias, cos, sin)


def pieces(cuts, half):
    found = []
    for p, (start, stop) in enumerate(cuts):
        for b in range(2):
            low, high = max(start, b * half), min(stop, (b + 1) * half)
            if low < high:
                found.append((p, low - start, low - b * half, high - low, b))
    return found


def attend_kernel(
    flips, cuts, heads, where_ref, range_ref, queries, starts, places, weight, *refs
):
    parts, (kv, attended, attended_b, logs, branch) = refs[: 2 * len(cuts)], refs[2 * len(cuts) :]
    chip = where_ref[0]
    rows = queries.shape[2]
    half = rows // 2
    count = parts[0].shape[0]
    chips = 2 * count
    for p, first, at, size, b in pieces(cuts, half):
        for k, flip in enumerate(flips[p]):
            part = parts[2 * p + k // count]
            source = chip ^ flip
            block = source if b == 0 else 2 * chips - 1 - source
            place = pl.multiple_of(block * half + at, 16)
            for s in range(2):
                kv[s, pl.ds(place, size), :] = part[k % count, s, first : first + size, :]

    for s in range(2):
        for b in range(2):
            mine = slice(b * half, (b + 1) * half)
            q = queries[s, :, mine, :].reshape(heads * half, HD)
            start = jnp.concatenate([starts[s, mine, :]] * heads, axis=0)
            place = jnp.concatenate([places[s, mine, :]] * heads, axis=0)

            def step(i, state):
                top, total, out = state
                first = pl.multiple_of(i * CHUNK, CHUNK)
                keys = kv[s, pl.ds(first, CHUNK), :HD]
                values = kv[s, pl.ds(first, CHUNK), HD:]
                scores = dot(q, keys, 1, 1) * SCALE
                key_place = first + lax.broadcasted_iota(jnp.int32, scores.shape, 1)
                seen = (key_place >= start) & (key_place <= place)
                scores = jnp.where(seen, scores, NEVER)
                new_top = jnp.maximum(top, jnp.max(scores, axis=1, keepdims=True))
                fade = jnp.exp(top - new_top)
                weights = jnp.exp(scores - new_top)
                total = total * fade + jnp.sum(weights, axis=1, keepdims=True)
                out = out * fade + dot(weights.astype(bf16), values, 1, 0)
                return new_top, total, out

            at = 4 * s + 2 * b
            top, total, out = lax.fori_loop(
                range_ref[at],
                range_ref[at + 1],
                step,
                (
                    jnp.full((heads * half, 1), NEVER, f32),
                    jnp.zeros((heads * half, 1), f32),
                    jnp.zeros((heads * half, HD), f32),
                ),
            )
            out = out / total
            logs[s, b] = top + jnp.log(total)
            attended[s, b] = out
            for h in range(heads):
                attended_b[s, mine, h * HD : (h + 1) * HD] = out[h * half : (h + 1) * half].astype(
                    bf16
                )
        branch[s] = dot(attended_b[s], weight[...], 1, 1)


def attend(where, ranges, queries, starts, places, weight, parts, flips, cuts):
    _, heads, rows, _ = queries.shape
    keys = 2 * parts[0].shape[0] * rows
    half = rows // 2
    return pl.pallas_call(
        functools.partial(attend_kernel, flips, cuts, heads),
        out_shape=[
            jax.ShapeDtypeStruct((2, keys, 2 * HD), bf16),
            jax.ShapeDtypeStruct((2, 2, heads * half, HD), f32),
            jax.ShapeDtypeStruct((2, rows, heads * HD), bf16),
            jax.ShapeDtypeStruct((2, 2, heads * half, 1), f32),
            jax.ShapeDtypeStruct((2, rows, weight.shape[0]), f32),
        ],
        in_specs=[SMEM] * 2 + [VMEM] * (4 + len(parts)),
        out_specs=[VMEM] * 5,
        compiler_params=BIG,
        name="attend",
    )(where, ranges, queries, starts, places, weight, *parts)


def attend_back_kernel(
    heads,
    range_ref,
    branch_own,
    branch_other,
    weight,
    queries,
    kv,
    attended,
    logs,
    starts,
    places,
    cos,
    sin,
    query_out,
    kv_out,
    grads,
    kv_sum,
):
    rows = queries.shape[2]
    half = rows // 2
    chips = kv.shape[1] // rows
    kv_sum[...] = jnp.zeros_like(kv_sum)
    for s, branch in enumerate((branch_own, branch_other)):
        grads[s] = dot(branch[...], weight[...], 1, 0).astype(bf16)
    for s in range(2):
        for b in range(2):
            mine = slice(b * half, (b + 1) * half)
            q = queries[s, :, mine, :].reshape(heads * half, HD)
            start = jnp.concatenate([starts[s, mine, :]] * heads, axis=0)
            place = jnp.concatenate([places[s, mine, :]] * heads, axis=0)
            grad = jnp.concatenate(
                [grads[s, mine, h * HD : (h + 1) * HD] for h in range(heads)], axis=0
            )
            delta = jnp.sum(grad.astype(f32) * attended[s, b], axis=1, keepdims=True)
            log_total = logs[s, b]

            def step(i, query_grad):
                first = pl.multiple_of(i * CHUNK, CHUNK)
                keys = kv[s, pl.ds(first, CHUNK), :HD]
                values = kv[s, pl.ds(first, CHUNK), HD:]
                scores = dot(q, keys, 1, 1) * SCALE
                key_place = first + lax.broadcasted_iota(jnp.int32, scores.shape, 1)
                seen = (key_place >= start) & (key_place <= place)
                weights = jnp.where(seen, jnp.exp(scores - log_total), 0.0)
                weight_grad = dot(grad, values, 1, 1)
                score_grad = (weights * (weight_grad - delta)).astype(bf16)
                kv_sum[s, pl.ds(first, CHUNK), :HD] += dot(score_grad, q, 0, 0)
                kv_sum[s, pl.ds(first, CHUNK), HD:] += dot(weights.astype(bf16), grad, 0, 0)
                return query_grad + dot(score_grad, keys, 1, 0)

            at = 4 * s + 2 * b
            query_grad = lax.fori_loop(
                range_ref[at], range_ref[at + 1], step, jnp.zeros((heads * half, HD), f32)
            )
            cos_b, sin_b = cos[s, mine, :] * SCALE, sin[s, mine, :] * SCALE
            for h in range(heads):
                z = query_grad[h * half : (h + 1) * half]
                z = z * cos_b - pltpu.roll(z, HD // 2, 1) * sin_b
                query_out[s, mine, h * HD : (h + 1) * HD] = z.astype(bf16)

    def give(chip, carry):
        for s in range(2):
            for b in range(2):
                block = chip if b == 0 else 2 * chips - 1 - chip
                place = pl.multiple_of(block * half, half)
                mine = slice(b * half, (b + 1) * half)
                source = kv_sum[s, pl.ds(place, half), :]
                kv_out[chip % 8, chip // 8, s, mine, :HD] = (source[:, :HD] * SCALE).astype(bf16)
                kv_out[chip % 8, chip // 8, s, mine, HD:] = source[:, HD:].astype(bf16)
        return carry

    lax.fori_loop(0, chips, give, 0)


def attend_back(
    ranges, branch_own, branch_other, weight, queries, kv, attended, logs, starts, places, cos, sin
):
    _, heads, rows, _ = queries.shape
    keys = kv.shape[1]
    chips = keys // rows
    return pl.pallas_call(
        functools.partial(attend_back_kernel, heads),
        out_shape=[
            jax.ShapeDtypeStruct((2, rows, heads * HD), bf16),
            jax.ShapeDtypeStruct((8, chips // 8, 2, rows, 2 * HD), bf16),
        ],
        in_specs=[SMEM] + [VMEM] * 11,
        out_specs=[VMEM] * 2,
        scratch_shapes=[
            pltpu.VMEM((2, rows, heads * HD), bf16),
            pltpu.VMEM((2, keys, 2 * HD), f32),
        ],
        compiler_params=BIG,
        name="attend_back",
    )(
        ranges,
        branch_own,
        branch_other,
        weight,
        queries,
        kv,
        attended,
        logs,
        starts,
        places,
        cos,
        sin,
    )


def on_device(
    tokens, cotangent, doc_lengths, norm_attn, w_qkv, b_qkv, w_out, norm_mlp, w_gate, w_up, w_down
):
    ctx_size = lax.axis_size("ctx")
    chip = lax.axis_index("ctx")
    core = lax.axis_index("wshard")
    where = jnp.stack([chip, core]).astype(jnp.int32)
    high = high_bits()
    groups = ctx_size // 8
    tok_dev, width = tokens.shape[1], tokens.shape[2]
    ff = w_gate.shape[1]
    ff_own = ff // 8
    heads = H // KVH
    hq = heads * HD
    rows_dev = w_qkv.shape[0]
    cuts = row_parts(tok_dev)
    half = tok_dev // 2
    flips = [relative_flips(high + order) for order in ORDERS]
    group_flips = relative_flips(group_bits())
    low, middle, upper = member_bits()

    n_gain, n_bias = norm_attn.shape[0], b_qkv.shape[0]
    small = jnp.concatenate([norm_attn, b_qkv, norm_mlp])[None]
    small = jnp.pad(small, ((0, 15), (hq, 2 * HD - small.shape[1])))
    qkv_send = jnp.concatenate([head_columns(w_qkv, 1 - core), small])
    qkv_own = jnp.concatenate([head_columns(w_qkv, core), small])
    token_own, out_grad_b = tokens[0], cotangent[0]
    out_t = w_out.T
    qkv_other = core_swap(qkv_send)
    token_other = core_swap(token_own)
    length_other = core_swap(doc_lengths[0])
    out_other = core_swap(half_of(out_t, 1 - core, 1))
    down_found = gather_list(w_down, group_bits())
    length_pair = jnp.stack([doc_lengths[0], length_other])
    qkv_pair = jnp.stack([qkv_own, qkv_other])[None]
    qkv_pair, w_gate, out_other = together(qkv_pair, w_gate, out_other)
    out_pair = by_core(half_of(out_t, core, 1), out_other, core)
    out_w = lax.all_gather(out_pair, "ctx", axis=0, tiled=False).reshape(width, hq)
    out_grad_all = lax.all_gather(
        after(out_grad_b, out_w), "ctx", axis=0, tiled=True, axis_index_groups=group_lists()
    )
    qkv_pair = gather_relative(qkv_pair, high)
    packed = pack_members(w_gate, w_up)
    qkv_pair, packed, down_found = together(qkv_pair, packed, down_found)
    column_cuts = ((0, hq // 2, rows_dev), (hq // 2, hq, rows_dev), (hq, hq + 2 * HD, rows_dev + 16))
    qkv_parts = [qkv_pair[:, :, :rows, start:stop] for start, stop, rows in column_cuts]
    qkv_parts = doubled(qkv_parts, [order[0] for order in ORDERS])
    packed = group_exchange(packed)
    down_other = [core_swap(x) for x in down_found]
    qkv_parts = doubled(qkv_parts, [order[1] for order in ORDERS])
    qkv_parts, packed = together(qkv_parts, packed)
    packed_other = core_swap(packed)
    qkv_parts = with_arrived(qkv_parts, [order[2] for order in ORDERS])
    shares = ((0, 3), (3, 8))
    qkv_parts, packed = together(qkv_parts, packed)
    packed_found = [gather_list(packed[:3], group_bits())]

    inner = jnp.arange(tok_dev, dtype=jnp.int32)
    blocks = jnp.where(inner < half, chip, 2 * ctx_size - 1 - chip)
    places = (blocks * half + inner % half).astype(jnp.int32)
    ends = jnp.cumsum(length_pair, axis=1)
    passed = ends[:, None, :] <= places[None, :, None]
    starts = jnp.sum(jnp.where(passed, length_pair[:, None, :], 0), axis=2)
    places = jnp.broadcast_to(places[None], starts.shape)
    frequency = ROPE_BASE ** (-jnp.arange(HD // 2, dtype=f32) * 2.0 / HD)
    angles = (places - starts).astype(f32)[..., None] * frequency
    cos_half, sin_half = jnp.cos(angles), jnp.sin(angles)
    cos = jnp.concatenate([cos_half, cos_half], axis=-1)
    sin = jnp.concatenate([-sin_half, sin_half], axis=-1)
    first = jnp.min(starts.reshape(2, 2, half), axis=2) // CHUNK
    last = jnp.max(places.reshape(2, 2, half), axis=2) // CHUNK + 1
    ranges = jnp.stack([first, last], axis=-1).reshape(-1).astype(jnp.int32)
    starts, places = starts[..., None], places[..., None]

    qkv_w, small_all = order_weights(qkv_parts, flips, where)
    qkv_w = qkv_w.reshape(width, hq + 2 * HD)
    small_all = small_all.reshape(2 * ctx_size, 2 * HD)
    gain_one = small_all[:, :n_gain].reshape(1, -1)
    bias = small_all[:, n_gain : n_gain + n_bias].reshape(1, -1)
    gain_two = small_all[:, n_gain + n_bias : 2 * n_gain + n_bias].reshape(1, -1)
    bias = head_columns(bias, core)
    normed_one, queries, kv_own = project(token_own, token_other, gain_one, qkv_w, bias, cos, sin)
    kv_own, packed_found, packed = together(kv_own, packed_found, packed)

    kv_own = gather_relative(kv_own[None], high)
    kv_own, packed = together(kv_own, packed)
    packed_found.append(gather_list(packed[3:], group_bits()))
    kv_parts = [kv_own[:, :, start:stop] for start, stop in cuts]
    for step in range(2):
        kv_parts = doubled(kv_parts, [order[step] for order in ORDERS])
    kv_parts, packed_found, packed = together(kv_parts, packed_found, packed)
    down = order_rows([x[None] for x in down_found], [x[None] for x in down_other], group_flips, where)
    down = down.reshape(ff_own, width)
    kv_parts = with_arrived(kv_parts, [order[2] for order in ORDERS])
    kv_parts, down, out_w = together(kv_parts, down, out_w)
    kv, attended, attended_b, logs, branch = attend(
        where, ranges, queries, starts, places, out_w, kv_parts, flips, cuts
    )
    branch_other = core_swap(branch[1])
    inputs = token_own.astype(f32)
    hidden_res = inputs + branch[0] + branch_other
    scale_two = lax.rsqrt(jnp.mean(hidden_res * hidden_res, axis=-1, keepdims=True) + EPSILON)
    normed_two = (hidden_res * scale_two * gain_two).astype(bf16)

    group_orders = ((upper, middle, low), (upper, low, middle))
    group_cuts = ((0, half), (half, tok_dev))
    token_parts = gather_relative(normed_two[None], (upper,))
    token_parts = [token_parts[:, start:stop] for start, stop in group_cuts]
    token_parts = doubled(token_parts, [order[1] for order in group_orders])
    token_parts = with_arrived(token_parts, [order[2] for order in group_orders])
    token_flips = [relative_flips(order) for order in group_orders]
    normed_all = order_tokens(token_parts, token_flips, group_cuts, groups, where)
    normed_all = normed_all.reshape(8 * tok_dev, width)

    sources, loads = [packed, packed_other], [(0, 0, 0), (0, 1, 0)]
    for found, (first, _) in zip(packed_found, shares):
        for piece, flip in list(zip(found, group_flips))[1:]:
            sources.extend([piece, core_swap(piece)])
            loads.extend([(flip, 0, first), (flip, 1, first)])
    if rows_dev % 16:
        own, other = [], []
        for flip in group_flips:
            for core_flip, side in enumerate((own, other)):
                found = [x for x, load in zip(sources, loads) if load[:2] == (flip, core_flip)]
                side.append(jnp.concatenate(found))
        sources, loads = [order_rows(own, other, group_flips, where).reshape(width, -1)], [(None, 0, 0)]
    out_grad = out_grad_b.astype(f32)
    pre_grad, activated, normed_grad_part = mlp(
        where, groups, normed_all, out_grad_all, down, sources, loads
    )

    normed_grad_part = normed_grad_part.reshape(2, 2, 2, tok_dev, width)
    scatter = Scatter(
        [normed_grad_part[:, :, :, start:stop] for start, stop in group_cuts], (upper, middle, low)
    )
    bits = [order[2] for order in group_orders]
    kept, sent = scatter.split(bits)
    gu_keep, gu_send = gate_up_grads(normed_all, after(pre_grad, *sent), rows_dev, where)
    scatter.step(bits, kept, sent)
    scatter.parts, gu_keep, gu_send = together(scatter.parts, gu_keep, gu_send)

    bits = [order[1] for order in group_orders]
    kept, sent = scatter.split(bits)
    gu_arrived = core_swap(gu_send)
    branch_part = dot(after(activated, *sent), down, 1, 0).astype(bf16)
    scatter.step(bits, kept, sent)
    scatter.parts, branch_part, gu_arrived = together(scatter.parts, branch_part, gu_arrived)

    kept, sent = scatter.split((upper, upper))
    gu_sum = (gu_keep.astype(f32) + gu_arrived.astype(f32)).astype(bf16)
    scatter.step((upper, upper), kept, sent)
    scatter.parts, gu_sum, branch_part = together(scatter.parts, gu_sum, branch_part)
    branch_mlp = lax.psum_scatter(
        branch_part, "ctx", scatter_dimension=0, tiled=True, axis_index_groups=group_lists()
    )
    normed_two_grad = jnp.concatenate(scatter.parts)
    gain_two_grad = jnp.sum(normed_two_grad * hidden_res * scale_two, axis=0)
    hidden_grad = out_grad + rms_back(normed_two_grad, hidden_res, scale_two, gain_two)

    wide = gu_sum.shape[2] // 2
    column = wide // 256 * 128
    gu_cuts = ((0, column), (column, wide), (wide, wide + column), (wide + column, 2 * wide))
    gu_pieces = [gu_sum.reshape(8, groups, rows_dev, -1)[..., a:b] for a, b in gu_cuts]
    falling = tuple(reversed(group_bits()))
    gu_done = []

    def weight_parts(x):
        return x.astype(bf16).reshape(ctx_size // 8, 8, 2, rows_dev, x.shape[1])

    branch_own = hidden_grad.astype(bf16)
    branch_other = core_swap(branch_own)
    gu_done.append(sum_over(gu_pieces[0], 1, falling).astype(bf16))
    branch_own, branch_other, gu_pieces, gu_done = together(
        branch_own, branch_other, gu_pieces, gu_done
    )
    gu_done.append(sum_over(gu_pieces[1], 1, falling).astype(bf16))
    project_grad_q, kv_grad = attend_back(
        ranges, branch_own, branch_other, out_w, queries, kv, attended, logs, starts, places, cos, sin
    )
    (kv_grad, project_grad_q), gu_done, gu_pieces, activated = together(
        (kv_grad, project_grad_q), gu_done, gu_pieces, activated
    )
    kv_sum = cube_exchange(kv_grad)
    gu_third = sum_over(gu_pieces[2], 1, falling).astype(bf16)
    down_keep, down_send = down_grads(activated, out_grad_all, groups, where)
    branch_grad = jnp.concatenate([branch_own, branch_other])
    normed_one = normed_one.reshape(-1, width)
    project_grad_q = project_grad_q.reshape(-1, hq)
    grad_out_part = weight_parts(dot(branch_grad, attended_b.reshape(-1, hq), 0, 0))
    grad_q_part = weight_parts(dot(normed_one, project_grad_q, 0, 0))
    wide_part = jnp.concatenate([grad_q_part, grad_out_part], axis=-1)
    names = tuple(reversed(high)) + (2, 1, 0)
    wide_part = wide_part.reshape((2,) * len(names) + wide_part.shape[2:])
    third = 2 * hq // 3
    scatter = Scatter([wide_part[..., i * third : (i + 1) * third] for i in range(3)], names)
    bits = [order[0] for order in ORDERS]
    kept, sent = scatter.split(bits)
    kv_sum, sent, down_send = together(kv_sum, sent, down_send)

    kv_sum = jnp.sum(kv_sum.astype(f32), axis=0).astype(bf16)
    kv_sum = sum_over_high(kv_sum, high)
    grad_gate = group_exchange(jnp.concatenate(gu_done, axis=2))
    arrived = [chip_swap(x, 1 << bit) for x, bit in zip(sent, bits)]
    key_pre = kv_sum[..., :HD]
    key_pre = key_pre * cos - jnp.roll(key_pre, HD // 2, axis=-1) * sin
    project_grad_kv = jnp.concatenate([key_pre, kv_sum[..., HD:]], axis=-1).astype(bf16)
    project_grad_kv = project_grad_kv.reshape(-1, 2 * HD)
    grad_kv = weight_parts(dot(normed_one, project_grad_kv, 0, 0)).swapaxes(0, 1)
    grad_kv, grad_gate, arrived, gu_third, gu_pieces = together(
        grad_kv, grad_gate, arrived, gu_third, gu_pieces
    )

    grad_kv = cube_exchange(grad_kv)
    gu_last = sum_over(gu_pieces[3], 1, falling).astype(bf16)
    scatter.add(kept, arrived)
    scatter.step([order[1] for order in ORDERS])
    down_arrived = core_swap(down_send)
    project_grad = jnp.concatenate([project_grad_q, project_grad_kv], axis=1)
    normed_one_grad = dot(project_grad, qkv_w, 1, 1)
    normed_one_grad = normed_one_grad[:tok_dev] + core_swap(normed_one_grad[tok_dev:])
    grad_kv, gu_last, scatter.parts, down_arrived = together(
        grad_kv, gu_last, scatter.parts, down_arrived
    )
    grad_up = group_exchange(jnp.concatenate([gu_third, gu_last], axis=2))
    grad_kv = jnp.sum(grad_kv.astype(f32), axis=0).astype(bf16)
    grad_kv = sum_over_high(grad_kv, high)
    down_sum = (down_keep.astype(f32) + down_arrived.astype(f32)).astype(bf16)
    grad_down = sum_over(down_sum, 0, falling)
    scatter.step([order[2] for order in ORDERS])
    scatter.parts = [jnp.concatenate(scatter.parts, axis=-1)]
    scale_one = lax.rsqrt(jnp.mean(inputs * inputs, axis=-1, keepdims=True) + EPSILON)
    gain_one_grad = jnp.sum(normed_one_grad * inputs * scale_one, axis=0)
    input_grad = hidden_grad + rms_back(normed_one_grad, inputs, scale_one, gain_one)
    grad_kv, grad_up, scatter.parts, gain_one_grad, grad_down, branch_mlp = together(
        grad_kv, grad_up, scatter.parts, gain_one_grad, grad_down, branch_mlp
    )
    output = (hidden_res + branch_mlp.astype(f32)).astype(bf16)
    for bit in reversed(high):
        scatter.step((bit,))
    scattered = scatter.parts[0]

    grad_gate, grad_up = unpack_members(grad_gate, grad_up, ff)
    chip_grad = jnp.concatenate([scattered[..., :hq], grad_kv, scattered[..., hq:]], axis=-1)

    def pick(x, which):
        return lax.dynamic_index_in_dim(x, which, 0, keepdims=False)

    def whole_columns(x):
        return jnp.concatenate(
            [
                x[0, :, :hq],
                x[1, :, :hq],
                x[0, :, hq : hq + HD],
                x[1, :, hq : hq + HD],
                x[0, :, hq + HD : hq + 2 * HD],
                x[1, :, hq + HD : hq + 2 * HD],
            ],
            axis=1,
        )

    pair = by_core(pick(chip_grad, core), core_swap(pick(chip_grad, 1 - core)), core)
    grad_qkv = whole_columns(pair)
    grad_out = pair[:, :, hq + 2 * HD :].transpose(1, 0, 2).reshape(-1, 2 * hq).T

    bias_grad = jnp.sum(project_grad.astype(f32), axis=0, keepdims=True)
    zeros = jnp.zeros_like(bias_grad)
    bias_full = whole_columns(
        jnp.stack([jnp.where(core == 0, bias_grad, zeros), jnp.where(core == 0, zeros, bias_grad)])
    )[0]
    qk_width = (H + KVH) * HD
    sums = jnp.concatenate(
        [
            x.reshape(ctx_size, 1, -1)
            for x in (gain_one_grad, gain_two_grad, bias_full[:qk_width], bias_full[qk_width:])
        ],
        axis=2,
    )
    sums = lax.all_to_all(sums, "ctx", split_axis=0, concat_axis=0, tiled=True)
    sums = jnp.sum(sums, axis=0)
    sums = (sums + core_swap(sums))[0]

    def owned(start, size):
        return lax.dynamic_slice_in_dim(sums, start + core * (size // 2), size // 2, 0)

    own_width, own_qk, own_v = width // ctx_size, qk_width // ctx_size, KVH * HD // ctx_size
    return (
        output[None],
        input_grad[None],
        owned(0, own_width),
        grad_qkv,
        owned(2 * own_width, own_qk),
        owned(2 * own_width + own_qk, own_v),
        grad_out,
        owned(own_width, own_width),
        grad_gate,
        grad_up,
        grad_down,
    )


def solution(mesh):
    whole = ("ctx", "wshard")
    rows, columns, flat = P(whole, None), P(None, whole), P(whole)
    tokens = P("wshard", "ctx", None)
    return jax.shard_map(
        on_device,
        mesh=mesh,
        in_specs=(tokens, tokens, P("wshard", None), flat, rows, flat, columns, flat, rows, rows, rows),
        out_specs=(tokens, tokens, flat, rows, flat, flat, columns, flat, rows, rows, rows),
        check_vma=False,
    )
```

time: 830 us -> 612 us (0.74)
  Pallas kernels: 0 us -> 89.9 us
  waiting for transfers between devices: 362 us -> 274 us
  local copies, waits for them, and re-layouts: 112 us -> 36.8 us
  matrix products: 89.3 us -> 15 us
  starting transfers between devices: 181 us -> 116 us
  other arithmetic: 73.8 us -> 56.3 us
  between operations: 4.57 us -> 15.7 us
    ppermute x146 -> x51, starting transfers between devices: 178 us -> 71.4 us  [chip_swap(): return lax.ppermute(x, 'ctx', [(i, i ^ flip) for i in range(count)])]
    ppermute x146 -> x51, waiting for transfers between devices: 361 us -> 264 us  [chip_swap(): return lax.ppermute(x, 'ctx', [(i, i ^ flip) for i in range(count)])]
    pallas_call x0 -> x11, Pallas kernels: none -> 89.9 us  [the longest x1 27.7 us: mlp(): pl.pallas_call(functools.partial(mlp_kernel, loads, groups), grid=(rows /...]
    dot_general x13 -> x5, matrix products: 62.1 us -> 15 us  [dot(): lax.dot_general(left, right, (((left_axis,), (right_axis,)), ((), ())), p...]
    all_to_all x0 -> x6, starting transfers between devices: none -> 42.2 us  [the longest x3 25 us: group_exchange(): lax.all_to_all(x, 'ctx', split_axis=0, concat_axis=0, tiled=True, axis_in...]
    convert_element_type x11 -> x0, local copies, waits for them, and re-layouts: 27.6 us -> none  [the longest x6 16.7 us: to_columns(): return x.reshape(rows_dev, ff).astype(f32)]
    unnamed x253 -> x126, local copies, waits for them, and re-layouts: 29.9 us -> 7.48 us
    dot_general x5 -> x0, matrix products: 19.8 us -> none  [the longest x1 5.77 us: on_device(): jnp.einsum('sthd,skd->shtk', grad_heads, values, preferred_element_type=f32)]
  transfers between devices with their start and end apart: 161 -> 76, of which waited for: 88 -> 35; matrix products, arithmetic and copies ran while one was open for 23% -> 16% of each run, Pallas kernels for 0% -> 10%
where the time goes in v2:
time: 612 us; the launch traced here: 603 us
  waiting for transfers between devices  274 us (45%)
  starting transfers between devices  116 us (19%)
  Pallas kernels  89.9 us (15%)
  other arithmetic  56.3 us (9%)
  local copies, waits for them, and re-layouts  36.8 us (6%)
  between operations  15.7 us (3%)
  matrix products  15 us (2%)
    ppermute x51, waiting for transfers between devices, chip_swap(): return lax.ppermute(x, 'ctx', [(i, i ^ flip) for i in range(count)])  264 us
    ppermute x51, starting transfers between devices, chip_swap(): return lax.ppermute(x, 'ctx', [(i, i ^ flip) for i in range(count)])  71.4 us
    pallas_call x1, Pallas kernels, mlp(): pl.pallas_call(functools.partial(mlp_kernel, loads, groups), grid=(rows /...  27.7 us
    all_to_all x3, starting transfers between devices, group_exchange(): lax.all_to_all(x, 'ctx', split_axis=0, concat_axis=0, tiled=True, axis_in...  25 us
    dot_general x5, matrix products, dot(): lax.dot_general(left, right, (((left_axis,), (right_axis,)), ((), ())), p...  15 us
    pallas_call x1, Pallas kernels, gate_up_grads(): pl.pallas_call(functools.partial(gate_up_grads_kernel, rows_dev), grid=(w...  12.3 us
  transfers between devices with their start and end apart: 76, of which 35 were waited for; matrix products, arithmetic and copies ran while one was open for 16% of the time, Pallas kernels for 10%

profile of v2, /device:TPU:0, one launch (start us, length us, event | category | flops | bytes accessed | tf_op | source)
XLA Modules:
  0.0 603.5 jit_solution(9526046919555767707)
XLA Ops:
  20.8 9.4 %collective-permute-done.4 = bf16[1,2,64,1024]{3,2,1,0:T(8,128)(2,1)S(1)} collective-permute-done((bf16[1,2,64,1024]{3,2,1,0:T(8,128)(2,1)S(1)}, bf16[1,2,64,1024]{3,2,1,0:T(8,128)(2,1)S(1)}, u32[]{:S(2)}, u32[]{:S(2)}) %collective-permute-start.4) | collective-permute-done | bytes 262176 | tf_op jit(solution)/shard_map/ppermute | solution.py:42
  30.3 5.9 all-to-all-start
  42.9 29.2 %collective-permute-done.10 = bf16[2,2,64,256]{3,2,1,0:T(8,128)(2,1)S(1)} collective-permute-done((bf16[2,2,64,256]{3,2,1,0:T(8,128)(2,1)S(1)}, bf16[2,2,64,256]{3,2,1,0:T(8,128)(2,1)S(1)}, u32[]{:S(2)}, u32[]{:S(2)}) %collective-permute-start.10) | collective-permute-done | bytes 131104 | tf_op jit(solution)/shard_map/ppermute | solution.py:42
  77.5 7.1 %collective-permute-done.11 = bf16[4,2,64,256]{3,2,1,0:T(8,128)(2,1)} collective-permute-done((bf16[4,2,64,256]{3,2,1,0:T(8,128)(2,1)}, bf16[4,2,64,256]{3,2,1,0:T(8,128)(2,1)}, u32[]{:S(2)}, u32[]{:S(2)}) %collective-permute-start.11) | collective-permute-done | bytes 262176 | tf_op jit(solution)/shard_map/ppermute | solution.py:42
  86.4 7.0 %collective-permute-done.9 = bf16[4,2,48,384]{3,2,1,0:T(8,128)(2,1)} collective-permute-done((bf16[4,2,48,384]{3,2,1,0:T(8,128)(2,1)S(1)}, bf16[4,2,48,384]{3,2,1,0:T(8,128)(2,1)}, u32[]{:S(2)}, u32[]{:S(2)}) %collective-permute-start.9) | collective-permute-done | bytes 294944 | tf_op jit(solution)/shard_map/ppermute | solution.py:42
  98.9 18.9 %collective-permute-done.14.refs_5_ = bf16[8,2,64,256]{3,2,1,0:T(8,128)(2,1)S(1)} collective-permute-done((bf16[8,2,64,256]{3,2,1,0:T(8,128)(2,1)}, bf16[8,2,64,256]{3,2,1,0:T(8,128)(2,1)S(1)}, u32[]{:S(2)}, u32[]{:S(2)}) %collective-permute-start.14) | collective-permute-done | bytes 524320 | tf_op jit(solution)/shard_map/ppermute | solution.py:42
  117.7 5.6 collective-permute-done.12.refs_1_
  124.9 3.9 order_weights.1
  132.4 4.2 project.1
  136.6 11.0 %collective-permute-done.15.refs_2_ = bf16[3,48,2304]{2,1,0:T(8,128)(2,1)} collective-permute-done((bf16[3,48,2304]{2,1,0:T(8,128)(2,1)S(1)}, bf16[3,48,2304]{2,1,0:T(8,128)(2,1)}, u32[]{:S(2)}, u32[]{:S(2)}) %collective-permute-start.15) | collective-permute-done | bytes 663584 | tf_op jit(solution)/shard_map/ppermute | solution.py:42
  148.3 7.7 %collective-permute-done.16 = bf16[1,2,128,256]{3,2,1,0:T(8,128)(2,1)S(1)} collective-permute-done((bf16[1,2,128,256]{3,2,1,0:T(8,128)(2,1)}, bf16[1,2,128,256]{3,2,1,0:T(8,128)(2,1)S(1)}, u32[]{:S(2)}, u32[]{:S(2)}) %collective-permute-start.16) | collective-permute-done | bytes 131104 | tf_op jit(solution)/shard_map/ppermute | solution.py:42
  159.0 4.2 collective-permute-done.21
  165.5 22.0 %collective-permute-done.17 = bf16[2,2,48,256]{3,2,1,0:T(8,128)(2,1)S(1)} collective-permute-done((bf16[2,2,48,256]{3,2,1,0:T(8,128)(2,1)S(1)}, bf16[2,2,48,256]{3,2,1,0:T(8,128)(2,1)S(1)}, u32[]{:S(2)}, u32[]{:S(2)}) %collective-permute-start.17) | collective-permute-done | bytes 98336 | tf_op jit(solution)/shard_map/ppermute | solution.py:42
  189.3 4.4 collective-permute-done.20
  193.7 6.2 %collective-permute-done.18 = bf16[4,2,48,256]{3,2,1,0:T(8,128)(2,1)S(1)} collective-permute-done((bf16[4,2,48,256]{3,2,1,0:T(8,128)(2,1)S(1)}, bf16[4,2,48,256]{3,2,1,0:T(8,128)(2,1)S(1)}, u32[]{:S(2)}, u32[]{:S(2)}) %collective-permute-start.18) | collective-permute-done | bytes 196640 | tf_op jit(solution)/shard_map/ppermute | solution.py:42
  202.0 3.3 order_rows.1
  205.3 7.7 %collective-permute-done.26.refs_5_ = bf16[8,2,32,256]{3,2,1,0:T(8,128)(2,1)} collective-permute-done((bf16[8,2,32,256]{3,2,1,0:T(8,128)(2,1)S(1)}, bf16[8,2,32,256]{3,2,1,0:T(8,128)(2,1)}, u32[]{:S(2)}, u32[]{:S(2)}) %collective-permute-start.26) | collective-permute-done | bytes 262176 | tf_op jit(solution)/shard_map/ppermute | solution.py:42
  213.1 5.4 collective-permute-done.24.refs_1_
  219.3 9.6 %attend.1 = (bf16[2,2048,256]{2,1,0:T(8,128)(2,1)}, f32[2,2,384,128]{3,2,1,0:T(8,128)}, bf16[2,128,768]{2,1,0:T(8,128)(2,1)}, f32[2,2,384,1]{3,2,1,0:T(8,128)}, f32[2,128,1536]{2,1,0:T(8,128)}) custom-call(s32[2]{0:T(128)} %pad_add_fusion.2.where_ref, s32[8]{0:T(128)} %reshape.416.range_ref, bf16[2,6,128,128]{3,2,1,0:T(8,128)(2,1)} %get-tuple-element.137.queries, ...), custom_call_target="tpu_custom_call" | custom-call | tf_op jit(solution)/shard_map/attend/pallas_call | solution.py:566
  237.8 18.3 %collective-permute-done.30 = bf16[1,128,1536]{2,1,0:T(8,128)(2,1)S(1)} collective-permute-done((bf16[1,128,1536]{2,1,0:T(8,128)(2,1)S(1)}, bf16[1,128,1536]{2,1,0:T(8,128)(2,1)S(1)}, u32[]{:S(2)}, u32[]{:S(2)}) %collective-permute-start.30) | collective-permute-done | bytes 393248 | tf_op jit(solution)/shard_map/ppermute | solution.py:42
  256.5 5.0 collective-permute-start.33
  261.5 5.0 collective-permute-done.31
  267.5 4.9 collective-permute-start.32
  274.5 14.6 %collective-permute-done.32.refs_1_ = bf16[4,64,1536]{2,1,0:T(8,128)(2,1)} collective-permute-done((bf16[4,64,1536]{2,1,0:T(8,128)(2,1)}, bf16[4,64,1536]{2,1,0:T(8,128)(2,1)}, u32[]{:S(2)}, u32[]{:S(2)}) %collective-permute-start.32) | collective-permute-done | bytes 786464 | tf_op jit(solution)/shard_map/ppermute | solution.py:42
  291.5 3.8 order_tokens.1
  295.3 27.7 %mlp.1 = (bf16[1024,2304]{1,0:T(8,128)(2,1)}, bf16[1024,1120]{1,0:T(8,128)(2,1)}, bf16[1024,1536]{1,0:T(8,128)(2,1)}) custom-call(s32[2]{0:T(128)} %pad_add_fusion.2.where_ref, bf16[1024,1536]{1,0:T(8,128)(2,1)} %bitcast.276, bf16[1024,1536]{1,0:T(8,128)(2,1)} %all-gather.4.cloned.1.call-done.out_grad, bf16[1120,1536]{1,0:T(8,128)(2,1)} %bitcast.280, ...), custom_call_target="tpu_custom_call" | custom-call | tf_op jit(solution)/shard_map/mlp/pallas_call | solution.py:371
  328.4 12.3 %gate_up_grads.1 = (bf16[16,48,2304]{2,1,0:T(8,128)(2,1)}, bf16[16,48,2304]{2,1,0:T(8,128)(2,1)}) custom-call(s32[2]{0:T(128)} %pad_add_fusion.2.where_ref, bf16[1024,1536]{1,0:T(8,128)(2,1)} %bitcast.277, bf16[1024,2304]{1,0:T(8,128)(2,1)} %get-tuple-element.167.pre_grad), custom_call_target="tpu_custom_call" | custom-call | tf_op jit(solution)/shard_map/gate_up_grads/pallas_call | solution.py:408
  349.4 8.6 %convolution_convert_fusion = bf16[1024,1536]{1,0:T(8,128)(2,1)} fusion(bf16[1024,1120]{1,0:T(8,128)(2,1)} %get-tuple-element.197.activated, bf16[1120,1536]{1,0:T(8,128)(2,1)} %bitcast.281), kind=kOutput, calls=%fused_computation.2 | convolution fusion | flops 3524788224 | bytes 8880128 | tf_op jit(solution)/shard_map/dot_general | solution.py:166
  359.3 3.8 collective-permute-start.44
  363.1 3.9 add_convert_fusion
  367.1 9.8 %collective-permute-done.44 = bf16[64,1536]{1,0:T(8,128)(2,1)S(1)} collective-permute-done((bf16[64,1536]{1,0:T(8,128)(2,1)S(1)}, bf16[64,1536]{1,0:T(8,128)(2,1)S(1)}, u32[]{:S(2)}, u32[]{:S(2)}) %collective-permute-start.44) | collective-permute-done | bytes 196640 | tf_op jit(solution)/shard_map/ppermute | solution.py:42
  376.9 3.5 collective-permute-done.43
  385.9 5.7 collective-permute-done.46
  393.3 10.9 %attend_back.1 = (bf16[2,128,768]{2,1,0:T(8,128)(2,1)}, bf16[8,2,2,128,256]{4,3,2,1,0:T(8,128)(2,1)}) custom-call(s32[8]{0:T(128)} %reshape.416.range_ref, bf16[128,1536]{1,0:T(8,128)(2,1)} %copy-done.6, bf16[128,1536]{1,0:T(8,128)(2,1)} %copy-done.20, bf16[1536,768]{1,0:T(8,128)(2,1)} %bitcast.283, bf16[2,6,128,128]{3,2,1,0:T(8,128)(2,1)} %get-tuple-element.137.queries, ...), custom_call_target="tpu_custom_call" | custom-call | tf_op jit(solution)/shard_map/attend_back/pallas_call | solution.py:663
  405.1 6.2 %all-to-all-start.1 = ((bf16[8,2,2,128,256]{4,3,2,1,0:T(8,128)(2,1)}), bf16[8,2,2,128,256]{4,3,2,1,0:T(8,128)(2,1)}, u32[]{:S(2)}, u32[]{:S(2)}) async-start(bf16[8,2,2,128,256]{4,3,2,1,0:T(8,128)(2,1)} %get-tuple-element.194), calls=%async_computation.1 | async-start | bytes 4194304 | tf_op jit(solution)/shard_map/all_to_all | solution.py:51
  424.4 7.5 %down_grads.1 = (bf16[2,280,1536]{2,1,0:T(8,128)(2,1)}, bf16[2,280,1536]{2,1,0:T(8,128)(2,1)}) custom-call(s32[2]{0:T(128)} %pad_add_fusion.2.where_ref, bf16[1024,1120]{1,0:T(8,128)(2,1)} %get-tuple-element.197.activated, bf16[1024,1536]{1,0:T(8,128)(2,1)} %all-gather.4.cloned.1.call-done.out_grad), custom_call_target="tpu_custom_call" | custom-call | tf_op jit(solution)/shard_map/down_grads/pallas_call | solution.py:439
  432.9 6.2 %all-to-all-done.1 = bf16[8,2,2,128,256]{4,3,2,1,0:T(8,128)(2,1)} async-done(((bf16[8,2,2,128,256]{4,3,2,1,0:T(8,128)(2,1)}), bf16[8,2,2,128,256]{4,3,2,1,0:T(8,128)(2,1)}, u32[]{:S(2)}, u32[]{:S(2)}) %all-to-all-start.1) | async-done | bytes 2097184 | tf_op jit(solution)/shard_map/all_to_all | solution.py:51
  439.1 15.2 %all-to-all-start.2 = ((bf16[8,48,1152]{2,1,0:T(8,128)(2,1)}), bf16[8,48,1152]{2,1,0:T(8,128)(2,1)}, u32[]{:S(2)}, u32[]{:S(2)}) async-start(bf16[8,48,1152]{2,1,0:T(8,128)(2,1)} %pad_maximum_fusion), calls=%async_computation.2 | async-start | bytes 1769472 | tf_op jit(solution)/shard_map/all_to_all | solution.py:71
  463.0 5.8 collective-permute-start.49
  471.8 18.3 %collective-permute-done.48 = bf16[1,2,128,256]{3,2,1,0:T(8,128)(2,1)S(1)} collective-permute-done((bf16[1,2,128,256]{3,2,1,0:T(8,128)(2,1)S(1)}, bf16[1,2,128,256]{3,2,1,0:T(8,128)(2,1)S(1)}, u32[]{:S(2)}, u32[]{:S(2)}) %collective-permute-start.48) | collective-permute-done | bytes 131104 | tf_op jit(solution)/shard_map/ppermute | solution.py:42
  501.1 4.2 all-to-all-start.3
  519.8 6.0 collective-permute-done.56
  525.9 7.7 %collective-permute-done.55 = bf16[2,2,2,48,512]{4,3,2,1,0:T(8,128)(2,1)S(1)} collective-permute-done((bf16[2,2,2,48,512]{4,3,2,1,0:T(8,128)(2,1)S(1)}, bf16[2,2,2,48,512]{4,3,2,1,0:T(8,128)(2,1)S(1)}, u32[]{:S(2)}, u32[]{:S(2)}) %collective-permute-start.55) | collective-permute-done | bytes 393248 | tf_op jit(solution)/shard_map/ppermute | solution.py:42
  544.4 3.9 all-to-all-start.4
  555.9 14.0 %collective-permute-done.63 = bf16[1,280,1536]{2,1,0:T(8,128)(2,1)S(1)} collective-permute-done((bf16[1,280,1536]{2,1,0:T(8,128)(2,1)S(1)}, bf16[1,280,1536]{2,1,0:T(8,128)(2,1)S(1)}, u32[]{:S(2)}, u32[]{:S(2)}) %collective-permute-start.63) | collective-permute-done | bytes 860192 | tf_op jit(solution)/shard_map/ppermute | solution.py:42
  572.3 6.8 %all-to-all-start.5 = ((f32[16,1,320]{2,1,0:T(1,128)}), f32[16,1,320]{2,1,0:T(1,128)S(1)}, u32[]{:S(2)}, u32[]{:S(2)}) async-start(f32[16,1,320]{2,1,0:T(1,128)} %pad_maximum_fusion.27), calls=%async_computation.6 | async-start | bytes 49152 | tf_op jit(solution)/shard_map/all_to_all | solution.py:970
  583.8 3.6 unpack_members.1
  587.5 5.3 collective-permute-done.65
  (421 shorter events, 166.7 us)
Async XLA Ops:
  7.2 23.1 %collective-permute-start.5 = (bf16[280,1536]{1,0:T(8,128)(2,1)}, bf16[280,1536]{1,0:T(8,128)(2,1)}, u32[]{:S(2)}, u32[]{:S(2)}) collective-permute-start(bf16[280,1536]{1,0:T(8,128)(2,1)} %param.21), channel_id=1, source_target_pairs={{0,2},{2,0},{4,6},{6,4},{8,10},{10,8},{12,14},{14,12},{16,18},{18,... | collective-permute-start | bytes 2580488 | tf_op jit(solution)/shard_map/ppermute | solution.py:42
  30.3 65.6 %all-to-all-start = ((bf16[8,48,2304]{2,1,0:T(8,128)(2,1)}), bf16[8,48,2304]{2,1,0:T(8,128)(2,1)S(1)}, u32[]{:S(2)}, u32[]{:S(2)}) async-start(bf16[8,48,2304]{2,1,0:T(8,128)(2,1)} %pack_members.1), calls=%async_computation | async-start | bytes 3538944 | tf_op jit(solution)/shard_map/all_to_all | solution.py:71
  36.1 122.6 %all-gather.6.cloned.1.call-start = ((), (), s32[]{:S(2)}) async-start(), calls=%async_computation.9 | async-start | bytes 2506752 | tf_op jit(solution)/shard_map/all_gather | solution.py:730
  36.9 258.4 %all-gather.4.cloned.1.call-start = ((), (), s32[]{:S(2)}) async-start(), calls=%async_computation.7 | async-start | bytes 3538944 | tf_op jit(solution)/shard_map/all_gather | solution.py:731
  37.0 40.3 %collective-permute-start = (s32[4]{0:T(128)S(1)}, s32[4]{0:T(128)S(1)}, u32[]{:S(2)}, u32[]{:S(2)}) collective-permute-start(s32[4]{0:T(128)S(1)} %bitcast.312), channel_id=1, source_target_pairs={{0,1},{1,0},{2,3},{3,2},{4,5},{5,4},{6,7},{7,6},{8,9},{9,8},{10,11... | collective-permute-start | bytes 56 | tf_op jit(solution)/shard_map/ppermute | solution.py:37
  37.1 95.4 %collective-permute-start.1 = (bf16[128,1536]{1,0:T(8,128)(2,1)S(1)}, bf16[128,1536]{1,0:T(8,128)(2,1)}, u32[]{:S(2)}, u32[]{:S(2)}) collective-permute-start(bf16[128,1536]{1,0:T(8,128)(2,1)S(1)} %bitcast.285), channel_id=1, source_target_pairs={{0,1},{1,0},{2,3},{3,2},{4,5},{5,4},{6,7},{7,6},{8,9},{9,8},{10,11... | collective-permute-start | bytes 1179656 | tf_op jit(solution)/shard_map/ppermute | solution.py:37
  37.6 34.5 %collective-permute-start.10 = (bf16[2,2,64,256]{3,2,1,0:T(8,128)(2,1)S(1)}, bf16[2,2,64,256]{3,2,1,0:T(8,128)(2,1)S(1)}, u32[]{:S(2)}, u32[]{:S(2)}) collective-permute-start(bf16[2,2,64,256]{3,2,1,0:T(8,128)(2,1)S(1)} %slice.173), channel_id=1, source_target_pairs={{0,8},{2,10},{4,12},{6,14},{8,0},{10,2},{12,4},{14,6},{16,24},{18,... | collective-permute-start | bytes 393224 | tf_op jit(solution)/shard_map/ppermute | solution.py:42
  39.7 33.1 %collective-permute-start.8 = (bf16[2,2,48,384]{3,2,1,0:T(8,128)(2,1)S(1)}, bf16[2,2,48,384]{3,2,1,0:T(8,128)(2,1)S(1)}, u32[]{:S(2)}, u32[]{:S(2)}) collective-permute-start(bf16[2,2,48,384]{3,2,1,0:T(8,128)(2,1)S(1)} %get-tuple-element.259), channel_id=1, source_target_pairs={{0,4},{2,6},{4,0},{6,2},{8,12},{10,14},{12,8},{14,10},{16,20},{18,... | collective-permute-start | bytes 442376 | tf_op jit(solution)/shard_map/ppermute | solution.py:42
  41.8 33.6 %collective-permute-start.6 = (bf16[2,2,48,384]{3,2,1,0:T(8,128)(2,1)S(1)}, bf16[2,2,48,384]{3,2,1,0:T(8,128)(2,1)S(1)}, u32[]{:S(2)}, u32[]{:S(2)}) collective-permute-start(bf16[2,2,48,384]{3,2,1,0:T(8,128)(2,1)S(1)} %get-tuple-element.260), channel_id=1, source_target_pairs={{0,2},{2,0},{4,6},{6,4},{8,10},{10,8},{12,14},{14,12},{16,18},{18,... | collective-permute-start | bytes 442376 | tf_op jit(solution)/shard_map/ppermute | solution.py:42
  72.9 20.6 %collective-permute-start.9 = (bf16[4,2,48,384]{3,2,1,0:T(8,128)(2,1)S(1)}, bf16[4,2,48,384]{3,2,1,0:T(8,128)(2,1)}, u32[]{:S(2)}, u32[]{:S(2)}) collective-permute-start(bf16[4,2,48,384]{3,2,1,0:T(8,128)(2,1)S(1)} %pad_maximum_fusion.16), channel_id=1, source_target_pairs={{0,8},{2,10},{4,12},{6,14},{8,0},{10,2},{12,4},{14,6},{16,24},{18,... | collective-permute-start | bytes 884744 | tf_op jit(solution)/shard_map/ppermute | solution.py:42
  76.2 18.3 %collective-permute-start.7 = (bf16[4,2,48,384]{3,2,1,0:T(8,128)(2,1)}, bf16[4,2,48,384]{3,2,1,0:T(8,128)(2,1)}, u32[]{:S(2)}, u32[]{:S(2)}) collective-permute-start(bf16[4,2,48,384]{3,2,1,0:T(8,128)(2,1)} %pad_maximum_fusion.15), channel_id=1, source_target_pairs={{0,4},{2,6},{4,0},{6,2},{8,12},{10,14},{12,8},{14,10},{16,20},{18,... | collective-permute-start | bytes 884744 | tf_op jit(solution)/shard_map/ppermute | solution.py:42
  95.9 27.5 %collective-permute-start.12 = (bf16[8,2,48,384]{3,2,1,0:T(8,128)(2,1)S(1)}, bf16[8,2,48,384]{3,2,1,0:T(8,128)(2,1)S(1)}, u32[]{:S(2)}, u32[]{:S(2)}) collective-permute-start(bf16[8,2,48,384]{3,2,1,0:T(8,128)(2,1)S(1)} %pad_maximum_fusion.5.refs_0_), channel_id=1, source_target_pairs={{0,8},{2,10},{4,12},{6,14},{8,0},{10,2},{12,4},{14,6},{16,24},{18,... | collective-permute-start | bytes 1769480 | tf_op jit(solution)/shard_map/ppermute | solution.py:42
  95.9 27.4 %collective-permute-start.13 = (bf16[8,2,48,384]{3,2,1,0:T(8,128)(2,1)S(1)}, bf16[8,2,48,384]{3,2,1,0:T(8,128)(2,1)S(1)}, u32[]{:S(2)}, u32[]{:S(2)}) collective-permute-start(bf16[8,2,48,384]{3,2,1,0:T(8,128)(2,1)S(1)} %pad_maximum_fusion.6.refs_2_), channel_id=1, source_target_pairs={{0,2},{2,0},{4,6},{6,4},{8,10},{10,8},{12,14},{14,12},{16,18},{18,... | collective-permute-start | bytes 1769480 | tf_op jit(solution)/shard_map/ppermute | solution.py:42
  96.6 21.1 %collective-permute-start.14 = (bf16[8,2,64,256]{3,2,1,0:T(8,128)(2,1)}, bf16[8,2,64,256]{3,2,1,0:T(8,128)(2,1)S(1)}, u32[]{:S(2)}, u32[]{:S(2)}) collective-permute-start(bf16[8,2,64,256]{3,2,1,0:T(8,128)(2,1)} %pad_maximum_fusion.9.refs_4_), channel_id=1, source_target_pairs={{0,4},{2,6},{4,0},{6,2},{8,12},{10,14},{12,8},{14,10},{16,20},{18,... | collective-permute-start | bytes 1572872 | tf_op jit(solution)/shard_map/ppermute | solution.py:42
  130.7 16.9 %collective-permute-start.15 = (bf16[3,48,2304]{2,1,0:T(8,128)(2,1)S(1)}, bf16[3,48,2304]{2,1,0:T(8,128)(2,1)}, u32[]{:S(2)}, u32[]{:S(2)}) collective-permute-start(bf16[3,48,2304]{2,1,0:T(8,128)(2,1)S(1)} %slice.179), channel_id=1, source_target_pairs={{0,2},{2,0},{4,6},{6,4},{8,10},{10,8},{12,14},{14,12},{16,18},{18,... | collective-permute-start | bytes 1990664 | tf_op jit(solution)/shard_map/ppermute | solution.py:42
  158.0 42.0 %collective-permute-start.23 = (bf16[5,48,2304]{2,1,0:T(8,128)(2,1)}, bf16[5,48,2304]{2,1,0:T(8,128)(2,1)}, u32[]{:S(2)}, u32[]{:S(2)}) collective-permute-start(bf16[5,48,2304]{2,1,0:T(8,128)(2,1)} %slice.183), channel_id=1, source_target_pairs={{0,2},{2,0},{4,6},{6,4},{8,10},{10,8},{12,14},{14,12},{16,18},{18,... | collective-permute-start | bytes 3317768 | tf_op jit(solution)/shard_map/ppermute | solution.py:42
  158.2 43.8 %collective-permute-start.27 = (bf16[280,1536]{1,0:T(8,128)(2,1)}, bf16[280,1536]{1,0:T(8,128)(2,1)}, u32[]{:S(2)}, u32[]{:S(2)}) collective-permute-start(bf16[280,1536]{1,0:T(8,128)(2,1)} %param.21), channel_id=1, source_target_pairs={{0,1},{1,0},{2,3},{3,2},{4,5},{5,4},{6,7},{7,6},{8,9},{9,8},{10,11... | collective-permute-start | bytes 2580488 | tf_op jit(solution)/shard_map/ppermute | solution.py:37
  158.2 43.8 %collective-permute-start.28 = (bf16[280,1536]{1,0:T(8,128)(2,1)}, bf16[280,1536]{1,0:T(8,128)(2,1)}, u32[]{:S(2)}, u32[]{:S(2)}) collective-permute-start(bf16[280,1536]{1,0:T(8,128)(2,1)} %collective-permute-done.5), channel_id=1, source_target_pairs={{0,1},{1,0},{2,3},{3,2},{4,5},{5,4},{6,7},{7,6},{8,9},{9,8},{10,11... | collective-permute-start | bytes 2580488 | tf_op jit(solution)/shard_map/ppermute | solution.py:37
  163.1 24.4 %collective-permute-start.17 = (bf16[2,2,48,256]{3,2,1,0:T(8,128)(2,1)S(1)}, bf16[2,2,48,256]{3,2,1,0:T(8,128)(2,1)S(1)}, u32[]{:S(2)}, u32[]{:S(2)}) collective-permute-start(bf16[2,2,48,256]{3,2,1,0:T(8,128)(2,1)S(1)} %get-tuple-element.265), channel_id=1, source_target_pairs={{0,2},{2,0},{4,6},{6,4},{8,10},{10,8},{12,14},{14,12},{16,18},{18,... | collective-permute-start | bytes 294920 | tf_op jit(solution)/shard_map/ppermute | solution.py:42
  164.9 24.3 %collective-permute-start.22 = (bf16[4,2,32,256]{3,2,1,0:T(8,128)(2,1)S(1)}, bf16[4,2,32,256]{3,2,1,0:T(8,128)(2,1)S(1)}, u32[]{:S(2)}, u32[]{:S(2)}) collective-permute-start(bf16[4,2,32,256]{3,2,1,0:T(8,128)(2,1)S(1)} %pad_maximum_fusion.26), channel_id=1, source_target_pairs={{0,2},{2,0},{4,6},{6,4},{8,10},{10,8},{12,14},{14,12},{16,18},{18,... | collective-permute-start | bytes 393224 | tf_op jit(solution)/shard_map/ppermute | solution.py:42
  199.9 18.6 %collective-permute-start.24 = (bf16[8,2,48,256]{3,2,1,0:T(8,128)(2,1)S(1)}, bf16[8,2,48,256]{3,2,1,0:T(8,128)(2,1)S(1)}, u32[]{:S(2)}, u32[]{:S(2)}) collective-permute-start(bf16[8,2,48,256]{3,2,1,0:T(8,128)(2,1)S(1)} %pad_maximum_fusion.12.refs_0_), channel_id=1, source_target_pairs={{0,8},{2,10},{4,12},{6,14},{8,0},{10,2},{12,4},{14,6},{16,24},{18,... | collective-permute-start | bytes 1179656 | tf_op jit(solution)/shard_map/ppermute | solution.py:42
  200.0 18.5 %collective-permute-start.25 = (bf16[8,2,48,256]{3,2,1,0:T(8,128)(2,1)S(1)}, bf16[8,2,48,256]{3,2,1,0:T(8,128)(2,1)}, u32[]{:S(2)}, u32[]{:S(2)}) collective-permute-start(bf16[8,2,48,256]{3,2,1,0:T(8,128)(2,1)S(1)} %pad_maximum_fusion.13.refs_2_), channel_id=1, source_target_pairs={{0,2},{2,0},{4,6},{6,4},{8,10},{10,8},{12,14},{14,12},{16,18},{18,... | collective-permute-start | bytes 1179656 | tf_op jit(solution)/shard_map/ppermute | solution.py:42
  235.5 20.5 %collective-permute-start.30 = (bf16[1,128,1536]{2,1,0:T(8,128)(2,1)S(1)}, bf16[1,128,1536]{2,1,0:T(8,128)(2,1)S(1)}, u32[]{:S(2)}, u32[]{:S(2)}) collective-permute-start(bf16[1,128,1536]{2,1,0:T(8,128)(2,1)S(1)} %fusion.29), channel_id=1, source_target_pairs={{0,16},{2,18},{4,20},{6,22},{8,24},{10,26},{12,28},{14,30},{16,0},... | collective-permute-start | bytes 1179656 | tf_op jit(solution)/shard_map/ppermute | solution.py:42
  237.8 57.5 %collective-permute-start.35 = (bf16[8,48,2304]{2,1,0:T(8,128)(2,1)S(1)}, bf16[8,48,2304]{2,1,0:T(8,128)(2,1)}, u32[]{:S(2)}, u32[]{:S(2)}) collective-permute-start(bf16[8,48,2304]{2,1,0:T(8,128)(2,1)S(1)} %all-to-all-done.refs_0_), channel_id=1, source_target_pairs={{0,1},{1,0},{2,3},{3,2},{4,5},{5,4},{6,7},{7,6},{8,9},{9,8},{10,11... | collective-permute-start | bytes 5308424 | tf_op jit(solution)/shard_map/ppermute | solution.py:37
  261.5 33.8 %collective-permute-start.37 = (bf16[5,48,2304]{2,1,0:T(8,128)(2,1)}, bf16[5,48,2304]{2,1,0:T(8,128)(2,1)}, u32[]{:S(2)}, u32[]{:S(2)}) collective-permute-start(bf16[5,48,2304]{2,1,0:T(8,128)(2,1)} %collective-permute-done.23.refs_4_), channel_id=1, source_target_pairs={{0,1},{1,0},{2,3},{3,2},{4,5},{5,4},{6,7},{7,6},{8,9},{9,8},{10,11... | collective-permute-start | bytes 3317768 | tf_op jit(solution)/shard_map/ppermute | solution.py:37
  267.5 21.6 %collective-permute-start.32 = (bf16[4,64,1536]{2,1,0:T(8,128)(2,1)}, bf16[4,64,1536]{2,1,0:T(8,128)(2,1)}, u32[]{:S(2)}, u32[]{:S(2)}) collective-permute-start(bf16[4,64,1536]{2,1,0:T(8,128)(2,1)} %pad_maximum_fusion.2.refs_0_), channel_id=1, source_target_pairs={{0,4},{2,6},{4,0},{6,2},{8,12},{10,14},{12,8},{14,10},{16,20},{18,... | collective-permute-start | bytes 2359304 | tf_op jit(solution)/shard_map/ppermute | solution.py:42
  273.3 18.2 %collective-permute-start.34 = (bf16[4,64,1536]{2,1,0:T(8,128)(2,1)}, bf16[4,64,1536]{2,1,0:T(8,128)(2,1)}, u32[]{:S(2)}, u32[]{:S(2)}) collective-permute-start(bf16[4,64,1536]{2,1,0:T(8,128)(2,1)} %pad_maximum_fusion.3.refs_2_), channel_id=1, source_target_pairs={{0,8},{2,10},{4,12},{6,14},{8,0},{10,2},{12,4},{14,6},{16,24},{18,... | collective-permute-start | bytes 2359304 | tf_op jit(solution)/shard_map/ppermute | solution.py:42
  274.5 20.9 %collective-permute-start.36 = (bf16[3,48,2304]{2,1,0:T(8,128)(2,1)}, bf16[3,48,2304]{2,1,0:T(8,128)(2,1)}, u32[]{:S(2)}, u32[]{:S(2)}) collective-permute-start(bf16[3,48,2304]{2,1,0:T(8,128)(2,1)} %collective-permute-done.15.refs_2_), channel_id=1, source_target_pairs={{0,1},{1,0},{2,3},{3,2},{4,5},{5,4},{6,7},{7,6},{8,9},{9,8},{10,11... | collective-permute-start | bytes 1990664 | tf_op jit(solution)/shard_map/ppermute | solution.py:37
  326.3 17.6 %collective-permute-start.39 = (bf16[2,2,64,1536]{3,2,0,1:T(8,128)(2,1)}, bf16[2,2,64,1536]{3,2,0,1:T(8,128)(2,1)}, u32[]{:S(2)}, u32[]{:S(2)}) collective-permute-start(bf16[2,2,64,1536]{3,2,0,1:T(8,128)(2,1)} %bitcast.267), channel_id=1, source_target_pairs={{0,8},{2,10},{4,12},{6,14},{8,0},{10,2},{12,4},{14,6},{16,24},{18,... | collective-permute-start | bytes 2359304 | tf_op jit(solution)/shard_map/ppermute | solution.py:42
  328.0 17.2 %collective-permute-start.38 = (bf16[2,2,64,1536]{3,2,0,1:T(8,128)(2,1)S(1)}, bf16[2,2,64,1536]{3,2,0,1:T(8,128)(2,1)S(1)}, u32[]{:S(2)}, u32[]{:S(2)}) collective-permute-start(bf16[2,2,64,1536]{3,2,0,1:T(8,128)(2,1)S(1)} %bitcast.296), channel_id=1, source_target_pairs={{0,4},{2,6},{4,0},{6,2},{8,12},{10,14},{12,8},{14,10},{16,20},{18,... | collective-permute-start | bytes 2359304 | tf_op jit(solution)/shard_map/ppermute | solution.py:42
  359.3 17.6 %collective-permute-start.44 = (bf16[64,1536]{1,0:T(8,128)(2,1)S(1)}, bf16[64,1536]{1,0:T(8,128)(2,1)S(1)}, u32[]{:S(2)}, u32[]{:S(2)}) collective-permute-start(bf16[64,1536]{1,0:T(8,128)(2,1)S(1)} %dynamic-slice_bitcast_fusion.10), channel_id=1, source_target_pairs={{0,16},{2,18},{4,20},{6,22},{8,24},{10,26},{12,28},{14,30},{16,0},... | collective-permute-start | bytes 589832 | tf_op jit(solution)/shard_map/ppermute | solution.py:42
  363.0 17.3 %collective-permute-start.43 = (bf16[64,1536]{1,0:T(8,128)(2,1)S(1)}, bf16[64,1536]{1,0:T(8,128)(2,1)S(1)}, u32[]{:S(2)}, u32[]{:S(2)}) collective-permute-start(bf16[64,1536]{1,0:T(8,128)(2,1)S(1)} %dynamic-slice_bitcast_fusion.11), channel_id=1, source_target_pairs={{0,16},{2,18},{4,20},{6,22},{8,24},{10,26},{12,28},{14,30},{16,0},... | collective-permute-start | bytes 589832 | tf_op jit(solution)/shard_map/ppermute | solution.py:42
  405.1 34.0 %all-to-all-start.1 = ((bf16[8,2,2,128,256]{4,3,2,1,0:T(8,128)(2,1)}), bf16[8,2,2,128,256]{4,3,2,1,0:T(8,128)(2,1)}, u32[]{:S(2)}, u32[]{:S(2)}) async-start(bf16[8,2,2,128,256]{4,3,2,1,0:T(8,128)(2,1)} %get-tuple-element.194), calls=%async_computation.1 | async-start | bytes 4194304 | tf_op jit(solution)/shard_map/all_to_all | solution.py:51
  411.3 160.1 %reduce-scatter.2.cloned.1.call-start = ((), (), s32[]{:S(2)}) async-start(), calls=%async_computation.8 | async-start | bytes 3538944 | tf_op jit(solution)/shard_map/reduce_scatter | solution.py:845
  418.0 43.1 %collective-permute-start.52 = (bf16[8,1,48,512]{3,2,0,1:T(8,128)(2,1)}, bf16[8,1,48,512]{3,2,0,1:T(8,128)(2,1)}, u32[]{:S(2)}, u32[]{:S(2)}) collective-permute-start(bf16[8,1,48,512]{3,2,0,1:T(8,128)(2,1)} %constant_dynamic-slice_fusion.9), channel_id=1, source_target_pairs={{0,2},{2,0},{4,6},{6,4},{8,10},{10,8},{12,14},{14,12},{16,18},{18,... | collective-permute-start | bytes 1179656 | tf_op jit(solution)/shard_map/ppermute | solution.py:42
  439.1 62.0 %all-to-all-start.2 = ((bf16[8,48,1152]{2,1,0:T(8,128)(2,1)}), bf16[8,48,1152]{2,1,0:T(8,128)(2,1)}, u32[]{:S(2)}, u32[]{:S(2)}) async-start(bf16[8,48,1152]{2,1,0:T(8,128)(2,1)} %pad_maximum_fusion), calls=%async_computation.2 | async-start | bytes 1769472 | tf_op jit(solution)/shard_map/all_to_all | solution.py:71
  458.1 31.9 %collective-permute-start.48 = (bf16[1,2,128,256]{3,2,1,0:T(8,128)(2,1)S(1)}, bf16[1,2,128,256]{3,2,1,0:T(8,128)(2,1)S(1)}, u32[]{:S(2)}, u32[]{:S(2)}) collective-permute-start(bf16[1,2,128,256]{3,2,1,0:T(8,128)(2,1)S(1)} %constant_dynamic-slice_fusion.10), channel_id=1, source_target_pairs={{0,16},{2,18},{4,20},{6,22},{8,24},{10,26},{12,28},{14,30},{16,0},... | collective-permute-start | bytes 393224 | tf_op jit(solution)/shard_map/ppermute | solution.py:42
  463.0 38.1 %collective-permute-start.49 = (bf16[2,2,2,2,48,512]{5,4,3,0,1,2:T(8,128)(2,1)}, bf16[2,2,2,2,48,512]{5,4,3,0,1,2:T(8,128)(2,1)}, u32[]{:S(2)}, u32[]{:S(2)}) collective-permute-start(bf16[2,2,2,2,48,512]{5,4,3,0,1,2:T(8,128)(2,1)} %bitcast.295), channel_id=1, source_target_pairs={{0,2},{2,0},{4,6},{6,4},{8,10},{10,8},{12,14},{14,12},{16,18},{18,... | collective-permute-start | bytes 2359304 | tf_op jit(solution)/shard_map/ppermute | solution.py:42
  468.8 32.3 %collective-permute-start.50 = (bf16[2,2,2,2,48,512]{5,4,3,2,1,0:T(8,128)(2,1)}, bf16[2,2,2,2,48,512]{5,4,3,2,1,0:T(8,128)(2,1)}, u32[]{:S(2)}, u32[]{:S(2)}) collective-permute-start(bf16[2,2,2,2,48,512]{5,4,3,2,1,0:T(8,128)(2,1)} %fusion.9), channel_id=1, source_target_pairs={{0,4},{2,6},{4,0},{6,2},{8,12},{10,14},{12,8},{14,10},{16,20},{18,... | collective-permute-start | bytes 2359304 | tf_op jit(solution)/shard_map/ppermute | solution.py:42
  470.3 30.8 %collective-permute-start.51 = (bf16[2,2,2,2,48,512]{5,4,3,0,1,2:T(8,128)(2,1)}, bf16[2,2,2,2,48,512]{5,4,3,0,1,2:T(8,128)(2,1)}, u32[]{:S(2)}, u32[]{:S(2)}) collective-permute-start(bf16[2,2,2,2,48,512]{5,4,3,0,1,2:T(8,128)(2,1)} %bitcast.294), channel_id=1, source_target_pairs={{0,8},{2,10},{4,12},{6,14},{8,0},{10,2},{12,4},{14,6},{16,24},{18,... | collective-permute-start | bytes 2359304 | tf_op jit(solution)/shard_map/ppermute | solution.py:42
  471.7 64.3 %collective-permute-start.57 = (bf16[2,280,1536]{2,1,0:T(8,128)(2,1)}, bf16[2,280,1536]{2,1,0:T(8,128)(2,1)}, u32[]{:S(2)}, u32[]{:S(2)}) collective-permute-start(bf16[2,280,1536]{2,1,0:T(8,128)(2,1)} %get-tuple-element.212), channel_id=1, source_target_pairs={{0,1},{1,0},{2,3},{3,2},{4,5},{5,4},{6,7},{7,6},{8,9},{9,8},{10,11... | collective-permute-start | bytes 5160968 | tf_op jit(solution)/shard_map/ppermute | solution.py:37
  501.1 34.9 %all-to-all-start.3 = ((bf16[8,2,2,48,256]{4,3,2,1,0:T(8,128)(2,1)}), bf16[8,2,2,48,256]{4,3,2,1,0:T(8,128)(2,1)}, u32[]{:S(2)}, u32[]{:S(2)}) async-start(bf16[8,2,2,48,256]{4,3,2,1,0:T(8,128)(2,1)} %bitcast.287), calls=%async_computation.3 | async-start | bytes 1572864 | tf_op jit(solution)/shard_map/all_to_all | solution.py:51
  507.2 18.6 %collective-permute-start.56 = (bf16[2,2,2,48,512]{4,3,2,0,1:T(8,128)(2,1)S(1)}, bf16[2,2,2,48,512]{4,3,2,0,1:T(8,128)(2,1)S(1)}, u32[]{:S(2)}, u32[]{:S(2)}) collective-permute-start(bf16[2,2,2,48,512]{4,3,2,0,1:T(8,128)(2,1)S(1)} %dynamic-slice_bitcast_fusion), channel_id=1, source_target_pairs={{0,2},{2,0},{4,6},{6,4},{8,10},{10,8},{12,14},{14,12},{16,18},{18,... | collective-permute-start | bytes 1179656 | tf_op jit(solution)/shard_map/ppermute | solution.py:42
  510.6 23.0 %collective-permute-start.55 = (bf16[2,2,2,48,512]{4,3,2,1,0:T(8,128)(2,1)S(1)}, bf16[2,2,2,48,512]{4,3,2,1,0:T(8,128)(2,1)S(1)}, u32[]{:S(2)}, u32[]{:S(2)}) collective-permute-start(bf16[2,2,2,48,512]{4,3,2,1,0:T(8,128)(2,1)S(1)} %dynamic-slice_bitcast_fusion.1), channel_id=1, source_target_pairs={{0,8},{2,10},{4,12},{6,14},{8,0},{10,2},{12,4},{14,6},{16,24},{18,... | collective-permute-start | bytes 1179656 | tf_op jit(solution)/shard_map/ppermute | solution.py:42
  513.7 20.0 %collective-permute-start.54 = (bf16[2,2,2,48,512]{4,3,2,0,1:T(8,128)(2,1)S(1)}, bf16[2,2,2,48,512]{4,3,2,0,1:T(8,128)(2,1)S(1)}, u32[]{:S(2)}, u32[]{:S(2)}) collective-permute-start(bf16[2,2,2,48,512]{4,3,2,0,1:T(8,128)(2,1)S(1)} %dynamic-slice_bitcast_fusion.2), channel_id=1, source_target_pairs={{0,4},{2,6},{4,0},{6,2},{8,12},{10,14},{12,8},{14,10},{16,20},{18,... | collective-permute-start | bytes 1179656 | tf_op jit(solution)/shard_map/ppermute | solution.py:42
  515.3 20.6 %collective-permute-start.53 = (bf16[8,1,48,640]{3,2,0,1:T(8,128)(2,1)S(1)}, bf16[8,1,48,640]{3,2,0,1:T(8,128)(2,1)S(1)}, u32[]{:S(2)}, u32[]{:S(2)}) collective-permute-start(bf16[8,1,48,640]{3,2,0,1:T(8,128)(2,1)S(1)} %constant_dynamic-slice_fusion.8), channel_id=1, source_target_pairs={{0,2},{2,0},{4,6},{6,4},{8,10},{10,8},{12,14},{14,12},{16,18},{18,... | collective-permute-start | bytes 1474568 | tf_op jit(solution)/shard_map/ppermute | solution.py:42
  544.4 27.0 %all-to-all-start.4 = ((bf16[8,48,1152]{2,1,0:T(8,128)(2,1)}), bf16[8,48,1152]{2,1,0:T(8,128)(2,1)S(1)}, u32[]{:S(2)}, u32[]{:S(2)}) async-start(bf16[8,48,1152]{2,1,0:T(8,128)(2,1)} %pad_maximum_fusion.1), calls=%async_computation.4 | async-start | bytes 1769472 | tf_op jit(solution)/shard_map/all_to_all | solution.py:71
  550.3 19.7 %collective-permute-start.63 = (bf16[1,280,1536]{2,1,0:T(8,128)(2,1)S(1)}, bf16[1,280,1536]{2,1,0:T(8,128)(2,1)S(1)}, u32[]{:S(2)}, u32[]{:S(2)}) collective-permute-start(bf16[1,280,1536]{2,1,0:T(8,128)(2,1)S(1)} %constant_dynamic-slice_fusion.4), channel_id=1, source_target_pairs={{0,2},{2,0},{4,6},{6,4},{8,10},{10,8},{12,14},{14,12},{16,18},{18,... | collective-permute-start | bytes 2580488 | tf_op jit(solution)/shard_map/ppermute | solution.py:42
  (86 other events, 922.6 us)
Sparse Core Ops, SparseCore 0:
  39.8 84.1 all-gather.5
  158.9 69.2 all-gather.3
  415.7 109.4 reduce-scatter.1

commit v3 on v2

--- a/solution.py
+++ b/solution.py
@@ -25,7 +25,7 @@
 
 
 def after(x, *others):
-    return lax.optimization_barrier((x,) + others)[0]
+    return together(x, *others)[0]
 
 
 def together(*groups):
@@ -400,9 +400,9 @@
         send[i] = jnp.where(core == 0, upper, low)
 
 
-def gate_up_grads(normed, pre_grad, rows_dev, where, tile=384):
+def gate_up_grads(normed, pre_grad, side, rows_dev, where, tile=384):
     rows, width = normed.shape
-    wide = pre_grad.shape[1]
+    wide = pre_grad.shape[1] // 2
     chips, step = width // (2 * rows_dev), tile // (2 * rows_dev)
     result = pl.BlockSpec((step, rows_dev, wide), lambda i: (i, 0, 0))
     return pl.pallas_call(
@@ -412,7 +412,7 @@
         in_specs=[
             SMEM,
             pl.BlockSpec((rows, tile), lambda i: (0, i)),
-            pl.BlockSpec((rows, wide), lambda i: (0, 0), pipeline_mode=pl.Buffered(1)),
+            pl.BlockSpec((rows, wide), lambda i: (0, side), pipeline_mode=pl.Buffered(1)),
         ],
         out_specs=[result] * 2,
         compiler_params=BIG,
@@ -737,15 +737,13 @@
     column_cuts = ((0, hq // 2, rows_dev), (hq // 2, hq, rows_dev), (hq, hq + 2 * HD, rows_dev + 16))
     qkv_parts = [qkv_pair[:, :, :rows, start:stop] for start, stop, rows in column_cuts]
     qkv_parts = doubled(qkv_parts, [order[0] for order in ORDERS])
-    packed = group_exchange(packed)
     down_other = [core_swap(x) for x in down_found]
     qkv_parts = doubled(qkv_parts, [order[1] for order in ORDERS])
+    qkv_parts = with_arrived(qkv_parts, [order[2] for order in ORDERS])
     qkv_parts, packed = together(qkv_parts, packed)
-    packed_other = core_swap(packed)
-    qkv_parts = with_arrived(qkv_parts, [order[2] for order in ORDERS])
-    shares = ((0, 3), (3, 8))
-    qkv_parts, packed = together(qkv_parts, packed)
-    packed_found = [gather_list(packed[:3], group_bits())]
+    row_cut = rows_dev // 3
+    first_rows, later_rows = packed[:, :row_cut], packed[:, row_cut:]
+    first_rows = group_exchange(first_rows)
 
     inner = jnp.arange(tok_dev, dtype=jnp.int32)
     blocks = jnp.where(inner < half, chip, 2 * ctx_size - 1 - chip)
@@ -772,23 +770,26 @@
     gain_two = small_all[:, n_gain + n_bias : 2 * n_gain + n_bias].reshape(1, -1)
     bias = head_columns(bias, core)
     normed_one, queries, kv_own = project(token_own, token_other, gain_one, qkv_w, bias, cos, sin)
-    kv_own, packed_found, packed = together(kv_own, packed_found, packed)
-
     kv_own = gather_relative(kv_own[None], high)
-    kv_own, packed = together(kv_own, packed)
-    packed_found.append(gather_list(packed[3:], group_bits()))
+    kv_own, first_rows = together(kv_own, first_rows)
+
     kv_parts = [kv_own[:, :, start:stop] for start, stop in cuts]
     for step in range(2):
         kv_parts = doubled(kv_parts, [order[step] for order in ORDERS])
-    kv_parts, packed_found, packed = together(kv_parts, packed_found, packed)
     down = order_rows([x[None] for x in down_found], [x[None] for x in down_other], group_flips, where)
     down = down.reshape(ff_own, width)
     kv_parts = with_arrived(kv_parts, [order[2] for order in ORDERS])
-    kv_parts, down, out_w = together(kv_parts, down, out_w)
+    kv_parts, down, later_rows, first_rows = together(kv_parts, down, later_rows, first_rows)
+    later_rows = group_exchange(later_rows)
     kv, attended, attended_b, logs, branch = attend(
         where, ranges, queries, starts, places, out_w, kv_parts, flips, cuts
     )
     branch_other = core_swap(branch[1])
+    branch_other, later_rows, first_rows = together(branch_other, later_rows, first_rows)
+    packed = jnp.concatenate([first_rows, later_rows], axis=1)
+    shares = ((0, 4), (4, 8))
+    packed_found = [gather_list(packed[:4], group_bits())]
+    packed_other = core_swap(packed)
     inputs = token_own.astype(f32)
     hidden_res = inputs + branch[0] + branch_other
     scale_two = lax.rsqrt(jnp.mean(hidden_res * hidden_res, axis=-1, keepdims=True) + EPSILON)
@@ -797,9 +798,13 @@
     group_orders = ((upper, middle, low), (upper, low, middle))
     group_cuts = ((0, half), (half, tok_dev))
     token_parts = gather_relative(normed_two[None], (upper,))
+    token_parts, packed, packed_found = together(token_parts, packed, packed_found)
     token_parts = [token_parts[:, start:stop] for start, stop in group_cuts]
     token_parts = doubled(token_parts, [order[1] for order in group_orders])
+    packed_found.append(gather_list(packed[4:], group_bits()))
+    token_parts, out_grad_all = together(token_parts, out_grad_all)
     token_parts = with_arrived(token_parts, [order[2] for order in group_orders])
+    token_parts, packed_found = together(token_parts, packed_found)
     token_flips = [relative_flips(order) for order in group_orders]
     normed_all = order_tokens(token_parts, token_flips, group_cuts, groups, where)
     normed_all = normed_all.reshape(8 * tok_dev, width)
@@ -827,53 +832,60 @@
     )
     bits = [order[2] for order in group_orders]
     kept, sent = scatter.split(bits)
-    gu_keep, gu_send = gate_up_grads(normed_all, after(pre_grad, *sent), rows_dev, where)
+    gate_keep, gate_send = gate_up_grads(normed_all, after(pre_grad, *sent), 0, rows_dev, where)
+    gate_arrived = core_swap(gate_send)
+    branch_part = dot(after(activated, gate_send), down, 1, 0).astype(bf16)
     scatter.step(bits, kept, sent)
-    scatter.parts, gu_keep, gu_send = together(scatter.parts, gu_keep, gu_send)
+    scatter.parts, gate_arrived, branch_part = together(scatter.parts, gate_arrived, branch_part)
+
+    def of_cores(keep, arrived):
+        total = (keep.astype(f32) + arrived.astype(f32)).astype(bf16)
+        return total.reshape(8, groups, rows_dev, -1)
+
+    def of_group(total):
+        return sum_over(total, 1, tuple(reversed(group_bits()))).astype(bf16)
 
     bits = [order[1] for order in group_orders]
     kept, sent = scatter.split(bits)
-    gu_arrived = core_swap(gu_send)
-    branch_part = dot(after(activated, *sent), down, 1, 0).astype(bf16)
+    gate_total = of_cores(gate_keep, gate_arrived)
     scatter.step(bits, kept, sent)
-    scatter.parts, branch_part, gu_arrived = together(scatter.parts, branch_part, gu_arrived)
+    scatter.parts, gate_total, pre_grad = together(scatter.parts, gate_total, pre_grad)
 
     kept, sent = scatter.split((upper, upper))
-    gu_sum = (gu_keep.astype(f32) + gu_arrived.astype(f32)).astype(bf16)
+    grad_gate = of_group(gate_total)
+    up_keep, up_send = gate_up_grads(normed_all, after(pre_grad, *sent), 1, rows_dev, where)
+    branch_part = branch_part.reshape(2, 2, 2, tok_dev, width)
+    branch_sums = Scatter(
+        [branch_part[:, :, :, start:stop] for start, stop in group_cuts], (upper, middle, low)
+    )
+    bits = [order[2] for order in group_orders]
+    branch_kept, branch_sent = branch_sums.split(bits)
     scatter.step((upper, upper), kept, sent)
-    scatter.parts, gu_sum, branch_part = together(scatter.parts, gu_sum, branch_part)
-    branch_mlp = lax.psum_scatter(
-        branch_part, "ctx", scatter_dimension=0, tiled=True, axis_index_groups=group_lists()
-    )
+    branch_arrived = [chip_swap(x, 1 << bit) for x, bit in zip(branch_sent, bits)]
+    scatter.parts, grad_gate, up_send = together(scatter.parts, grad_gate, up_send)
+    grad_gate = group_exchange(grad_gate)
+    up_arrived = core_swap(up_send)
     normed_two_grad = jnp.concatenate(scatter.parts)
     gain_two_grad = jnp.sum(normed_two_grad * hidden_res * scale_two, axis=0)
     hidden_grad = out_grad + rms_back(normed_two_grad, hidden_res, scale_two, gain_two)
 
-    wide = gu_sum.shape[2] // 2
-    column = wide // 256 * 128
-    gu_cuts = ((0, column), (column, wide), (wide, wide + column), (wide + column, 2 * wide))
-    gu_pieces = [gu_sum.reshape(8, groups, rows_dev, -1)[..., a:b] for a, b in gu_cuts]
     falling = tuple(reversed(group_bits()))
-    gu_done = []
-
     def weight_parts(x):
         return x.astype(bf16).reshape(ctx_size // 8, 8, 2, rows_dev, x.shape[1])
 
     branch_own = hidden_grad.astype(bf16)
     branch_other = core_swap(branch_own)
-    gu_done.append(sum_over(gu_pieces[0], 1, falling).astype(bf16))
-    branch_own, branch_other, gu_pieces, gu_done = together(
-        branch_own, branch_other, gu_pieces, gu_done
-    )
-    gu_done.append(sum_over(gu_pieces[1], 1, falling).astype(bf16))
+    branch_own, branch_other, up_arrived, branch_arrived = together(
+        branch_own, branch_other, up_arrived, branch_arrived
+    )
+    grad_up = of_group(of_cores(up_keep, up_arrived))
     project_grad_q, kv_grad = attend_back(
         ranges, branch_own, branch_other, out_w, queries, kv, attended, logs, starts, places, cos, sin
     )
-    (kv_grad, project_grad_q), gu_done, gu_pieces, activated = together(
-        (kv_grad, project_grad_q), gu_done, gu_pieces, activated
+    (kv_grad, project_grad_q), grad_gate, grad_up, activated = together(
+        (kv_grad, project_grad_q), grad_gate, grad_up, activated
     )
     kv_sum = cube_exchange(kv_grad)
-    gu_third = sum_over(gu_pieces[2], 1, falling).astype(bf16)
     down_keep, down_send = down_grads(activated, out_grad_all, groups, where)
     branch_grad = jnp.concatenate([branch_own, branch_other])
     normed_one = normed_one.reshape(-1, width)
@@ -887,55 +899,40 @@
     scatter = Scatter([wide_part[..., i * third : (i + 1) * third] for i in range(3)], names)
     bits = [order[0] for order in ORDERS]
     kept, sent = scatter.split(bits)
-    kv_sum, sent, down_send = together(kv_sum, sent, down_send)
+    arrived = [chip_swap(x, 1 << bit) for x, bit in zip(sent, bits)]
+    kv_sum, arrived, down_send, branch_arrived = together(
+        kv_sum, arrived, down_send, branch_arrived
+    )
 
     kv_sum = jnp.sum(kv_sum.astype(f32), axis=0).astype(bf16)
+    kv_sum, grad_up = together(kv_sum, grad_up)
     kv_sum = sum_over_high(kv_sum, high)
-    grad_gate = group_exchange(jnp.concatenate(gu_done, axis=2))
-    arrived = [chip_swap(x, 1 << bit) for x, bit in zip(sent, bits)]
+    down_arrived = core_swap(down_send)
+    grad_up = group_exchange(grad_up)
     key_pre = kv_sum[..., :HD]
     key_pre = key_pre * cos - jnp.roll(key_pre, HD // 2, axis=-1) * sin
     project_grad_kv = jnp.concatenate([key_pre, kv_sum[..., HD:]], axis=-1).astype(bf16)
     project_grad_kv = project_grad_kv.reshape(-1, 2 * HD)
     grad_kv = weight_parts(dot(normed_one, project_grad_kv, 0, 0)).swapaxes(0, 1)
-    grad_kv, grad_gate, arrived, gu_third, gu_pieces = together(
-        grad_kv, grad_gate, arrived, gu_third, gu_pieces
-    )
-
-    grad_kv = cube_exchange(grad_kv)
-    gu_last = sum_over(gu_pieces[3], 1, falling).astype(bf16)
-    scatter.add(kept, arrived)
-    scatter.step([order[1] for order in ORDERS])
-    down_arrived = core_swap(down_send)
     project_grad = jnp.concatenate([project_grad_q, project_grad_kv], axis=1)
     normed_one_grad = dot(project_grad, qkv_w, 1, 1)
     normed_one_grad = normed_one_grad[:tok_dev] + core_swap(normed_one_grad[tok_dev:])
-    grad_kv, gu_last, scatter.parts, down_arrived = together(
-        grad_kv, gu_last, scatter.parts, down_arrived
-    )
-    grad_up = group_exchange(jnp.concatenate([gu_third, gu_last], axis=2))
-    grad_kv = jnp.sum(grad_kv.astype(f32), axis=0).astype(bf16)
-    grad_kv = sum_over_high(grad_kv, high)
+    scatter.add(kept, arrived)
+    branch_sums.add(branch_kept, branch_arrived)
+    branch_sums.step([order[1] for order in group_orders])
     down_sum = (down_keep.astype(f32) + down_arrived.astype(f32)).astype(bf16)
-    grad_down = sum_over(down_sum, 0, falling)
+    grad_kv, grad_up, scatter.parts, branch_sums.parts, down_sum, normed_one_grad = together(
+        grad_kv, grad_up, scatter.parts, branch_sums.parts, down_sum, normed_one_grad
+    )
+    grad_kv = cube_exchange(grad_kv)
+    branch_sums.parts = [jnp.concatenate(branch_sums.parts, axis=-2)]
+    branch_sums.step((upper,))
+    scatter.step([order[1] for order in ORDERS])
     scatter.step([order[2] for order in ORDERS])
     scatter.parts = [jnp.concatenate(scatter.parts, axis=-1)]
     scale_one = lax.rsqrt(jnp.mean(inputs * inputs, axis=-1, keepdims=True) + EPSILON)
     gain_one_grad = jnp.sum(normed_one_grad * inputs * scale_one, axis=0)
     input_grad = hidden_grad + rms_back(normed_one_grad, inputs, scale_one, gain_one)
-    grad_kv, grad_up, scatter.parts, gain_one_grad, grad_down, branch_mlp = together(
-        grad_kv, grad_up, scatter.parts, gain_one_grad, grad_down, branch_mlp
-    )
-    output = (hidden_res + branch_mlp.astype(f32)).astype(bf16)
-    for bit in reversed(high):
-        scatter.step((bit,))
-    scattered = scatter.parts[0]
-
-    grad_gate, grad_up = unpack_members(grad_gate, grad_up, ff)
-    chip_grad = jnp.concatenate([scattered[..., :hq], grad_kv, scattered[..., hq:]], axis=-1)
-
-    def pick(x, which):
-        return lax.dynamic_index_in_dim(x, which, 0, keepdims=False)
 
     def whole_columns(x):
         return jnp.concatenate(
@@ -950,10 +947,6 @@
             axis=1,
         )
 
-    pair = by_core(pick(chip_grad, core), core_swap(pick(chip_grad, 1 - core)), core)
-    grad_qkv = whole_columns(pair)
-    grad_out = pair[:, :, hq + 2 * HD :].transpose(1, 0, 2).reshape(-1, 2 * hq).T
-
     bias_grad = jnp.sum(project_grad.astype(f32), axis=0, keepdims=True)
     zeros = jnp.zeros_like(bias_grad)
     bias_full = whole_columns(
@@ -967,9 +960,29 @@
         ],
         axis=2,
     )
+    grad_kv, scatter.parts, branch_sums.parts, sums, down_sum = together(
+        grad_kv, scatter.parts, branch_sums.parts, sums, down_sum
+    )
     sums = lax.all_to_all(sums, "ctx", split_axis=0, concat_axis=0, tiled=True)
+    grad_kv = jnp.sum(grad_kv.astype(f32), axis=0).astype(bf16)
+    grad_kv = sum_over_high(grad_kv, high)
+    grad_down = sum_over(down_sum, 0, falling)
+    for bit in reversed(high):
+        scatter.step((bit,))
+    scattered = scatter.parts[0]
     sums = jnp.sum(sums, axis=0)
     sums = (sums + core_swap(sums))[0]
+    output = (hidden_res + branch_sums.parts[0]).astype(bf16)
+
+    grad_gate, grad_up = unpack_members(grad_gate, grad_up, ff)
+    chip_grad = jnp.concatenate([scattered[..., :hq], grad_kv, scattered[..., hq:]], axis=-1)
+
+    def pick(x, which):
+        return lax.dynamic_index_in_dim(x, which, 0, keepdims=False)
+
+    pair = by_core(pick(chip_grad, core), core_swap(pick(chip_grad, 1 - core)), core)
+    grad_qkv = whole_columns(pair)
+    grad_out = pair[:, :, hq + 2 * HD :].transpose(1, 0, 2).reshape(-1, 2 * hq).T
 
     def owned(start, size):
         return lax.dynamic_slice_in_dim(sums, start + core * (size // 2), size // 2, 0)

time: 612 us -> 571 us (0.933)
  waiting for transfers between devices: 274 us -> 223 us
  local copies, waits for them, and re-layouts: 36.8 us -> 48.9 us
    ppermute x51 -> x54, waiting for transfers between devices: 264 us -> 197 us  [chip_swap(): return lax.ppermute(x, 'ctx', [(i, i ^ flip) for i in range(count)])]
    all_to_all x3 -> x4, waiting for transfers between devices: 0.01 us -> 22.5 us  [group_exchange(): lax.all_to_all(x, 'ctx', split_axis=0, concat_axis=0, tiled=True, axis_in...]
    convert_element_type x13 -> x17, other arithmetic: 9.63 us -> 18.8 us  [add(): self.parts = [x.astype(bf16) for x in self.parts]]
    unnamed x126 -> x164, local copies, waits for them, and re-layouts: 7.48 us -> 15.6 us
    all_to_all x3 -> x4, starting transfers between devices: 25 us -> 17.7 us  [group_exchange(): lax.all_to_all(x, 'ctx', split_axis=0, concat_axis=0, tiled=True, axis_in...]
    ppermute x51 -> x54, starting transfers between devices: 71.4 us -> 78.1 us  [chip_swap(): return lax.ppermute(x, 'ctx', [(i, i ^ flip) for i in range(count)])]
    all_to_all x2, waiting for transfers between devices: 6.22 us -> 0.01 us  [cube_exchange(): lax.all_to_all(x, 'ctx', split_axis=0, concat_axis=0, tiled=True, axis_in...]
    pallas_call x1 -> x2, Pallas kernels: 12.3 us -> 16.6 us  [gate_up_grads(): pl.pallas_call(functools.partial(gate_up_grads_kernel, rows_dev), grid=(w...]
  transfers between devices with their start and end apart: 76 -> 80, of which waited for: 35 -> 43; matrix products, arithmetic and copies ran while one was open for 16% -> 16% of each run, Pallas kernels for 10% -> 12%
where the time goes in v3:
time: 571 us; the launch traced here: 562 us
  waiting for transfers between devices  223 us (39%)
  starting transfers between devices  112 us (20%)
  Pallas kernels  94.5 us (17%)
  other arithmetic  55.6 us (10%)
  local copies, waits for them, and re-layouts  48.9 us (9%)
  between operations  16.1 us (3%)
  matrix products  12.4 us (2%)
    ppermute x54, waiting for transfers between devices, chip_swap(): return lax.ppermute(x, 'ctx', [(i, i ^ flip) for i in range(count)])  197 us
    ppermute x54, starting transfers between devices, chip_swap(): return lax.ppermute(x, 'ctx', [(i, i ^ flip) for i in range(count)])  78.1 us
    pallas_call x1, Pallas kernels, mlp(): pl.pallas_call(functools.partial(mlp_kernel, loads, groups), grid=(rows /...  27.8 us
    all_to_all x4, waiting for transfers between devices, group_exchange(): lax.all_to_all(x, 'ctx', split_axis=0, concat_axis=0, tiled=True, axis_in...  22.5 us
    convert_element_type x17, other arithmetic, add(): self.parts = [x.astype(bf16) for x in self.parts]  18.8 us
    all_to_all x4, starting transfers between devices, group_exchange(): lax.all_to_all(x, 'ctx', split_axis=0, concat_axis=0, tiled=True, axis_in...  17.7 us
    pallas_call x2, Pallas kernels, gate_up_grads(): pl.pallas_call(functools.partial(gate_up_grads_kernel, rows_dev), grid=(w...  16.6 us
    unnamed x164, local copies, waits for them, and re-layouts  15.6 us
  transfers between devices with their start and end apart: 80, of which 43 were waited for; matrix products, arithmetic and copies ran while one was open for 16% of the time, Pallas kernels for 12%

profile of v3, /device:TPU:0, one launch (start us, length us, event | category | flops | bytes accessed | tf_op | source)
XLA Modules:
  0.0 561.8 jit_solution(5441155873259294307)
XLA Ops:
  8.7 2.9 collective-permute-start.5
  19.0 3.1 pack_members.1
  22.1 9.4 %collective-permute-done.4 = bf16[1,2,64,1024]{3,2,1,0:T(8,128)(2,1)S(1)} collective-permute-done((bf16[1,2,64,1024]{3,2,1,0:T(8,128)(2,1)S(1)}, bf16[1,2,64,1024]{3,2,1,0:T(8,128)(2,1)S(1)}, u32[]{:S(2)}, u32[]{:S(2)}) %collective-permute-start.4) | collective-permute-done | bytes 262176 | tf_op jit(solution)/shard_map/ppermute | solution.py:42
  42.8 4.6 collective-permute-done.7
  49.2 3.5 collective-permute-done.10
  58.2 6.3 %collective-permute-done.14.refs_5_ = bf16[8,2,64,256]{3,2,1,0:T(8,128)(2,1)S(1)} collective-permute-done((bf16[8,2,64,256]{3,2,1,0:T(8,128)(2,1)S(1)}, bf16[8,2,64,256]{3,2,1,0:T(8,128)(2,1)S(1)}, u32[]{:S(2)}, u32[]{:S(2)}) %collective-permute-start.14) | collective-permute-done | bytes 524320 | tf_op jit(solution)/shard_map/ppermute | solution.py:42
  68.5 4.1 order_weights.1
  74.3 5.6 %all-to-all-start = ((bf16[8,16,2304]{2,1,0:T(8,128)(2,1)}), bf16[8,16,2304]{2,1,0:T(8,128)(2,1)S(1)}, u32[]{:S(2)}, u32[]{:S(2)}) async-start(bf16[8,16,2304]{2,1,0:T(8,128)(2,1)} %slice.179), calls=%async_computation | async-start | bytes 1179648 | tf_op jit(solution)/shard_map/all_to_all | solution.py:71
  82.8 4.2 project.1
  87.0 2.9 collective-permute-start.15
  89.9 12.8 %collective-permute-done.15 = bf16[1,2,128,256]{3,2,1,0:T(8,128)(2,1)S(1)} collective-permute-done((bf16[1,2,128,256]{3,2,1,0:T(8,128)(2,1)}, bf16[1,2,128,256]{3,2,1,0:T(8,128)(2,1)S(1)}, u32[]{:S(2)}, u32[]{:S(2)}) %collective-permute-start.15) | collective-permute-done | bytes 131104 | tf_op jit(solution)/shard_map/ppermute | solution.py:42
  121.5 3.4 order_rows.1
  127.8 3.6 all-to-all-start.1
  134.7 9.6 %attend.1 = (bf16[2,2048,256]{2,1,0:T(8,128)(2,1)}, f32[2,2,384,128]{3,2,1,0:T(8,128)}, bf16[2,128,768]{2,1,0:T(8,128)(2,1)}, f32[2,2,384,1]{3,2,1,0:T(8,128)}, f32[2,128,1536]{2,1,0:T(8,128)}) custom-call(s32[2]{0:T(128)} %pad_add_fusion.2.where_ref, s32[8]{0:T(128)} %reshape.417.range_ref, bf16[2,6,128,128]{3,2,1,0:T(8,128)(2,1)} %get-tuple-element.135.queries, ...), custom_call_target="tpu_custom_call" | custom-call | tf_op jit(solution)/shard_map/attend/pallas_call | solution.py:566
  148.8 22.5 %all-to-all-done.1 = bf16[8,32,2304]{2,1,0:T(8,128)(2,1)S(1)} async-done(((bf16[8,32,2304]{2,1,0:T(8,128)(2,1)}), bf16[8,32,2304]{2,1,0:T(8,128)(2,1)S(1)}, u32[]{:S(2)}, u32[]{:S(2)}) %all-to-all-start.1) | async-done | bytes 1179680 | tf_op jit(solution)/shard_map/all_to_all | solution.py:71
  175.4 33.0 %collective-permute-done.28 = bf16[1,128,1536]{2,1,0:T(8,128)(2,1)S(1)} collective-permute-done((bf16[1,128,1536]{2,1,0:T(8,128)(2,1)S(1)}, bf16[1,128,1536]{2,1,0:T(8,128)(2,1)S(1)}, u32[]{:S(2)}, u32[]{:S(2)}) %collective-permute-start.28) | collective-permute-done | bytes 393248 | tf_op jit(solution)/shard_map/ppermute | solution.py:42
  208.5 7.4 %collective-permute-start.31 = (bf16[2,64,1536]{2,1,0:T(8,128)(2,1)S(1)}, bf16[2,64,1536]{2,1,0:T(8,128)(2,1)S(1)}, u32[]{:S(2)}, u32[]{:S(2)}) collective-permute-start(bf16[2,64,1536]{2,1,0:T(8,128)(2,1)S(1)} %get-tuple-element.261), channel_id=1, source_target_pairs={{0,4},{2,6},{4,0},{6,2},{8,12},{10,14},{12,8},{14,10},{16,20},{18,... | collective-permute-start | bytes 1179656 | tf_op jit(solution)/shard_map/ppermute | solution.py:42
  217.7 3.9 collective-permute-done.31
  224.7 3.5 collective-permute-start.32
  228.4 10.9 %collective-permute-done.34.refs_4_ = bf16[4,48,2304]{2,1,0:T(8,128)(2,1)} collective-permute-done((bf16[4,48,2304]{2,1,0:T(8,128)(2,1)}, bf16[4,48,2304]{2,1,0:T(8,128)(2,1)}, u32[]{:S(2)}, u32[]{:S(2)}) %collective-permute-start.34) | collective-permute-done | bytes 884768 | tf_op jit(solution)/shard_map/ppermute | solution.py:42
  239.2 6.0 %collective-permute-done.32.refs_1_ = bf16[4,64,1536]{2,1,0:T(8,128)(2,1)} collective-permute-done((bf16[4,64,1536]{2,1,0:T(8,128)(2,1)}, bf16[4,64,1536]{2,1,0:T(8,128)(2,1)}, u32[]{:S(2)}, u32[]{:S(2)}) %collective-permute-start.32) | collective-permute-done | bytes 786464 | tf_op jit(solution)/shard_map/ppermute | solution.py:42
  247.2 3.7 order_tokens.1
  250.9 27.8 %mlp.1 = (bf16[1024,2304]{1,0:T(8,128)(2,1)}, bf16[1024,1120]{1,0:T(8,128)(2,1)}, bf16[1024,1536]{1,0:T(8,128)(2,1)}) custom-call(s32[2]{0:T(128)} %pad_add_fusion.2.where_ref, bf16[1024,1536]{1,0:T(8,128)(2,1)} %bitcast.306, bf16[1024,1536]{1,0:T(8,128)(2,1)} %all-gather.4.cloned.1.call-done.out_grad, bf16[1120,1536]{1,0:T(8,128)(2,1)} %bitcast.315, ...), custom_call_target="tpu_custom_call" | custom-call | tf_op jit(solution)/shard_map/mlp/pallas_call | solution.py:371
  285.2 8.2 %gate_up_grads.2 = (bf16[16,48,1152]{2,1,0:T(8,128)(2,1)}, bf16[16,48,1152]{2,1,0:T(8,128)(2,1)}) custom-call(s32[2]{0:T(128)} %pad_add_fusion.2.where_ref, bf16[1024,1536]{1,0:T(8,128)(2,1)} %bitcast.307, bf16[1024,2304]{1,0:T(8,128)(2,1)} %get-tuple-element.184.pre_grad), custom_call_target="tpu_custom_call" | custom-call | tf_op jit(solution)/shard_map/gate_up_grads/pallas_call | solution.py:408
  293.5 6.2 %convolution_convert_fusion = bf16[1024,1536]{1,0:T(8,128)(2,1)S(1)} fusion(bf16[1024,1120]{1,0:T(8,128)(2,1)} %get-tuple-element.203.activated, bf16[1120,1536]{1,0:T(8,128)(2,1)S(1)} %bitcast.316), kind=kOutput, calls=%fused_computation.1 | convolution fusion | flops 3524788224 | bytes 8880128 | tf_op jit(solution)/shard_map/dot_general | solution.py:166
  314.6 5.6 collective-permute-done.42
  320.2 4.4 collective-permute-done.41
  324.9 2.9 collective-permute-start.43
  327.9 8.3 %gate_up_grads.3 = (bf16[16,48,1152]{2,1,0:T(8,128)(2,1)}, bf16[16,48,1152]{2,1,0:T(8,128)(2,1)}) custom-call(s32[2]{0:T(128)} %pad_add_fusion.2.where_ref, bf16[1024,1536]{1,0:T(8,128)(2,1)} %bitcast.308, bf16[1024,2304]{1,0:T(8,128)(2,1)} %get-tuple-element.184.pre_grad), custom_call_target="tpu_custom_call" | custom-call | tf_op jit(solution)/shard_map/gate_up_grads/pallas_call | solution.py:408
  337.1 3.2 collective-permute-done.44
  342.6 6.8 %collective-permute-done.45 = bf16[8,1,48,1152]{3,2,0,1:T(8,128)(2,1)S(1)} collective-permute-done((bf16[8,1,48,1152]{3,2,0,1:T(8,128)(2,1)S(1)}, bf16[8,1,48,1152]{3,2,0,1:T(8,128)(2,1)S(1)}, u32[]{:S(2)}, u32[]{:S(2)}) %collective-permute-start.45) | collective-permute-done | bytes 884768 | tf_op jit(solution)/shard_map/ppermute | solution.py:42
  353.0 3.6 all-to-all-start.2
  360.4 11.0 %attend_back.1 = (bf16[2,128,768]{2,1,0:T(8,128)(2,1)}, bf16[8,2,2,128,256]{4,3,2,1,0:T(8,128)(2,1)}) custom-call(s32[8]{0:T(128)} %reshape.417.range_ref, bf16[128,1536]{1,0:T(8,128)(2,1)} %copy-done.6, bf16[128,1536]{1,0:T(8,128)(2,1)} %copy-done.29, bf16[1536,768]{1,0:T(8,128)(2,1)} %bitcast.318, bf16[2,6,128,128]{3,2,1,0:T(8,128)(2,1)} %get-tuple-element.135.queries, ...), custom_call_target="tpu_custom_call" | custom-call | tf_op jit(solution)/shard_map/attend_back/pallas_call | solution.py:663
  371.5 9.6 %collective-permute-done.50 = bf16[8,1,48,1152]{3,2,0,1:T(8,128)(2,1)S(1)} collective-permute-done((bf16[8,1,48,1152]{3,2,0,1:T(8,128)(2,1)S(1)}, bf16[8,1,48,1152]{3,2,0,1:T(8,128)(2,1)S(1)}, u32[]{:S(2)}, u32[]{:S(2)}) %collective-permute-start.50) | collective-permute-done | bytes 884768 | tf_op jit(solution)/shard_map/ppermute | solution.py:42
  383.1 4.4 all-to-all-start.3
  403.7 7.5 %down_grads.1 = (bf16[2,280,1536]{2,1,0:T(8,128)(2,1)}, bf16[2,280,1536]{2,1,0:T(8,128)(2,1)}) custom-call(s32[2]{0:T(128)} %pad_add_fusion.2.where_ref, bf16[1024,1120]{1,0:T(8,128)(2,1)} %get-tuple-element.203.activated, bf16[1024,1536]{1,0:T(8,128)(2,1)} %all-gather.4.cloned.1.call-done.out_grad), custom_call_target="tpu_custom_call" | custom-call | tf_op jit(solution)/shard_map/down_grads/pallas_call | solution.py:439
  411.2 17.7 %collective-permute-done.53 = bf16[2,2,2,2,48,512]{5,4,3,0,1,2:T(8,128)(2,1)} collective-permute-done((bf16[2,2,2,2,48,512]{5,4,3,0,1,2:T(8,128)(2,1)}, bf16[2,2,2,2,48,512]{5,4,3,0,1,2:T(8,128)(2,1)}, u32[]{:S(2)}, u32[]{:S(2)}) %collective-permute-start.53) | collective-permute-done | bytes 786464 | tf_op jit(solution)/shard_map/ppermute | solution.py:42
  434.2 4.9 all-to-all-start.4
  439.2 3.0 collective-permute-start.54
  454.0 13.2 %collective-permute-done.54 = bf16[1,2,128,256]{3,2,1,0:T(8,128)(2,1)S(1)} collective-permute-done((bf16[1,2,128,256]{3,2,1,0:T(8,128)(2,1)S(1)}, bf16[1,2,128,256]{3,2,1,0:T(8,128)(2,1)S(1)}, u32[]{:S(2)}, u32[]{:S(2)}) %collective-permute-start.54) | collective-permute-done | bytes 131104 | tf_op jit(solution)/shard_map/ppermute | solution.py:42
  470.5 2.9 fusion.43
  478.5 3.1 add_convert_fusion.2
  481.7 4.4 all-to-all-start.5
  500.5 3.6 unpack_members.1
  508.3 4.7 collective-permute-done.61
  524.4 4.1 all-to-all-start.6
  536.1 6.1 %collective-permute-done.68 = bf16[1,2,48,256]{3,2,1,0:T(8,128)(2,1)S(1)} collective-permute-done((bf16[1,2,48,256]{3,2,1,0:T(8,128)(2,1)S(1)}, bf16[1,2,48,256]{3,2,1,0:T(8,128)(2,1)S(1)}, u32[]{:S(2)}, u32[]{:S(2)}) %collective-permute-start.68) | collective-permute-done | bytes 49184 | tf_op jit(solution)/shard_map/ppermute | solution.py:42
  542.2 5.6 collective-permute-done.67
  (474 shorter events, 196.2 us)
Async XLA Ops:
  7.2 124.2 %all-gather.6.cloned.1.call-start = ((), (), s32[]{:S(2)}) async-start(), calls=%async_computation.8 | async-start | bytes 2506752 | tf_op jit(solution)/shard_map/all_gather | solution.py:730
  7.2 29.1 %collective-permute-start = (s32[4]{0:T(128)}, s32[4]{0:T(128)S(1)}, u32[]{:S(2)}, u32[]{:S(2)}) collective-permute-start(s32[4]{0:T(128)} %bitcast.352), channel_id=1, source_target_pairs={{0,1},{1,0},{2,3},{3,2},{4,5},{5,4},{6,7},{7,6},{8,9},{9,8},{10,11... | collective-permute-start | bytes 56 | tf_op jit(solution)/shard_map/ppermute | solution.py:37
  8.7 23.7 %collective-permute-start.5 = (bf16[280,1536]{1,0:T(8,128)(2,1)}, bf16[280,1536]{1,0:T(8,128)(2,1)}, u32[]{:S(2)}, u32[]{:S(2)}) collective-permute-start(bf16[280,1536]{1,0:T(8,128)(2,1)} %param.21), channel_id=1, source_target_pairs={{0,2},{2,0},{4,6},{6,4},{8,10},{10,8},{12,14},{14,12},{16,18},{18,... | collective-permute-start | bytes 2580488 | tf_op jit(solution)/shard_map/ppermute | solution.py:42
  14.2 67.8 %collective-permute-start.1 = (bf16[128,1536]{1,0:T(8,128)(2,1)}, bf16[128,1536]{1,0:T(8,128)(2,1)S(1)}, u32[]{:S(2)}, u32[]{:S(2)}) collective-permute-start(bf16[128,1536]{1,0:T(8,128)(2,1)} %bitcast.323), channel_id=1, source_target_pairs={{0,1},{1,0},{2,3},{3,2},{4,5},{5,4},{6,7},{7,6},{8,9},{9,8},{10,11... | collective-permute-start | bytes 1179656 | tf_op jit(solution)/shard_map/ppermute | solution.py:37
  15.6 15.9 %collective-permute-start.4 = (bf16[1,2,64,1024]{3,2,1,0:T(8,128)(2,1)S(1)}, bf16[1,2,64,1024]{3,2,1,0:T(8,128)(2,1)S(1)}, u32[]{:S(2)}, u32[]{:S(2)}) collective-permute-start(bf16[1,2,64,1024]{3,2,1,0:T(8,128)(2,1)S(1)} %maximum_bitcast_fusion), channel_id=1, source_target_pairs={{0,16},{2,18},{4,20},{6,22},{8,24},{10,26},{12,28},{14,30},{16,0},... | collective-permute-start | bytes 786440 | tf_op jit(solution)/shard_map/ppermute | solution.py:42
  42.6 12.5 %collective-permute-start.13 = (bf16[4,2,64,256]{3,2,1,0:T(8,128)(2,1)S(1)}, bf16[4,2,64,256]{3,2,1,0:T(8,128)(2,1)S(1)}, u32[]{:S(2)}, u32[]{:S(2)}) collective-permute-start(bf16[4,2,64,256]{3,2,1,0:T(8,128)(2,1)S(1)} %pad_maximum_fusion.15), channel_id=1, source_target_pairs={{0,2},{2,0},{4,6},{6,4},{8,10},{10,8},{12,14},{14,12},{16,18},{18,... | collective-permute-start | bytes 786440 | tf_op jit(solution)/shard_map/ppermute | solution.py:42
  47.5 19.4 %collective-permute-start.8 = (bf16[8,2,48,384]{3,2,1,0:T(8,128)(2,1)S(1)}, bf16[8,2,48,384]{3,2,1,0:T(8,128)(2,1)S(1)}, u32[]{:S(2)}, u32[]{:S(2)}) collective-permute-start(bf16[8,2,48,384]{3,2,1,0:T(8,128)(2,1)S(1)} %pad_maximum_fusion.4.refs_0_), channel_id=1, source_target_pairs={{0,8},{2,10},{4,12},{6,14},{8,0},{10,2},{12,4},{14,6},{16,24},{18,... | collective-permute-start | bytes 1769480 | tf_op jit(solution)/shard_map/ppermute | solution.py:42
  52.8 14.1 %collective-permute-start.11 = (bf16[8,2,48,384]{3,2,1,0:T(8,128)(2,1)S(1)}, bf16[8,2,48,384]{3,2,1,0:T(8,128)(2,1)S(1)}, u32[]{:S(2)}, u32[]{:S(2)}) collective-permute-start(bf16[8,2,48,384]{3,2,1,0:T(8,128)(2,1)S(1)} %pad_maximum_fusion.5.refs_2_), channel_id=1, source_target_pairs={{0,2},{2,0},{4,6},{6,4},{8,10},{10,8},{12,14},{14,12},{16,18},{18,... | collective-permute-start | bytes 1769480 | tf_op jit(solution)/shard_map/ppermute | solution.py:42
  74.3 29.3 %all-to-all-start = ((bf16[8,16,2304]{2,1,0:T(8,128)(2,1)}), bf16[8,16,2304]{2,1,0:T(8,128)(2,1)S(1)}, u32[]{:S(2)}, u32[]{:S(2)}) async-start(bf16[8,16,2304]{2,1,0:T(8,128)(2,1)} %slice.179), calls=%async_computation | async-start | bytes 1179648 | tf_op jit(solution)/shard_map/all_to_all | solution.py:71
  87.0 15.7 %collective-permute-start.15 = (bf16[1,2,128,256]{3,2,1,0:T(8,128)(2,1)}, bf16[1,2,128,256]{3,2,1,0:T(8,128)(2,1)S(1)}, u32[]{:S(2)}, u32[]{:S(2)}) collective-permute-start(bf16[1,2,128,256]{3,2,1,0:T(8,128)(2,1)} %bitcast.344), channel_id=1, source_target_pairs={{0,16},{2,18},{4,20},{6,22},{8,24},{10,26},{12,28},{14,30},{16,0},... | collective-permute-start | bytes 393224 | tf_op jit(solution)/shard_map/ppermute | solution.py:42
  105.2 15.1 %collective-permute-start.25 = (bf16[280,1536]{1,0:T(8,128)(2,1)}, bf16[280,1536]{1,0:T(8,128)(2,1)S(1)}, u32[]{:S(2)}, u32[]{:S(2)}) collective-permute-start(bf16[280,1536]{1,0:T(8,128)(2,1)} %param.21), channel_id=1, source_target_pairs={{0,1},{1,0},{2,3},{3,2},{4,5},{5,4},{6,7},{7,6},{8,9},{9,8},{10,11... | collective-permute-start | bytes 2580488 | tf_op jit(solution)/shard_map/ppermute | solution.py:37
  105.2 15.1 %collective-permute-start.26 = (bf16[280,1536]{1,0:T(8,128)(2,1)}, bf16[280,1536]{1,0:T(8,128)(2,1)S(1)}, u32[]{:S(2)}, u32[]{:S(2)}) collective-permute-start(bf16[280,1536]{1,0:T(8,128)(2,1)} %collective-permute-done.5), channel_id=1, source_target_pairs={{0,1},{1,0},{2,3},{3,2},{4,5},{5,4},{6,7},{7,6},{8,9},{9,8},{10,11... | collective-permute-start | bytes 2580488 | tf_op jit(solution)/shard_map/ppermute | solution.py:37
  127.8 43.6 %all-to-all-start.1 = ((bf16[8,32,2304]{2,1,0:T(8,128)(2,1)}), bf16[8,32,2304]{2,1,0:T(8,128)(2,1)S(1)}, u32[]{:S(2)}, u32[]{:S(2)}) async-start(bf16[8,32,2304]{2,1,0:T(8,128)(2,1)} %slice.183), calls=%async_computation.1 | async-start | bytes 2359296 | tf_op jit(solution)/shard_map/all_to_all | solution.py:71
  131.4 93.3 %all-gather.4.cloned.1.call-start = ((), (), s32[]{:S(2)}) async-start(), calls=%async_computation.7 | async-start | bytes 3538944 | tf_op jit(solution)/shard_map/all_gather | solution.py:731
  171.6 36.8 %collective-permute-start.29 = (bf16[4,48,2304]{2,1,0:T(8,128)(2,1)S(1)}, bf16[4,48,2304]{2,1,0:T(8,128)(2,1)S(1)}, u32[]{:S(2)}, u32[]{:S(2)}) collective-permute-start(bf16[4,48,2304]{2,1,0:T(8,128)(2,1)S(1)} %slice.225), channel_id=1, source_target_pairs={{0,2},{2,0},{4,6},{6,4},{8,10},{10,8},{12,14},{14,12},{16,18},{18,... | collective-permute-start | bytes 2654216 | tf_op jit(solution)/shard_map/ppermute | solution.py:42
  175.3 33.0 %collective-permute-start.28 = (bf16[1,128,1536]{2,1,0:T(8,128)(2,1)S(1)}, bf16[1,128,1536]{2,1,0:T(8,128)(2,1)S(1)}, u32[]{:S(2)}, u32[]{:S(2)}) collective-permute-start(bf16[1,128,1536]{2,1,0:T(8,128)(2,1)S(1)} %fusion.34), channel_id=1, source_target_pairs={{0,16},{2,18},{4,20},{6,22},{8,24},{10,26},{12,28},{14,30},{16,0},... | collective-permute-start | bytes 1179656 | tf_op jit(solution)/shard_map/ppermute | solution.py:42
  208.5 13.2 %collective-permute-start.31 = (bf16[2,64,1536]{2,1,0:T(8,128)(2,1)S(1)}, bf16[2,64,1536]{2,1,0:T(8,128)(2,1)S(1)}, u32[]{:S(2)}, u32[]{:S(2)}) collective-permute-start(bf16[2,64,1536]{2,1,0:T(8,128)(2,1)S(1)} %get-tuple-element.261), channel_id=1, source_target_pairs={{0,4},{2,6},{4,0},{6,2},{8,12},{10,14},{12,8},{14,10},{16,20},{18,... | collective-permute-start | bytes 1179656 | tf_op jit(solution)/shard_map/ppermute | solution.py:42
  215.9 35.0 %collective-permute-start.35 = (bf16[8,48,2304]{2,1,0:T(8,128)(2,1)S(1)}, bf16[8,48,2304]{2,1,0:T(8,128)(2,1)}, u32[]{:S(2)}, u32[]{:S(2)}) collective-permute-start(bf16[8,48,2304]{2,1,0:T(8,128)(2,1)S(1)} %constant_dynamic-update-slice_fusion.refs_0_), channel_id=1, source_target_pairs={{0,1},{1,0},{2,3},{3,2},{4,5},{5,4},{6,7},{7,6},{8,9},{9,8},{10,11... | collective-permute-start | bytes 5308424 | tf_op jit(solution)/shard_map/ppermute | solution.py:37
  216.9 22.4 %collective-permute-start.34 = (bf16[4,48,2304]{2,1,0:T(8,128)(2,1)}, bf16[4,48,2304]{2,1,0:T(8,128)(2,1)}, u32[]{:S(2)}, u32[]{:S(2)}) collective-permute-start(bf16[4,48,2304]{2,1,0:T(8,128)(2,1)} %slice.190), channel_id=1, source_target_pairs={{0,2},{2,0},{4,6},{6,4},{8,10},{10,8},{12,14},{14,12},{16,18},{18,... | collective-permute-start | bytes 2654216 | tf_op jit(solution)/shard_map/ppermute | solution.py:42
  224.7 20.5 %collective-permute-start.32 = (bf16[4,64,1536]{2,1,0:T(8,128)(2,1)}, bf16[4,64,1536]{2,1,0:T(8,128)(2,1)}, u32[]{:S(2)}, u32[]{:S(2)}) collective-permute-start(bf16[4,64,1536]{2,1,0:T(8,128)(2,1)} %pad_maximum_fusion.1.refs_0_), channel_id=1, source_target_pairs={{0,4},{2,6},{4,0},{6,2},{8,12},{10,14},{12,8},{14,10},{16,20},{18,... | collective-permute-start | bytes 2359304 | tf_op jit(solution)/shard_map/ppermute | solution.py:42
  228.2 18.5 %collective-permute-start.33 = (bf16[4,64,1536]{2,1,0:T(8,128)(2,1)}, bf16[4,64,1536]{2,1,0:T(8,128)(2,1)}, u32[]{:S(2)}, u32[]{:S(2)}) collective-permute-start(bf16[4,64,1536]{2,1,0:T(8,128)(2,1)} %pad_maximum_fusion.2.refs_2_), channel_id=1, source_target_pairs={{0,8},{2,10},{4,12},{6,14},{8,0},{10,2},{12,4},{14,6},{16,24},{18,... | collective-permute-start | bytes 2359304 | tf_op jit(solution)/shard_map/ppermute | solution.py:42
  282.7 19.8 %collective-permute-start.39 = (bf16[2,2,64,1536]{3,2,0,1:T(8,128)(2,1)}, bf16[2,2,64,1536]{3,2,0,1:T(8,128)(2,1)}, u32[]{:S(2)}, u32[]{:S(2)}) collective-permute-start(bf16[2,2,64,1536]{3,2,0,1:T(8,128)(2,1)} %bitcast.303), channel_id=1, source_target_pairs={{0,8},{2,10},{4,12},{6,14},{8,0},{10,2},{12,4},{14,6},{16,24},{18,... | collective-permute-start | bytes 2359304 | tf_op jit(solution)/shard_map/ppermute | solution.py:42
  284.9 19.5 %collective-permute-start.38 = (bf16[2,2,64,1536]{3,2,0,1:T(8,128)(2,1)}, bf16[2,2,64,1536]{3,2,0,1:T(8,128)(2,1)}, u32[]{:S(2)}, u32[]{:S(2)}) collective-permute-start(bf16[2,2,64,1536]{3,2,0,1:T(8,128)(2,1)} %bitcast.304), channel_id=1, source_target_pairs={{0,4},{2,6},{4,0},{6,2},{8,12},{10,14},{12,8},{14,10},{16,20},{18,... | collective-permute-start | bytes 2359304 | tf_op jit(solution)/shard_map/ppermute | solution.py:42
  308.4 16.3 %collective-permute-start.41 = (bf16[2,64,1536]{2,1,0:T(8,128)(2,1)S(1)}, bf16[2,64,1536]{2,1,0:T(8,128)(2,1)S(1)}, u32[]{:S(2)}, u32[]{:S(2)}) collective-permute-start(bf16[2,64,1536]{2,1,0:T(8,128)(2,1)S(1)} %dynamic-slice_bitcast_fusion.8), channel_id=1, source_target_pairs={{0,8},{2,10},{4,12},{6,14},{8,0},{10,2},{12,4},{14,6},{16,24},{18,... | collective-permute-start | bytes 1179656 | tf_op jit(solution)/shard_map/ppermute | solution.py:42
  312.0 44.6 %collective-permute-start.49 = (bf16[2,2,64,1536]{3,2,0,1:T(8,128)(2,1)}, bf16[2,2,64,1536]{3,2,0,1:T(8,128)(2,1)}, u32[]{:S(2)}, u32[]{:S(2)}) collective-permute-start(bf16[2,2,64,1536]{3,2,0,1:T(8,128)(2,1)} %bitcast.301), channel_id=1, source_target_pairs={{0,8},{2,10},{4,12},{6,14},{8,0},{10,2},{12,4},{14,6},{16,24},{18,... | collective-permute-start | bytes 2359304 | tf_op jit(solution)/shard_map/ppermute | solution.py:42
  312.3 44.3 %collective-permute-start.48 = (bf16[2,2,64,1536]{3,2,0,1:T(8,128)(2,1)}, bf16[2,2,64,1536]{3,2,0,1:T(8,128)(2,1)}, u32[]{:S(2)}, u32[]{:S(2)}) collective-permute-start(bf16[2,2,64,1536]{3,2,0,1:T(8,128)(2,1)} %bitcast.302), channel_id=1, source_target_pairs={{0,4},{2,6},{4,0},{6,2},{8,12},{10,14},{12,8},{14,10},{16,20},{18,... | collective-permute-start | bytes 2359304 | tf_op jit(solution)/shard_map/ppermute | solution.py:42
  324.8 15.6 %collective-permute-start.44 = (bf16[64,1536]{1,0:T(8,128)(2,1)S(1)}, bf16[64,1536]{1,0:T(8,128)(2,1)S(1)}, u32[]{:S(2)}, u32[]{:S(2)}) collective-permute-start(bf16[64,1536]{1,0:T(8,128)(2,1)S(1)} %dynamic-slice_bitcast_fusion.14), channel_id=1, source_target_pairs={{0,16},{2,18},{4,20},{6,22},{8,24},{10,26},{12,28},{14,30},{16,0},... | collective-permute-start | bytes 589832 | tf_op jit(solution)/shard_map/ppermute | solution.py:42
  324.9 17.6 %collective-permute-start.43 = (bf16[64,1536]{1,0:T(8,128)(2,1)S(1)}, bf16[64,1536]{1,0:T(8,128)(2,1)S(1)}, u32[]{:S(2)}, u32[]{:S(2)}) collective-permute-start(bf16[64,1536]{1,0:T(8,128)(2,1)S(1)} %dynamic-slice_bitcast_fusion.15), channel_id=1, source_target_pairs={{0,16},{2,18},{4,20},{6,22},{8,24},{10,26},{12,28},{14,30},{16,0},... | collective-permute-start | bytes 589832 | tf_op jit(solution)/shard_map/ppermute | solution.py:42
  336.2 13.1 %collective-permute-start.45 = (bf16[8,1,48,1152]{3,2,0,1:T(8,128)(2,1)S(1)}, bf16[8,1,48,1152]{3,2,0,1:T(8,128)(2,1)S(1)}, u32[]{:S(2)}, u32[]{:S(2)}) collective-permute-start(bf16[8,1,48,1152]{3,2,0,1:T(8,128)(2,1)S(1)} %constant_dynamic-slice_fusion.15), channel_id=1, source_target_pairs={{0,2},{2,0},{4,6},{6,4},{8,10},{10,8},{12,14},{14,12},{16,18},{18,... | collective-permute-start | bytes 2654216 | tf_op jit(solution)/shard_map/ppermute | solution.py:42
  353.0 29.1 %all-to-all-start.2 = ((bf16[8,48,1152]{2,1,0:T(8,128)(2,1)}), bf16[8,48,1152]{2,1,0:T(8,128)(2,1)S(1)}, u32[]{:S(2)}, u32[]{:S(2)}) async-start(bf16[8,48,1152]{2,1,0:T(8,128)(2,1)} %fusion.9), calls=%async_computation.2 | async-start | bytes 1769472 | tf_op jit(solution)/shard_map/all_to_all | solution.py:71
  359.3 21.7 %collective-permute-start.50 = (bf16[8,1,48,1152]{3,2,0,1:T(8,128)(2,1)S(1)}, bf16[8,1,48,1152]{3,2,0,1:T(8,128)(2,1)S(1)}, u32[]{:S(2)}, u32[]{:S(2)}) collective-permute-start(bf16[8,1,48,1152]{3,2,0,1:T(8,128)(2,1)S(1)} %dynamic-slice_bitcast_fusion), channel_id=1, source_target_pairs={{0,2},{2,0},{4,6},{6,4},{8,10},{10,8},{12,14},{14,12},{16,18},{18,... | collective-permute-start | bytes 2654216 | tf_op jit(solution)/shard_map/ppermute | solution.py:42
  383.1 46.7 %all-to-all-start.3 = ((bf16[8,2,2,128,256]{4,3,2,1,0:T(8,128)(2,1)}), bf16[8,2,2,128,256]{4,3,2,1,0:T(8,128)(2,1)}, u32[]{:S(2)}, u32[]{:S(2)}) async-start(bf16[8,2,2,128,256]{4,3,2,1,0:T(8,128)(2,1)} %get-tuple-element.200), calls=%async_computation.3 | async-start | bytes 4194304 | tf_op jit(solution)/shard_map/all_to_all | solution.py:51
  391.7 37.2 %collective-permute-start.53 = (bf16[2,2,2,2,48,512]{5,4,3,0,1,2:T(8,128)(2,1)}, bf16[2,2,2,2,48,512]{5,4,3,0,1,2:T(8,128)(2,1)}, u32[]{:S(2)}, u32[]{:S(2)}) collective-permute-start(bf16[2,2,2,2,48,512]{5,4,3,0,1,2:T(8,128)(2,1)} %bitcast.299), channel_id=1, source_target_pairs={{0,8},{2,10},{4,12},{6,14},{8,0},{10,2},{12,4},{14,6},{16,24},{18,... | collective-permute-start | bytes 2359304 | tf_op jit(solution)/shard_map/ppermute | solution.py:42
  396.2 33.6 %collective-permute-start.52 = (bf16[2,2,2,2,48,512]{5,4,3,2,1,0:T(8,128)(2,1)}, bf16[2,2,2,2,48,512]{5,4,3,2,1,0:T(8,128)(2,1)}, u32[]{:S(2)}, u32[]{:S(2)}) collective-permute-start(bf16[2,2,2,2,48,512]{5,4,3,2,1,0:T(8,128)(2,1)} %fusion.14), channel_id=1, source_target_pairs={{0,4},{2,6},{4,0},{6,2},{8,12},{10,14},{12,8},{14,10},{16,20},{18,... | collective-permute-start | bytes 2359304 | tf_op jit(solution)/shard_map/ppermute | solution.py:42
  399.6 30.2 %collective-permute-start.51 = (bf16[2,2,2,2,48,512]{5,4,3,0,1,2:T(8,128)(2,1)}, bf16[2,2,2,2,48,512]{5,4,3,0,1,2:T(8,128)(2,1)}, u32[]{:S(2)}, u32[]{:S(2)}) collective-permute-start(bf16[2,2,2,2,48,512]{5,4,3,0,1,2:T(8,128)(2,1)} %bitcast.300), channel_id=1, source_target_pairs={{0,2},{2,0},{4,6},{6,4},{8,10},{10,8},{12,14},{14,12},{16,18},{18,... | collective-permute-start | bytes 2359304 | tf_op jit(solution)/shard_map/ppermute | solution.py:42
  434.2 47.5 %all-to-all-start.4 = ((bf16[8,48,1152]{2,1,0:T(8,128)(2,1)}), bf16[8,48,1152]{2,1,0:T(8,128)(2,1)S(1)}, u32[]{:S(2)}, u32[]{:S(2)}) async-start(bf16[8,48,1152]{2,1,0:T(8,128)(2,1)} %fusion.10), calls=%async_computation.4 | async-start | bytes 1769472 | tf_op jit(solution)/shard_map/all_to_all | solution.py:71
  439.2 28.1 %collective-permute-start.54 = (bf16[1,2,128,256]{3,2,1,0:T(8,128)(2,1)S(1)}, bf16[1,2,128,256]{3,2,1,0:T(8,128)(2,1)S(1)}, u32[]{:S(2)}, u32[]{:S(2)}) collective-permute-start(bf16[1,2,128,256]{3,2,1,0:T(8,128)(2,1)S(1)} %constant_dynamic-slice_fusion.10), channel_id=1, source_target_pairs={{0,16},{2,18},{4,20},{6,22},{8,24},{10,26},{12,28},{14,30},{16,0},... | collective-permute-start | bytes 393224 | tf_op jit(solution)/shard_map/ppermute | solution.py:42
  444.3 29.3 %collective-permute-start.56 = (bf16[2,64,1536]{2,1,0:T(8,128)(2,1)}, bf16[2,64,1536]{2,1,0:T(8,128)(2,1)}, u32[]{:S(2)}, u32[]{:S(2)}) collective-permute-start(bf16[2,64,1536]{2,1,0:T(8,128)(2,1)} %dynamic-slice_bitcast_fusion.5), channel_id=1, source_target_pairs={{0,4},{2,6},{4,0},{6,2},{8,12},{10,14},{12,8},{14,10},{16,20},{18,... | collective-permute-start | bytes 1179656 | tf_op jit(solution)/shard_map/ppermute | solution.py:42
  445.7 32.8 %collective-permute-start.57 = (bf16[2,280,1536]{2,1,0:T(8,128)(2,1)}, bf16[2,280,1536]{2,1,0:T(8,128)(2,1)}, u32[]{:S(2)}, u32[]{:S(2)}) collective-permute-start(bf16[2,280,1536]{2,1,0:T(8,128)(2,1)} %get-tuple-element.217), channel_id=1, source_target_pairs={{0,1},{1,0},{2,3},{3,2},{4,5},{5,4},{6,7},{7,6},{8,9},{9,8},{10,11... | collective-permute-start | bytes 5160968 | tf_op jit(solution)/shard_map/ppermute | solution.py:37
  452.5 23.9 %collective-permute-start.55 = (bf16[2,64,1536]{2,1,0:T(8,128)(2,1)}, bf16[2,64,1536]{2,1,0:T(8,128)(2,1)}, u32[]{:S(2)}, u32[]{:S(2)}) collective-permute-start(bf16[2,64,1536]{2,1,0:T(8,128)(2,1)} %dynamic-slice_bitcast_fusion.6), channel_id=1, source_target_pairs={{0,8},{2,10},{4,12},{6,14},{8,0},{10,2},{12,4},{14,6},{16,24},{18,... | collective-permute-start | bytes 1179656 | tf_op jit(solution)/shard_map/ppermute | solution.py:42
  481.7 40.6 %all-to-all-start.5 = ((bf16[8,2,2,48,256]{4,3,2,1,0:T(8,128)(2,1)}), bf16[8,2,2,48,256]{4,3,2,1,0:T(8,128)(2,1)}, u32[]{:S(2)}, u32[]{:S(2)}) async-start(bf16[8,2,2,48,256]{4,3,2,1,0:T(8,128)(2,1)} %bitcast.327), calls=%async_computation.5 | async-start | bytes 1572864 | tf_op jit(solution)/shard_map/all_to_all | solution.py:51
  489.8 15.9 %collective-permute-start.63 = (bf16[2,2,2,48,512]{4,3,2,0,1:T(8,128)(2,1)S(1)}, bf16[2,2,2,48,512]{4,3,2,0,1:T(8,128)(2,1)}, u32[]{:S(2)}, u32[]{:S(2)}) collective-permute-start(bf16[2,2,2,48,512]{4,3,2,0,1:T(8,128)(2,1)S(1)} %dynamic-slice_bitcast_fusion.2), channel_id=1, source_target_pairs={{0,2},{2,0},{4,6},{6,4},{8,10},{10,8},{12,14},{14,12},{16,18},{18,... | collective-permute-start | bytes 1179656 | tf_op jit(solution)/shard_map/ppermute | solution.py:42
  491.9 21.1 %collective-permute-start.61 = (bf16[2,2,2,48,512]{4,3,2,1,0:T(8,128)(2,1)S(1)}, bf16[2,2,2,48,512]{4,3,2,1,0:T(8,128)(2,1)}, u32[]{:S(2)}, u32[]{:S(2)}) collective-permute-start(bf16[2,2,2,48,512]{4,3,2,1,0:T(8,128)(2,1)S(1)} %dynamic-slice_bitcast_fusion.3), channel_id=1, source_target_pairs={{0,8},{2,10},{4,12},{6,14},{8,0},{10,2},{12,4},{14,6},{16,24},{18,... | collective-permute-start | bytes 1179656 | tf_op jit(solution)/shard_map/ppermute | solution.py:42
  493.3 23.0 %collective-permute-start.59 = (bf16[2,2,2,48,512]{4,3,2,0,1:T(8,128)(2,1)S(1)}, bf16[2,2,2,48,512]{4,3,2,0,1:T(8,128)(2,1)S(1)}, u32[]{:S(2)}, u32[]{:S(2)}) collective-permute-start(bf16[2,2,2,48,512]{4,3,2,0,1:T(8,128)(2,1)S(1)} %dynamic-slice_bitcast_fusion.4), channel_id=1, source_target_pairs={{0,4},{2,6},{4,0},{6,2},{8,12},{10,14},{12,8},{14,10},{16,20},{18,... | collective-permute-start | bytes 1179656 | tf_op jit(solution)/shard_map/ppermute | solution.py:42
  496.9 19.6 %collective-permute-start.65 = (bf16[128,1536]{1,0:T(8,128)(2,1)S(1)}, bf16[128,1536]{1,0:T(8,128)(2,1)S(1)}, u32[]{:S(2)}, u32[]{:S(2)}) collective-permute-start(bf16[128,1536]{1,0:T(8,128)(2,1)S(1)} %dynamic-slice_bitcast_fusion.1), channel_id=1, source_target_pairs={{0,16},{2,18},{4,20},{6,22},{8,24},{10,26},{12,28},{14,30},{16,0},... | collective-permute-start | bytes 1179656 | tf_op jit(solution)/shard_map/ppermute | solution.py:42
  533.4 14.4 %collective-permute-start.67 = (bf16[2,48,1536]{2,1,0:T(8,128)(2,1)}, bf16[2,48,1536]{2,1,0:T(8,128)(2,1)}, u32[]{:S(2)}, u32[]{:S(2)}) collective-permute-start(bf16[2,48,1536]{2,1,0:T(8,128)(2,1)} %dynamic-slice_bitcast_fusion.10), channel_id=1, source_target_pairs={{0,16},{2,18},{4,20},{6,22},{8,24},{10,26},{12,28},{14,30},{16,0},... | collective-permute-start | bytes 884744 | tf_op jit(solution)/shard_map/ppermute | solution.py:42
  533.5 18.2 %collective-permute-start.70 = (bf16[1,280,1536]{2,1,0:T(8,128)(2,1)S(1)}, bf16[1,280,1536]{2,1,0:T(8,128)(2,1)}, u32[]{:S(2)}, u32[]{:S(2)}) collective-permute-start(bf16[1,280,1536]{2,1,0:T(8,128)(2,1)S(1)} %constant_dynamic-slice_fusion), channel_id=1, source_target_pairs={{0,2},{2,0},{4,6},{6,4},{8,10},{10,8},{12,14},{14,12},{16,18},{18,... | collective-permute-start | bytes 2580488 | tf_op jit(solution)/shard_map/ppermute | solution.py:42
  536.1 13.0 %collective-permute-start.66 = (f32[1,320]{1,0:T(1,128)S(1)}, f32[1,320]{1,0:T(1,128)S(1)}, u32[]{:S(2)}, u32[]{:S(2)}) collective-permute-start(f32[1,320]{1,0:T(1,128)S(1)} %reduce_sum.120), channel_id=1, source_target_pairs={{0,1},{1,0},{2,3},{3,2},{4,5},{5,4},{6,7},{7,6},{8,9},{9,8},{10,11... | collective-permute-start | bytes 3848 | tf_op jit(solution)/shard_map/ppermute | solution.py:37
  (107 other events, 844.2 us)
Sparse Core Ops, SparseCore 0:
  19.1 67.4 all-gather.5
  134.4 79.7 all-gather.3

commit v4 on v3

--- a/solution.py
+++ b/solution.py
@@ -451,15 +451,15 @@
     )(where, activated, out_grad)
 
 
-def project_kernel(heads, own, other, gain, weight, bias, cos, sin, normed, queries, kv):
+def project_streams(heads, own, other, gain, weight, bias, cos, sin, normed, queries, kv):
     hq = heads * HD
     for s, tokens in enumerate((own, other)):
         x = tokens[...].astype(f32)
         scale = lax.rsqrt(jnp.mean(x * x, axis=-1, keepdims=True) + EPSILON)
-        n = (x * scale * gain[...]).astype(bf16)
+        n = (x * scale * gain).astype(bf16)
         normed[s] = n
         cos_s, sin_s = cos[s], sin[s]
-        project = dot(n, weight[...], 1, 0) + bias[...]
+        project = dot(n, weight[...], 1, 0) + bias
 
         def turn(z):
             return z * cos_s + pltpu.roll(z, HD // 2, 1) * sin_s
@@ -468,6 +468,12 @@
             queries[s, h] = turn(project[:, h * HD : (h + 1) * HD]).astype(bf16)
         kv[s, :, :HD] = turn(project[:, hq : hq + HD]).astype(bf16)
         kv[s, :, HD:] = project[:, hq + HD :].astype(bf16)
+
+
+def project_kernel(heads, own, other, gain, weight, bias, cos, sin, normed, queries, kv):
+    project_streams(
+        heads, own, other, gain[...], weight, bias[...], cos, sin, normed, queries, kv
+    )
 
 
 def project(own, other, gain, weight, bias, cos, sin):
@@ -485,6 +491,73 @@
         compiler_params=BIG,
         name="project",
     )(own, other, gain, weight, bias, cos, sin)
+
+
+def order_project_kernel(
+    heads, flips, n_gain, n_bias, rows, where_ref, own, other, cos, sin, *refs
+):
+    parts = refs[: 2 * len(flips)]
+    normed, queries, kv, weight, gains, small, line = refs[2 * len(flips) :]
+    chip, core = where_ref[0], where_ref[1]
+    count = parts[0].shape[0]
+    at = 0
+    for p, part_flips in enumerate(flips):
+        columns = parts[2 * p].shape[3]
+        for k, flip in enumerate(part_flips):
+            part = parts[2 * p + k // count]
+            for h in range(2):
+                device = 2 * (chip ^ flip) + (core ^ h)
+                first = pl.multiple_of(device * rows, 16)
+                weight[pl.ds(first, rows), at : at + columns] = part[k % count, h, :rows]
+                if p == len(flips) - 1:
+                    small[pl.ds(device, 1), :] = part[k % count, h, rows:].astype(f32)[:1]
+        at += columns
+    devices = small.shape[0]
+    total = devices * n_bias
+    for d in range(devices):
+        row = small[d : d + 1, :]
+        gains[0:1, d * n_gain : (d + 1) * n_gain] = row[:, :n_gain]
+        line[1:2, d * n_bias : (d + 1) * n_bias] = row[:, n_gain : n_gain + n_bias]
+        gains[1:2, d * n_gain : (d + 1) * n_gain] = row[
+            :, n_gain + n_bias : 2 * n_gain + n_bias
+        ]
+    hq, v = heads * HD, 2 * heads * HD + 2 * HD
+    bias = jnp.where(
+        core == 0,
+        jnp.concatenate(
+            [line[1:2, :hq], line[1:2, 2 * hq : 2 * hq + HD], line[1:2, v : v + HD]], axis=1
+        ),
+        jnp.concatenate(
+            [line[1:2, hq : 2 * hq], line[1:2, 2 * hq + HD : v], line[1:2, v + HD : total]], axis=1
+        ),
+    )
+    gain = gains[0:1, :]
+    project_streams(heads, own, other, gain, weight, bias, cos, sin, normed, queries, kv)
+
+
+def order_project(where, own, other, cos, sin, parts, flips, n_gain, n_bias, rows):
+    tokens, width = own.shape
+    heads = H // KVH
+    columns = sum(p.shape[3] for p in parts[::2])
+    devices = 4 * parts[0].shape[0]
+    return pl.pallas_call(
+        functools.partial(order_project_kernel, heads, flips, n_gain, n_bias, rows),
+        out_shape=[
+            jax.ShapeDtypeStruct((2, tokens, width), bf16),
+            jax.ShapeDtypeStruct((2, heads, tokens, HD), bf16),
+            jax.ShapeDtypeStruct((2, tokens, 2 * HD), bf16),
+            jax.ShapeDtypeStruct((width, columns), bf16),
+            jax.ShapeDtypeStruct((2, width), f32),
+        ],
+        in_specs=[SMEM] + [VMEM] * (4 + len(parts)),
+        out_specs=[VMEM] * 5,
+        scratch_shapes=[
+            pltpu.VMEM((devices, parts[-1].shape[3]), f32),
+            pltpu.VMEM((8, devices * n_bias), f32),
+        ],
+        compiler_params=BIG,
+        name="order_project",
+    )(where, own, other, cos, sin, *parts)
 
 
 def pieces(cuts, half):
@@ -762,14 +835,20 @@
     ranges = jnp.stack([first, last], axis=-1).reshape(-1).astype(jnp.int32)
     starts, places = starts[..., None], places[..., None]
 
-    qkv_w, small_all = order_weights(qkv_parts, flips, where)
-    qkv_w = qkv_w.reshape(width, hq + 2 * HD)
-    small_all = small_all.reshape(2 * ctx_size, 2 * HD)
-    gain_one = small_all[:, :n_gain].reshape(1, -1)
-    bias = small_all[:, n_gain : n_gain + n_bias].reshape(1, -1)
-    gain_two = small_all[:, n_gain + n_bias : 2 * n_gain + n_bias].reshape(1, -1)
-    bias = head_columns(bias, core)
-    normed_one, queries, kv_own = project(token_own, token_other, gain_one, qkv_w, bias, cos, sin)
+    if rows_dev % 16:
+        qkv_w, small_all = order_weights(qkv_parts, flips, where)
+        qkv_w = qkv_w.reshape(width, hq + 2 * HD)
+        small_all = small_all.reshape(2 * ctx_size, 2 * HD)
+        gain_one = small_all[:, :n_gain].reshape(1, -1)
+        bias = small_all[:, n_gain : n_gain + n_bias].reshape(1, -1)
+        gain_two = small_all[:, n_gain + n_bias : 2 * n_gain + n_bias].reshape(1, -1)
+        bias = head_columns(bias, core)
+        normed_one, queries, kv_own = project(token_own, token_other, gain_one, qkv_w, bias, cos, sin)
+    else:
+        normed_one, queries, kv_own, qkv_w, gains = order_project(
+            where, token_own, token_other, cos, sin, qkv_parts, flips, n_gain, n_bias, rows_dev
+        )
+        gain_one, gain_two = gains[:1], gains[1:]
     kv_own = gather_relative(kv_own[None], high)
     kv_own, first_rows = together(kv_own, first_rows)
 

time: 571 us -> 563 us (0.986)
  waiting for transfers between devices: 223 us -> 207 us
  other arithmetic: 55.6 us -> 63.3 us
    ppermute x54, waiting for transfers between devices: 197 us -> 171 us  [chip_swap(): return lax.ppermute(x, 'ctx', [(i, i ^ flip) for i in range(count)])]
    all_to_all x1, waiting for transfers between devices: 0.49 us -> 8.75 us  [on_device(): sums = lax.all_to_all(sums, 'ctx', split_axis=0, concat_axis=0, tiled=True)]
    unnamed x164 -> x148, local copies, waits for them, and re-layouts: 15.6 us -> 15.3 us
  transfers between devices with their start and end apart: 80 -> 80, of which waited for: 43 -> 32; matrix products, arithmetic and copies ran while one was open for 16% -> 18% of each run, Pallas kernels for 12% -> 11%
where the time goes in v4:
time: 563 us; the launch traced here: 554 us
  waiting for transfers between devices  207 us (37%)
  starting transfers between devices  116 us (21%)
  Pallas kernels  89.8 us (16%)
  other arithmetic  63.3 us (11%)
  local copies, waits for them, and re-layouts  51.2 us (9%)
  between operations  15.9 us (3%)
  matrix products  10.5 us (2%)
    ppermute x54, waiting for transfers between devices, chip_swap(): return lax.ppermute(x, 'ctx', [(i, i ^ flip) for i in range(count)])  171 us
    ppermute x54, starting transfers between devices, chip_swap(): return lax.ppermute(x, 'ctx', [(i, i ^ flip) for i in range(count)])  78.9 us
    pallas_call x1, Pallas kernels, mlp(): pl.pallas_call(functools.partial(mlp_kernel, loads, groups), grid=(rows /...  27.7 us
    all_to_all x4, waiting for transfers between devices, group_exchange(): lax.all_to_all(x, 'ctx', split_axis=0, concat_axis=0, tiled=True, axis_in...  23.4 us
    all_to_all x4, starting transfers between devices, group_exchange(): lax.all_to_all(x, 'ctx', split_axis=0, concat_axis=0, tiled=True, axis_in...  21.2 us
    convert_element_type x17, other arithmetic, add(): self.parts = [x.astype(bf16) for x in self.parts]  20.5 us
    pallas_call x2, Pallas kernels, gate_up_grads(): pl.pallas_call(functools.partial(gate_up_grads_kernel, rows_dev), grid=(w...  16.6 us
    unnamed x148, local copies, waits for them, and re-layouts  15.3 us
  transfers between devices with their start and end apart: 80, of which 32 were waited for; matrix products, arithmetic and copies ran while one was open for 18% of the time, Pallas kernels for 11%

profile of v4, /device:TPU:0, one launch (start us, length us, event | category | flops | bytes accessed | tf_op | source)
XLA Modules:
  0.0 553.6 jit_solution(16347479254077459069)
XLA Ops:
  7.2 3.0 collective-permute-start.5
  15.2 2.6 collective-permute-start.4
  18.5 3.1 pack_members.1
  21.5 9.8 %collective-permute-done.4 = bf16[1,2,64,1024]{3,2,1,0:T(8,128)(2,1)S(1)} collective-permute-done((bf16[1,2,64,1024]{3,2,1,0:T(8,128)(2,1)S(1)}, bf16[1,2,64,1024]{3,2,1,0:T(8,128)(2,1)S(1)}, u32[]{:S(2)}, u32[]{:S(2)}) %collective-permute-start.4) | collective-permute-done | bytes 262176 | tf_op jit(solution)/shard_map/ppermute | solution.py:42
  34.0 2.7 collective-permute-done.9
  40.5 9.1 %collective-permute-done.12 = bf16[2,2,64,256]{3,2,1,0:T(8,128)(2,1)S(1)} collective-permute-done((bf16[2,2,64,256]{3,2,1,0:T(8,128)(2,1)S(1)}, bf16[2,2,64,256]{3,2,1,0:T(8,128)(2,1)S(1)}, u32[]{:S(2)}, u32[]{:S(2)}) %collective-permute-start.12) | collective-permute-done | bytes 131104 | tf_op jit(solution)/shard_map/ppermute | solution.py:42
  54.6 4.4 collective-permute-done.13
  62.6 17.6 %collective-permute-done.14.refs_5_ = bf16[8,2,64,256]{3,2,1,0:T(8,128)(2,1)} collective-permute-done((bf16[8,2,64,256]{3,2,1,0:T(8,128)(2,1)}, bf16[8,2,64,256]{3,2,1,0:T(8,128)(2,1)}, u32[]{:S(2)}, u32[]{:S(2)}) %collective-permute-start.14) | collective-permute-done | bytes 524320 | tf_op jit(solution)/shard_map/ppermute | solution.py:42
  81.0 7.0 %all-to-all-start = ((bf16[8,16,2304]{2,1,0:T(8,128)(2,1)}), bf16[8,16,2304]{2,1,0:T(8,128)(2,1)}, u32[]{:S(2)}, u32[]{:S(2)}) async-start(bf16[8,16,2304]{2,1,0:T(8,128)(2,1)} %slice.162), calls=%async_computation | async-start | bytes 1179648 | tf_op jit(solution)/shard_map/all_to_all | solution.py:71
  89.8 4.8 order_project.1
  94.6 3.0 collective-permute-start.15
  97.6 3.2 collective-permute-done.15
  101.7 3.5 collective-permute-start.19
  120.8 3.4 order_rows.1
  126.9 4.7 all-to-all-start.1
  135.0 9.1 %attend.1 = (bf16[2,2048,256]{2,1,0:T(8,128)(2,1)}, f32[2,2,384,128]{3,2,1,0:T(8,128)}, bf16[2,128,768]{2,1,0:T(8,128)(2,1)}, f32[2,2,384,1]{3,2,1,0:T(8,128)}, f32[2,128,1536]{2,1,0:T(8,128)}) custom-call(s32[2]{0:T(128)} %pad_add_fusion.2.where_ref, s32[8]{0:T(128)} %reshape.402.range_ref, bf16[2,6,128,128]{3,2,1,0:T(8,128)(2,1)} %get-tuple-element.133.queries, ...), custom_call_target="tpu_custom_call" | custom-call | tf_op jit(solution)/shard_map/attend/pallas_call | solution.py:639
  147.9 23.4 %all-to-all-done.1 = bf16[8,32,2304]{2,1,0:T(8,128)(2,1)S(1)} async-done(((bf16[8,32,2304]{2,1,0:T(8,128)(2,1)}), bf16[8,32,2304]{2,1,0:T(8,128)(2,1)S(1)}, u32[]{:S(2)}, u32[]{:S(2)}) %all-to-all-start.1) | async-done | bytes 1179680 | tf_op jit(solution)/shard_map/all_to_all | solution.py:71
  177.5 34.7 %collective-permute-done.28 = bf16[1,128,1536]{2,1,0:T(8,128)(2,1)S(1)} collective-permute-done((bf16[1,128,1536]{2,1,0:T(8,128)(2,1)S(1)}, bf16[1,128,1536]{2,1,0:T(8,128)(2,1)S(1)}, u32[]{:S(2)}, u32[]{:S(2)}) %collective-permute-start.28) | collective-permute-done | bytes 393248 | tf_op jit(solution)/shard_map/ppermute | solution.py:42
  212.4 5.4 collective-permute-start.31
  219.2 6.5 %collective-permute-done.31 = bf16[2,64,1536]{2,1,0:T(8,128)(2,1)S(1)} collective-permute-done((bf16[2,64,1536]{2,1,0:T(8,128)(2,1)S(1)}, bf16[2,64,1536]{2,1,0:T(8,128)(2,1)S(1)}, u32[]{:S(2)}, u32[]{:S(2)}) %collective-permute-start.31) | collective-permute-done | bytes 393248 | tf_op jit(solution)/shard_map/ppermute | solution.py:42
  229.6 11.5 %collective-permute-done.34.refs_4_ = bf16[4,48,2304]{2,1,0:T(8,128)(2,1)} collective-permute-done((bf16[4,48,2304]{2,1,0:T(8,128)(2,1)}, bf16[4,48,2304]{2,1,0:T(8,128)(2,1)}, u32[]{:S(2)}, u32[]{:S(2)}) %collective-permute-start.34) | collective-permute-done | bytes 884768 | tf_op jit(solution)/shard_map/ppermute | solution.py:42
  241.1 5.4 collective-permute-done.32.refs_1_
  248.5 3.7 order_tokens.1
  252.2 27.7 %mlp.1 = (bf16[1024,2304]{1,0:T(8,128)(2,1)}, bf16[1024,1120]{1,0:T(8,128)(2,1)}, bf16[1024,1536]{1,0:T(8,128)(2,1)}) custom-call(s32[2]{0:T(128)} %pad_add_fusion.2.where_ref, bf16[1024,1536]{1,0:T(8,128)(2,1)} %bitcast.305, bf16[1024,1536]{1,0:T(8,128)(2,1)} %all-gather.4.cloned.1.call-done.out_grad, bf16[1120,1536]{1,0:T(8,128)(2,1)} %bitcast.314, ...), custom_call_target="tpu_custom_call" | custom-call | tf_op jit(solution)/shard_map/mlp/pallas_call | solution.py:371
  286.5 8.2 %gate_up_grads.2 = (bf16[16,48,1152]{2,1,0:T(8,128)(2,1)}, bf16[16,48,1152]{2,1,0:T(8,128)(2,1)}) custom-call(s32[2]{0:T(128)} %pad_add_fusion.2.where_ref, bf16[1024,1536]{1,0:T(8,128)(2,1)} %bitcast.306, bf16[1024,2304]{1,0:T(8,128)(2,1)} %get-tuple-element.183.pre_grad), custom_call_target="tpu_custom_call" | custom-call | tf_op jit(solution)/shard_map/gate_up_grads/pallas_call | solution.py:408
  294.8 6.2 %convolution_convert_fusion = bf16[1024,1536]{1,0:T(8,128)(2,1)S(1)} fusion(bf16[1024,1120]{1,0:T(8,128)(2,1)} %get-tuple-element.202.activated, bf16[1120,1536]{1,0:T(8,128)(2,1)S(1)} %bitcast.315), kind=kOutput, calls=%fused_computation.1 | convolution fusion | flops 3524788224 | bytes 8880128 | tf_op jit(solution)/shard_map/dot_general | solution.py:166
  301.0 4.7 collective-permute-done.39
  317.4 3.2 collective-permute-done.42
  320.7 4.5 collective-permute-done.41
  328.4 8.4 %gate_up_grads.3 = (bf16[16,48,1152]{2,1,0:T(8,128)(2,1)}, bf16[16,48,1152]{2,1,0:T(8,128)(2,1)}) custom-call(s32[2]{0:T(128)} %pad_add_fusion.2.where_ref, bf16[1024,1536]{1,0:T(8,128)(2,1)} %bitcast.307, bf16[1024,2304]{1,0:T(8,128)(2,1)} %get-tuple-element.183.pre_grad), custom_call_target="tpu_custom_call" | custom-call | tf_op jit(solution)/shard_map/gate_up_grads/pallas_call | solution.py:408
  342.0 7.9 %collective-permute-done.45 = bf16[8,1,48,1152]{3,2,0,1:T(8,128)(2,1)S(1)} collective-permute-done((bf16[8,1,48,1152]{3,2,0,1:T(8,128)(2,1)S(1)}, bf16[8,1,48,1152]{3,2,0,1:T(8,128)(2,1)S(1)}, u32[]{:S(2)}, u32[]{:S(2)}) %collective-permute-start.45) | collective-permute-done | bytes 884768 | tf_op jit(solution)/shard_map/ppermute | solution.py:42
  353.6 5.0 all-to-all-start.2
  361.4 10.3 %attend_back.1 = (bf16[2,128,768]{2,1,0:T(8,128)(2,1)}, bf16[8,2,2,128,256]{4,3,2,1,0:T(8,128)(2,1)}) custom-call(s32[8]{0:T(128)} %reshape.402.range_ref, bf16[128,1536]{1,0:T(8,128)(2,1)} %copy-done.8, bf16[128,1536]{1,0:T(8,128)(2,1)} %copy-done.33, bf16[1536,768]{1,0:T(8,128)(2,1)} %bitcast.317, bf16[2,6,128,128]{3,2,1,0:T(8,128)(2,1)} %get-tuple-element.133.queries, ...), custom_call_target="tpu_custom_call" | custom-call | tf_op jit(solution)/shard_map/attend_back/pallas_call | solution.py:736
  371.7 11.0 %collective-permute-done.50 = bf16[8,1,48,1152]{3,2,0,1:T(8,128)(2,1)S(1)} collective-permute-done((bf16[8,1,48,1152]{3,2,0,1:T(8,128)(2,1)S(1)}, bf16[8,1,48,1152]{3,2,0,1:T(8,128)(2,1)S(1)}, u32[]{:S(2)}, u32[]{:S(2)}) %collective-permute-start.50) | collective-permute-done | bytes 884768 | tf_op jit(solution)/shard_map/ppermute | solution.py:42
  384.8 4.4 all-to-all-start.3
  404.6 7.5 %down_grads.1 = (bf16[2,280,1536]{2,1,0:T(8,128)(2,1)}, bf16[2,280,1536]{2,1,0:T(8,128)(2,1)}) custom-call(s32[2]{0:T(128)} %pad_add_fusion.2.where_ref, bf16[1024,1120]{1,0:T(8,128)(2,1)} %get-tuple-element.202.activated, bf16[1024,1536]{1,0:T(8,128)(2,1)} %all-gather.4.cloned.1.call-done.out_grad), custom_call_target="tpu_custom_call" | custom-call | tf_op jit(solution)/shard_map/down_grads/pallas_call | solution.py:439
  412.1 18.2 %collective-permute-done.53 = bf16[2,2,2,2,48,512]{5,4,3,0,1,2:T(8,128)(2,1)} collective-permute-done((bf16[2,2,2,2,48,512]{5,4,3,0,1,2:T(8,128)(2,1)}, bf16[2,2,2,2,48,512]{5,4,3,0,1,2:T(8,128)(2,1)}, u32[]{:S(2)}, u32[]{:S(2)}) %collective-permute-start.53) | collective-permute-done | bytes 786464 | tf_op jit(solution)/shard_map/ppermute | solution.py:42
  431.1 2.7 reduce_sum.113
  445.3 4.5 all-to-all-start.4
  449.8 2.6 fusion.4
  470.4 3.1 add_convert_fusion.2
  477.9 2.9 collective-permute-start.65
  488.6 4.2 all-to-all-start.5
  496.3 3.6 unpack_members.1
  511.0 3.8 collective-permute-done.60
  523.5 4.0 all-to-all-start.6
  529.4 8.8 %all-to-all-done.6 = f32[16,1,320]{2,1,0:T(1,128)S(1)} async-done(((f32[16,1,320]{2,1,0:T(1,128)}), f32[16,1,320]{2,1,0:T(1,128)S(1)}, u32[]{:S(2)}, u32[]{:S(2)}) %all-to-all-start.6) | async-done | bytes 20512 | tf_op jit(solution)/shard_map/all_to_all | solution.py:1045
  543.6 2.7 add_bitcast_fusion
  (444 shorter events, 186.0 us)
Async XLA Ops:
  7.2 124.5 %all-gather.6.cloned.1.call-start = ((), (), s32[]{:S(2)}) async-start(), calls=%async_computation.8 | async-start | bytes 2506752 | tf_op jit(solution)/shard_map/all_gather | solution.py:803
  7.2 24.1 %collective-permute-start.5 = (bf16[280,1536]{1,0:T(8,128)(2,1)}, bf16[280,1536]{1,0:T(8,128)(2,1)S(1)}, u32[]{:S(2)}, u32[]{:S(2)}) collective-permute-start(bf16[280,1536]{1,0:T(8,128)(2,1)} %param.21), channel_id=1, source_target_pairs={{0,2},{2,0},{4,6},{6,4},{8,10},{10,8},{12,14},{14,12},{16,18},{18,... | collective-permute-start | bytes 2580488 | tf_op jit(solution)/shard_map/ppermute | solution.py:42
  15.2 16.2 %collective-permute-start.4 = (bf16[1,2,64,1024]{3,2,1,0:T(8,128)(2,1)S(1)}, bf16[1,2,64,1024]{3,2,1,0:T(8,128)(2,1)S(1)}, u32[]{:S(2)}, u32[]{:S(2)}) collective-permute-start(bf16[1,2,64,1024]{3,2,1,0:T(8,128)(2,1)S(1)} %maximum_bitcast_fusion), channel_id=1, source_target_pairs={{0,16},{2,18},{4,20},{6,22},{8,24},{10,26},{12,28},{14,30},{16,0},... | collective-permute-start | bytes 786440 | tf_op jit(solution)/shard_map/ppermute | solution.py:42
  49.9 30.3 %collective-permute-start.11 = (bf16[8,2,48,384]{3,2,1,0:T(8,128)(2,1)S(1)}, bf16[8,2,48,384]{3,2,1,0:T(8,128)(2,1)}, u32[]{:S(2)}, u32[]{:S(2)}) collective-permute-start(bf16[8,2,48,384]{3,2,1,0:T(8,128)(2,1)S(1)} %pad_maximum_fusion.5.refs_2_), channel_id=1, source_target_pairs={{0,2},{2,0},{4,6},{6,4},{8,10},{10,8},{12,14},{14,12},{16,18},{18,... | collective-permute-start | bytes 1769480 | tf_op jit(solution)/shard_map/ppermute | solution.py:42
  52.0 28.1 %collective-permute-start.8 = (bf16[8,2,48,384]{3,2,1,0:T(8,128)(2,1)S(1)}, bf16[8,2,48,384]{3,2,1,0:T(8,128)(2,1)}, u32[]{:S(2)}, u32[]{:S(2)}) collective-permute-start(bf16[8,2,48,384]{3,2,1,0:T(8,128)(2,1)S(1)} %pad_maximum_fusion.4.refs_0_), channel_id=1, source_target_pairs={{0,8},{2,10},{4,12},{6,14},{8,0},{10,2},{12,4},{14,6},{16,24},{18,... | collective-permute-start | bytes 1769480 | tf_op jit(solution)/shard_map/ppermute | solution.py:42
  59.9 20.3 %collective-permute-start.14 = (bf16[8,2,64,256]{3,2,1,0:T(8,128)(2,1)}, bf16[8,2,64,256]{3,2,1,0:T(8,128)(2,1)}, u32[]{:S(2)}, u32[]{:S(2)}) collective-permute-start(bf16[8,2,64,256]{3,2,1,0:T(8,128)(2,1)} %pad_maximum_fusion.8.refs_4_), channel_id=1, source_target_pairs={{0,4},{2,6},{4,0},{6,2},{8,12},{10,14},{12,8},{14,10},{16,20},{18,... | collective-permute-start | bytes 1572872 | tf_op jit(solution)/shard_map/ppermute | solution.py:42
  61.5 26.6 %collective-permute-start = (s32[4]{0:T(128)S(1)}, s32[4]{0:T(128)S(1)}, u32[]{:S(2)}, u32[]{:S(2)}) collective-permute-start(s32[4]{0:T(128)S(1)} %bitcast.349), channel_id=1, source_target_pairs={{0,1},{1,0},{2,3},{3,2},{4,5},{5,4},{6,7},{7,6},{8,9},{9,8},{10,11... | collective-permute-start | bytes 56 | tf_op jit(solution)/shard_map/ppermute | solution.py:37
  61.5 28.3 %collective-permute-start.1 = (bf16[128,1536]{1,0:T(8,128)(2,1)S(1)}, bf16[128,1536]{1,0:T(8,128)(2,1)}, u32[]{:S(2)}, u32[]{:S(2)}) collective-permute-start(bf16[128,1536]{1,0:T(8,128)(2,1)S(1)} %bitcast.323), channel_id=1, source_target_pairs={{0,1},{1,0},{2,3},{3,2},{4,5},{5,4},{6,7},{7,6},{8,9},{9,8},{10,11... | collective-permute-start | bytes 1179656 | tf_op jit(solution)/shard_map/ppermute | solution.py:37
  81.0 20.7 %all-to-all-start = ((bf16[8,16,2304]{2,1,0:T(8,128)(2,1)}), bf16[8,16,2304]{2,1,0:T(8,128)(2,1)}, u32[]{:S(2)}, u32[]{:S(2)}) async-start(bf16[8,16,2304]{2,1,0:T(8,128)(2,1)} %slice.162), calls=%async_computation | async-start | bytes 1179648 | tf_op jit(solution)/shard_map/all_to_all | solution.py:71
  105.2 14.4 %collective-permute-start.25 = (bf16[280,1536]{1,0:T(8,128)(2,1)}, bf16[280,1536]{1,0:T(8,128)(2,1)S(1)}, u32[]{:S(2)}, u32[]{:S(2)}) collective-permute-start(bf16[280,1536]{1,0:T(8,128)(2,1)} %param.21), channel_id=1, source_target_pairs={{0,1},{1,0},{2,3},{3,2},{4,5},{5,4},{6,7},{7,6},{8,9},{9,8},{10,11... | collective-permute-start | bytes 2580488 | tf_op jit(solution)/shard_map/ppermute | solution.py:37
  105.2 14.4 %collective-permute-start.26 = (bf16[280,1536]{1,0:T(8,128)(2,1)}, bf16[280,1536]{1,0:T(8,128)(2,1)S(1)}, u32[]{:S(2)}, u32[]{:S(2)}) collective-permute-start(bf16[280,1536]{1,0:T(8,128)(2,1)} %copy-done.47), channel_id=1, source_target_pairs={{0,1},{1,0},{2,3},{3,2},{4,5},{5,4},{6,7},{7,6},{8,9},{9,8},{10,11... | collective-permute-start | bytes 2580488 | tf_op jit(solution)/shard_map/ppermute | solution.py:37
  126.9 44.4 %all-to-all-start.1 = ((bf16[8,32,2304]{2,1,0:T(8,128)(2,1)}), bf16[8,32,2304]{2,1,0:T(8,128)(2,1)S(1)}, u32[]{:S(2)}, u32[]{:S(2)}) async-start(bf16[8,32,2304]{2,1,0:T(8,128)(2,1)} %slice.166), calls=%async_computation.1 | async-start | bytes 2359296 | tf_op jit(solution)/shard_map/all_to_all | solution.py:71
  131.7 96.5 %all-gather.4.cloned.1.call-start = ((), (), s32[]{:S(2)}) async-start(), calls=%async_computation.7 | async-start | bytes 3538944 | tf_op jit(solution)/shard_map/all_gather | solution.py:804
  172.6 39.7 %collective-permute-start.29 = (bf16[4,48,2304]{2,1,0:T(8,128)(2,1)S(1)}, bf16[4,48,2304]{2,1,0:T(8,128)(2,1)S(1)}, u32[]{:S(2)}, u32[]{:S(2)}) collective-permute-start(bf16[4,48,2304]{2,1,0:T(8,128)(2,1)S(1)} %slice.203), channel_id=1, source_target_pairs={{0,2},{2,0},{4,6},{6,4},{8,10},{10,8},{12,14},{14,12},{16,18},{18,... | collective-permute-start | bytes 2654216 | tf_op jit(solution)/shard_map/ppermute | solution.py:42
  177.4 34.8 %collective-permute-start.28 = (bf16[1,128,1536]{2,1,0:T(8,128)(2,1)S(1)}, bf16[1,128,1536]{2,1,0:T(8,128)(2,1)S(1)}, u32[]{:S(2)}, u32[]{:S(2)}) collective-permute-start(bf16[1,128,1536]{2,1,0:T(8,128)(2,1)S(1)} %fusion.34), channel_id=1, source_target_pairs={{0,16},{2,18},{4,20},{6,22},{8,24},{10,26},{12,28},{14,30},{16,0},... | collective-permute-start | bytes 1179656 | tf_op jit(solution)/shard_map/ppermute | solution.py:42
  217.7 34.5 %collective-permute-start.35 = (bf16[8,48,2304]{2,1,0:T(8,128)(2,1)S(1)}, bf16[8,48,2304]{2,1,0:T(8,128)(2,1)}, u32[]{:S(2)}, u32[]{:S(2)}) collective-permute-start(bf16[8,48,2304]{2,1,0:T(8,128)(2,1)S(1)} %constant_dynamic-update-slice_fusion.refs_0_), channel_id=1, source_target_pairs={{0,1},{1,0},{2,3},{3,2},{4,5},{5,4},{6,7},{7,6},{8,9},{9,8},{10,11... | collective-permute-start | bytes 5308424 | tf_op jit(solution)/shard_map/ppermute | solution.py:37
  218.7 22.4 %collective-permute-start.34 = (bf16[4,48,2304]{2,1,0:T(8,128)(2,1)}, bf16[4,48,2304]{2,1,0:T(8,128)(2,1)}, u32[]{:S(2)}, u32[]{:S(2)}) collective-permute-start(bf16[4,48,2304]{2,1,0:T(8,128)(2,1)} %slice.173), channel_id=1, source_target_pairs={{0,2},{2,0},{4,6},{6,4},{8,10},{10,8},{12,14},{14,12},{16,18},{18,... | collective-permute-start | bytes 2654216 | tf_op jit(solution)/shard_map/ppermute | solution.py:42
  228.2 18.3 %collective-permute-start.32 = (bf16[4,64,1536]{2,1,0:T(8,128)(2,1)}, bf16[4,64,1536]{2,1,0:T(8,128)(2,1)}, u32[]{:S(2)}, u32[]{:S(2)}) collective-permute-start(bf16[4,64,1536]{2,1,0:T(8,128)(2,1)} %pad_maximum_fusion.1.refs_0_), channel_id=1, source_target_pairs={{0,4},{2,6},{4,0},{6,2},{8,12},{10,14},{12,8},{14,10},{16,20},{18,... | collective-permute-start | bytes 2359304 | tf_op jit(solution)/shard_map/ppermute | solution.py:42
  229.6 18.4 %collective-permute-start.33 = (bf16[4,64,1536]{2,1,0:T(8,128)(2,1)}, bf16[4,64,1536]{2,1,0:T(8,128)(2,1)}, u32[]{:S(2)}, u32[]{:S(2)}) collective-permute-start(bf16[4,64,1536]{2,1,0:T(8,128)(2,1)} %pad_maximum_fusion.2.refs_2_), channel_id=1, source_target_pairs={{0,8},{2,10},{4,12},{6,14},{8,0},{10,2},{12,4},{14,6},{16,24},{18,... | collective-permute-start | bytes 2359304 | tf_op jit(solution)/shard_map/ppermute | solution.py:42
  286.0 19.8 %collective-permute-start.39 = (bf16[2,2,64,1536]{3,2,0,1:T(8,128)(2,1)}, bf16[2,2,64,1536]{3,2,0,1:T(8,128)(2,1)}, u32[]{:S(2)}, u32[]{:S(2)}) collective-permute-start(bf16[2,2,64,1536]{3,2,0,1:T(8,128)(2,1)} %bitcast.302), channel_id=1, source_target_pairs={{0,8},{2,10},{4,12},{6,14},{8,0},{10,2},{12,4},{14,6},{16,24},{18,... | collective-permute-start | bytes 2359304 | tf_op jit(solution)/shard_map/ppermute | solution.py:42
  286.3 20.8 %collective-permute-start.38 = (bf16[2,2,64,1536]{3,2,0,1:T(8,128)(2,1)}, bf16[2,2,64,1536]{3,2,0,1:T(8,128)(2,1)}, u32[]{:S(2)}, u32[]{:S(2)}) collective-permute-start(bf16[2,2,64,1536]{3,2,0,1:T(8,128)(2,1)} %bitcast.303), channel_id=1, source_target_pairs={{0,4},{2,6},{4,0},{6,2},{8,12},{10,14},{12,8},{14,10},{16,20},{18,... | collective-permute-start | bytes 2359304 | tf_op jit(solution)/shard_map/ppermute | solution.py:42
  294.8 13.7 %collective-permute-start.40 = (bf16[16,48,1152]{2,1,0:T(8,128)(2,1)}, bf16[16,48,1152]{2,1,0:T(8,128)(2,1)S(1)}, u32[]{:S(2)}, u32[]{:S(2)}) collective-permute-start(bf16[16,48,1152]{2,1,0:T(8,128)(2,1)} %get-tuple-element.172), channel_id=1, source_target_pairs={{0,1},{1,0},{2,3},{3,2},{4,5},{5,4},{6,7},{7,6},{8,9},{9,8},{10,11... | collective-permute-start | bytes 5308424 | tf_op jit(solution)/shard_map/ppermute | solution.py:37
  308.9 16.3 %collective-permute-start.41 = (bf16[2,64,1536]{2,1,0:T(8,128)(2,1)S(1)}, bf16[2,64,1536]{2,1,0:T(8,128)(2,1)S(1)}, u32[]{:S(2)}, u32[]{:S(2)}) collective-permute-start(bf16[2,64,1536]{2,1,0:T(8,128)(2,1)S(1)} %dynamic-slice_bitcast_fusion.8), channel_id=1, source_target_pairs={{0,8},{2,10},{4,12},{6,14},{8,0},{10,2},{12,4},{14,6},{16,24},{18,... | collective-permute-start | bytes 1179656 | tf_op jit(solution)/shard_map/ppermute | solution.py:42
  311.5 47.1 %collective-permute-start.48 = (bf16[2,2,64,1536]{3,2,0,1:T(8,128)(2,1)}, bf16[2,2,64,1536]{3,2,0,1:T(8,128)(2,1)}, u32[]{:S(2)}, u32[]{:S(2)}) collective-permute-start(bf16[2,2,64,1536]{3,2,0,1:T(8,128)(2,1)} %bitcast.301), channel_id=1, source_target_pairs={{0,4},{2,6},{4,0},{6,2},{8,12},{10,14},{12,8},{14,10},{16,20},{18,... | collective-permute-start | bytes 2359304 | tf_op jit(solution)/shard_map/ppermute | solution.py:42
  315.2 43.3 %collective-permute-start.49 = (bf16[2,2,64,1536]{3,2,0,1:T(8,128)(2,1)}, bf16[2,2,64,1536]{3,2,0,1:T(8,128)(2,1)}, u32[]{:S(2)}, u32[]{:S(2)}) collective-permute-start(bf16[2,2,64,1536]{3,2,0,1:T(8,128)(2,1)} %bitcast.300), channel_id=1, source_target_pairs={{0,8},{2,10},{4,12},{6,14},{8,0},{10,2},{12,4},{14,6},{16,24},{18,... | collective-permute-start | bytes 2359304 | tf_op jit(solution)/shard_map/ppermute | solution.py:42
  325.3 14.0 %collective-permute-start.44 = (bf16[64,1536]{1,0:T(8,128)(2,1)S(1)}, bf16[64,1536]{1,0:T(8,128)(2,1)S(1)}, u32[]{:S(2)}, u32[]{:S(2)}) collective-permute-start(bf16[64,1536]{1,0:T(8,128)(2,1)S(1)} %dynamic-slice_bitcast_fusion.14), channel_id=1, source_target_pairs={{0,16},{2,18},{4,20},{6,22},{8,24},{10,26},{12,28},{14,30},{16,0},... | collective-permute-start | bytes 589832 | tf_op jit(solution)/shard_map/ppermute | solution.py:42
  326.2 15.7 %collective-permute-start.43 = (bf16[64,1536]{1,0:T(8,128)(2,1)S(1)}, bf16[64,1536]{1,0:T(8,128)(2,1)S(1)}, u32[]{:S(2)}, u32[]{:S(2)}) collective-permute-start(bf16[64,1536]{1,0:T(8,128)(2,1)S(1)} %dynamic-slice_bitcast_fusion.15), channel_id=1, source_target_pairs={{0,16},{2,18},{4,20},{6,22},{8,24},{10,26},{12,28},{14,30},{16,0},... | collective-permute-start | bytes 589832 | tf_op jit(solution)/shard_map/ppermute | solution.py:42
  353.6 30.3 %all-to-all-start.2 = ((bf16[8,48,1152]{2,1,0:T(8,128)(2,1)}), bf16[8,48,1152]{2,1,0:T(8,128)(2,1)S(1)}, u32[]{:S(2)}, u32[]{:S(2)}) async-start(bf16[8,48,1152]{2,1,0:T(8,128)(2,1)} %fusion.9), calls=%async_computation.2 | async-start | bytes 1769472 | tf_op jit(solution)/shard_map/all_to_all | solution.py:71
  361.3 21.4 %collective-permute-start.50 = (bf16[8,1,48,1152]{3,2,0,1:T(8,128)(2,1)S(1)}, bf16[8,1,48,1152]{3,2,0,1:T(8,128)(2,1)S(1)}, u32[]{:S(2)}, u32[]{:S(2)}) collective-permute-start(bf16[8,1,48,1152]{3,2,0,1:T(8,128)(2,1)S(1)} %dynamic-slice_bitcast_fusion), channel_id=1, source_target_pairs={{0,2},{2,0},{4,6},{6,4},{8,10},{10,8},{12,14},{14,12},{16,18},{18,... | collective-permute-start | bytes 2654216 | tf_op jit(solution)/shard_map/ppermute | solution.py:42
  384.8 46.2 %all-to-all-start.3 = ((bf16[8,2,2,128,256]{4,3,2,1,0:T(8,128)(2,1)}), bf16[8,2,2,128,256]{4,3,2,1,0:T(8,128)(2,1)}, u32[]{:S(2)}, u32[]{:S(2)}) async-start(bf16[8,2,2,128,256]{4,3,2,1,0:T(8,128)(2,1)} %get-tuple-element.199), calls=%async_computation.3 | async-start | bytes 4194304 | tf_op jit(solution)/shard_map/all_to_all | solution.py:51
  393.4 36.9 %collective-permute-start.53 = (bf16[2,2,2,2,48,512]{5,4,3,0,1,2:T(8,128)(2,1)}, bf16[2,2,2,2,48,512]{5,4,3,0,1,2:T(8,128)(2,1)}, u32[]{:S(2)}, u32[]{:S(2)}) collective-permute-start(bf16[2,2,2,2,48,512]{5,4,3,0,1,2:T(8,128)(2,1)} %bitcast.298), channel_id=1, source_target_pairs={{0,8},{2,10},{4,12},{6,14},{8,0},{10,2},{12,4},{14,6},{16,24},{18,... | collective-permute-start | bytes 2359304 | tf_op jit(solution)/shard_map/ppermute | solution.py:42
  397.9 33.2 %collective-permute-start.52 = (bf16[2,2,2,2,48,512]{5,4,3,2,1,0:T(8,128)(2,1)}, bf16[2,2,2,2,48,512]{5,4,3,2,1,0:T(8,128)(2,1)}, u32[]{:S(2)}, u32[]{:S(2)}) collective-permute-start(bf16[2,2,2,2,48,512]{5,4,3,2,1,0:T(8,128)(2,1)} %fusion.14), channel_id=1, source_target_pairs={{0,4},{2,6},{4,0},{6,2},{8,12},{10,14},{12,8},{14,10},{16,20},{18,... | collective-permute-start | bytes 2359304 | tf_op jit(solution)/shard_map/ppermute | solution.py:42
  401.3 29.8 %collective-permute-start.51 = (bf16[2,2,2,2,48,512]{5,4,3,0,1,2:T(8,128)(2,1)}, bf16[2,2,2,2,48,512]{5,4,3,0,1,2:T(8,128)(2,1)}, u32[]{:S(2)}, u32[]{:S(2)}) collective-permute-start(bf16[2,2,2,2,48,512]{5,4,3,0,1,2:T(8,128)(2,1)} %bitcast.299), channel_id=1, source_target_pairs={{0,2},{2,0},{4,6},{6,4},{8,10},{10,8},{12,14},{14,12},{16,18},{18,... | collective-permute-start | bytes 2359304 | tf_op jit(solution)/shard_map/ppermute | solution.py:42
  435.4 21.8 %collective-permute-start.54 = (bf16[1,2,128,256]{3,2,1,0:T(8,128)(2,1)}, bf16[1,2,128,256]{3,2,1,0:T(8,128)(2,1)}, u32[]{:S(2)}, u32[]{:S(2)}) collective-permute-start(bf16[1,2,128,256]{3,2,1,0:T(8,128)(2,1)} %constant_dynamic-slice_fusion.10), channel_id=1, source_target_pairs={{0,16},{2,18},{4,20},{6,22},{8,24},{10,26},{12,28},{14,30},{16,0},... | collective-permute-start | bytes 393224 | tf_op jit(solution)/shard_map/ppermute | solution.py:42
  437.6 32.8 %collective-permute-start.57 = (bf16[2,280,1536]{2,1,0:T(8,128)(2,1)}, bf16[2,280,1536]{2,1,0:T(8,128)(2,1)}, u32[]{:S(2)}, u32[]{:S(2)}) collective-permute-start(bf16[2,280,1536]{2,1,0:T(8,128)(2,1)} %get-tuple-element.216), channel_id=1, source_target_pairs={{0,1},{1,0},{2,3},{3,2},{4,5},{5,4},{6,7},{7,6},{8,9},{9,8},{10,11... | collective-permute-start | bytes 5160968 | tf_op jit(solution)/shard_map/ppermute | solution.py:37
  440.0 26.4 %collective-permute-start.56 = (bf16[2,64,1536]{2,1,0:T(8,128)(2,1)}, bf16[2,64,1536]{2,1,0:T(8,128)(2,1)}, u32[]{:S(2)}, u32[]{:S(2)}) collective-permute-start(bf16[2,64,1536]{2,1,0:T(8,128)(2,1)} %dynamic-slice_bitcast_fusion.5), channel_id=1, source_target_pairs={{0,4},{2,6},{4,0},{6,2},{8,12},{10,14},{12,8},{14,10},{16,20},{18,... | collective-permute-start | bytes 1179656 | tf_op jit(solution)/shard_map/ppermute | solution.py:42
  444.5 23.9 %collective-permute-start.55 = (bf16[2,64,1536]{2,1,0:T(8,128)(2,1)}, bf16[2,64,1536]{2,1,0:T(8,128)(2,1)}, u32[]{:S(2)}, u32[]{:S(2)}) collective-permute-start(bf16[2,64,1536]{2,1,0:T(8,128)(2,1)} %dynamic-slice_bitcast_fusion.6), channel_id=1, source_target_pairs={{0,8},{2,10},{4,12},{6,14},{8,0},{10,2},{12,4},{14,6},{16,24},{18,... | collective-permute-start | bytes 1179656 | tf_op jit(solution)/shard_map/ppermute | solution.py:42
  445.3 28.2 %all-to-all-start.4 = ((bf16[8,48,1152]{2,1,0:T(8,128)(2,1)}), bf16[8,48,1152]{2,1,0:T(8,128)(2,1)}, u32[]{:S(2)}, u32[]{:S(2)}) async-start(bf16[8,48,1152]{2,1,0:T(8,128)(2,1)} %fusion.10), calls=%async_computation.4 | async-start | bytes 1769472 | tf_op jit(solution)/shard_map/all_to_all | solution.py:71
  477.9 31.1 %collective-permute-start.65 = (bf16[128,1536]{1,0:T(8,128)(2,1)}, bf16[128,1536]{1,0:T(8,128)(2,1)}, u32[]{:S(2)}, u32[]{:S(2)}) collective-permute-start(bf16[128,1536]{1,0:T(8,128)(2,1)} %dynamic-slice_bitcast_fusion.1), channel_id=1, source_target_pairs={{0,16},{2,18},{4,20},{6,22},{8,24},{10,26},{12,28},{14,30},{16,0},... | collective-permute-start | bytes 1179656 | tf_op jit(solution)/shard_map/ppermute | solution.py:42
  481.6 18.3 %collective-permute-start.59 = (bf16[2,2,2,48,512]{4,3,2,0,1:T(8,128)(2,1)}, bf16[2,2,2,48,512]{4,3,2,0,1:T(8,128)(2,1)}, u32[]{:S(2)}, u32[]{:S(2)}) collective-permute-start(bf16[2,2,2,48,512]{4,3,2,0,1:T(8,128)(2,1)} %dynamic-slice_bitcast_fusion.4), channel_id=1, source_target_pairs={{0,4},{2,6},{4,0},{6,2},{8,12},{10,14},{12,8},{14,10},{16,20},{18,... | collective-permute-start | bytes 1179656 | tf_op jit(solution)/shard_map/ppermute | solution.py:42
  483.9 19.5 %collective-permute-start.61 = (bf16[2,2,2,48,512]{4,3,2,1,0:T(8,128)(2,1)}, bf16[2,2,2,48,512]{4,3,2,1,0:T(8,128)(2,1)}, u32[]{:S(2)}, u32[]{:S(2)}) collective-permute-start(bf16[2,2,2,48,512]{4,3,2,1,0:T(8,128)(2,1)} %dynamic-slice_bitcast_fusion.3), channel_id=1, source_target_pairs={{0,8},{2,10},{4,12},{6,14},{8,0},{10,2},{12,4},{14,6},{16,24},{18,... | collective-permute-start | bytes 1179656 | tf_op jit(solution)/shard_map/ppermute | solution.py:42
  486.1 20.9 %collective-permute-start.63 = (bf16[2,2,2,48,512]{4,3,2,0,1:T(8,128)(2,1)}, bf16[2,2,2,48,512]{4,3,2,0,1:T(8,128)(2,1)}, u32[]{:S(2)}, u32[]{:S(2)}) collective-permute-start(bf16[2,2,2,48,512]{4,3,2,0,1:T(8,128)(2,1)} %dynamic-slice_bitcast_fusion.2), channel_id=1, source_target_pairs={{0,2},{2,0},{4,6},{6,4},{8,10},{10,8},{12,14},{14,12},{16,18},{18,... | collective-permute-start | bytes 1179656 | tf_op jit(solution)/shard_map/ppermute | solution.py:42
  488.6 26.5 %all-to-all-start.5 = ((bf16[8,2,2,48,256]{4,3,2,1,0:T(8,128)(2,1)}), bf16[8,2,2,48,256]{4,3,2,1,0:T(8,128)(2,1)}, u32[]{:S(2)}, u32[]{:S(2)}) async-start(bf16[8,2,2,48,256]{4,3,2,1,0:T(8,128)(2,1)} %bitcast.304), calls=%async_computation.5 | async-start | bytes 1572864 | tf_op jit(solution)/shard_map/all_to_all | solution.py:51
  501.1 13.7 %collective-permute-start.60 = (bf16[2,2,48,512]{3,2,1,0:T(8,128)(2,1)S(1)}, bf16[2,2,48,512]{3,2,1,0:T(8,128)(2,1)S(1)}, u32[]{:S(2)}, u32[]{:S(2)}) collective-permute-start(bf16[2,2,48,512]{3,2,1,0:T(8,128)(2,1)S(1)} %dynamic-slice_bitcast_fusion.13), channel_id=1, source_target_pairs={{0,8},{2,10},{4,12},{6,14},{8,0},{10,2},{12,4},{14,6},{16,24},{18,... | collective-permute-start | bytes 589832 | tf_op jit(solution)/shard_map/ppermute | solution.py:42
  516.1 27.5 %collective-permute-start.70 = (bf16[1,280,1536]{2,1,0:T(8,128)(2,1)}, bf16[1,280,1536]{2,1,0:T(8,128)(2,1)}, u32[]{:S(2)}, u32[]{:S(2)}) collective-permute-start(bf16[1,280,1536]{2,1,0:T(8,128)(2,1)} %constant_dynamic-slice_fusion), channel_id=1, source_target_pairs={{0,2},{2,0},{4,6},{6,4},{8,10},{10,8},{12,14},{14,12},{16,18},{18,... | collective-permute-start | bytes 2580488 | tf_op jit(solution)/shard_map/ppermute | solution.py:42
  520.5 17.9 %collective-permute-start.68 = (bf16[1,2,48,256]{3,2,1,0:T(8,128)(2,1)}, bf16[1,2,48,256]{3,2,1,0:T(8,128)(2,1)}, u32[]{:S(2)}, u32[]{:S(2)}) collective-permute-start(bf16[1,2,48,256]{3,2,1,0:T(8,128)(2,1)} %constant_dynamic-slice_fusion.4), channel_id=1, source_target_pairs={{0,16},{2,18},{4,20},{6,22},{8,24},{10,26},{12,28},{14,30},{16,0},... | collective-permute-start | bytes 147464 | tf_op jit(solution)/shard_map/ppermute | solution.py:42
  521.2 18.0 %collective-permute-start.67 = (bf16[2,48,1536]{2,1,0:T(8,128)(2,1)S(1)}, bf16[2,48,1536]{2,1,0:T(8,128)(2,1)}, u32[]{:S(2)}, u32[]{:S(2)}) collective-permute-start(bf16[2,48,1536]{2,1,0:T(8,128)(2,1)S(1)} %dynamic-slice_bitcast_fusion.10), channel_id=1, source_target_pairs={{0,16},{2,18},{4,20},{6,22},{8,24},{10,26},{12,28},{14,30},{16,0},... | collective-permute-start | bytes 884744 | tf_op jit(solution)/shard_map/ppermute | solution.py:42
  523.5 14.7 %all-to-all-start.6 = ((f32[16,1,320]{2,1,0:T(1,128)}), f32[16,1,320]{2,1,0:T(1,128)S(1)}, u32[]{:S(2)}, u32[]{:S(2)}) async-start(f32[16,1,320]{2,1,0:T(1,128)} %pad_maximum_fusion.25), calls=%async_computation.6 | async-start | bytes 49152 | tf_op jit(solution)/shard_map/all_to_all | solution.py:1045
  (99 other events, 733.8 us)
Sparse Core Ops, SparseCore 0:
  18.6 71.6 all-gather.5
  134.7 81.6 all-gather.3

commit v5 on v4

--- a/solution.py
+++ b/solution.py
@@ -971,22 +971,20 @@
     project_grad_q = project_grad_q.reshape(-1, hq)
     grad_out_part = weight_parts(dot(branch_grad, attended_b.reshape(-1, hq), 0, 0))
     grad_q_part = weight_parts(dot(normed_one, project_grad_q, 0, 0))
-    wide_part = jnp.concatenate([grad_q_part, grad_out_part], axis=-1)
     names = tuple(reversed(high)) + (2, 1, 0)
-    wide_part = wide_part.reshape((2,) * len(names) + wide_part.shape[2:])
-    third = 2 * hq // 3
-    scatter = Scatter([wide_part[..., i * third : (i + 1) * third] for i in range(3)], names)
-    bits = [order[0] for order in ORDERS]
+    wide_parts = [
+        x.reshape((2,) * len(names) + x.shape[2:]) for x in (grad_q_part, grad_out_part)
+    ]
+    scatter = Scatter(wide_parts, names)
+    bits = (0, 1)
     kept, sent = scatter.split(bits)
     arrived = [chip_swap(x, 1 << bit) for x, bit in zip(sent, bits)]
-    kv_sum, arrived, down_send, branch_arrived = together(
-        kv_sum, arrived, down_send, branch_arrived
-    )
+    kv_sum, down_send, branch_arrived = together(kv_sum, down_send, branch_arrived)
 
     kv_sum = jnp.sum(kv_sum.astype(f32), axis=0).astype(bf16)
-    kv_sum, grad_up = together(kv_sum, grad_up)
     kv_sum = sum_over_high(kv_sum, high)
     down_arrived = core_swap(down_send)
+    kv_sum, arrived, grad_up = together(kv_sum, arrived, grad_up)
     grad_up = group_exchange(grad_up)
     key_pre = kv_sum[..., :HD]
     key_pre = key_pre * cos - jnp.roll(key_pre, HD // 2, axis=-1) * sin
@@ -1006,8 +1004,8 @@
     grad_kv = cube_exchange(grad_kv)
     branch_sums.parts = [jnp.concatenate(branch_sums.parts, axis=-2)]
     branch_sums.step((upper,))
-    scatter.step([order[1] for order in ORDERS])
-    scatter.step([order[2] for order in ORDERS])
+    scatter.step((2, 0))
+    scatter.step((1, 2))
     scatter.parts = [jnp.concatenate(scatter.parts, axis=-1)]
     scale_one = lax.rsqrt(jnp.mean(inputs * inputs, axis=-1, keepdims=True) + EPSILON)
     gain_one_grad = jnp.sum(normed_one_grad * inputs * scale_one, axis=0)

time: 563 us -> 570 us (1.012); the launches traced: 554 us -> 567 us
  waiting for transfers between devices: 207 us -> 235 us
  Pallas kernels: 89.8 us -> 105 us
  starting transfers between devices: 116 us -> 104 us
  other arithmetic: 63.3 us -> 53.4 us
    pallas_call x2, Pallas kernels: 16.6 us -> 29 us  [gate_up_grads(): pl.pallas_call(functools.partial(gate_up_grads_kernel, rows_dev), grid=(w...]
    all_to_all x2, waiting for transfers between devices: 0.01 us -> 10.5 us  [cube_exchange(): lax.all_to_all(x, 'ctx', split_axis=0, concat_axis=0, tiled=True, axis_in...]
    ppermute x54 -> x51, starting transfers between devices: 78.9 us -> 68.8 us  [chip_swap(): return lax.ppermute(x, 'ctx', [(i, i ^ flip) for i in range(count)])]
    all_to_all x4, waiting for transfers between devices: 23.4 us -> 33 us  [group_exchange(): lax.all_to_all(x, 'ctx', split_axis=0, concat_axis=0, tiled=True, axis_in...]
    ppermute x54 -> x51, waiting for transfers between devices: 171 us -> 178 us  [chip_swap(): return lax.ppermute(x, 'ctx', [(i, i ^ flip) for i in range(count)])]
    convert_element_type x17 -> x14, other arithmetic: 20.5 us -> 18.1 us  [add(): self.parts = [x.astype(bf16) for x in self.parts]]
    unnamed x148 -> x132, local copies, waits for them, and re-layouts: 15.3 us -> 12.9 us
  transfers between devices with their start and end apart: 80 -> 77, of which waited for: 32 -> 32; matrix products, arithmetic and copies ran while one was open for 18% -> 16% of each run, Pallas kernels for 11% -> 14%
where the time goes in v5:
time: 570 us; the launch traced here: 567 us
  waiting for transfers between devices  235 us (41%)
  Pallas kernels  105 us (18%)
  starting transfers between devices  104 us (18%)
  other arithmetic  53.4 us (9%)
  local copies, waits for them, and re-layouts  47 us (8%)
  between operations  15.6 us (3%)
  matrix products  7.55 us (1%)
    ppermute x51, waiting for transfers between devices, chip_swap(): return lax.ppermute(x, 'ctx', [(i, i ^ flip) for i in range(count)])  178 us
    ppermute x51, starting transfers between devices, chip_swap(): return lax.ppermute(x, 'ctx', [(i, i ^ flip) for i in range(count)])  68.8 us
    all_to_all x4, waiting for transfers between devices, group_exchange(): lax.all_to_all(x, 'ctx', split_axis=0, concat_axis=0, tiled=True, axis_in...  33 us
    pallas_call x2, Pallas kernels, gate_up_grads(): pl.pallas_call(functools.partial(gate_up_grads_kernel, rows_dev), grid=(w...  29 us
    pallas_call x1, Pallas kernels, mlp(): pl.pallas_call(functools.partial(mlp_kernel, loads, groups), grid=(rows /...  27.8 us
    all_to_all x4, starting transfers between devices, group_exchange(): lax.all_to_all(x, 'ctx', split_axis=0, concat_axis=0, tiled=True, axis_in...  20.3 us
    convert_element_type x14, other arithmetic, add(): self.parts = [x.astype(bf16) for x in self.parts]  18.1 us
    unnamed x132, local copies, waits for them, and re-layouts  12.9 us
  transfers between devices with their start and end apart: 77, of which 32 were waited for; matrix products, arithmetic and copies ran while one was open for 16% of the time, Pallas kernels for 14%

profile of v5, /device:TPU:0, one launch (start us, length us, event | category | flops | bytes accessed | tf_op | source)
XLA Modules:
  0.0 567.5 jit_solution(14492395669850866216)
XLA Ops:
  7.2 3.0 collective-permute-start.5
  18.5 3.1 pack_members.1
  21.6 9.8 %collective-permute-done.4 = bf16[1,2,64,1024]{3,2,1,0:T(8,128)(2,1)S(1)} collective-permute-done((bf16[1,2,64,1024]{3,2,1,0:T(8,128)(2,1)S(1)}, bf16[1,2,64,1024]{3,2,1,0:T(8,128)(2,1)S(1)}, u32[]{:S(2)}, u32[]{:S(2)}) %collective-permute-start.4) | collective-permute-done | bytes 262176 | tf_op jit(solution)/shard_map/ppermute | solution.py:42
  40.5 9.0 %collective-permute-done.12 = bf16[2,2,64,256]{3,2,1,0:T(8,128)(2,1)S(1)} collective-permute-done((bf16[2,2,64,256]{3,2,1,0:T(8,128)(2,1)S(1)}, bf16[2,2,64,256]{3,2,1,0:T(8,128)(2,1)S(1)}, u32[]{:S(2)}, u32[]{:S(2)}) %collective-permute-start.12) | collective-permute-done | bytes 131104 | tf_op jit(solution)/shard_map/ppermute | solution.py:42
  54.5 4.3 collective-permute-done.13
  61.8 18.0 %collective-permute-done.14.refs_5_ = bf16[8,2,64,256]{3,2,1,0:T(8,128)(2,1)} collective-permute-done((bf16[8,2,64,256]{3,2,1,0:T(8,128)(2,1)}, bf16[8,2,64,256]{3,2,1,0:T(8,128)(2,1)}, u32[]{:S(2)}, u32[]{:S(2)}) %collective-permute-start.14) | collective-permute-done | bytes 524320 | tf_op jit(solution)/shard_map/ppermute | solution.py:42
  80.7 7.2 %all-to-all-start = ((bf16[8,16,2304]{2,1,0:T(8,128)(2,1)}), bf16[8,16,2304]{2,1,0:T(8,128)(2,1)}, u32[]{:S(2)}, u32[]{:S(2)}) async-start(bf16[8,16,2304]{2,1,0:T(8,128)(2,1)} %slice.151), calls=%async_computation | async-start | bytes 1179648 | tf_op jit(solution)/shard_map/all_to_all | solution.py:71
  90.4 4.8 order_project.1
  95.2 3.0 collective-permute-start.15
  98.2 3.2 collective-permute-done.15
  102.3 3.5 collective-permute-start.19
  121.4 3.3 order_rows.1
  127.2 4.8 all-to-all-start.1
  135.4 10.2 %attend.1 = (bf16[2,2048,256]{2,1,0:T(8,128)(2,1)}, f32[2,2,384,128]{3,2,1,0:T(8,128)}, bf16[2,128,768]{2,1,0:T(8,128)(2,1)}, f32[2,2,384,1]{3,2,1,0:T(8,128)}, f32[2,128,1536]{2,1,0:T(8,128)}) custom-call(s32[2]{0:T(128)} %pad_add_fusion.2.where_ref, s32[8]{0:T(128)} %reshape.389.range_ref, bf16[2,6,128,128]{3,2,1,0:T(8,128)(2,1)} %get-tuple-element.131.queries, ...), custom_call_target="tpu_custom_call" | custom-call | tf_op jit(solution)/shard_map/attend/pallas_call | solution.py:639
  149.1 23.1 %all-to-all-done.1 = bf16[8,32,2304]{2,1,0:T(8,128)(2,1)} async-done(((bf16[8,32,2304]{2,1,0:T(8,128)(2,1)}), bf16[8,32,2304]{2,1,0:T(8,128)(2,1)}, u32[]{:S(2)}, u32[]{:S(2)}) %all-to-all-start.1) | async-done | bytes 1179680 | tf_op jit(solution)/shard_map/all_to_all | solution.py:71
  176.1 33.5 %collective-permute-done.28 = bf16[1,128,1536]{2,1,0:T(8,128)(2,1)S(1)} collective-permute-done((bf16[1,128,1536]{2,1,0:T(8,128)(2,1)S(1)}, bf16[1,128,1536]{2,1,0:T(8,128)(2,1)S(1)}, u32[]{:S(2)}, u32[]{:S(2)}) %collective-permute-start.28) | collective-permute-done | bytes 393248 | tf_op jit(solution)/shard_map/ppermute | solution.py:42
  209.8 4.4 collective-permute-start.31
  216.2 3.8 collective-permute-done.31
  223.0 4.3 collective-permute-start.32
  227.3 10.3 %collective-permute-done.34.refs_4_ = bf16[4,48,2304]{2,1,0:T(8,128)(2,1)} collective-permute-done((bf16[4,48,2304]{2,1,0:T(8,128)(2,1)}, bf16[4,48,2304]{2,1,0:T(8,128)(2,1)}, u32[]{:S(2)}, u32[]{:S(2)}) %collective-permute-start.34) | collective-permute-done | bytes 884768 | tf_op jit(solution)/shard_map/ppermute | solution.py:42
  237.6 7.4 %collective-permute-done.32.refs_1_ = bf16[4,64,1536]{2,1,0:T(8,128)(2,1)S(1)} collective-permute-done((bf16[4,64,1536]{2,1,0:T(8,128)(2,1)}, bf16[4,64,1536]{2,1,0:T(8,128)(2,1)S(1)}, u32[]{:S(2)}, u32[]{:S(2)}) %collective-permute-start.32) | collective-permute-done | bytes 786464 | tf_op jit(solution)/shard_map/ppermute | solution.py:42
  247.1 3.7 order_tokens.1
  250.9 27.8 %mlp.1 = (bf16[1024,2304]{1,0:T(8,128)(2,1)}, bf16[1024,1120]{1,0:T(8,128)(2,1)}, bf16[1024,1536]{1,0:T(8,128)(2,1)}) custom-call(s32[2]{0:T(128)} %pad_add_fusion.2.where_ref, bf16[1024,1536]{1,0:T(8,128)(2,1)} %bitcast.285, bf16[1024,1536]{1,0:T(8,128)(2,1)} %all-gather.4.cloned.1.call-done.out_grad, bf16[1120,1536]{1,0:T(8,128)(2,1)} %bitcast.288, ...), custom_call_target="tpu_custom_call" | custom-call | tf_op jit(solution)/shard_map/mlp/pallas_call | solution.py:371
  284.2 8.2 %gate_up_grads.2 = (bf16[16,48,1152]{2,1,0:T(8,128)(2,1)}, bf16[16,48,1152]{2,1,0:T(8,128)(2,1)}) custom-call(s32[2]{0:T(128)} %pad_add_fusion.2.where_ref, bf16[1024,1536]{1,0:T(8,128)(2,1)} %bitcast.286, bf16[1024,2304]{1,0:T(8,128)(2,1)} %get-tuple-element.181.pre_grad), custom_call_target="tpu_custom_call" | custom-call | tf_op jit(solution)/shard_map/gate_up_grads/pallas_call | solution.py:408
  292.7 4.4 convolution_convert_fusion
  297.2 6.0 %collective-permute-done.39 = bf16[2,2,64,1536]{3,2,0,1:T(8,128)(2,1)} collective-permute-done((bf16[2,2,64,1536]{3,2,0,1:T(8,128)(2,1)}, bf16[2,2,64,1536]{3,2,0,1:T(8,128)(2,1)}, u32[]{:S(2)}, u32[]{:S(2)}) %collective-permute-start.39) | collective-permute-done | bytes 786464 | tf_op jit(solution)/shard_map/ppermute | solution.py:42
  313.9 4.1 collective-permute-done.42
  319.7 2.9 collective-permute-start.43
  322.7 20.8 %gate_up_grads.3 = (bf16[16,48,1152]{2,1,0:T(8,128)(2,1)}, bf16[16,48,1152]{2,1,0:T(8,128)(2,1)}) custom-call(s32[2]{0:T(128)} %pad_add_fusion.2.where_ref, bf16[1024,1536]{1,0:T(8,128)(2,1)} %bitcast.287, bf16[1024,2304]{1,0:T(8,128)(2,1)} %get-tuple-element.181.pre_grad), custom_call_target="tpu_custom_call" | custom-call | tf_op jit(solution)/shard_map/gate_up_grads/pallas_call | solution.py:408
  343.7 17.8 %collective-permute-done.45 = bf16[8,1,48,1152]{3,2,0,1:T(8,128)(2,1)S(1)} collective-permute-done((bf16[8,1,48,1152]{3,2,0,1:T(8,128)(2,1)S(1)}, bf16[8,1,48,1152]{3,2,0,1:T(8,128)(2,1)S(1)}, u32[]{:S(2)}, u32[]{:S(2)}) %collective-permute-start.45) | collective-permute-done | bytes 884768 | tf_op jit(solution)/shard_map/ppermute | solution.py:42
  364.8 3.6 all-to-all-start.2
  371.7 11.6 %attend_back.1 = (bf16[2,128,768]{2,1,0:T(8,128)(2,1)}, bf16[8,2,2,128,256]{4,3,2,1,0:T(8,128)(2,1)}) custom-call(s32[8]{0:T(128)} %reshape.389.range_ref, bf16[128,1536]{1,0:T(8,128)(2,1)} %copy-done.8, bf16[128,1536]{1,0:T(8,128)(2,1)} %copy-done.26, bf16[1536,768]{1,0:T(8,128)(2,1)} %bitcast.294, bf16[2,6,128,128]{3,2,1,0:T(8,128)(2,1)} %get-tuple-element.131.queries, ...), custom_call_target="tpu_custom_call" | custom-call | tf_op jit(solution)/shard_map/attend_back/pallas_call | solution.py:736
  383.2 10.0 %collective-permute-done.50 = bf16[8,1,48,1152]{3,2,0,1:T(8,128)(2,1)S(1)} collective-permute-done((bf16[8,1,48,1152]{3,2,0,1:T(8,128)(2,1)S(1)}, bf16[8,1,48,1152]{3,2,0,1:T(8,128)(2,1)S(1)}, u32[]{:S(2)}, u32[]{:S(2)}) %collective-permute-start.50) | collective-permute-done | bytes 884768 | tf_op jit(solution)/shard_map/ppermute | solution.py:42
  395.3 4.3 all-to-all-start.3
  408.8 7.5 %down_grads.1 = (bf16[2,280,1536]{2,1,0:T(8,128)(2,1)}, bf16[2,280,1536]{2,1,0:T(8,128)(2,1)}) custom-call(s32[2]{0:T(128)} %pad_add_fusion.2.where_ref, bf16[1024,1120]{1,0:T(8,128)(2,1)} %get-tuple-element.198.activated, bf16[1024,1536]{1,0:T(8,128)(2,1)} %all-gather.4.cloned.1.call-done.out_grad), custom_call_target="tpu_custom_call" | custom-call | tf_op jit(solution)/shard_map/down_grads/pallas_call | solution.py:439
  416.3 10.5 %all-to-all-done.3 = bf16[8,2,2,128,256]{4,3,2,1,0:T(8,128)(2,1)} async-done(((bf16[8,2,2,128,256]{4,3,2,1,0:T(8,128)(2,1)}), bf16[8,2,2,128,256]{4,3,2,1,0:T(8,128)(2,1)}, u32[]{:S(2)}, u32[]{:S(2)}) %all-to-all-start.3) | async-done | bytes 2097184 | tf_op jit(solution)/shard_map/all_to_all | solution.py:51
  438.5 12.8 %collective-permute-done.53 = bf16[2,2,2,2,48,768]{5,4,3,0,1,2:T(8,128)(2,1)} collective-permute-done((bf16[2,2,2,2,48,768]{5,4,3,0,1,2:T(8,128)(2,1)}, bf16[2,2,2,2,48,768]{5,4,3,0,1,2:T(8,128)(2,1)}, u32[]{:S(2)}, u32[]{:S(2)}) %collective-permute-start.53) | collective-permute-done | bytes 1179680 | tf_op jit(solution)/shard_map/ppermute | solution.py:42
  457.8 4.7 all-to-all-start.4
  462.5 2.9 fusion.1
  475.6 9.9 %all-to-all-done.4.packed_up = bf16[8,48,1152]{2,1,0:T(8,128)(2,1)} async-done(((bf16[8,48,1152]{2,1,0:T(8,128)(2,1)}), bf16[8,48,1152]{2,1,0:T(8,128)(2,1)}, u32[]{:S(2)}, u32[]{:S(2)}) %all-to-all-start.4) | async-done | bytes 884768 | tf_op jit(solution)/shard_map/all_to_all | solution.py:71
  495.6 4.2 all-to-all-start.5
  503.6 3.7 unpack_members.1
  508.1 7.5 %collective-permute-done.58 = bf16[2,2,2,48,768]{4,3,2,1,0:T(8,128)(2,1)} collective-permute-done((bf16[2,2,2,48,768]{4,3,2,1,0:T(8,128)(2,1)}, bf16[2,2,2,48,768]{4,3,2,1,0:T(8,128)(2,1)}, u32[]{:S(2)}, u32[]{:S(2)}) %collective-permute-start.58) | collective-permute-done | bytes 589856 | tf_op jit(solution)/shard_map/ppermute | solution.py:42
  520.5 7.1 %collective-permute-done.59 = bf16[2,2,48,768]{3,2,1,0:T(8,128)(2,1)S(1)} collective-permute-done((bf16[2,2,48,768]{3,2,1,0:T(8,128)(2,1)S(1)}, bf16[2,2,48,768]{3,2,1,0:T(8,128)(2,1)S(1)}, u32[]{:S(2)}, u32[]{:S(2)}) %collective-permute-start.59) | collective-permute-done | bytes 294944 | tf_op jit(solution)/shard_map/ppermute | solution.py:42
  536.2 2.9 collective-permute-start.64
  539.1 3.6 all-to-all-start.6
  543.6 9.4 %all-to-all-done.6 = f32[16,1,320]{2,1,0:T(1,128)S(1)} async-done(((f32[16,1,320]{2,1,0:T(1,128)}), f32[16,1,320]{2,1,0:T(1,128)S(1)}, u32[]{:S(2)}, u32[]{:S(2)}) %all-to-all-start.6) | async-done | bytes 20512 | tf_op jit(solution)/shard_map/all_to_all | solution.py:1043
  557.7 2.7 add_bitcast_fusion
  (415 shorter events, 163.3 us)
Async XLA Ops:
  7.2 124.9 %all-gather.6.cloned.1.call-start = ((), (), s32[]{:S(2)}) async-start(), calls=%async_computation.8 | async-start | bytes 2506752 | tf_op jit(solution)/shard_map/all_gather | solution.py:803
  7.2 24.1 %collective-permute-start.5 = (bf16[280,1536]{1,0:T(8,128)(2,1)}, bf16[280,1536]{1,0:T(8,128)(2,1)}, u32[]{:S(2)}, u32[]{:S(2)}) collective-permute-start(bf16[280,1536]{1,0:T(8,128)(2,1)} %param.21), channel_id=1, source_target_pairs={{0,2},{2,0},{4,6},{6,4},{8,10},{10,8},{12,14},{14,12},{16,18},{18,... | collective-permute-start | bytes 2580488 | tf_op jit(solution)/shard_map/ppermute | solution.py:42
  15.2 16.2 %collective-permute-start.4 = (bf16[1,2,64,1024]{3,2,1,0:T(8,128)(2,1)S(1)}, bf16[1,2,64,1024]{3,2,1,0:T(8,128)(2,1)S(1)}, u32[]{:S(2)}, u32[]{:S(2)}) collective-permute-start(bf16[1,2,64,1024]{3,2,1,0:T(8,128)(2,1)S(1)} %maximum_bitcast_fusion), channel_id=1, source_target_pairs={{0,16},{2,18},{4,20},{6,22},{8,24},{10,26},{12,28},{14,30},{16,0},... | collective-permute-start | bytes 786440 | tf_op jit(solution)/shard_map/ppermute | solution.py:42
  36.7 12.9 %collective-permute-start.10 = (bf16[4,2,48,384]{3,2,1,0:T(8,128)(2,1)S(1)}, bf16[4,2,48,384]{3,2,1,0:T(8,128)(2,1)S(1)}, u32[]{:S(2)}, u32[]{:S(2)}) collective-permute-start(bf16[4,2,48,384]{3,2,1,0:T(8,128)(2,1)S(1)} %pad_maximum_fusion.14), channel_id=1, source_target_pairs={{0,8},{2,10},{4,12},{6,14},{8,0},{10,2},{12,4},{14,6},{16,24},{18,... | collective-permute-start | bytes 884744 | tf_op jit(solution)/shard_map/ppermute | solution.py:42
  38.9 12.9 %collective-permute-start.7 = (bf16[4,2,48,384]{3,2,1,0:T(8,128)(2,1)S(1)}, bf16[4,2,48,384]{3,2,1,0:T(8,128)(2,1)S(1)}, u32[]{:S(2)}, u32[]{:S(2)}) collective-permute-start(bf16[4,2,48,384]{3,2,1,0:T(8,128)(2,1)S(1)} %pad_maximum_fusion.13), channel_id=1, source_target_pairs={{0,4},{2,6},{4,0},{6,2},{8,12},{10,14},{12,8},{14,10},{16,20},{18,... | collective-permute-start | bytes 884744 | tf_op jit(solution)/shard_map/ppermute | solution.py:42
  49.7 30.1 %collective-permute-start.11 = (bf16[8,2,48,384]{3,2,1,0:T(8,128)(2,1)S(1)}, bf16[8,2,48,384]{3,2,1,0:T(8,128)(2,1)}, u32[]{:S(2)}, u32[]{:S(2)}) collective-permute-start(bf16[8,2,48,384]{3,2,1,0:T(8,128)(2,1)S(1)} %pad_maximum_fusion.5.refs_2_), channel_id=1, source_target_pairs={{0,2},{2,0},{4,6},{6,4},{8,10},{10,8},{12,14},{14,12},{16,18},{18,... | collective-permute-start | bytes 1769480 | tf_op jit(solution)/shard_map/ppermute | solution.py:42
  52.7 27.2 %collective-permute-start.8 = (bf16[8,2,48,384]{3,2,1,0:T(8,128)(2,1)}, bf16[8,2,48,384]{3,2,1,0:T(8,128)(2,1)}, u32[]{:S(2)}, u32[]{:S(2)}) collective-permute-start(bf16[8,2,48,384]{3,2,1,0:T(8,128)(2,1)} %pad_maximum_fusion.4.refs_0_), channel_id=1, source_target_pairs={{0,8},{2,10},{4,12},{6,14},{8,0},{10,2},{12,4},{14,6},{16,24},{18,... | collective-permute-start | bytes 1769480 | tf_op jit(solution)/shard_map/ppermute | solution.py:42
  59.7 20.2 %collective-permute-start.14 = (bf16[8,2,64,256]{3,2,1,0:T(8,128)(2,1)}, bf16[8,2,64,256]{3,2,1,0:T(8,128)(2,1)}, u32[]{:S(2)}, u32[]{:S(2)}) collective-permute-start(bf16[8,2,64,256]{3,2,1,0:T(8,128)(2,1)} %pad_maximum_fusion.8.refs_4_), channel_id=1, source_target_pairs={{0,4},{2,6},{4,0},{6,2},{8,12},{10,14},{12,8},{14,10},{16,20},{18,... | collective-permute-start | bytes 1572872 | tf_op jit(solution)/shard_map/ppermute | solution.py:42
  60.7 27.3 %collective-permute-start = (s32[4]{0:T(128)S(1)}, s32[4]{0:T(128)S(1)}, u32[]{:S(2)}, u32[]{:S(2)}) collective-permute-start(s32[4]{0:T(128)S(1)} %bitcast.326), channel_id=1, source_target_pairs={{0,1},{1,0},{2,3},{3,2},{4,5},{5,4},{6,7},{7,6},{8,9},{9,8},{10,11... | collective-permute-start | bytes 56 | tf_op jit(solution)/shard_map/ppermute | solution.py:37
  60.7 28.9 %collective-permute-start.1 = (bf16[128,1536]{1,0:T(8,128)(2,1)S(1)}, bf16[128,1536]{1,0:T(8,128)(2,1)S(1)}, u32[]{:S(2)}, u32[]{:S(2)}) collective-permute-start(bf16[128,1536]{1,0:T(8,128)(2,1)S(1)} %bitcast.300), channel_id=1, source_target_pairs={{0,1},{1,0},{2,3},{3,2},{4,5},{5,4},{6,7},{7,6},{8,9},{9,8},{10,11... | collective-permute-start | bytes 1179656 | tf_op jit(solution)/shard_map/ppermute | solution.py:37
  80.7 21.6 %all-to-all-start = ((bf16[8,16,2304]{2,1,0:T(8,128)(2,1)}), bf16[8,16,2304]{2,1,0:T(8,128)(2,1)}, u32[]{:S(2)}, u32[]{:S(2)}) async-start(bf16[8,16,2304]{2,1,0:T(8,128)(2,1)} %slice.151), calls=%async_computation | async-start | bytes 1179648 | tf_op jit(solution)/shard_map/all_to_all | solution.py:71
  105.8 14.4 %collective-permute-start.25 = (bf16[280,1536]{1,0:T(8,128)(2,1)}, bf16[280,1536]{1,0:T(8,128)(2,1)S(1)}, u32[]{:S(2)}, u32[]{:S(2)}) collective-permute-start(bf16[280,1536]{1,0:T(8,128)(2,1)} %param.21), channel_id=1, source_target_pairs={{0,1},{1,0},{2,3},{3,2},{4,5},{5,4},{6,7},{7,6},{8,9},{9,8},{10,11... | collective-permute-start | bytes 2580488 | tf_op jit(solution)/shard_map/ppermute | solution.py:37
  105.8 14.4 %collective-permute-start.26 = (bf16[280,1536]{1,0:T(8,128)(2,1)}, bf16[280,1536]{1,0:T(8,128)(2,1)S(1)}, u32[]{:S(2)}, u32[]{:S(2)}) collective-permute-start(bf16[280,1536]{1,0:T(8,128)(2,1)} %collective-permute-done.5), channel_id=1, source_target_pairs={{0,1},{1,0},{2,3},{3,2},{4,5},{5,4},{6,7},{7,6},{8,9},{9,8},{10,11... | collective-permute-start | bytes 2580488 | tf_op jit(solution)/shard_map/ppermute | solution.py:37
  127.2 45.0 %all-to-all-start.1 = ((bf16[8,32,2304]{2,1,0:T(8,128)(2,1)}), bf16[8,32,2304]{2,1,0:T(8,128)(2,1)}, u32[]{:S(2)}, u32[]{:S(2)}) async-start(bf16[8,32,2304]{2,1,0:T(8,128)(2,1)} %slice.155), calls=%async_computation.1 | async-start | bytes 2359296 | tf_op jit(solution)/shard_map/all_to_all | solution.py:71
  132.1 91.0 %all-gather.4.cloned.1.call-start = ((), (), s32[]{:S(2)}) async-start(), calls=%async_computation.7 | async-start | bytes 3538944 | tf_op jit(solution)/shard_map/all_gather | solution.py:804
  175.2 34.6 %collective-permute-start.29 = (bf16[4,48,2304]{2,1,0:T(8,128)(2,1)S(1)}, bf16[4,48,2304]{2,1,0:T(8,128)(2,1)S(1)}, u32[]{:S(2)}, u32[]{:S(2)}) collective-permute-start(bf16[4,48,2304]{2,1,0:T(8,128)(2,1)S(1)} %slice.189), channel_id=1, source_target_pairs={{0,2},{2,0},{4,6},{6,4},{8,10},{10,8},{12,14},{14,12},{16,18},{18,... | collective-permute-start | bytes 2654216 | tf_op jit(solution)/shard_map/ppermute | solution.py:42
  176.0 33.6 %collective-permute-start.28 = (bf16[1,128,1536]{2,1,0:T(8,128)(2,1)S(1)}, bf16[1,128,1536]{2,1,0:T(8,128)(2,1)S(1)}, u32[]{:S(2)}, u32[]{:S(2)}) collective-permute-start(bf16[1,128,1536]{2,1,0:T(8,128)(2,1)S(1)} %fusion.30), channel_id=1, source_target_pairs={{0,16},{2,18},{4,20},{6,22},{8,24},{10,26},{12,28},{14,30},{16,0},... | collective-permute-start | bytes 1179656 | tf_op jit(solution)/shard_map/ppermute | solution.py:42
  214.2 36.7 %collective-permute-start.35 = (bf16[8,48,2304]{2,1,0:T(8,128)(2,1)S(1)}, bf16[8,48,2304]{2,1,0:T(8,128)(2,1)}, u32[]{:S(2)}, u32[]{:S(2)}) collective-permute-start(bf16[8,48,2304]{2,1,0:T(8,128)(2,1)S(1)} %constant_dynamic-update-slice_fusion.refs_0_), channel_id=1, source_target_pairs={{0,1},{1,0},{2,3},{3,2},{4,5},{5,4},{6,7},{7,6},{8,9},{9,8},{10,11... | collective-permute-start | bytes 5308424 | tf_op jit(solution)/shard_map/ppermute | solution.py:37
  215.2 22.4 %collective-permute-start.34 = (bf16[4,48,2304]{2,1,0:T(8,128)(2,1)}, bf16[4,48,2304]{2,1,0:T(8,128)(2,1)}, u32[]{:S(2)}, u32[]{:S(2)}) collective-permute-start(bf16[4,48,2304]{2,1,0:T(8,128)(2,1)} %slice.162), channel_id=1, source_target_pairs={{0,2},{2,0},{4,6},{6,4},{8,10},{10,8},{12,14},{14,12},{16,18},{18,... | collective-permute-start | bytes 2654216 | tf_op jit(solution)/shard_map/ppermute | solution.py:42
  223.0 22.0 %collective-permute-start.32 = (bf16[4,64,1536]{2,1,0:T(8,128)(2,1)}, bf16[4,64,1536]{2,1,0:T(8,128)(2,1)S(1)}, u32[]{:S(2)}, u32[]{:S(2)}) collective-permute-start(bf16[4,64,1536]{2,1,0:T(8,128)(2,1)} %pad_maximum_fusion.1.refs_0_), channel_id=1, source_target_pairs={{0,4},{2,6},{4,0},{6,2},{8,12},{10,14},{12,8},{14,10},{16,20},{18,... | collective-permute-start | bytes 2359304 | tf_op jit(solution)/shard_map/ppermute | solution.py:42
  227.3 18.9 %collective-permute-start.33 = (bf16[4,64,1536]{2,1,0:T(8,128)(2,1)S(1)}, bf16[4,64,1536]{2,1,0:T(8,128)(2,1)S(1)}, u32[]{:S(2)}, u32[]{:S(2)}) collective-permute-start(bf16[4,64,1536]{2,1,0:T(8,128)(2,1)S(1)} %pad_maximum_fusion.2.refs_2_), channel_id=1, source_target_pairs={{0,8},{2,10},{4,12},{6,14},{8,0},{10,2},{12,4},{14,6},{16,24},{18,... | collective-permute-start | bytes 2359304 | tf_op jit(solution)/shard_map/ppermute | solution.py:42
  282.9 20.3 %collective-permute-start.39 = (bf16[2,2,64,1536]{3,2,0,1:T(8,128)(2,1)}, bf16[2,2,64,1536]{3,2,0,1:T(8,128)(2,1)}, u32[]{:S(2)}, u32[]{:S(2)}) collective-permute-start(bf16[2,2,64,1536]{3,2,0,1:T(8,128)(2,1)} %bitcast.282), channel_id=1, source_target_pairs={{0,8},{2,10},{4,12},{6,14},{8,0},{10,2},{12,4},{14,6},{16,24},{18,... | collective-permute-start | bytes 2359304 | tf_op jit(solution)/shard_map/ppermute | solution.py:42
  283.1 21.3 %collective-permute-start.38 = (bf16[2,2,64,1536]{3,2,0,1:T(8,128)(2,1)}, bf16[2,2,64,1536]{3,2,0,1:T(8,128)(2,1)}, u32[]{:S(2)}, u32[]{:S(2)}) collective-permute-start(bf16[2,2,64,1536]{3,2,0,1:T(8,128)(2,1)} %bitcast.283), channel_id=1, source_target_pairs={{0,4},{2,6},{4,0},{6,2},{8,12},{10,14},{12,8},{14,10},{16,20},{18,... | collective-permute-start | bytes 2359304 | tf_op jit(solution)/shard_map/ppermute | solution.py:42
  292.5 13.3 %collective-permute-start.40 = (bf16[16,48,1152]{2,1,0:T(8,128)(2,1)}, bf16[16,48,1152]{2,1,0:T(8,128)(2,1)S(1)}, u32[]{:S(2)}, u32[]{:S(2)}) collective-permute-start(bf16[16,48,1152]{2,1,0:T(8,128)(2,1)} %get-tuple-element.170), channel_id=1, source_target_pairs={{0,1},{1,0},{2,3},{3,2},{4,5},{5,4},{6,7},{7,6},{8,9},{9,8},{10,11... | collective-permute-start | bytes 5308424 | tf_op jit(solution)/shard_map/ppermute | solution.py:37
  307.3 12.1 %collective-permute-start.41 = (bf16[2,64,1536]{2,1,0:T(8,128)(2,1)S(1)}, bf16[2,64,1536]{2,1,0:T(8,128)(2,1)S(1)}, u32[]{:S(2)}, u32[]{:S(2)}) collective-permute-start(bf16[2,64,1536]{2,1,0:T(8,128)(2,1)S(1)} %dynamic-slice_bitcast_fusion.8), channel_id=1, source_target_pairs={{0,8},{2,10},{4,12},{6,14},{8,0},{10,2},{12,4},{14,6},{16,24},{18,... | collective-permute-start | bytes 1179656 | tf_op jit(solution)/shard_map/ppermute | solution.py:42
  309.1 59.3 %collective-permute-start.48 = (bf16[2,2,64,1536]{3,2,0,1:T(8,128)(2,1)S(1)}, bf16[2,2,64,1536]{3,2,0,1:T(8,128)(2,1)}, u32[]{:S(2)}, u32[]{:S(2)}) collective-permute-start(bf16[2,2,64,1536]{3,2,0,1:T(8,128)(2,1)S(1)} %bitcast.310), channel_id=1, source_target_pairs={{0,4},{2,6},{4,0},{6,2},{8,12},{10,14},{12,8},{14,10},{16,20},{18,... | collective-permute-start | bytes 2359304 | tf_op jit(solution)/shard_map/ppermute | solution.py:42
  311.8 56.6 %collective-permute-start.49 = (bf16[2,2,64,1536]{3,2,0,1:T(8,128)(2,1)}, bf16[2,2,64,1536]{3,2,0,1:T(8,128)(2,1)}, u32[]{:S(2)}, u32[]{:S(2)}) collective-permute-start(bf16[2,2,64,1536]{3,2,0,1:T(8,128)(2,1)} %bitcast.280), channel_id=1, source_target_pairs={{0,8},{2,10},{4,12},{6,14},{8,0},{10,2},{12,4},{14,6},{16,24},{18,... | collective-permute-start | bytes 2359304 | tf_op jit(solution)/shard_map/ppermute | solution.py:42
  319.6 23.9 %collective-permute-start.44 = (bf16[64,1536]{1,0:T(8,128)(2,1)S(1)}, bf16[64,1536]{1,0:T(8,128)(2,1)S(1)}, u32[]{:S(2)}, u32[]{:S(2)}) collective-permute-start(bf16[64,1536]{1,0:T(8,128)(2,1)S(1)} %dynamic-slice_bitcast_fusion.13), channel_id=1, source_target_pairs={{0,16},{2,18},{4,20},{6,22},{8,24},{10,26},{12,28},{14,30},{16,0},... | collective-permute-start | bytes 589832 | tf_op jit(solution)/shard_map/ppermute | solution.py:42
  319.7 23.9 %collective-permute-start.43 = (bf16[64,1536]{1,0:T(8,128)(2,1)S(1)}, bf16[64,1536]{1,0:T(8,128)(2,1)S(1)}, u32[]{:S(2)}, u32[]{:S(2)}) collective-permute-start(bf16[64,1536]{1,0:T(8,128)(2,1)S(1)} %dynamic-slice_bitcast_fusion.14), channel_id=1, source_target_pairs={{0,16},{2,18},{4,20},{6,22},{8,24},{10,26},{12,28},{14,30},{16,0},... | collective-permute-start | bytes 589832 | tf_op jit(solution)/shard_map/ppermute | solution.py:42
  343.5 18.0 %collective-permute-start.45 = (bf16[8,1,48,1152]{3,2,0,1:T(8,128)(2,1)S(1)}, bf16[8,1,48,1152]{3,2,0,1:T(8,128)(2,1)S(1)}, u32[]{:S(2)}, u32[]{:S(2)}) collective-permute-start(bf16[8,1,48,1152]{3,2,0,1:T(8,128)(2,1)S(1)} %constant_dynamic-slice_fusion.13), channel_id=1, source_target_pairs={{0,2},{2,0},{4,6},{6,4},{8,10},{10,8},{12,14},{14,12},{16,18},{18,... | collective-permute-start | bytes 2654216 | tf_op jit(solution)/shard_map/ppermute | solution.py:42
  364.8 29.5 %all-to-all-start.2 = ((bf16[8,48,1152]{2,1,0:T(8,128)(2,1)}), bf16[8,48,1152]{2,1,0:T(8,128)(2,1)S(1)}, u32[]{:S(2)}, u32[]{:S(2)}) async-start(bf16[8,48,1152]{2,1,0:T(8,128)(2,1)} %fusion.10), calls=%async_computation.2 | async-start | bytes 1769472 | tf_op jit(solution)/shard_map/all_to_all | solution.py:71
  371.1 22.1 %collective-permute-start.50 = (bf16[8,1,48,1152]{3,2,0,1:T(8,128)(2,1)S(1)}, bf16[8,1,48,1152]{3,2,0,1:T(8,128)(2,1)S(1)}, u32[]{:S(2)}, u32[]{:S(2)}) collective-permute-start(bf16[8,1,48,1152]{3,2,0,1:T(8,128)(2,1)S(1)} %dynamic-slice_bitcast_fusion.1), channel_id=1, source_target_pairs={{0,2},{2,0},{4,6},{6,4},{8,10},{10,8},{12,14},{14,12},{16,18},{18,... | collective-permute-start | bytes 2654216 | tf_op jit(solution)/shard_map/ppermute | solution.py:42
  395.3 31.4 %all-to-all-start.3 = ((bf16[8,2,2,128,256]{4,3,2,1,0:T(8,128)(2,1)}), bf16[8,2,2,128,256]{4,3,2,1,0:T(8,128)(2,1)}, u32[]{:S(2)}, u32[]{:S(2)}) async-start(bf16[8,2,2,128,256]{4,3,2,1,0:T(8,128)(2,1)} %get-tuple-element.197), calls=%async_computation.3 | async-start | bytes 4194304 | tf_op jit(solution)/shard_map/all_to_all | solution.py:51
  403.5 47.7 %collective-permute-start.53 = (bf16[2,2,2,2,48,768]{5,4,3,0,1,2:T(8,128)(2,1)}, bf16[2,2,2,2,48,768]{5,4,3,0,1,2:T(8,128)(2,1)}, u32[]{:S(2)}, u32[]{:S(2)}) collective-permute-start(bf16[2,2,2,2,48,768]{5,4,3,0,1,2:T(8,128)(2,1)} %bitcast.279), channel_id=1, source_target_pairs={{0,4},{2,6},{4,0},{6,2},{8,12},{10,14},{12,8},{14,10},{16,20},{18,... | collective-permute-start | bytes 3538952 | tf_op jit(solution)/shard_map/ppermute | solution.py:42
  407.3 43.9 %collective-permute-start.52 = (bf16[2,2,2,2,48,768]{5,4,3,2,1,0:T(8,128)(2,1)}, bf16[2,2,2,2,48,768]{5,4,3,2,1,0:T(8,128)(2,1)}, u32[]{:S(2)}, u32[]{:S(2)}) collective-permute-start(bf16[2,2,2,2,48,768]{5,4,3,2,1,0:T(8,128)(2,1)} %dynamic-slice_bitcast_fusion), channel_id=1, source_target_pairs={{0,2},{2,0},{4,6},{6,4},{8,10},{10,8},{12,14},{14,12},{16,18},{18,... | collective-permute-start | bytes 3538952 | tf_op jit(solution)/shard_map/ppermute | solution.py:42
  432.9 40.7 %collective-permute-start.56 = (bf16[2,280,1536]{2,1,0:T(8,128)(2,1)}, bf16[2,280,1536]{2,1,0:T(8,128)(2,1)}, u32[]{:S(2)}, u32[]{:S(2)}) collective-permute-start(bf16[2,280,1536]{2,1,0:T(8,128)(2,1)} %get-tuple-element.213), channel_id=1, source_target_pairs={{0,1},{1,0},{2,3},{3,2},{4,5},{5,4},{6,7},{7,6},{8,9},{9,8},{10,11... | collective-permute-start | bytes 5160968 | tf_op jit(solution)/shard_map/ppermute | solution.py:37
  435.3 33.1 %collective-permute-start.55 = (bf16[2,64,1536]{2,1,0:T(8,128)(2,1)}, bf16[2,64,1536]{2,1,0:T(8,128)(2,1)}, u32[]{:S(2)}, u32[]{:S(2)}) collective-permute-start(bf16[2,64,1536]{2,1,0:T(8,128)(2,1)} %dynamic-slice_bitcast_fusion.5), channel_id=1, source_target_pairs={{0,4},{2,6},{4,0},{6,2},{8,12},{10,14},{12,8},{14,10},{16,20},{18,... | collective-permute-start | bytes 1179656 | tf_op jit(solution)/shard_map/ppermute | solution.py:42
  438.1 32.3 %collective-permute-start.54 = (bf16[2,64,1536]{2,1,0:T(8,128)(2,1)}, bf16[2,64,1536]{2,1,0:T(8,128)(2,1)}, u32[]{:S(2)}, u32[]{:S(2)}) collective-permute-start(bf16[2,64,1536]{2,1,0:T(8,128)(2,1)} %dynamic-slice_bitcast_fusion.6), channel_id=1, source_target_pairs={{0,8},{2,10},{4,12},{6,14},{8,0},{10,2},{12,4},{14,6},{16,24},{18,... | collective-permute-start | bytes 1179656 | tf_op jit(solution)/shard_map/ppermute | solution.py:42
  456.9 15.5 %collective-permute-start.57 = (f32[128,1536]{1,0:T(8,128)}, f32[128,1536]{1,0:T(8,128)}, u32[]{:S(2)}, u32[]{:S(2)}) collective-permute-start(f32[128,1536]{1,0:T(8,128)} %slice.195), channel_id=1, source_target_pairs={{0,1},{1,0},{2,3},{3,2},{4,5},{5,4},{6,7},{7,6},{8,9},{9,8},{10,11... | collective-permute-start | bytes 2359304 | tf_op jit(solution)/shard_map/ppermute | solution.py:37
  457.8 27.7 %all-to-all-start.4 = ((bf16[8,48,1152]{2,1,0:T(8,128)(2,1)}), bf16[8,48,1152]{2,1,0:T(8,128)(2,1)}, u32[]{:S(2)}, u32[]{:S(2)}) async-start(bf16[8,48,1152]{2,1,0:T(8,128)(2,1)} %fusion.11), calls=%async_computation.4 | async-start | bytes 1769472 | tf_op jit(solution)/shard_map/all_to_all | solution.py:71
  489.4 30.0 %collective-permute-start.62 = (bf16[128,1536]{1,0:T(8,128)(2,1)}, bf16[128,1536]{1,0:T(8,128)(2,1)}, u32[]{:S(2)}, u32[]{:S(2)}) collective-permute-start(bf16[128,1536]{1,0:T(8,128)(2,1)} %dynamic-slice_bitcast_fusion.4), channel_id=1, source_target_pairs={{0,16},{2,18},{4,20},{6,22},{8,24},{10,26},{12,28},{14,30},{16,0},... | collective-permute-start | bytes 1179656 | tf_op jit(solution)/shard_map/ppermute | solution.py:42
  490.3 25.2 %collective-permute-start.58 = (bf16[2,2,2,48,768]{4,3,2,1,0:T(8,128)(2,1)}, bf16[2,2,2,48,768]{4,3,2,1,0:T(8,128)(2,1)}, u32[]{:S(2)}, u32[]{:S(2)}) collective-permute-start(bf16[2,2,2,48,768]{4,3,2,1,0:T(8,128)(2,1)} %dynamic-slice_bitcast_fusion.3), channel_id=1, source_target_pairs={{0,8},{2,10},{4,12},{6,14},{8,0},{10,2},{12,4},{14,6},{16,24},{18,... | collective-permute-start | bytes 1769480 | tf_op jit(solution)/shard_map/ppermute | solution.py:42
  493.6 24.5 %collective-permute-start.60 = (bf16[2,2,2,48,768]{4,3,2,0,1:T(8,128)(2,1)}, bf16[2,2,2,48,768]{4,3,2,0,1:T(8,128)(2,1)}, u32[]{:S(2)}, u32[]{:S(2)}) collective-permute-start(bf16[2,2,2,48,768]{4,3,2,0,1:T(8,128)(2,1)} %dynamic-slice_bitcast_fusion.2), channel_id=1, source_target_pairs={{0,2},{2,0},{4,6},{6,4},{8,10},{10,8},{12,14},{14,12},{16,18},{18,... | collective-permute-start | bytes 1769480 | tf_op jit(solution)/shard_map/ppermute | solution.py:42
  495.6 34.6 %all-to-all-start.5 = ((bf16[8,2,2,48,256]{4,3,2,1,0:T(8,128)(2,1)}), bf16[8,2,2,48,256]{4,3,2,1,0:T(8,128)(2,1)}, u32[]{:S(2)}, u32[]{:S(2)}) async-start(bf16[8,2,2,48,256]{4,3,2,1,0:T(8,128)(2,1)} %bitcast.303), calls=%async_computation.5 | async-start | bytes 1572864 | tf_op jit(solution)/shard_map/all_to_all | solution.py:51
  531.1 26.5 %collective-permute-start.67 = (bf16[1,280,1536]{2,1,0:T(8,128)(2,1)}, bf16[1,280,1536]{2,1,0:T(8,128)(2,1)}, u32[]{:S(2)}, u32[]{:S(2)}) collective-permute-start(bf16[1,280,1536]{2,1,0:T(8,128)(2,1)} %constant_dynamic-slice_fusion), channel_id=1, source_target_pairs={{0,2},{2,0},{4,6},{6,4},{8,10},{10,8},{12,14},{14,12},{16,18},{18,... | collective-permute-start | bytes 2580488 | tf_op jit(solution)/shard_map/ppermute | solution.py:42
  534.4 18.7 %collective-permute-start.65 = (bf16[1,2,48,256]{3,2,1,0:T(8,128)(2,1)S(1)}, bf16[1,2,48,256]{3,2,1,0:T(8,128)(2,1)S(1)}, u32[]{:S(2)}, u32[]{:S(2)}) collective-permute-start(bf16[1,2,48,256]{3,2,1,0:T(8,128)(2,1)S(1)} %constant_dynamic-slice_fusion.4), channel_id=1, source_target_pairs={{0,16},{2,18},{4,20},{6,22},{8,24},{10,26},{12,28},{14,30},{16,0},... | collective-permute-start | bytes 147464 | tf_op jit(solution)/shard_map/ppermute | solution.py:42
  536.2 16.9 %collective-permute-start.64 = (bf16[2,48,1536]{2,1,0:T(8,128)(2,1)}, bf16[2,48,1536]{2,1,0:T(8,128)(2,1)}, u32[]{:S(2)}, u32[]{:S(2)}) collective-permute-start(bf16[2,48,1536]{2,1,0:T(8,128)(2,1)} %dynamic-slice_bitcast_fusion.10), channel_id=1, source_target_pairs={{0,16},{2,18},{4,20},{6,22},{8,24},{10,26},{12,28},{14,30},{16,0},... | collective-permute-start | bytes 884744 | tf_op jit(solution)/shard_map/ppermute | solution.py:42
  539.1 13.9 %all-to-all-start.6 = ((f32[16,1,320]{2,1,0:T(1,128)}), f32[16,1,320]{2,1,0:T(1,128)S(1)}, u32[]{:S(2)}, u32[]{:S(2)}) async-start(f32[16,1,320]{2,1,0:T(1,128)} %pad_maximum_fusion.25), calls=%async_computation.6 | async-start | bytes 49152 | tf_op jit(solution)/shard_map/all_to_all | solution.py:1043
  (89 other events, 653.4 us)
Sparse Core Ops, SparseCore 0:
  18.6 71.5 all-gather.5
  135.1 79.4 all-gather.3

commit v6 on v4

--- a/solution.py
+++ b/solution.py
@@ -14,7 +14,7 @@
 EPSILON = 1e-06
 ROPE_BASE = 1000000.0
 ORDERS = ((0, 1, 2), (1, 2, 0), (2, 0, 1))
-CHUNK = 256
+CHUNK = 512
 NEVER = -1e30
 SCALE = 1.0 / math.sqrt(HD)
 bf16 = jnp.bfloat16

time: 563 us -> 563 us (level)
  transfers between devices with their start and end apart: 80 -> 80, of which waited for: 32 -> 31; matrix products, arithmetic and copies ran while one was open for 18% -> 18% of each run, Pallas kernels for 11% -> 12%
where the time goes in v6:
time: 563 us; the launch traced here: 553 us
  waiting for transfers between devices  204 us (36%)
  starting transfers between devices  116 us (21%)
  Pallas kernels  93 us (17%)
  other arithmetic  63.3 us (11%)
  local copies, waits for them, and re-layouts  51.2 us (9%)
  between operations  15.7 us (3%)
  matrix products  10.6 us (2%)
    ppermute x54, waiting for transfers between devices, chip_swap(): return lax.ppermute(x, 'ctx', [(i, i ^ flip) for i in range(count)])  168 us
    ppermute x54, starting transfers between devices, chip_swap(): return lax.ppermute(x, 'ctx', [(i, i ^ flip) for i in range(count)])  78.8 us
    pallas_call x1, Pallas kernels, mlp(): pl.pallas_call(functools.partial(mlp_kernel, loads, groups), grid=(rows /...  27.8 us
    all_to_all x4, waiting for transfers between devices, group_exchange(): lax.all_to_all(x, 'ctx', split_axis=0, concat_axis=0, tiled=True, axis_in...  22.5 us
    all_to_all x4, starting transfers between devices, group_exchange(): lax.all_to_all(x, 'ctx', split_axis=0, concat_axis=0, tiled=True, axis_in...  21 us
    convert_element_type x17, other arithmetic, add(): self.parts = [x.astype(bf16) for x in self.parts]  20.5 us
    pallas_call x2, Pallas kernels, gate_up_grads(): pl.pallas_call(functools.partial(gate_up_grads_kernel, rows_dev), grid=(w...  16.8 us
    unnamed x148, local copies, waits for them, and re-layouts  15.3 us
  transfers between devices with their start and end apart: 80, of which 31 were waited for; matrix products, arithmetic and copies ran while one was open for 18% of the time, Pallas kernels for 12%

profile of v6, /device:TPU:0, one launch (start us, length us, event | category | flops | bytes accessed | tf_op | source)
XLA Modules:
  0.0 553.4 jit_solution(2012259876521323639)
XLA Ops:
  7.2 3.0 collective-permute-start.5
  15.2 2.6 collective-permute-start.4
  18.5 3.1 pack_members.1
  21.5 9.8 %collective-permute-done.4 = bf16[1,2,64,1024]{3,2,1,0:T(8,128)(2,1)S(1)} collective-permute-done((bf16[1,2,64,1024]{3,2,1,0:T(8,128)(2,1)S(1)}, bf16[1,2,64,1024]{3,2,1,0:T(8,128)(2,1)S(1)}, u32[]{:S(2)}, u32[]{:S(2)}) %collective-permute-start.4) | collective-permute-done | bytes 262176 | tf_op jit(solution)/shard_map/ppermute | solution.py:42
  34.0 2.7 collective-permute-done.9
  40.5 9.1 %collective-permute-done.12 = bf16[2,2,64,256]{3,2,1,0:T(8,128)(2,1)S(1)} collective-permute-done((bf16[2,2,64,256]{3,2,1,0:T(8,128)(2,1)S(1)}, bf16[2,2,64,256]{3,2,1,0:T(8,128)(2,1)S(1)}, u32[]{:S(2)}, u32[]{:S(2)}) %collective-permute-start.12) | collective-permute-done | bytes 131104 | tf_op jit(solution)/shard_map/ppermute | solution.py:42
  54.6 4.4 collective-permute-done.13
  62.6 17.6 %collective-permute-done.14.refs_5_ = bf16[8,2,64,256]{3,2,1,0:T(8,128)(2,1)} collective-permute-done((bf16[8,2,64,256]{3,2,1,0:T(8,128)(2,1)}, bf16[8,2,64,256]{3,2,1,0:T(8,128)(2,1)}, u32[]{:S(2)}, u32[]{:S(2)}) %collective-permute-start.14) | collective-permute-done | bytes 524320 | tf_op jit(solution)/shard_map/ppermute | solution.py:42
  81.0 7.0 %all-to-all-start = ((bf16[8,16,2304]{2,1,0:T(8,128)(2,1)}), bf16[8,16,2304]{2,1,0:T(8,128)(2,1)}, u32[]{:S(2)}, u32[]{:S(2)}) async-start(bf16[8,16,2304]{2,1,0:T(8,128)(2,1)} %slice.162), calls=%async_computation | async-start | bytes 1179648 | tf_op jit(solution)/shard_map/all_to_all | solution.py:71
  89.8 4.8 order_project.1
  94.6 3.0 collective-permute-start.15
  97.6 3.2 collective-permute-done.15
  101.7 3.5 collective-permute-start.19
  120.8 3.4 order_rows.1
  126.9 4.7 all-to-all-start.1
  135.0 10.1 %attend.1 = (bf16[2,2048,256]{2,1,0:T(8,128)(2,1)}, f32[2,2,384,128]{3,2,1,0:T(8,128)}, bf16[2,128,768]{2,1,0:T(8,128)(2,1)}, f32[2,2,384,1]{3,2,1,0:T(8,128)}, f32[2,128,1536]{2,1,0:T(8,128)}) custom-call(s32[2]{0:T(128)} %pad_add_fusion.2.where_ref, s32[8]{0:T(128)} %reshape.402.range_ref, bf16[2,6,128,128]{3,2,1,0:T(8,128)(2,1)} %get-tuple-element.133.queries, ...), custom_call_target="tpu_custom_call" | custom-call | tf_op jit(solution)/shard_map/attend/pallas_call | solution.py:639
  148.8 22.5 %all-to-all-done.1 = bf16[8,32,2304]{2,1,0:T(8,128)(2,1)S(1)} async-done(((bf16[8,32,2304]{2,1,0:T(8,128)(2,1)}), bf16[8,32,2304]{2,1,0:T(8,128)(2,1)S(1)}, u32[]{:S(2)}, u32[]{:S(2)}) %all-to-all-start.1) | async-done | bytes 1179680 | tf_op jit(solution)/shard_map/all_to_all | solution.py:71
  177.5 34.7 %collective-permute-done.28 = bf16[1,128,1536]{2,1,0:T(8,128)(2,1)S(1)} collective-permute-done((bf16[1,128,1536]{2,1,0:T(8,128)(2,1)S(1)}, bf16[1,128,1536]{2,1,0:T(8,128)(2,1)S(1)}, u32[]{:S(2)}, u32[]{:S(2)}) %collective-permute-start.28) | collective-permute-done | bytes 393248 | tf_op jit(solution)/shard_map/ppermute | solution.py:42
  212.4 5.4 collective-permute-start.31
  219.2 6.5 %collective-permute-done.31 = bf16[2,64,1536]{2,1,0:T(8,128)(2,1)S(1)} collective-permute-done((bf16[2,64,1536]{2,1,0:T(8,128)(2,1)S(1)}, bf16[2,64,1536]{2,1,0:T(8,128)(2,1)S(1)}, u32[]{:S(2)}, u32[]{:S(2)}) %collective-permute-start.31) | collective-permute-done | bytes 393248 | tf_op jit(solution)/shard_map/ppermute | solution.py:42
  229.6 11.5 %collective-permute-done.34.refs_4_ = bf16[4,48,2304]{2,1,0:T(8,128)(2,1)} collective-permute-done((bf16[4,48,2304]{2,1,0:T(8,128)(2,1)}, bf16[4,48,2304]{2,1,0:T(8,128)(2,1)}, u32[]{:S(2)}, u32[]{:S(2)}) %collective-permute-start.34) | collective-permute-done | bytes 884768 | tf_op jit(solution)/shard_map/ppermute | solution.py:42
  241.1 5.4 collective-permute-done.32.refs_1_
  248.5 3.7 order_tokens.1
  252.2 27.8 %mlp.1 = (bf16[1024,2304]{1,0:T(8,128)(2,1)}, bf16[1024,1120]{1,0:T(8,128)(2,1)}, bf16[1024,1536]{1,0:T(8,128)(2,1)}) custom-call(s32[2]{0:T(128)} %pad_add_fusion.2.where_ref, bf16[1024,1536]{1,0:T(8,128)(2,1)} %bitcast.305, bf16[1024,1536]{1,0:T(8,128)(2,1)} %all-gather.4.cloned.1.call-done.out_grad, bf16[1120,1536]{1,0:T(8,128)(2,1)} %bitcast.314, ...), custom_call_target="tpu_custom_call" | custom-call | tf_op jit(solution)/shard_map/mlp/pallas_call | solution.py:371
  286.5 8.2 %gate_up_grads.2 = (bf16[16,48,1152]{2,1,0:T(8,128)(2,1)}, bf16[16,48,1152]{2,1,0:T(8,128)(2,1)}) custom-call(s32[2]{0:T(128)} %pad_add_fusion.2.where_ref, bf16[1024,1536]{1,0:T(8,128)(2,1)} %bitcast.306, bf16[1024,2304]{1,0:T(8,128)(2,1)} %get-tuple-element.183.pre_grad), custom_call_target="tpu_custom_call" | custom-call | tf_op jit(solution)/shard_map/gate_up_grads/pallas_call | solution.py:408
  294.8 6.2 %convolution_convert_fusion = bf16[1024,1536]{1,0:T(8,128)(2,1)S(1)} fusion(bf16[1024,1120]{1,0:T(8,128)(2,1)} %get-tuple-element.202.activated, bf16[1120,1536]{1,0:T(8,128)(2,1)S(1)} %bitcast.315), kind=kOutput, calls=%fused_computation.1 | convolution fusion | flops 3524788224 | bytes 8880128 | tf_op jit(solution)/shard_map/dot_general | solution.py:166
  301.0 4.7 collective-permute-done.39
  317.4 3.2 collective-permute-done.42
  320.7 4.5 collective-permute-done.41
  328.4 8.6 %gate_up_grads.3 = (bf16[16,48,1152]{2,1,0:T(8,128)(2,1)}, bf16[16,48,1152]{2,1,0:T(8,128)(2,1)}) custom-call(s32[2]{0:T(128)} %pad_add_fusion.2.where_ref, bf16[1024,1536]{1,0:T(8,128)(2,1)} %bitcast.307, bf16[1024,2304]{1,0:T(8,128)(2,1)} %get-tuple-element.183.pre_grad), custom_call_target="tpu_custom_call" | custom-call | tf_op jit(solution)/shard_map/gate_up_grads/pallas_call | solution.py:408
  342.0 8.1 %collective-permute-done.45 = bf16[8,1,48,1152]{3,2,0,1:T(8,128)(2,1)S(1)} collective-permute-done((bf16[8,1,48,1152]{3,2,0,1:T(8,128)(2,1)S(1)}, bf16[8,1,48,1152]{3,2,0,1:T(8,128)(2,1)S(1)}, u32[]{:S(2)}, u32[]{:S(2)}) %collective-permute-start.45) | collective-permute-done | bytes 884768 | tf_op jit(solution)/shard_map/ppermute | solution.py:42
  353.8 5.0 all-to-all-start.2
  361.6 12.3 %attend_back.1 = (bf16[2,128,768]{2,1,0:T(8,128)(2,1)}, bf16[8,2,2,128,256]{4,3,2,1,0:T(8,128)(2,1)}) custom-call(s32[8]{0:T(128)} %reshape.402.range_ref, bf16[128,1536]{1,0:T(8,128)(2,1)} %copy-done.8, bf16[128,1536]{1,0:T(8,128)(2,1)} %copy-done.33, bf16[1536,768]{1,0:T(8,128)(2,1)} %bitcast.317, bf16[2,6,128,128]{3,2,1,0:T(8,128)(2,1)} %get-tuple-element.133.queries, ...), custom_call_target="tpu_custom_call" | custom-call | tf_op jit(solution)/shard_map/attend_back/pallas_call | solution.py:736
  373.9 9.0 %collective-permute-done.50 = bf16[8,1,48,1152]{3,2,0,1:T(8,128)(2,1)S(1)} collective-permute-done((bf16[8,1,48,1152]{3,2,0,1:T(8,128)(2,1)S(1)}, bf16[8,1,48,1152]{3,2,0,1:T(8,128)(2,1)S(1)}, u32[]{:S(2)}, u32[]{:S(2)}) %collective-permute-start.50) | collective-permute-done | bytes 884768 | tf_op jit(solution)/shard_map/ppermute | solution.py:42
  385.0 4.5 all-to-all-start.3
  405.1 7.5 %down_grads.1 = (bf16[2,280,1536]{2,1,0:T(8,128)(2,1)}, bf16[2,280,1536]{2,1,0:T(8,128)(2,1)}) custom-call(s32[2]{0:T(128)} %pad_add_fusion.2.where_ref, bf16[1024,1120]{1,0:T(8,128)(2,1)} %get-tuple-element.202.activated, bf16[1024,1536]{1,0:T(8,128)(2,1)} %all-gather.4.cloned.1.call-done.out_grad), custom_call_target="tpu_custom_call" | custom-call | tf_op jit(solution)/shard_map/down_grads/pallas_call | solution.py:439
  412.5 18.2 %collective-permute-done.53 = bf16[2,2,2,2,48,512]{5,4,3,0,1,2:T(8,128)(2,1)} collective-permute-done((bf16[2,2,2,2,48,512]{5,4,3,0,1,2:T(8,128)(2,1)}, bf16[2,2,2,2,48,512]{5,4,3,0,1,2:T(8,128)(2,1)}, u32[]{:S(2)}, u32[]{:S(2)}) %collective-permute-start.53) | collective-permute-done | bytes 786464 | tf_op jit(solution)/shard_map/ppermute | solution.py:42
  431.5 2.7 reduce_sum.113
  445.7 4.2 all-to-all-start.4
  449.9 2.6 fusion.4
  470.5 3.1 add_convert_fusion.2
  478.1 2.8 collective-permute-start.65
  488.6 4.4 all-to-all-start.5
  496.6 3.6 unpack_members.1
  511.1 3.8 collective-permute-done.60
  523.5 4.0 all-to-all-start.6
  529.5 8.8 %all-to-all-done.6 = f32[16,1,320]{2,1,0:T(1,128)S(1)} async-done(((f32[16,1,320]{2,1,0:T(1,128)}), f32[16,1,320]{2,1,0:T(1,128)S(1)}, u32[]{:S(2)}, u32[]{:S(2)}) %all-to-all-start.6) | async-done | bytes 20512 | tf_op jit(solution)/shard_map/all_to_all | solution.py:1045
  543.6 2.7 add_bitcast_fusion
  (444 shorter events, 185.5 us)
Async XLA Ops:
  7.2 124.5 %all-gather.6.cloned.1.call-start = ((), (), s32[]{:S(2)}) async-start(), calls=%async_computation.8 | async-start | bytes 2506752 | tf_op jit(solution)/shard_map/all_gather | solution.py:803
  7.2 24.1 %collective-permute-start.5 = (bf16[280,1536]{1,0:T(8,128)(2,1)}, bf16[280,1536]{1,0:T(8,128)(2,1)S(1)}, u32[]{:S(2)}, u32[]{:S(2)}) collective-permute-start(bf16[280,1536]{1,0:T(8,128)(2,1)} %param.21), channel_id=1, source_target_pairs={{0,2},{2,0},{4,6},{6,4},{8,10},{10,8},{12,14},{14,12},{16,18},{18,... | collective-permute-start | bytes 2580488 | tf_op jit(solution)/shard_map/ppermute | solution.py:42
  15.2 16.2 %collective-permute-start.4 = (bf16[1,2,64,1024]{3,2,1,0:T(8,128)(2,1)S(1)}, bf16[1,2,64,1024]{3,2,1,0:T(8,128)(2,1)S(1)}, u32[]{:S(2)}, u32[]{:S(2)}) collective-permute-start(bf16[1,2,64,1024]{3,2,1,0:T(8,128)(2,1)S(1)} %maximum_bitcast_fusion), channel_id=1, source_target_pairs={{0,16},{2,18},{4,20},{6,22},{8,24},{10,26},{12,28},{14,30},{16,0},... | collective-permute-start | bytes 786440 | tf_op jit(solution)/shard_map/ppermute | solution.py:42
  49.9 30.3 %collective-permute-start.11 = (bf16[8,2,48,384]{3,2,1,0:T(8,128)(2,1)S(1)}, bf16[8,2,48,384]{3,2,1,0:T(8,128)(2,1)}, u32[]{:S(2)}, u32[]{:S(2)}) collective-permute-start(bf16[8,2,48,384]{3,2,1,0:T(8,128)(2,1)S(1)} %pad_maximum_fusion.5.refs_2_), channel_id=1, source_target_pairs={{0,2},{2,0},{4,6},{6,4},{8,10},{10,8},{12,14},{14,12},{16,18},{18,... | collective-permute-start | bytes 1769480 | tf_op jit(solution)/shard_map/ppermute | solution.py:42
  52.0 28.1 %collective-permute-start.8 = (bf16[8,2,48,384]{3,2,1,0:T(8,128)(2,1)S(1)}, bf16[8,2,48,384]{3,2,1,0:T(8,128)(2,1)}, u32[]{:S(2)}, u32[]{:S(2)}) collective-permute-start(bf16[8,2,48,384]{3,2,1,0:T(8,128)(2,1)S(1)} %pad_maximum_fusion.4.refs_0_), channel_id=1, source_target_pairs={{0,8},{2,10},{4,12},{6,14},{8,0},{10,2},{12,4},{14,6},{16,24},{18,... | collective-permute-start | bytes 1769480 | tf_op jit(solution)/shard_map/ppermute | solution.py:42
  59.9 20.3 %collective-permute-start.14 = (bf16[8,2,64,256]{3,2,1,0:T(8,128)(2,1)}, bf16[8,2,64,256]{3,2,1,0:T(8,128)(2,1)}, u32[]{:S(2)}, u32[]{:S(2)}) collective-permute-start(bf16[8,2,64,256]{3,2,1,0:T(8,128)(2,1)} %pad_maximum_fusion.8.refs_4_), channel_id=1, source_target_pairs={{0,4},{2,6},{4,0},{6,2},{8,12},{10,14},{12,8},{14,10},{16,20},{18,... | collective-permute-start | bytes 1572872 | tf_op jit(solution)/shard_map/ppermute | solution.py:42
  61.5 26.6 %collective-permute-start = (s32[4]{0:T(128)S(1)}, s32[4]{0:T(128)S(1)}, u32[]{:S(2)}, u32[]{:S(2)}) collective-permute-start(s32[4]{0:T(128)S(1)} %bitcast.349), channel_id=1, source_target_pairs={{0,1},{1,0},{2,3},{3,2},{4,5},{5,4},{6,7},{7,6},{8,9},{9,8},{10,11... | collective-permute-start | bytes 56 | tf_op jit(solution)/shard_map/ppermute | solution.py:37
  61.5 28.3 %collective-permute-start.1 = (bf16[128,1536]{1,0:T(8,128)(2,1)S(1)}, bf16[128,1536]{1,0:T(8,128)(2,1)}, u32[]{:S(2)}, u32[]{:S(2)}) collective-permute-start(bf16[128,1536]{1,0:T(8,128)(2,1)S(1)} %bitcast.323), channel_id=1, source_target_pairs={{0,1},{1,0},{2,3},{3,2},{4,5},{5,4},{6,7},{7,6},{8,9},{9,8},{10,11... | collective-permute-start | bytes 1179656 | tf_op jit(solution)/shard_map/ppermute | solution.py:37
  81.0 20.7 %all-to-all-start = ((bf16[8,16,2304]{2,1,0:T(8,128)(2,1)}), bf16[8,16,2304]{2,1,0:T(8,128)(2,1)}, u32[]{:S(2)}, u32[]{:S(2)}) async-start(bf16[8,16,2304]{2,1,0:T(8,128)(2,1)} %slice.162), calls=%async_computation | async-start | bytes 1179648 | tf_op jit(solution)/shard_map/all_to_all | solution.py:71
  105.2 14.4 %collective-permute-start.25 = (bf16[280,1536]{1,0:T(8,128)(2,1)}, bf16[280,1536]{1,0:T(8,128)(2,1)S(1)}, u32[]{:S(2)}, u32[]{:S(2)}) collective-permute-start(bf16[280,1536]{1,0:T(8,128)(2,1)} %param.21), channel_id=1, source_target_pairs={{0,1},{1,0},{2,3},{3,2},{4,5},{5,4},{6,7},{7,6},{8,9},{9,8},{10,11... | collective-permute-start | bytes 2580488 | tf_op jit(solution)/shard_map/ppermute | solution.py:37
  105.2 14.4 %collective-permute-start.26 = (bf16[280,1536]{1,0:T(8,128)(2,1)}, bf16[280,1536]{1,0:T(8,128)(2,1)S(1)}, u32[]{:S(2)}, u32[]{:S(2)}) collective-permute-start(bf16[280,1536]{1,0:T(8,128)(2,1)} %copy-done.47), channel_id=1, source_target_pairs={{0,1},{1,0},{2,3},{3,2},{4,5},{5,4},{6,7},{7,6},{8,9},{9,8},{10,11... | collective-permute-start | bytes 2580488 | tf_op jit(solution)/shard_map/ppermute | solution.py:37
  126.9 44.4 %all-to-all-start.1 = ((bf16[8,32,2304]{2,1,0:T(8,128)(2,1)}), bf16[8,32,2304]{2,1,0:T(8,128)(2,1)S(1)}, u32[]{:S(2)}, u32[]{:S(2)}) async-start(bf16[8,32,2304]{2,1,0:T(8,128)(2,1)} %slice.166), calls=%async_computation.1 | async-start | bytes 2359296 | tf_op jit(solution)/shard_map/all_to_all | solution.py:71
  131.7 96.5 %all-gather.4.cloned.1.call-start = ((), (), s32[]{:S(2)}) async-start(), calls=%async_computation.7 | async-start | bytes 3538944 | tf_op jit(solution)/shard_map/all_gather | solution.py:804
  172.6 39.7 %collective-permute-start.29 = (bf16[4,48,2304]{2,1,0:T(8,128)(2,1)S(1)}, bf16[4,48,2304]{2,1,0:T(8,128)(2,1)S(1)}, u32[]{:S(2)}, u32[]{:S(2)}) collective-permute-start(bf16[4,48,2304]{2,1,0:T(8,128)(2,1)S(1)} %slice.203), channel_id=1, source_target_pairs={{0,2},{2,0},{4,6},{6,4},{8,10},{10,8},{12,14},{14,12},{16,18},{18,... | collective-permute-start | bytes 2654216 | tf_op jit(solution)/shard_map/ppermute | solution.py:42
  177.4 34.8 %collective-permute-start.28 = (bf16[1,128,1536]{2,1,0:T(8,128)(2,1)S(1)}, bf16[1,128,1536]{2,1,0:T(8,128)(2,1)S(1)}, u32[]{:S(2)}, u32[]{:S(2)}) collective-permute-start(bf16[1,128,1536]{2,1,0:T(8,128)(2,1)S(1)} %fusion.34), channel_id=1, source_target_pairs={{0,16},{2,18},{4,20},{6,22},{8,24},{10,26},{12,28},{14,30},{16,0},... | collective-permute-start | bytes 1179656 | tf_op jit(solution)/shard_map/ppermute | solution.py:42
  217.7 34.5 %collective-permute-start.35 = (bf16[8,48,2304]{2,1,0:T(8,128)(2,1)S(1)}, bf16[8,48,2304]{2,1,0:T(8,128)(2,1)}, u32[]{:S(2)}, u32[]{:S(2)}) collective-permute-start(bf16[8,48,2304]{2,1,0:T(8,128)(2,1)S(1)} %constant_dynamic-update-slice_fusion.refs_0_), channel_id=1, source_target_pairs={{0,1},{1,0},{2,3},{3,2},{4,5},{5,4},{6,7},{7,6},{8,9},{9,8},{10,11... | collective-permute-start | bytes 5308424 | tf_op jit(solution)/shard_map/ppermute | solution.py:37
  218.7 22.4 %collective-permute-start.34 = (bf16[4,48,2304]{2,1,0:T(8,128)(2,1)}, bf16[4,48,2304]{2,1,0:T(8,128)(2,1)}, u32[]{:S(2)}, u32[]{:S(2)}) collective-permute-start(bf16[4,48,2304]{2,1,0:T(8,128)(2,1)} %slice.173), channel_id=1, source_target_pairs={{0,2},{2,0},{4,6},{6,4},{8,10},{10,8},{12,14},{14,12},{16,18},{18,... | collective-permute-start | bytes 2654216 | tf_op jit(solution)/shard_map/ppermute | solution.py:42
  228.2 18.3 %collective-permute-start.32 = (bf16[4,64,1536]{2,1,0:T(8,128)(2,1)}, bf16[4,64,1536]{2,1,0:T(8,128)(2,1)}, u32[]{:S(2)}, u32[]{:S(2)}) collective-permute-start(bf16[4,64,1536]{2,1,0:T(8,128)(2,1)} %pad_maximum_fusion.1.refs_0_), channel_id=1, source_target_pairs={{0,4},{2,6},{4,0},{6,2},{8,12},{10,14},{12,8},{14,10},{16,20},{18,... | collective-permute-start | bytes 2359304 | tf_op jit(solution)/shard_map/ppermute | solution.py:42
  229.6 18.4 %collective-permute-start.33 = (bf16[4,64,1536]{2,1,0:T(8,128)(2,1)}, bf16[4,64,1536]{2,1,0:T(8,128)(2,1)}, u32[]{:S(2)}, u32[]{:S(2)}) collective-permute-start(bf16[4,64,1536]{2,1,0:T(8,128)(2,1)} %pad_maximum_fusion.2.refs_2_), channel_id=1, source_target_pairs={{0,8},{2,10},{4,12},{6,14},{8,0},{10,2},{12,4},{14,6},{16,24},{18,... | collective-permute-start | bytes 2359304 | tf_op jit(solution)/shard_map/ppermute | solution.py:42
  286.0 19.8 %collective-permute-start.39 = (bf16[2,2,64,1536]{3,2,0,1:T(8,128)(2,1)}, bf16[2,2,64,1536]{3,2,0,1:T(8,128)(2,1)}, u32[]{:S(2)}, u32[]{:S(2)}) collective-permute-start(bf16[2,2,64,1536]{3,2,0,1:T(8,128)(2,1)} %bitcast.302), channel_id=1, source_target_pairs={{0,8},{2,10},{4,12},{6,14},{8,0},{10,2},{12,4},{14,6},{16,24},{18,... | collective-permute-start | bytes 2359304 | tf_op jit(solution)/shard_map/ppermute | solution.py:42
  286.3 20.8 %collective-permute-start.38 = (bf16[2,2,64,1536]{3,2,0,1:T(8,128)(2,1)}, bf16[2,2,64,1536]{3,2,0,1:T(8,128)(2,1)}, u32[]{:S(2)}, u32[]{:S(2)}) collective-permute-start(bf16[2,2,64,1536]{3,2,0,1:T(8,128)(2,1)} %bitcast.303), channel_id=1, source_target_pairs={{0,4},{2,6},{4,0},{6,2},{8,12},{10,14},{12,8},{14,10},{16,20},{18,... | collective-permute-start | bytes 2359304 | tf_op jit(solution)/shard_map/ppermute | solution.py:42
  294.8 13.7 %collective-permute-start.40 = (bf16[16,48,1152]{2,1,0:T(8,128)(2,1)}, bf16[16,48,1152]{2,1,0:T(8,128)(2,1)S(1)}, u32[]{:S(2)}, u32[]{:S(2)}) collective-permute-start(bf16[16,48,1152]{2,1,0:T(8,128)(2,1)} %get-tuple-element.172), channel_id=1, source_target_pairs={{0,1},{1,0},{2,3},{3,2},{4,5},{5,4},{6,7},{7,6},{8,9},{9,8},{10,11... | collective-permute-start | bytes 5308424 | tf_op jit(solution)/shard_map/ppermute | solution.py:37
  308.9 16.3 %collective-permute-start.41 = (bf16[2,64,1536]{2,1,0:T(8,128)(2,1)S(1)}, bf16[2,64,1536]{2,1,0:T(8,128)(2,1)S(1)}, u32[]{:S(2)}, u32[]{:S(2)}) collective-permute-start(bf16[2,64,1536]{2,1,0:T(8,128)(2,1)S(1)} %dynamic-slice_bitcast_fusion.8), channel_id=1, source_target_pairs={{0,8},{2,10},{4,12},{6,14},{8,0},{10,2},{12,4},{14,6},{16,24},{18,... | collective-permute-start | bytes 1179656 | tf_op jit(solution)/shard_map/ppermute | solution.py:42
  311.5 47.3 %collective-permute-start.48 = (bf16[2,2,64,1536]{3,2,0,1:T(8,128)(2,1)}, bf16[2,2,64,1536]{3,2,0,1:T(8,128)(2,1)}, u32[]{:S(2)}, u32[]{:S(2)}) collective-permute-start(bf16[2,2,64,1536]{3,2,0,1:T(8,128)(2,1)} %bitcast.301), channel_id=1, source_target_pairs={{0,4},{2,6},{4,0},{6,2},{8,12},{10,14},{12,8},{14,10},{16,20},{18,... | collective-permute-start | bytes 2359304 | tf_op jit(solution)/shard_map/ppermute | solution.py:42
  315.2 43.5 %collective-permute-start.49 = (bf16[2,2,64,1536]{3,2,0,1:T(8,128)(2,1)}, bf16[2,2,64,1536]{3,2,0,1:T(8,128)(2,1)}, u32[]{:S(2)}, u32[]{:S(2)}) collective-permute-start(bf16[2,2,64,1536]{3,2,0,1:T(8,128)(2,1)} %bitcast.300), channel_id=1, source_target_pairs={{0,8},{2,10},{4,12},{6,14},{8,0},{10,2},{12,4},{14,6},{16,24},{18,... | collective-permute-start | bytes 2359304 | tf_op jit(solution)/shard_map/ppermute | solution.py:42
  325.3 14.0 %collective-permute-start.44 = (bf16[64,1536]{1,0:T(8,128)(2,1)S(1)}, bf16[64,1536]{1,0:T(8,128)(2,1)S(1)}, u32[]{:S(2)}, u32[]{:S(2)}) collective-permute-start(bf16[64,1536]{1,0:T(8,128)(2,1)S(1)} %dynamic-slice_bitcast_fusion.14), channel_id=1, source_target_pairs={{0,16},{2,18},{4,20},{6,22},{8,24},{10,26},{12,28},{14,30},{16,0},... | collective-permute-start | bytes 589832 | tf_op jit(solution)/shard_map/ppermute | solution.py:42
  326.2 15.7 %collective-permute-start.43 = (bf16[64,1536]{1,0:T(8,128)(2,1)S(1)}, bf16[64,1536]{1,0:T(8,128)(2,1)S(1)}, u32[]{:S(2)}, u32[]{:S(2)}) collective-permute-start(bf16[64,1536]{1,0:T(8,128)(2,1)S(1)} %dynamic-slice_bitcast_fusion.15), channel_id=1, source_target_pairs={{0,16},{2,18},{4,20},{6,22},{8,24},{10,26},{12,28},{14,30},{16,0},... | collective-permute-start | bytes 589832 | tf_op jit(solution)/shard_map/ppermute | solution.py:42
  353.8 30.3 %all-to-all-start.2 = ((bf16[8,48,1152]{2,1,0:T(8,128)(2,1)}), bf16[8,48,1152]{2,1,0:T(8,128)(2,1)S(1)}, u32[]{:S(2)}, u32[]{:S(2)}) async-start(bf16[8,48,1152]{2,1,0:T(8,128)(2,1)} %fusion.9), calls=%async_computation.2 | async-start | bytes 1769472 | tf_op jit(solution)/shard_map/all_to_all | solution.py:71
  361.5 21.4 %collective-permute-start.50 = (bf16[8,1,48,1152]{3,2,0,1:T(8,128)(2,1)S(1)}, bf16[8,1,48,1152]{3,2,0,1:T(8,128)(2,1)S(1)}, u32[]{:S(2)}, u32[]{:S(2)}) collective-permute-start(bf16[8,1,48,1152]{3,2,0,1:T(8,128)(2,1)S(1)} %dynamic-slice_bitcast_fusion), channel_id=1, source_target_pairs={{0,2},{2,0},{4,6},{6,4},{8,10},{10,8},{12,14},{14,12},{16,18},{18,... | collective-permute-start | bytes 2654216 | tf_op jit(solution)/shard_map/ppermute | solution.py:42
  385.0 46.4 %all-to-all-start.3 = ((bf16[8,2,2,128,256]{4,3,2,1,0:T(8,128)(2,1)}), bf16[8,2,2,128,256]{4,3,2,1,0:T(8,128)(2,1)}, u32[]{:S(2)}, u32[]{:S(2)}) async-start(bf16[8,2,2,128,256]{4,3,2,1,0:T(8,128)(2,1)} %get-tuple-element.199), calls=%async_computation.3 | async-start | bytes 4194304 | tf_op jit(solution)/shard_map/all_to_all | solution.py:51
  393.8 36.9 %collective-permute-start.53 = (bf16[2,2,2,2,48,512]{5,4,3,0,1,2:T(8,128)(2,1)}, bf16[2,2,2,2,48,512]{5,4,3,0,1,2:T(8,128)(2,1)}, u32[]{:S(2)}, u32[]{:S(2)}) collective-permute-start(bf16[2,2,2,2,48,512]{5,4,3,0,1,2:T(8,128)(2,1)} %bitcast.298), channel_id=1, source_target_pairs={{0,8},{2,10},{4,12},{6,14},{8,0},{10,2},{12,4},{14,6},{16,24},{18,... | collective-permute-start | bytes 2359304 | tf_op jit(solution)/shard_map/ppermute | solution.py:42
  398.3 33.2 %collective-permute-start.52 = (bf16[2,2,2,2,48,512]{5,4,3,2,1,0:T(8,128)(2,1)}, bf16[2,2,2,2,48,512]{5,4,3,2,1,0:T(8,128)(2,1)}, u32[]{:S(2)}, u32[]{:S(2)}) collective-permute-start(bf16[2,2,2,2,48,512]{5,4,3,2,1,0:T(8,128)(2,1)} %fusion.14), channel_id=1, source_target_pairs={{0,4},{2,6},{4,0},{6,2},{8,12},{10,14},{12,8},{14,10},{16,20},{18,... | collective-permute-start | bytes 2359304 | tf_op jit(solution)/shard_map/ppermute | solution.py:42
  401.7 29.7 %collective-permute-start.51 = (bf16[2,2,2,2,48,512]{5,4,3,0,1,2:T(8,128)(2,1)}, bf16[2,2,2,2,48,512]{5,4,3,0,1,2:T(8,128)(2,1)}, u32[]{:S(2)}, u32[]{:S(2)}) collective-permute-start(bf16[2,2,2,2,48,512]{5,4,3,0,1,2:T(8,128)(2,1)} %bitcast.299), channel_id=1, source_target_pairs={{0,2},{2,0},{4,6},{6,4},{8,10},{10,8},{12,14},{14,12},{16,18},{18,... | collective-permute-start | bytes 2359304 | tf_op jit(solution)/shard_map/ppermute | solution.py:42
  435.8 21.5 %collective-permute-start.54 = (bf16[1,2,128,256]{3,2,1,0:T(8,128)(2,1)}, bf16[1,2,128,256]{3,2,1,0:T(8,128)(2,1)}, u32[]{:S(2)}, u32[]{:S(2)}) collective-permute-start(bf16[1,2,128,256]{3,2,1,0:T(8,128)(2,1)} %constant_dynamic-slice_fusion.10), channel_id=1, source_target_pairs={{0,16},{2,18},{4,20},{6,22},{8,24},{10,26},{12,28},{14,30},{16,0},... | collective-permute-start | bytes 393224 | tf_op jit(solution)/shard_map/ppermute | solution.py:42
  437.9 32.6 %collective-permute-start.57 = (bf16[2,280,1536]{2,1,0:T(8,128)(2,1)}, bf16[2,280,1536]{2,1,0:T(8,128)(2,1)}, u32[]{:S(2)}, u32[]{:S(2)}) collective-permute-start(bf16[2,280,1536]{2,1,0:T(8,128)(2,1)} %get-tuple-element.216), channel_id=1, source_target_pairs={{0,1},{1,0},{2,3},{3,2},{4,5},{5,4},{6,7},{7,6},{8,9},{9,8},{10,11... | collective-permute-start | bytes 5160968 | tf_op jit(solution)/shard_map/ppermute | solution.py:37
  440.3 26.2 %collective-permute-start.56 = (bf16[2,64,1536]{2,1,0:T(8,128)(2,1)}, bf16[2,64,1536]{2,1,0:T(8,128)(2,1)}, u32[]{:S(2)}, u32[]{:S(2)}) collective-permute-start(bf16[2,64,1536]{2,1,0:T(8,128)(2,1)} %dynamic-slice_bitcast_fusion.5), channel_id=1, source_target_pairs={{0,4},{2,6},{4,0},{6,2},{8,12},{10,14},{12,8},{14,10},{16,20},{18,... | collective-permute-start | bytes 1179656 | tf_op jit(solution)/shard_map/ppermute | solution.py:42
  444.8 23.6 %collective-permute-start.55 = (bf16[2,64,1536]{2,1,0:T(8,128)(2,1)}, bf16[2,64,1536]{2,1,0:T(8,128)(2,1)}, u32[]{:S(2)}, u32[]{:S(2)}) collective-permute-start(bf16[2,64,1536]{2,1,0:T(8,128)(2,1)} %dynamic-slice_bitcast_fusion.6), channel_id=1, source_target_pairs={{0,8},{2,10},{4,12},{6,14},{8,0},{10,2},{12,4},{14,6},{16,24},{18,... | collective-permute-start | bytes 1179656 | tf_op jit(solution)/shard_map/ppermute | solution.py:42
  445.7 28.0 %all-to-all-start.4 = ((bf16[8,48,1152]{2,1,0:T(8,128)(2,1)}), bf16[8,48,1152]{2,1,0:T(8,128)(2,1)}, u32[]{:S(2)}, u32[]{:S(2)}) async-start(bf16[8,48,1152]{2,1,0:T(8,128)(2,1)} %fusion.10), calls=%async_computation.4 | async-start | bytes 1769472 | tf_op jit(solution)/shard_map/all_to_all | solution.py:71
  478.1 31.0 %collective-permute-start.65 = (bf16[128,1536]{1,0:T(8,128)(2,1)}, bf16[128,1536]{1,0:T(8,128)(2,1)}, u32[]{:S(2)}, u32[]{:S(2)}) collective-permute-start(bf16[128,1536]{1,0:T(8,128)(2,1)} %dynamic-slice_bitcast_fusion.1), channel_id=1, source_target_pairs={{0,16},{2,18},{4,20},{6,22},{8,24},{10,26},{12,28},{14,30},{16,0},... | collective-permute-start | bytes 1179656 | tf_op jit(solution)/shard_map/ppermute | solution.py:42
  481.6 18.5 %collective-permute-start.59 = (bf16[2,2,2,48,512]{4,3,2,0,1:T(8,128)(2,1)}, bf16[2,2,2,48,512]{4,3,2,0,1:T(8,128)(2,1)}, u32[]{:S(2)}, u32[]{:S(2)}) collective-permute-start(bf16[2,2,2,48,512]{4,3,2,0,1:T(8,128)(2,1)} %dynamic-slice_bitcast_fusion.4), channel_id=1, source_target_pairs={{0,4},{2,6},{4,0},{6,2},{8,12},{10,14},{12,8},{14,10},{16,20},{18,... | collective-permute-start | bytes 1179656 | tf_op jit(solution)/shard_map/ppermute | solution.py:42
  483.9 19.5 %collective-permute-start.61 = (bf16[2,2,2,48,512]{4,3,2,1,0:T(8,128)(2,1)}, bf16[2,2,2,48,512]{4,3,2,1,0:T(8,128)(2,1)}, u32[]{:S(2)}, u32[]{:S(2)}) collective-permute-start(bf16[2,2,2,48,512]{4,3,2,1,0:T(8,128)(2,1)} %dynamic-slice_bitcast_fusion.3), channel_id=1, source_target_pairs={{0,8},{2,10},{4,12},{6,14},{8,0},{10,2},{12,4},{14,6},{16,24},{18,... | collective-permute-start | bytes 1179656 | tf_op jit(solution)/shard_map/ppermute | solution.py:42
  486.2 20.9 %collective-permute-start.63 = (bf16[2,2,2,48,512]{4,3,2,0,1:T(8,128)(2,1)}, bf16[2,2,2,48,512]{4,3,2,0,1:T(8,128)(2,1)}, u32[]{:S(2)}, u32[]{:S(2)}) collective-permute-start(bf16[2,2,2,48,512]{4,3,2,0,1:T(8,128)(2,1)} %dynamic-slice_bitcast_fusion.2), channel_id=1, source_target_pairs={{0,2},{2,0},{4,6},{6,4},{8,10},{10,8},{12,14},{14,12},{16,18},{18,... | collective-permute-start | bytes 1179656 | tf_op jit(solution)/shard_map/ppermute | solution.py:42
  488.6 26.5 %all-to-all-start.5 = ((bf16[8,2,2,48,256]{4,3,2,1,0:T(8,128)(2,1)}), bf16[8,2,2,48,256]{4,3,2,1,0:T(8,128)(2,1)}, u32[]{:S(2)}, u32[]{:S(2)}) async-start(bf16[8,2,2,48,256]{4,3,2,1,0:T(8,128)(2,1)} %bitcast.304), calls=%async_computation.5 | async-start | bytes 1572864 | tf_op jit(solution)/shard_map/all_to_all | solution.py:51
  501.4 13.5 %collective-permute-start.60 = (bf16[2,2,48,512]{3,2,1,0:T(8,128)(2,1)S(1)}, bf16[2,2,48,512]{3,2,1,0:T(8,128)(2,1)S(1)}, u32[]{:S(2)}, u32[]{:S(2)}) collective-permute-start(bf16[2,2,48,512]{3,2,1,0:T(8,128)(2,1)S(1)} %dynamic-slice_bitcast_fusion.13), channel_id=1, source_target_pairs={{0,8},{2,10},{4,12},{6,14},{8,0},{10,2},{12,4},{14,6},{16,24},{18,... | collective-permute-start | bytes 589832 | tf_op jit(solution)/shard_map/ppermute | solution.py:42
  516.1 27.5 %collective-permute-start.70 = (bf16[1,280,1536]{2,1,0:T(8,128)(2,1)}, bf16[1,280,1536]{2,1,0:T(8,128)(2,1)}, u32[]{:S(2)}, u32[]{:S(2)}) collective-permute-start(bf16[1,280,1536]{2,1,0:T(8,128)(2,1)} %constant_dynamic-slice_fusion), channel_id=1, source_target_pairs={{0,2},{2,0},{4,6},{6,4},{8,10},{10,8},{12,14},{14,12},{16,18},{18,... | collective-permute-start | bytes 2580488 | tf_op jit(solution)/shard_map/ppermute | solution.py:42
  520.5 17.9 %collective-permute-start.68 = (bf16[1,2,48,256]{3,2,1,0:T(8,128)(2,1)}, bf16[1,2,48,256]{3,2,1,0:T(8,128)(2,1)}, u32[]{:S(2)}, u32[]{:S(2)}) collective-permute-start(bf16[1,2,48,256]{3,2,1,0:T(8,128)(2,1)} %constant_dynamic-slice_fusion.4), channel_id=1, source_target_pairs={{0,16},{2,18},{4,20},{6,22},{8,24},{10,26},{12,28},{14,30},{16,0},... | collective-permute-start | bytes 147464 | tf_op jit(solution)/shard_map/ppermute | solution.py:42
  521.2 18.0 %collective-permute-start.67 = (bf16[2,48,1536]{2,1,0:T(8,128)(2,1)S(1)}, bf16[2,48,1536]{2,1,0:T(8,128)(2,1)}, u32[]{:S(2)}, u32[]{:S(2)}) collective-permute-start(bf16[2,48,1536]{2,1,0:T(8,128)(2,1)S(1)} %dynamic-slice_bitcast_fusion.10), channel_id=1, source_target_pairs={{0,16},{2,18},{4,20},{6,22},{8,24},{10,26},{12,28},{14,30},{16,0},... | collective-permute-start | bytes 884744 | tf_op jit(solution)/shard_map/ppermute | solution.py:42
  523.5 14.7 %all-to-all-start.6 = ((f32[16,1,320]{2,1,0:T(1,128)}), f32[16,1,320]{2,1,0:T(1,128)S(1)}, u32[]{:S(2)}, u32[]{:S(2)}) async-start(f32[16,1,320]{2,1,0:T(1,128)} %pad_maximum_fusion.25), calls=%async_computation.6 | async-start | bytes 49152 | tf_op jit(solution)/shard_map/all_to_all | solution.py:1045
  (99 other events, 734.4 us)
Sparse Core Ops, SparseCore 0:
  18.6 71.6 all-gather.5
  134.7 81.6 all-gather.3
